TPU v7x, 32 devices: a whole 2x2x4 slice. The times are simulated.
32 devices in a mesh: ha: 4 (over x, core), wa: 8 (over z, y).
Axes of the slice: x: 2, y: 2, z: 4, core: 2. Of those that a mesh axis runs over, the one named last changes fastest.
Arguments:
- tokens: bfloat16 [1, 8, 32, 16, 1152], P(None, None, 'ha', 'wa'), may hold values from -36 to 36
- cotangent: bfloat16 [1, 8, 32, 16, 1152], P(None, None, 'ha', 'wa'), may hold values from -6 to 6
- w_qkv: bfloat16 [3, 1152, 1728], P(None, 'wa'), may hold values from -0.1875 to 0.1875
- w_out: bfloat16 [3, 576, 1152], P(None, 'wa'), may hold values from -0.25 to 0.25
- gains: float32 [3, 1152], replicated, may hold values from 0.1 to 1.9
- gates: float32 [3, 8], replicated, may hold values from 0.5 to 2
Outputs:
- token_grad: bfloat16 [1, 8, 32, 16, 1152], P(None, None, 'ha', 'wa')
- head_sens: bfloat16 [1, 3, 8, 32, 16, 8], P(None, None, None, 'ha', 'wa')
All inputs are finite; a program needn't handle non-finite values.
Results may differ from a plain program's by a relative error of at most 0.02.
Values may be sent and summed in bfloat16 or wider, within the bound.
No kernel may reach another device: no remote copies, remote signals or barrier semaphores. Data moves between devices by JAX's collectives and lax.ppermute only.
A program may use at most 128 MiB of HBM per device.

v0:
```python
import jax
import jax.numpy as jnp
from jax import lax
from jax.sharding import PartitionSpec as P


def letter_forms(attend_axis):
    letters = "bfhw"
    query_side = letters + "nc"
    key_side = letters[:attend_axis] + "g" + letters[attend_axis + 1 :] + "nc"
    score_side = (
        letters[:attend_axis] + letters[attend_axis + 1 :] + "n" + letters[attend_axis] + "g"
    )
    return (
        query_side + "," + key_side + "->" + score_side,
        score_side + "," + key_side + "->" + query_side,
        score_side + "," + query_side + "->" + key_side,
    )


def product(form, left, right):
    return jnp.einsum(form, left, right, preferred_element_type=jnp.float32)


def forward_sublayer(inputs, w_qkv, w_out, gain, gate, attend_axis, keep_output):
    scores_form, mixing_form, keyward_form = letter_forms(attend_axis)
    heads = gate.shape[0]
    hidden = w_out.shape[0]
    head_dim = hidden // heads
    leading = inputs.shape[:4]
    inputs_f = inputs.astype(jnp.float32)
    inverse = lax.rsqrt(jnp.mean(inputs_f * inputs_f, axis=-1, keepdims=True) + 1e-06)
    normed = (inputs_f * inverse * gain).astype(jnp.bfloat16)
    projected = jnp.dot(normed, w_qkv, preferred_element_type=jnp.float32).astype(jnp.bfloat16)
    split = projected.reshape(leading + (3, heads, head_dim))
    queries = split[..., 0, :, :]
    keys_all = split[..., 1, :, :]
    values = split[..., 2, :, :]
    scores = product(scores_form, queries, keys_all) * head_dim ** (-0.5)
    raised = jnp.exp(scores)
    probs = raised / jnp.sum(raised, axis=-1, keepdims=True)
    probs_half = probs.astype(jnp.bfloat16)
    attended = product(mixing_form, probs_half, values).astype(jnp.bfloat16)
    saved = (inverse, queries, keys_all, values, probs, probs_half, attended)
    if not keep_output:
        return (inputs, saved)
    gated = (
        (attended.astype(jnp.float32) * gate[:, None])
        .astype(jnp.bfloat16)
        .reshape(leading + (hidden,))
    )
    outputs = (inputs_f + jnp.dot(gated, w_out, preferred_element_type=jnp.float32)).astype(
        jnp.bfloat16
    )
    return (outputs, saved)


def backward_sublayer(outgrad, inputs, saved, w_qkv, w_out, gain, gate, attend_axis):
    scores_form, mixing_form, keyward_form = letter_forms(attend_axis)
    inverse, queries, keys_all, values, probs, probs_half, attended = saved
    heads = gate.shape[0]
    hidden = w_out.shape[0]
    head_dim = hidden // heads
    leading = inputs.shape[:4]
    d_gated = jnp.dot(outgrad, w_out.T, preferred_element_type=jnp.float32).astype(jnp.bfloat16)
    d_gated = d_gated.reshape(leading + (heads, head_dim))
    sens = jnp.sum(d_gated.astype(jnp.float32) * attended.astype(jnp.float32), axis=-1).astype(
        jnp.bfloat16
    )
    d_attended = (d_gated.astype(jnp.float32) * gate[:, None]).astype(jnp.bfloat16)
    d_probs = product(scores_form, d_attended, values)
    d_values = product(keyward_form, probs_half, d_attended)
    d_scores = (
        probs * (d_probs - jnp.sum(d_probs * probs, axis=-1, keepdims=True)) * head_dim ** (-0.5)
    ).astype(jnp.bfloat16)
    d_queries = product(mixing_form, d_scores, keys_all)
    d_keys = product(keyward_form, d_scores, queries)
    d_proj = (
        jnp.stack([d_queries, d_keys, d_values], axis=4)
        .reshape(leading + (3 * hidden,))
        .astype(jnp.bfloat16)
    )
    d_normed = jnp.dot(d_proj, w_qkv.T, preferred_element_type=jnp.float32) * gain
    inputs_f = inputs.astype(jnp.float32)
    ingrad = (
        outgrad.astype(jnp.float32)
        + inverse * d_normed
        - inputs_f
        * inverse
        * inverse
        * inverse
        * jnp.mean(inputs_f * d_normed, axis=-1, keepdims=True)
    )
    return (ingrad.astype(jnp.bfloat16), sens)


def per_device(tokens, cotangent, w_qkv, w_out, gains, gates):
    heads = gates.shape[1]
    full_qkv, full_out = (
        lax.all_gather(w_qkv, "wa", axis=1, tiled=True),
        lax.all_gather(w_out, "wa", axis=1, tiled=True),
    )

    def weights_for(sublayer):
        return (full_qkv[sublayer], full_out[sublayer])

    qkv_first, out_first = weights_for(0)
    after_time, saved_time = forward_sublayer(
        tokens, qkv_first, out_first, gains[0], gates[0], 1, True
    )
    qkv_second, out_second = weights_for(1)
    tall_input = lax.all_to_all(after_time, "ha", split_axis=1, concat_axis=2, tiled=True)
    after_height, saved_height = forward_sublayer(
        tall_input, qkv_second, out_second, gains[1], gates[1], 2, True
    )
    qkv_third, out_third = weights_for(2)
    wide_input = lax.all_to_all(after_height, "wa", split_axis=2, concat_axis=3, tiled=True)
    wide_same, saved_width = forward_sublayer(
        wide_input, qkv_third, out_third, gains[2], gates[2], 3, False
    )
    tall_cot = lax.all_to_all(cotangent, "ha", split_axis=1, concat_axis=2, tiled=True)
    wide_cot = lax.all_to_all(tall_cot, "wa", split_axis=2, concat_axis=3, tiled=True)
    grad_width, sens_width = backward_sublayer(
        wide_cot, wide_input, saved_width, qkv_third, out_third, gains[2], gates[2], 3
    )
    tall_grad, tall_sens = (
        lax.all_to_all(grad_width, "wa", split_axis=3, concat_axis=2, tiled=True),
        lax.all_to_all(sens_width, "wa", split_axis=3, concat_axis=2, tiled=True),
    )
    grad_height, sens_height = backward_sublayer(
        tall_grad, tall_input, saved_height, qkv_second, out_second, gains[1], gates[1], 2
    )
    home_cot, both_sens = (
        lax.all_to_all(grad_height, "ha", split_axis=2, concat_axis=1, tiled=True),
        lax.all_to_all(
            jnp.concatenate([tall_sens, sens_height], axis=-1),
            "ha",
            split_axis=2,
            concat_axis=1,
            tiled=True,
        ),
    )
    home_sens_width = both_sens[..., :heads]
    home_sens_height = both_sens[..., heads:]
    token_grad, sens_time = backward_sublayer(
        home_cot, tokens, saved_time, qkv_first, out_first, gains[0], gates[0], 1
    )
    head_sens = jnp.stack([sens_time, home_sens_height, home_sens_width], axis=1)
    return (token_grad, head_sens)


def solution(mesh):
    in_specs = (
        P(None, None, "ha", "wa", None),
        P(None, None, "ha", "wa", None),
        P(None, "wa", None),
        P(None, "wa", None),
        P(),
        P(),
    )
    out_specs = (P(None, None, "ha", "wa", None), P(None, None, None, "ha", "wa", None))
    return jax.shard_map(
        per_device, mesh=mesh, in_specs=in_specs, out_specs=out_specs, check_vma=False
    )
```

profile of v0, /device:TPU:0, one launch (start us, length us, event | category | flops | bytes accessed | tf_op | source)
XLA Modules:
  0.0 389.7 jit_solution(5976131492476311820)
XLA Ops:
  8.6 1.7 copy.378
  10.3 4.2 %all-to-all-start = ((bf16[1,8,8,2,1152]{4,2,3,0,1:T(8,128)(2,1)}), bf16[1,8,8,2,1152]{4,2,3,0,1:T(8,128)(2,1)S(1)}, u32[]{:S(2)}, u32[]{:S(2)}) async-start(bf16[1,8,8,2,1152]{4,2,3,0,1:T(8,128)(2,1)} %copy.378), calls=%async_computation | async-start | bytes 589824 | tf_op jit(solution)/shard_map/all_to_all | solution.py:121
  15.5 1.1 fusion.79
  17.4 169.6 %all-gather.3.cloned.1.call-done = bf16[3,1152,1728]{2,1,0:T(8,128)(2,1)} async-done(((bf16[3,144,1728]{2,1,0:T(8,128)(2,1)}), bf16[3,1152,1728]{2,1,0:T(8,128)(2,1)}) %all-gather.3.cloned.1.call-update) | async-done | bytes 11943952 | tf_op jit(solution)/shard_map/all_gather | solution.py:100
  187.0 3.1 fusion.17
  191.7 1.2 multiply_convert_fusion.3
  193.1 65.0 %all-gather.5.cloned.1.call-done = bf16[3,576,1152]{2,1,0:T(8,128)(2,1)} async-done(((bf16[3,72,1152]{2,1,0:T(8,128)(2,1)}), bf16[3,576,1152]{2,1,0:T(8,128)(2,1)}) %all-gather.5.cloned.1.call-update) | async-done | bytes 3981328 | tf_op jit(solution)/shard_map/all_gather | solution.py:101
  258.1 2.4 fusion.19
  260.6 3.5 all-to-all-start.2
  264.1 1.0 copy.380
  265.0 5.4 %all-to-all-done.2 = bf16[1,8,8,2,1152]{4,2,3,0,1:T(8,128)(2,1)S(1)} async-done(((bf16[1,8,8,2,1152]{4,2,3,0,1:T(8,128)(2,1)}), bf16[1,8,8,2,1152]{4,2,3,0,1:T(8,128)(2,1)S(1)}, u32[]{:S(2)}, u32[]{:S(2)}) %all-to-all-start.2) | async-done | bytes 294944 | tf_op jit(solution)/shard_map/all_to_all | solution.py:112
  270.4 3.4 all-to-all-start.1
  274.0 3.0 fusion.16
  278.7 1.1 multiply_convert_fusion.2
  280.1 1.7 fusion.18
  281.9 0.9 copy.402
  283.4 5.4 %all-to-all-start.3 = ((bf16[1,2,32,2,1152]{4,3,1,0,2:T(2,128)(2,1)}), bf16[1,2,32,2,1152]{4,3,1,0,2:T(2,128)(2,1)S(1)}, u32[]{:S(2)}, u32[]{:S(2)}) async-start(bf16[1,2,32,2,1152]{4,3,1,0,2:T(2,128)(2,1)} %copy.402), calls=%async_computation.3 | async-start | bytes 589824 | tf_op jit(solution)/shard_map/all_to_all | solution.py:117
  290.0 1.9 fusion.57
  292.2 1.1 reshape.691
  293.2 4.6 %all-to-all-done.3 = bf16[1,2,32,2,1152]{4,3,1,0,2:T(2,128)(2,1)S(1)} async-done(((bf16[1,2,32,2,1152]{4,3,1,0,2:T(2,128)(2,1)}), bf16[1,2,32,2,1152]{4,3,1,0,2:T(2,128)(2,1)S(1)}, u32[]{:S(2)}, u32[]{:S(2)}) %all-to-all-start.3) | async-done | bytes 294944 | tf_op jit(solution)/shard_map/all_to_all | solution.py:117
  298.8 2.9 fusion.15
  303.6 1.4 fusion.102
  305.0 1.2 fusion.115
  306.4 1.6 fusion.42
  308.0 2.3 fusion.43
  310.6 1.5 fusion.55
  312.7 3.6 all-to-all-start.6
  316.4 1.1 pad_maximum_fusion
  318.3 3.7 multiply_reduce_fusion.3
  323.1 6.0 %all-to-all-start.4 = ((bf16[1,2,4,16,1152]{4,2,1,0,3:T(4,128)(2,1)}), bf16[1,2,4,16,1152]{4,2,1,0,3:T(4,128)(2,1)S(1)}, u32[]{:S(2)}, u32[]{:S(2)}) async-start(bf16[1,2,4,16,1152]{4,2,1,0,3:T(4,128)(2,1)} %copy.422), calls=%async_computation.4 | async-start | bytes 589824 | tf_op jit(solution)/shard_map/all_to_all | solution.py:127
  329.8 7.9 %all-to-all-done.4 = bf16[1,2,4,16,1152]{4,2,1,0,3:T(4,128)(2,1)S(1)} async-done(((bf16[1,2,4,16,1152]{4,2,1,0,3:T(4,128)(2,1)}), bf16[1,2,4,16,1152]{4,2,1,0,3:T(4,128)(2,1)S(1)}, u32[]{:S(2)}, u32[]{:S(2)}) %all-to-all-start.4) | async-done | bytes 294944 | tf_op jit(solution)/shard_map/all_to_all | solution.py:127
  337.9 2.7 fusion.59
  340.6 1.2 reshape.688
  341.8 1.2 reshape.692
  343.0 1.1 fusion.114
  344.4 1.6 fusion.45
  346.1 1.5 fusion.46
  348.7 3.5 all-to-all-start.7
  353.2 3.7 fusion.86
  357.2 0.9 copy.427
  358.1 3.5 all-to-all-start.5
  362.0 5.9 %all-to-all-done.5 = bf16[1,2,32,2,1152]{4,3,1,0,2:T(2,128)(2,1)S(1)} async-done(((bf16[1,2,32,2,1152]{4,3,1,0,2:T(2,128)(2,1)}), bf16[1,2,32,2,1152]{4,3,1,0,2:T(2,128)(2,1)S(1)}, u32[]{:S(2)}, u32[]{:S(2)}) %all-to-all-start.5) | async-done | bytes 294944 | tf_op jit(solution)/shard_map/all_to_all | solution.py:134
  368.0 1.9 fusion.58
  371.5 2.1 fusion.48
  373.6 1.1 fusion.49
  376.0 1.2 pad_maximum_fusion.2
  377.9 3.7 fusion.80
  381.9 0.9 copy.445
  (128 shorter events, 22.8 us)
Async XLA Ops:
  7.2 179.8 %all-gather.3.cloned.1.call-start = ((), (), s32[]{:S(2)}) async-start(), calls=%async_computation.8 | async-start | bytes 13934592 | tf_op jit(solution)/shard_map/all_gather | solution.py:100
  7.9 250.2 %all-gather.5.cloned.1.call-start = ((), (), s32[]{:S(2)}) async-start(), calls=%async_computation.9 | async-start | bytes 4478976 | tf_op jit(solution)/shard_map/all_gather | solution.py:101
  10.3 250.2 %all-to-all-start = ((bf16[1,8,8,2,1152]{4,2,3,0,1:T(8,128)(2,1)}), bf16[1,8,8,2,1152]{4,2,3,0,1:T(8,128)(2,1)S(1)}, u32[]{:S(2)}, u32[]{:S(2)}) async-start(bf16[1,8,8,2,1152]{4,2,3,0,1:T(8,128)(2,1)} %copy.378), calls=%async_computation | async-start | bytes 589824 | tf_op jit(solution)/shard_map/all_to_all | solution.py:121
  15.4 174.6 %copy-start.20 = (f32[1152]{0:T(1024)}, f32[1152]{0:T(1024)S(1)}, u32[]{:S(2)}) copy-start(f32[1152]{0:T(1024)S(1)} %get-tuple-element.19) | copy-start | bytes 13828
  15.4 258.5 %copy-start.22 = (f32[1152]{0:T(1024)}, f32[1152]{0:T(1024)S(1)}, u32[]{:S(2)}) copy-start(f32[1152]{0:T(1024)S(1)} %get-tuple-element.20) | copy-start | bytes 13828
  190.1 68.1 %copy-start.10 = (bf16[1,8,8,2,1152]{4,3,2,1,0:T(2,128)(2,1)S(1)}, bf16[1,8,8,2,1152]{4,3,2,1,0:T(2,128)(2,1)}, u32[]{:S(2)}) copy-start(bf16[1,8,8,2,1152]{4,3,2,1,0:T(2,128)(2,1)} %param.6) | copy-start | bytes 884740
  191.2 69.4 %copy-start = (bf16[1,8,8,2,1,8,72]{6,5,4,2,3,1,0:T(8,128)(2,1)}, bf16[1,8,8,2,1,8,72]{6,5,4,2,3,1,0:T(8,128)(2,1)S(1)}, u32[]{:S(2)}) copy-start(bf16[1,8,8,2,1,8,72]{6,5,4,2,3,1,0:T(8,128)(2,1)S(1)} %get-tuple-element.27) | copy-start | bytes 442372
  191.2 69.4 %copy-start.12 = (bf16[1,8,8,2,1,8,72]{6,5,4,2,3,1,0:T(8,128)(2,1)}, bf16[1,8,8,2,1,8,72]{6,5,4,2,3,1,0:T(8,128)(2,1)S(1)}, u32[]{:S(2)}) copy-start(bf16[1,8,8,2,1,8,72]{6,5,4,2,3,1,0:T(8,128)(2,1)S(1)} %get-tuple-element.28) | copy-start | bytes 442372
  191.2 79.2 %copy-start.14 = (bf16[1,8,8,2,1,8,72]{6,5,4,2,3,1,0:T(8,128)(2,1)}, bf16[1,8,8,2,1,8,72]{6,5,4,2,3,1,0:T(8,128)(2,1)S(1)}, u32[]{:S(2)}) copy-start(bf16[1,8,8,2,1,8,72]{6,5,4,2,3,1,0:T(8,128)(2,1)S(1)} %get-tuple-element.29) | copy-start | bytes 442372
  260.6 9.8 %all-to-all-start.2 = ((bf16[1,8,8,2,1152]{4,2,3,0,1:T(8,128)(2,1)}), bf16[1,8,8,2,1152]{4,2,3,0,1:T(8,128)(2,1)S(1)}, u32[]{:S(2)}, u32[]{:S(2)}) async-start(bf16[1,8,8,2,1152]{4,2,3,0,1:T(8,128)(2,1)} %fusion.19), calls=%async_computation.2 | async-start | bytes 589824 | tf_op jit(solution)/shard_map/all_to_all | solution.py:112
  270.4 13.0 %all-to-all-start.1 = ((bf16[1,2,32,2,1152]{4,3,1,0,2:T(2,128)(2,1)}), bf16[1,2,32,2,1152]{4,3,1,0,2:T(2,128)(2,1)S(1)}, u32[]{:S(2)}, u32[]{:S(2)}) async-start(bf16[1,2,32,2,1152]{4,3,1,0,2:T(2,128)(2,1)} %copy.380), calls=%async_computation.1 | async-start | bytes 589824 | tf_op jit(solution)/shard_map/all_to_all | solution.py:122
  278.0 0.7 copy-start.15
  278.0 5.4 %copy-start.2 = (bf16[1,2,32,2,1,8,72]{6,5,4,2,3,1,0:T(8,128)(2,1)}, bf16[1,2,32,2,1,8,72]{6,5,4,2,3,1,0:T(8,128)(2,1)S(1)}, u32[]{:S(2)}) copy-start(bf16[1,2,32,2,1,8,72]{6,5,4,2,3,1,0:T(8,128)(2,1)S(1)} %get-tuple-element.24) | copy-start | bytes 442372
  278.1 5.3 %copy-start.16 = (bf16[1,2,32,2,1,8,72]{6,5,4,2,3,1,0:T(8,128)(2,1)}, bf16[1,2,32,2,1,8,72]{6,5,4,2,3,1,0:T(8,128)(2,1)S(1)}, u32[]{:S(2)}) copy-start(bf16[1,2,32,2,1,8,72]{6,5,4,2,3,1,0:T(8,128)(2,1)S(1)} %get-tuple-element.26) | copy-start | bytes 442372
  278.4 13.6 %copy-start.4 = (f32[2,2,8,32,32]{3,4,2,1,0:T(8,128)}, f32[2,2,8,32,32]{3,4,2,1,0:T(8,128)S(1)}, u32[]{:S(2)}) copy-start(f32[2,2,8,32,32]{3,4,2,1,0:T(8,128)S(1)} %fusion.106) | copy-start | bytes 393220
  283.4 14.4 %all-to-all-start.3 = ((bf16[1,2,32,2,1152]{4,3,1,0,2:T(2,128)(2,1)}), bf16[1,2,32,2,1152]{4,3,1,0,2:T(2,128)(2,1)S(1)}, u32[]{:S(2)}, u32[]{:S(2)}) async-start(bf16[1,2,32,2,1152]{4,3,1,0,2:T(2,128)(2,1)} %copy.402), calls=%async_computation.3 | async-start | bytes 589824 | tf_op jit(solution)/shard_map/all_to_all | solution.py:117
  289.3 0.7 copy-start.8
  303.6 1.4 copy-start.17
  303.6 2.8 copy-start.18
  312.7 10.3 %all-to-all-start.6 = ((bf16[1,2,4,16,8]{4,2,1,0,3:T(4,128)(2,1)}), bf16[1,2,4,16,8]{4,2,1,0,3:T(4,128)(2,1)S(1)}, u32[]{:S(2)}, u32[]{:S(2)}) async-start(bf16[1,2,4,16,8]{4,2,1,0,3:T(4,128)(2,1)} %copy.435), calls=%async_computation.6 | async-start | bytes 65536 | tf_op jit(solution)/shard_map/all_to_all | solution.py:128
  317.7 4.2 %copy-start.9 = (bf16[2,4,16,1152]{3,2,1,0:T(8,128)(2,1)S(1)}, bf16[2,4,16,1152]{3,2,1,0:T(8,128)(2,1)}, u32[]{:S(2)}) copy-start(bf16[2,4,16,1152]{3,2,1,0:T(8,128)(2,1)} %copy-done.8) | copy-start | bytes 884740
  322.0 21.1 %copy-start.3 = (bf16[1,2,32,2,1,8,72]{6,5,4,2,3,1,0:T(8,128)(2,1)S(1)}, bf16[1,2,32,2,1,8,72]{6,5,4,2,3,1,0:T(8,128)(2,1)}, u32[]{:S(2)}) copy-start(bf16[1,2,32,2,1,8,72]{6,5,4,2,3,1,0:T(8,128)(2,1)} %copy-done.2) | copy-start | bytes 442372
  322.2 21.9 %copy-start.5 = (f32[2,2,8,32,32]{3,4,2,1,0:T(8,128)S(1)}, f32[2,2,8,32,32]{3,4,2,1,0:T(8,128)}, u32[]{:S(2)}) copy-start(f32[2,2,8,32,32]{3,4,2,1,0:T(8,128)} %copy-done.4) | copy-start | bytes 393220
  323.1 14.6 %all-to-all-start.4 = ((bf16[1,2,4,16,1152]{4,2,1,0,3:T(4,128)(2,1)}), bf16[1,2,4,16,1152]{4,2,1,0,3:T(4,128)(2,1)S(1)}, u32[]{:S(2)}, u32[]{:S(2)}) async-start(bf16[1,2,4,16,1152]{4,2,1,0,3:T(4,128)(2,1)} %copy.422), calls=%async_computation.4 | async-start | bytes 589824 | tf_op jit(solution)/shard_map/all_to_all | solution.py:127
  337.9 9.7 %copy-start.7 = (f32[1,2,32,2,8,72]{5,2,4,3,1,0:T(8,128)S(1)}, f32[1,2,32,2,8,72]{5,2,4,3,1,0:T(8,128)}, u32[]{:S(2)}) copy-start(f32[1,2,32,2,8,72]{5,2,4,3,1,0:T(8,128)} %get-tuple-element.38) | copy-start | bytes 884740
  348.7 9.4 %all-to-all-start.7 = ((bf16[4,2,256]{2,1,0:T(2,128)(2,1)}), bf16[4,2,256]{2,1,0:T(2,128)(2,1)S(1)}, u32[]{:S(2)}, u32[]{:S(2)}) async-start(bf16[4,2,256]{2,1,0:T(2,128)(2,1)} %reshape.709), calls=%async_computation.7 | async-start | bytes 8192 | tf_op jit(solution)/shard_map/all_to_all | solution.py:135
  352.7 4.2 %copy-start.19 = (f32[2,32,2]{1,2,0:T(2,128)S(1)}, f32[2,32,2]{1,2,0:T(2,128)}, u32[]{:S(2)}) copy-start(f32[2,32,2]{1,2,0:T(2,128)} %rsqrt.36) | copy-start | bytes 1540
  356.9 13.5 %copy-start.1 = (bf16[1,8,8,2,1,8,72]{6,5,4,2,3,1,0:T(8,128)(2,1)S(1)}, bf16[1,8,8,2,1,8,72]{6,5,4,2,3,1,0:T(8,128)(2,1)}, u32[]{:S(2)}) copy-start(bf16[1,8,8,2,1,8,72]{6,5,4,2,3,1,0:T(8,128)(2,1)} %copy-done) | copy-start | bytes 442372
  358.1 9.8 %all-to-all-start.5 = ((bf16[1,2,32,2,1152]{4,3,1,0,2:T(2,128)(2,1)}), bf16[1,2,32,2,1152]{4,3,1,0,2:T(2,128)(2,1)S(1)}, u32[]{:S(2)}, u32[]{:S(2)}) async-start(bf16[1,2,32,2,1152]{4,3,1,0,2:T(2,128)(2,1)} %copy.427), calls=%async_computation.5 | async-start | bytes 589824 | tf_op jit(solution)/shard_map/all_to_all | solution.py:134
  367.9 5.7 %copy-start.13 = (bf16[1,8,8,2,1,8,72]{6,5,4,2,3,1,0:T(8,128)(2,1)S(1)}, bf16[1,8,8,2,1,8,72]{6,5,4,2,3,1,0:T(8,128)(2,1)}, u32[]{:S(2)}) copy-start(bf16[1,8,8,2,1,8,72]{6,5,4,2,3,1,0:T(8,128)(2,1)} %copy-done.12) | copy-start | bytes 442372
  369.9 4.8 %copy-start.6 = (f32[1,8,8,2,8,72]{5,1,4,3,2,0:T(8,128)S(1)}, f32[1,8,8,2,8,72]{5,1,4,3,2,0:T(8,128)}, u32[]{:S(2)}) copy-start(f32[1,8,8,2,8,72]{5,1,4,3,2,0:T(8,128)} %get-tuple-element.36) | copy-start | bytes 884740
  371.4 6.5 %copy-start.11 = (bf16[1,8,8,2,1152]{4,3,2,1,0:T(2,128)(2,1)S(1)}, bf16[1,8,8,2,1152]{4,3,2,1,0:T(2,128)(2,1)}, u32[]{:S(2)}) copy-start(bf16[1,8,8,2,1152]{4,3,2,1,0:T(2,128)(2,1)} %param.6) | copy-start | bytes 884740
  371.4 6.5 %copy-start.21 = (f32[1152]{0:T(1024)S(1)}, f32[1152]{0:T(1024)}, u32[]{:S(2)}) copy-start(f32[1152]{0:T(1024)} %copy-done.20) | copy-start | bytes 13828
Sparse Core Ops, SparseCore 0:
  10.2 176.7 all-gather.2
  189.2 68.8 all-gather.4
where the time goes:
time: 391 us; the launch traced here: 390 us
  waiting for transfers between devices  260 us (66%)
  matrix products  50.6 us (13%)
  starting transfers between devices  33.1 us (8%)
  local copies, waits for them, and re-layouts  24.9 us (6%)
  between operations  14.8 us (4%)
  other arithmetic  5.96 us (2%)
    all_gather x1, waiting for transfers between devices, per_device(): lax.all_gather(w_qkv, 'wa', axis=1, tiled=True)  170 us
    all_gather x1, waiting for transfers between devices, per_device(): lax.all_gather(w_out, 'wa', axis=1, tiled=True)  65 us
    dot_general x15, matrix products, product(): return jnp.einsum(form, left, right, preferred_element_type=jnp.float32)  17.8 us
    dot_general x3, matrix products, backward_sublayer(): jnp.dot(d_proj, w_qkv.T, preferred_element_type=jnp.float32) * gain  11 us
    dot_general x3, matrix products, forward_sublayer(): jnp.dot(normed, w_qkv, preferred_element_type=jnp.float32)  8.99 us
    all_to_all x1, waiting for transfers between devices, per_device(): lax.all_to_all(grad_width, 'wa', split_axis=3, concat_axis=2, tiled=True)  7.85 us
  transfers between devices with their start and end apart: 10, of which 7 were waited for; matrix products, arithmetic and copies ran while one was open for 10% of the time, Pallas kernels for 0%

commit v1 on v0

v1 whole, which is shorter than its diff:
```python
import functools

import jax
import jax.numpy as jnp
from jax import lax
from jax.experimental import pallas as pl
from jax.experimental.pallas import tpu as pltpu
from jax.sharding import PartitionSpec as P

LANES = 128
ROWS = 16
AXES = ("ha", "wa")
NT = (((1,), (1,)), ((), ()))
TN = (((0,), (0,)), ((), ()))


def ceil_to(value, unit):
    return -(-value // unit) * unit


def tile_qkv(w):
    lead, (rows, cols) = w.shape[:-2], w.shape[-2:]
    wide = ceil_to(cols, LANES)
    w = jnp.pad(w, [(0, 0)] * (len(lead) + 1) + [(0, wide - cols)])
    w = w.reshape(lead + (rows // ROWS, ROWS, wide // LANES, LANES))
    return jnp.moveaxis(w, -2, -4)


def tile_out(w):
    lead, (rows, cols) = w.shape[:-2], w.shape[-2:]
    tall = ceil_to(rows, ROWS)
    w = jnp.pad(w, [(0, 0)] * len(lead) + [(0, tall - rows), (0, 0)])
    w = w.reshape(lead + (tall // ROWS, ROWS, cols // LANES, LANES))
    return jnp.swapaxes(w, -3, -2)


class Routes:
    def __init__(self, n_ha, n_wa):
        self.n_ha, self.n_wa = n_ha, n_wa

    def send(self, value, ha_bits=0, wa_bits=0, only_core=None):
        pairs = []
        for a in range(self.n_ha):
            for b in range(self.n_wa):
                if only_core is None or a % 2 == only_core:
                    source = a * self.n_wa + b
                    target = (a ^ ha_bits) * self.n_wa + (b ^ wa_bits)
                    pairs.append((source, target))
        return lax.ppermute(value, AXES, pairs)

    def y(self, value):
        return self.send(value, wa_bits=1)

    def z(self, value, k):
        return self.send(value, wa_bits=2 * k)

    def x(self, value, core):
        return self.send(value, ha_bits=2, only_core=core)

    def core(self, value):
        return self.send(value, ha_bits=1)

    def core_from(self, value, core):
        return self.send(value, ha_bits=1, only_core=core)


def spread(routes, groups, part, core_of):
    out = []
    for (buffer, offsets), home in zip(groups, core_of):
        other = routes.core(buffer)
        out.append((buffer, None, offsets, 0, 0))
        out.append((other, None, offsets, 1, 0))
        across = routes.x(buffer if home == 1 else other, home)
        copied = routes.core_from(across, home)
        out.append((across, copied, offsets, 2, home))
    return out


def gather_early(routes, own):
    r1 = routes.z(own, 1)
    ry = routes.y(own)
    far = [routes.z(own, k) for k in range(2, routes.n_wa // 2)]
    ry1 = routes.y(r1)
    near = jnp.stack([r1, ry, ry1])
    far_own = jnp.stack(far)
    far_y = routes.y(far_own)
    ks = range(2, routes.n_wa // 2)
    groups = [
        (near, [2, 1, 3]),
        (far_own, [2 * k for k in ks]),
        (far_y, [2 * k + 1 for k in ks]),
    ]
    return spread(routes, groups, None, (1, 0, 1))


def gather_late(routes, own):
    stack = own[None]
    k = 1
    while 2 * k < routes.n_wa:
        stack = jnp.concatenate([stack, routes.z(stack, k)])
        k *= 2
    across = routes.y(stack)
    n = stack.shape[0]
    groups = [
        (stack, [2 * k for k in range(n)]),
        (across, [2 * k + 1 for k in range(n)]),
    ]
    return spread(routes, groups, None, (1, 0))


def load_weights(plan, place_ref, refs, sems, w_scr, o_scr, start):
    count = [0]

    def move(src, dst):
        copy = pltpu.make_async_copy(src, dst, sems.at[count[0]])
        count[0] += 1
        if start:
            copy.start()
        else:
            copy.wait()

    if plan["full"]:
        move(refs[0], w_scr)
        move(refs[1], o_scr)
        return
    tiles, rg, og, ot = plan["tiles"], plan["rg"], plan["og"], plan["ot"]

    def put(src, slot, part):
        move(src.at[pl.ds(0, tiles)], w_scr.at[:, pl.ds(slot * 3 * rg + part * rg, rg)])
        move(src.at[pl.ds(tiles, og)], o_scr.at[slot, :, pl.ds(part * ot, ot)])

    own_ref = refs[0]
    for part in range(3):
        put(own_ref.at[part], place_ref[0], part)
    at = 1
    for offsets, kind, home, double in plan["groups"]:
        if not double:
            for i, offset in enumerate(offsets):
                if offset != 0:
                    put(refs[at].at[i], place_ref[offset], place_ref[plan["n_wa"] + kind])
            at += 1
        else:
            here, there = refs[at], refs[at + 1]
            base = count[0]
            for ref, cond in ((here, True), (there, False)):
                count[0] = base
                at_home = place_ref[plan["n_wa"] + 3] == home

                @pl.when(at_home if cond else jnp.logical_not(at_home))
                def _():
                    for i, offset in enumerate(offsets):
                        if offset != 0:
                            put(ref.at[i], place_ref[offset], place_ref[plan["n_wa"] + kind])

            at += 2


def dims_of(plan):
    return plan["T"], plan["D"], plan["heads"], plan["hd"], plan["tiles"] * LANES


def project(plan, x, gain, w_scr, proj_scr):
    T, D, heads, hd, wide = dims_of(plan)
    xf = x.astype(jnp.float32)
    inverse = lax.rsqrt(jnp.mean(xf * xf, axis=-1, keepdims=True) + 1e-06)
    normed = (xf * inverse * gain).astype(jnp.bfloat16)
    for j in range(0, plan["tiles"], 2):
        js = range(j, min(j + 2, plan["tiles"]))
        w = jnp.concatenate([w_scr[i].reshape(D, LANES) for i in js], axis=1)
        proj_scr[:, j * LANES : j * LANES + LANES * len(js)] = jnp.dot(
            normed, w, preferred_element_type=jnp.float32
        ).astype(jnp.bfloat16)
    return inverse


def qkv_of(plan, proj_ref, h):
    hd, hidden = plan["hd"], plan["heads"] * plan["hd"]
    return [proj_ref[:, m * hidden + h * hd : m * hidden + (h + 1) * hd] for m in range(3)]


def attend(plan, h, proj_ref, bias):
    q, k, v = qkv_of(plan, proj_ref, h)
    scores = lax.dot_general(q, k, NT, preferred_element_type=jnp.float32)
    raised = jnp.exp(scores * plan["hd"] ** (-0.5) + bias)
    probs = raised / jnp.sum(raised, axis=-1, keepdims=True)
    attended = jnp.dot(probs.astype(jnp.bfloat16), v, preferred_element_type=jnp.float32)
    return probs, attended.astype(jnp.bfloat16)


def fwd_kernel(plan, place_ref, gates_ref, x_ref, gain_ref, bias_ref, *rest):
    n = plan["n_refs"]
    refs, rest = rest[:n], rest[n:]
    y_ref, proj_ref, probs_ref, att_ref, inv_ref, w_scr, o_scr, gated_scr, sems = rest
    T, D, heads, hd, wide = dims_of(plan)
    layer, stride = plan["layer"], plan["og"] * ROWS
    load_weights(plan, place_ref, refs, sems, w_scr, o_scr, True)
    load_weights(plan, place_ref, refs, sems, w_scr, o_scr, False)
    x = x_ref[...]
    inv_ref[...] = project(plan, x, gain_ref[layer : layer + 1, :], w_scr, proj_ref)
    bias = bias_ref[...]
    gated_scr[...] = jnp.zeros_like(gated_scr)
    for h in range(heads):
        probs, attended = attend(plan, h, proj_ref, bias)
        probs_ref[h] = probs
        att_ref[:, h * hd : (h + 1) * hd] = attended
        gated = (attended.astype(jnp.float32) * gates_ref[layer, h]).astype(jnp.bfloat16)
        gated_scr[:, h * stride : h * stride + hd] = gated
    gated = gated_scr[...]
    lane_tiles = D // LANES
    for j in range(0, lane_tiles, 2):
        js = range(j, min(j + 2, lane_tiles))
        w = jnp.concatenate([o_scr[:, :, i].reshape(heads * stride, LANES) for i in js], axis=1)
        cols = slice(j * LANES, j * LANES + LANES * len(js))
        y_ref[:, cols] = (
            x_ref[:, cols].astype(jnp.float32)
            + jnp.dot(gated, w, preferred_element_type=jnp.float32)
        ).astype(jnp.bfloat16)


def backward(plan, gates_ref, outgrad_ref, x_ref, gain, inverse, proj_ref, probs_of, att_of,
             w_scr, o_scr, dgated_scr, dproj_scr, g_ref):
    T, D, heads, hd, wide = dims_of(plan)
    layer, stride, hidden = plan["layer"], plan["og"] * ROWS, heads * hd
    lane_tiles = D // LANES
    outgrad = outgrad_ref[:, :D]
    rows = heads * stride
    for r in range(0, heads, 2):
        hs = min(2, heads - r)
        w = jnp.concatenate(
            [o_scr[r : r + hs, :, i].reshape(hs * stride, LANES) for i in range(lane_tiles)],
            axis=1,
        )
        out = lax.dot_general(outgrad, w, NT, preferred_element_type=jnp.float32)
        dgated_scr[:, r * stride : (r + hs) * stride] = out.astype(jnp.bfloat16)
    if wide > 3 * hidden:
        dproj_scr[:, wide - LANES :] = jnp.zeros((T, LANES), jnp.bfloat16)
    lane = lax.broadcasted_iota(jnp.int32, (T, LANES), 1)
    sens = jnp.zeros((T, LANES), jnp.float32)
    if plan["carry"]:
        sens = outgrad_ref[:, D : D + LANES].astype(jnp.float32)
    for h in range(heads):
        q, k, v = qkv_of(plan, proj_ref, h)
        probs = probs_of(h)
        dgated = dgated_scr[:, h * stride : h * stride + hd].astype(jnp.float32)
        own = jnp.sum(dgated * att_of(h).astype(jnp.float32), axis=-1, keepdims=True)
        sens = jnp.where(lane == layer * heads + h, own, sens)
        datt = (dgated * gates_ref[layer, h]).astype(jnp.bfloat16)
        dprobs = lax.dot_general(datt, v, NT, preferred_element_type=jnp.float32)
        dvalues = lax.dot_general(
            probs.astype(jnp.bfloat16), datt, TN, preferred_element_type=jnp.float32
        )
        inner = jnp.sum(dprobs * probs, axis=-1, keepdims=True)
        dscores = (probs * (dprobs - inner) * hd ** (-0.5)).astype(jnp.bfloat16)
        dqueries = jnp.dot(dscores, k, preferred_element_type=jnp.float32)
        dkeys = lax.dot_general(dscores, q, TN, preferred_element_type=jnp.float32)
        for m, d in enumerate((dqueries, dkeys, dvalues)):
            at = m * hidden + h * hd
            dproj_scr[:, at : at + hd] = d.astype(jnp.bfloat16)
    g_ref[:, D : D + LANES] = sens.astype(jnp.bfloat16)
    dproj = dproj_scr[...]
    step = 2 * LANES
    groups = w_scr.shape[1]
    parts = []
    for r in range(0, D, step):
        rr = min(step, D - r)
        w = jnp.concatenate(
            [
                w_scr[i, r // ROWS : (r + rr) // ROWS].reshape(rr, LANES)
                for i in range(plan["tiles"])
            ],
            axis=1,
        )
        parts.append(lax.dot_general(dproj, w, NT, preferred_element_type=jnp.float32))
    dnormed = jnp.concatenate(parts, axis=1) * gain
    xf = x_ref[...].astype(jnp.float32)
    mean = jnp.mean(xf * dnormed, axis=-1, keepdims=True)
    ingrad = (
        outgrad.astype(jnp.float32)
        + inverse * dnormed
        - xf * (inverse * inverse * inverse) * mean
    )
    g_ref[:, :D] = ingrad.astype(jnp.bfloat16)


def both_kernel(plan, place_ref, gates_ref, x_ref, gain_ref, bias_ref, outgrad_ref, *rest):
    n = plan["n_refs"]
    refs, rest = rest[:n], rest[n:]
    g_ref, w_scr, o_scr, proj_scr, probs_scr, att_scr, dgated_scr, dproj_scr, sems = rest
    T, D, heads, hd, wide = dims_of(plan)
    layer = plan["layer"]
    load_weights(plan, place_ref, refs, sems, w_scr, o_scr, True)
    load_weights(plan, place_ref, refs, sems, w_scr, o_scr, False)
    gain = gain_ref[layer : layer + 1, :]
    inverse = project(plan, x_ref[...], gain, w_scr, proj_scr)
    bias = bias_ref[...]
    for h in range(heads):
        probs, attended = attend(plan, h, proj_scr, bias)
        probs_scr[h] = probs
        att_scr[:, h * hd : (h + 1) * hd] = attended
    backward(
        plan, gates_ref, outgrad_ref, x_ref, gain, inverse, proj_scr,
        lambda h: probs_scr[h], lambda h: att_scr[:, h * hd : (h + 1) * hd],
        w_scr, o_scr, dgated_scr, dproj_scr, g_ref,
    )


def bwd_kernel(plan, place_ref, gates_ref, x_ref, gain_ref, outgrad_ref, proj_ref, probs_ref,
               att_ref, inv_ref, *rest):
    n = plan["n_refs"]
    refs, rest = rest[:n], rest[n:]
    g_ref, w_scr, o_scr, dgated_scr, dproj_scr, sems = rest
    layer, hd = plan["layer"], plan["hd"]
    load_weights(plan, place_ref, refs, sems, w_scr, o_scr, True)
    load_weights(plan, place_ref, refs, sems, w_scr, o_scr, False)
    backward(
        plan, gates_ref, outgrad_ref, x_ref, gain_ref[layer : layer + 1, :], inv_ref[...],
        proj_ref, lambda h: probs_ref[h], lambda h: att_ref[:, h * hd : (h + 1) * hd],
        w_scr, o_scr, dgated_scr, dproj_scr, g_ref,
    )


def call(kernel, plan, place, gates, arrays, weights, outs, scratch, flops):
    vmem = pl.BlockSpec(memory_space=pltpu.VMEM)
    smem = pl.BlockSpec(memory_space=pltpu.SMEM)
    plan = dict(plan, n_refs=len(weights))
    D, heads = plan["D"], plan["heads"]
    w_shape = (plan["tiles"], D // ROWS, ROWS, LANES)
    o_shape = (heads, plan["og"], D // LANES, ROWS, LANES)
    n_sems = 2 * 3 * plan["n_wa"] + 2
    return pl.pallas_call(
        functools.partial(kernel, plan),
        out_shape=outs,
        in_specs=[smem, smem] + [vmem] * len(arrays) + [pl.BlockSpec(memory_space=pl.ANY)] * len(weights),
        out_specs=jax.tree.map(lambda _: vmem, outs),
        scratch_shapes=[pltpu.VMEM(w_shape, jnp.bfloat16), pltpu.VMEM(o_shape, jnp.bfloat16)]
        + scratch
        + [pltpu.SemaphoreType.DMA((n_sems,))],
        compiler_params=pltpu.CompilerParams(vmem_limit_bytes=40 * 1024 * 1024),
        cost_estimate=pl.CostEstimate(flops=flops, bytes_accessed=6 * 1024 * 1024, transcendentals=0),
    )(place, gates, *arrays, *weights)


def per_device(n_ha, n_wa, tokens, cotangent, w_qkv, w_out, gains, gates):
    videos, frames, rows, cols, D = tokens.shape
    layers, heads = gates.shape
    T = videos * frames * rows * cols
    width = w_qkv.shape[2]
    hidden = width // 3
    hd = hidden // heads
    tiles = ceil_to(width, LANES) // LANES
    og = ceil_to(hd, ROWS) // ROWS
    lane_tiles = D // LANES
    wide = tiles * LANES

    def flat(value):
        return jnp.swapaxes(value, 0, 1).reshape(T, D)

    idx = jnp.arange(T)
    fl = frames // n_ha * videos
    lines = [
        idx % (videos * rows * cols),
        (idx // (rows * cols)) % fl * cols + idx % cols,
        (idx // cols) % (T // (n_wa * cols)),
    ]
    biases = [jnp.where(line[:, None] == line[None, :], 0.0, -1e30).astype(jnp.float32) for line in lines]

    shard = w_qkv.shape[1]
    fast = (
        n_ha % 4 == 0
        and n_wa % 4 == 0
        and n_wa & (n_wa - 1) == 0
        and shard % (3 * ROWS) == 0
        and w_out.shape[1] == hd
        and lane_tiles % 3 == 0
    )
    ha, wa = lax.axis_index("ha"), lax.axis_index("wa")
    base = dict(T=T, D=D, heads=heads, hd=hd, tiles=tiles, og=og, n_wa=n_wa, carry=False)
    weights, plans = [], []
    if fast:
        rg, ot = shard // (3 * ROWS), lane_tiles // 3
        core, xbit = ha % 2, (ha // 2) % 2
        part = jnp.where(core == 0, 0, 1 + xbit)
        part_core = jnp.where(core == 0, 1 + xbit, 0)
        place = jnp.stack(
            [wa ^ offset for offset in range(n_wa)] + [part, part_core, 2 - xbit, core]
        ).astype(jnp.int32)
        routes = Routes(n_ha, n_wa)
        for layer in range(layers):
            thirds_q = tile_qkv(w_qkv[layer].reshape(3, shard // 3, width))
            thirds_o = tile_out(w_out[layer]).reshape(og, 3, ot, ROWS, LANES)
            thirds_o = jnp.swapaxes(thirds_o, 0, 1)
            own = jnp.concatenate([thirds_q, thirds_o], axis=1)
            mine = lax.dynamic_index_in_dim(own, part, 0, keepdims=False)
            groups = (gather_early if layer == 0 else gather_late)(routes, mine)
            arrays, meta = [own], []
            for here, there, offsets, kind, home in groups:
                arrays += [here] if there is None else [here, there]
                meta.append((offsets, kind, home, there is not None))
            weights.append(arrays)
            plans.append(dict(base, full=False, layer=layer, rg=rg, ot=ot, groups=meta))
    else:
        place = jnp.zeros((1,), jnp.int32)
        full_qkv = lax.all_gather(w_qkv, "wa", axis=1, tiled=True)
        full_out = lax.all_gather(w_out, "wa", axis=1, tiled=True)
        for layer in range(layers):
            weights.append([tile_qkv(full_qkv[layer]), tile_out(full_out[layer].reshape(heads, hd, D))])
            plans.append(dict(base, full=True, layer=layer))

    def swap(value, axis):
        return lax.all_to_all(value, axis, split_axis=0, concat_axis=0, tiled=True)

    bf16, f32 = jnp.bfloat16, jnp.float32
    act = jax.ShapeDtypeStruct((T, D), bf16)
    loaded = jax.ShapeDtypeStruct((T, D + LANES), bf16)
    dense = 2 * T * D * (width + hidden)

    def forward(layer, x):
        return call(
            fwd_kernel, plans[layer], place, gates, [x, gains, biases[layer]], weights[layer],
            [
                act,
                jax.ShapeDtypeStruct((T, wide), bf16),
                jax.ShapeDtypeStruct((heads, T, T), f32),
                jax.ShapeDtypeStruct((T, hidden), bf16),
                jax.ShapeDtypeStruct((T, 1), f32),
            ],
            [pltpu.VMEM((T, heads * og * ROWS), bf16)],
            dense,
        )

    grads = [pltpu.VMEM((T, heads * og * ROWS), bf16), pltpu.VMEM((T, wide), bf16)]

    def back(layer, x, outgrad, saved):
        return call(
            bwd_kernel, dict(plans[layer], carry=True), place, gates, [x, gains, outgrad] + list(saved),
            weights[layer], loaded, grads, dense,
        )

    home = flat(tokens)
    cot = swap(swap(flat(cotangent), "ha"), "wa")
    after_time, *saved_time = forward(0, home)
    tall = swap(after_time, "ha")
    after_height, *saved_height = forward(1, tall)
    across = swap(after_height, "wa")
    grad = call(
        both_kernel, plans[2], place, gates, [across, gains, biases[2], cot], weights[2], loaded,
        [
            pltpu.VMEM((T, wide), bf16),
            pltpu.VMEM((heads, T, T), f32),
            pltpu.VMEM((T, hidden), bf16),
        ]
        + grads,
        2 * dense,
    )
    grad = back(1, tall, swap(grad, "wa"), saved_height)
    grad = back(0, home, swap(grad, "ha"), saved_time)

    def unflat(value):
        value = value.reshape(frames, videos, rows, cols, value.shape[-1])
        return jnp.swapaxes(value, 0, 1)

    token_grad = unflat(grad[:, :D])
    sens = unflat(grad[:, D : D + layers * heads]).reshape(videos, frames, rows, cols, layers, heads)
    return (token_grad, jnp.moveaxis(sens, 4, 1))


def solution(mesh):
    spec = P(None, None, "ha", "wa", None)
    in_specs = (spec, spec, P(None, "wa", None), P(None, "wa", None), P(), P())
    out_specs = (spec, P(None, None, None, "ha", "wa", None))
    n_ha, n_wa = mesh.shape["ha"], mesh.shape["wa"]
    return jax.shard_map(
        functools.partial(per_device, n_ha, n_wa),
        mesh=mesh, in_specs=in_specs, out_specs=out_specs, check_vma=False,
    )
```

time: 391 us -> 259 us (0.66)
  waiting for transfers between devices: 260 us -> 71.3 us
  matrix products: 50.6 us -> 0 us
  starting transfers between devices: 33.1 us -> 70.9 us
  Pallas kernels: 0 us -> 37.6 us
  blocking collectives: 0 us -> 31.9 us
  between operations: 14.8 us -> 1.68 us
  local copies, waits for them, and re-layouts: 24.9 us -> 35 us
    all_gather x2 -> x0, waiting for transfers between devices: 235 us -> none  [the longest x1 170 us: per_device(): lax.all_gather(w_qkv, 'wa', axis=1, tiled=True)]
    ppermute x0 -> x33, waiting for transfers between devices: none -> 65.6 us  [send(): return lax.ppermute(value, AXES, pairs)]
    ppermute x0 -> x33, starting transfers between devices: none -> 54 us  [send(): return lax.ppermute(value, AXES, pairs)]
    dot_general x26 -> x0, matrix products: 48.5 us -> none  [the longest x15 17.8 us: product(): return jnp.einsum(form, left, right, preferred_element_type=jnp.float32)]
    pallas_call x0 -> x5, Pallas kernels: none -> 37.6 us  [call(): pl.pallas_call(functools.partial(kernel, plan), out_shape=outs, in_specs=...]
    all_to_all x0 -> x3, blocking collectives: none -> 31.9 us  [swap(): return lax.all_to_all(value, axis, split_axis=0, concat_axis=0, tiled=True)]
    unnamed x53 -> x133, local copies, waits for them, and re-layouts: 5.62 us -> 26.1 us
    all_to_all x8 -> x3, waiting for transfers between devices: 24.4 us -> 5.71 us  [swap(): return lax.all_to_all(value, axis, split_axis=0, concat_axis=0, tiled=True)]
  transfers between devices with their start and end apart: 10 -> 36, of which waited for: 7 -> 9; matrix products, arithmetic and copies ran while one was open for 10% -> 4% of each run, Pallas kernels for 0% -> 5%
where the time goes in v1:
time: 259 us; the launch traced here: 257 us
  waiting for transfers between devices  71.3 us (28%)
  starting transfers between devices  70.9 us (27%)
  Pallas kernels  37.6 us (15%)
  local copies, waits for them, and re-layouts  35 us (14%)
  blocking collectives  31.9 us (12%)
  other arithmetic  8.74 us (3%)
    ppermute x33, waiting for transfers between devices, send(): return lax.ppermute(value, AXES, pairs)  65.6 us
    ppermute x33, starting transfers between devices, send(): return lax.ppermute(value, AXES, pairs)  54 us
    pallas_call x5, Pallas kernels, call(): pl.pallas_call(functools.partial(kernel, plan), out_shape=outs, in_specs=...  37.6 us
    all_to_all x3, blocking collectives, swap(): return lax.all_to_all(value, axis, split_axis=0, concat_axis=0, tiled=True)  31.9 us
    unnamed x133, local copies, waits for them, and re-layouts  26.1 us
    all_to_all x3, starting transfers between devices, swap(): return lax.all_to_all(value, axis, split_axis=0, concat_axis=0, tiled=True)  16.9 us
    all_to_all x3, waiting for transfers between devices, swap(): return lax.all_to_all(value, axis, split_axis=0, concat_axis=0, tiled=True)  5.71 us
  transfers between devices with their start and end apart: 36, of which 9 were waited for; matrix products, arithmetic and copies ran while one was open for 4% of the time, Pallas kernels for 5%

profile of v1, /device:TPU:0, one launch (start us, length us, event | category | flops | bytes accessed | tf_op | source)
XLA Modules:
  0.0 257.1 jit_solution(2438483366692739676)
XLA Ops:
  0.7 1.1 slice_bitcast_fusion
  2.0 1.5 fusion.8
  4.2 3.1 %collective-permute-start.15 = (bf16[1,19,3,16,128]{4,3,2,1,0:T(8,128)(2,1)S(1)}, bf16[1,19,3,16,128]{4,3,2,1,0:T(8,128)(2,1)S(1)}, u32[]{:S(2)}, u32[]{:S(2)}) collective-permute-start(bf16[1,19,3,16,128]{4,3,2,1,0:T(8,128)(2,1)S(1)} %fusion.1), channel_id=1, source_target_pairs={{0,2},{1,3},{2,0},{3,1},{4,6},{5,7},{6,4},{7,5},{8,10},{9,11},{10,... | collective-permute-start | bytes 700424 | tf_op jit(solution)/shard_map/ppermute | solution.py:49
  7.3 5.7 %collective-permute-done.15 = bf16[1,19,3,16,128]{4,3,2,1,0:T(8,128)(2,1)S(1)} collective-permute-done((bf16[1,19,3,16,128]{4,3,2,1,0:T(8,128)(2,1)S(1)}, bf16[1,19,3,16,128]{4,3,2,1,0:T(8,128)(2,1)S(1)}, u32[]{:S(2)}, u32[]{:S(2)}) %collective-permute-start.15) | collective-permute-done | bytes 233504 | tf_op jit(solution)/shard_map/ppermute | solution.py:49
  13.8 2.8 %collective-permute-start.16 = (bf16[2,19,3,16,128]{4,3,2,1,0:T(8,128)(2,1)}, bf16[2,19,3,16,128]{4,3,2,1,0:T(8,128)(2,1)}, u32[]{:S(2)}, u32[]{:S(2)}) collective-permute-start(bf16[2,19,3,16,128]{4,3,2,1,0:T(8,128)(2,1)} %pad_maximum_fusion.7), channel_id=1, source_target_pairs={{0,4},{1,5},{2,6},{3,7},{4,0},{5,1},{6,2},{7,3},{8,12},{9,13},{10,... | collective-permute-start | bytes 1400840 | tf_op jit(solution)/shard_map/ppermute | solution.py:49
  18.2 1.6 collective-permute-start.24
  21.8 21.2 %collective-permute-done.16 = bf16[2,19,3,16,128]{4,3,2,1,0:T(8,128)(2,1)} collective-permute-done((bf16[2,19,3,16,128]{4,3,2,1,0:T(8,128)(2,1)}, bf16[2,19,3,16,128]{4,3,2,1,0:T(8,128)(2,1)}, u32[]{:S(2)}, u32[]{:S(2)}) %collective-permute-start.16) | collective-permute-done | bytes 466976 | tf_op jit(solution)/shard_map/ppermute | solution.py:49
  43.0 1.1 pad_maximum_fusion.rest_1_
  44.1 1.6 collective-permute-start.20
  45.8 3.0 %collective-permute-start.25 = (bf16[2,19,3,16,128]{4,3,2,1,0:T(8,128)(2,1)S(1)}, bf16[2,19,3,16,128]{4,3,2,1,0:T(8,128)(2,1)S(1)}, u32[]{:S(2)}, u32[]{:S(2)}) collective-permute-start(bf16[2,19,3,16,128]{4,3,2,1,0:T(8,128)(2,1)S(1)} %pad_maximum_fusion.8), channel_id=1, source_target_pairs={{0,4},{1,5},{2,6},{3,7},{4,0},{5,1},{6,2},{7,3},{8,12},{9,13},{10,... | collective-permute-start | bytes 1400840 | tf_op jit(solution)/shard_map/ppermute | solution.py:49
  49.3 1.5 collective-permute-start.2
  50.8 18.0 %collective-permute-done.6 = bf16[19,3,16,128]{3,2,1,0:T(8,128)(2,1)S(1)} collective-permute-done((bf16[19,3,16,128]{3,2,1,0:T(8,128)(2,1)S(1)}, bf16[19,3,16,128]{3,2,1,0:T(8,128)(2,1)S(1)}, u32[]{:S(2)}, u32[]{:S(2)}) %collective-permute-start.6) | collective-permute-done | bytes 233504 | tf_op jit(solution)/shard_map/ppermute | solution.py:49
  69.4 3.4 %collective-permute-done.1 = bf16[19,3,16,128]{3,2,1,0:T(8,128)(2,1)S(1)} collective-permute-done((bf16[19,3,16,128]{3,2,1,0:T(8,128)(2,1)S(1)}, bf16[19,3,16,128]{3,2,1,0:T(8,128)(2,1)S(1)}, u32[]{:S(2)}, u32[]{:S(2)}) %collective-permute-start.1) | collective-permute-done | bytes 233504 | tf_op jit(solution)/shard_map/ppermute | solution.py:49
  72.8 5.0 %collective-permute-done.2 = bf16[19,3,16,128]{3,2,1,0:T(8,128)(2,1)S(1)} collective-permute-done((bf16[19,3,16,128]{3,2,1,0:T(8,128)(2,1)S(1)}, bf16[19,3,16,128]{3,2,1,0:T(8,128)(2,1)S(1)}, u32[]{:S(2)}, u32[]{:S(2)}) %collective-permute-start.2) | collective-permute-done | bytes 233504 | tf_op jit(solution)/shard_map/ppermute | solution.py:49
  77.9 1.6 collective-permute-start.4
  80.5 1.5 collective-permute-start.29
  82.1 3.8 %collective-permute-done.11.rest_9_ = bf16[2,19,3,16,128]{4,3,2,1,0:T(8,128)(2,1)S(1)} collective-permute-done((bf16[2,19,3,16,128]{4,3,2,1,0:T(8,128)(2,1)S(1)}, bf16[2,19,3,16,128]{4,3,2,1,0:T(8,128)(2,1)S(1)}, u32[]{:S(2)}, u32[]{:S(2)}) %collective-permute-start.11) | collective-permute-done | bytes 466976 | tf_op jit(solution)/shard_map/ppermute | solution.py:49
  89.1 3.5 %collective-permute-start.12 = (bf16[2,19,3,16,128]{4,3,2,1,0:T(8,128)(2,1)S(1)}, bf16[2,19,3,16,128]{4,3,2,1,0:T(8,128)(2,1)S(1)}, u32[]{:S(2)}, u32[]{:S(2)}) collective-permute-start(bf16[2,19,3,16,128]{4,3,2,1,0:T(8,128)(2,1)S(1)} %collective-permute-done.11.rest_9_), channel_id=1, source_target_pairs={{0,8},{1,9},{2,10},{3,11},{4,12},{5,13},{6,14},{7,15},{8,0},{9,1},... | collective-permute-start | bytes 1400840 | tf_op jit(solution)/shard_map/ppermute | solution.py:49
  93.4 2.8 %collective-permute-start.9 = (bf16[2,19,3,16,128]{4,3,2,1,0:T(8,128)(2,1)S(1)}, bf16[2,19,3,16,128]{4,3,2,1,0:T(8,128)(2,1)S(1)}, u32[]{:S(2)}, u32[]{:S(2)}) collective-permute-start(bf16[2,19,3,16,128]{4,3,2,1,0:T(8,128)(2,1)S(1)} %collective-permute-done.8.rest_6_), channel_id=1, source_target_pairs={{0,16},{1,17},{2,18},{3,19},{4,20},{5,21},{6,22},{7,23},{16,0},{17... | collective-permute-start | bytes 1400840 | tf_op jit(solution)/shard_map/ppermute | solution.py:49
  97.0 7.9 %collective-permute-done.29.rest_5_ = bf16[4,19,3,16,128]{4,3,2,1,0:T(8,128)(2,1)S(1)} collective-permute-done((bf16[4,19,3,16,128]{4,3,2,1,0:T(8,128)(2,1)}, bf16[4,19,3,16,128]{4,3,2,1,0:T(8,128)(2,1)S(1)}, u32[]{:S(2)}, u32[]{:S(2)}) %collective-permute-start.29) | collective-permute-done | bytes 933920 | tf_op jit(solution)/shard_map/ppermute | solution.py:49
  105.9 3.1 %collective-permute-start.22 = (bf16[4,19,3,16,128]{4,3,2,1,0:T(8,128)(2,1)}, bf16[4,19,3,16,128]{4,3,2,1,0:T(8,128)(2,1)}, u32[]{:S(2)}, u32[]{:S(2)}) collective-permute-start(bf16[4,19,3,16,128]{4,3,2,1,0:T(8,128)(2,1)} %collective-permute-done.21.rest_6_), channel_id=1, source_target_pairs={{0,16},{1,17},{2,18},{3,19},{4,20},{5,21},{6,22},{7,23},{16,0},{17... | collective-permute-start | bytes 2801672 | tf_op jit(solution)/shard_map/ppermute | solution.py:49
  109.7 1.3 collective-permute-start.5
  111.0 1.3 collective-permute-start.14
  113.1 3.9 %collective-permute-start.10 = (bf16[2,19,3,16,128]{4,3,2,1,0:T(8,128)(2,1)S(1)}, bf16[2,19,3,16,128]{4,3,2,1,0:T(8,128)(2,1)S(1)}, u32[]{:S(2)}, u32[]{:S(2)}) collective-permute-start(bf16[2,19,3,16,128]{4,3,2,1,0:T(8,128)(2,1)S(1)} %collective-permute-done.9.rest_7_), channel_id=1, source_target_pairs={{0,8},{1,9},{2,10},{3,11},{4,12},{5,13},{6,14},{7,15},{16,24},{17,... | collective-permute-start | bytes 1400840 | tf_op jit(solution)/shard_map/ppermute | solution.py:49
  118.6 1.6 collective-permute-start.27
  121.3 3.1 %collective-permute-start.31 = (bf16[4,19,3,16,128]{4,3,2,1,0:T(8,128)(2,1)}, bf16[4,19,3,16,128]{4,3,2,1,0:T(8,128)(2,1)}, u32[]{:S(2)}, u32[]{:S(2)}) collective-permute-start(bf16[4,19,3,16,128]{4,3,2,1,0:T(8,128)(2,1)} %collective-permute-done.30.rest_6_), channel_id=1, source_target_pairs={{0,16},{1,17},{2,18},{3,19},{4,20},{5,21},{6,22},{7,23},{16,0},{17... | collective-permute-start | bytes 2801672 | tf_op jit(solution)/shard_map/ppermute | solution.py:49
  124.4 1.8 all_to_all.47
  126.2 4.1 %all-to-all-start.2 = ((bf16[4,32,1152]{2,1,0:T(8,128)(2,1)}), bf16[4,32,1152]{2,1,0:T(8,128)(2,1)}, u32[]{:S(2)}, u32[]{:S(2)}) async-start(bf16[4,32,1152]{2,1,0:T(8,128)(2,1)} %all_to_all.47), calls=%async_computation.2 | async-start | bytes 589824 | tf_op jit(solution)/shard_map/all_to_all | solution.py:410
  130.3 1.3 collective-permute-start.19
  131.6 4.9 %collective-permute-start.23 = (bf16[4,19,3,16,128]{4,3,2,1,0:T(8,128)(2,1)}, bf16[4,19,3,16,128]{4,3,2,1,0:T(8,128)(2,1)}, u32[]{:S(2)}, u32[]{:S(2)}) collective-permute-start(bf16[4,19,3,16,128]{4,3,2,1,0:T(8,128)(2,1)} %collective-permute-done.22.rest_7_), channel_id=1, source_target_pairs={{0,8},{1,9},{2,10},{3,11},{4,12},{5,13},{6,14},{7,15},{16,24},{17,... | collective-permute-start | bytes 2801672 | tf_op jit(solution)/shard_map/ppermute | solution.py:49
  137.9 1.3 pad_maximum_fusion.2.rest_0_
  145.5 5.7 %shard_map.77 = (bf16[128,1152]{1,0:T(8,128)(2,1)S(1)}, bf16[128,1792]{1,0:T(8,128)(2,1)S(1)}, f32[8,128,128]{2,1,0:T(8,128)S(1)}, bf16[128,576]{1,0:T(8,128)(2,1)S(1)}, f32[128,1]{1,0:T(8,128)S(1)}) custom-call(s32[12]{0:T(128)S(1)} %stack.72.place_ref, f32[3,8]{1,0:T(4,128)S(1)} %copy-done.57, bf16[128,1152]{1,0:T(8,128)(2,1)S(1)} %reshape_transpose.4.x_ref, ...), custom_call_target="tpu_custom_call" | custom-call | flops 679477248 | bytes 6291456 | tf_op jit(solution)/shard_map/pallas_call | solution.py:330
  154.1 10.5 %all_to_all.64 = bf16[4,32,1152]{2,1,0:T(8,128)(2,1)} all-to-all(bf16[4,32,1152]{2,1,0:T(8,128)(2,1)} %bitcast.70), channel_id=1, replica_groups=mesh['ha'=4,'wa'=8] {'ha'}, dimensions={0} | all-to-all | bytes 589824 | tf_op jit(solution)/shard_map/all_to_all | solution.py:410
  164.7 6.8 %all-to-all-start.3 = ((bf16[8,16,1152]{2,1,0:T(8,128)(2,1)}), bf16[8,16,1152]{2,1,0:T(8,128)(2,1)}, u32[]{:S(2)}, u32[]{:S(2)}) async-start(bf16[8,16,1152]{2,1,0:T(8,128)(2,1)} %bitcast.34), calls=%async_computation.3 | async-start | bytes 589824 | tf_op jit(solution)/shard_map/all_to_all | solution.py:410
  171.6 1.4 collective-permute-start.28
  173.0 4.9 %collective-permute-start.32 = (bf16[4,19,3,16,128]{4,3,2,1,0:T(8,128)(2,1)}, bf16[4,19,3,16,128]{4,3,2,1,0:T(8,128)(2,1)}, u32[]{:S(2)}, u32[]{:S(2)}) collective-permute-start(bf16[4,19,3,16,128]{4,3,2,1,0:T(8,128)(2,1)} %collective-permute-done.31.rest_7_), channel_id=1, source_target_pairs={{0,8},{1,9},{2,10},{3,11},{4,12},{5,13},{6,14},{7,15},{16,24},{17,... | collective-permute-start | bytes 2801672 | tf_op jit(solution)/shard_map/ppermute | solution.py:49
  178.0 1.2 pad_maximum_fusion.3.rest_0_
  179.3 1.2 copy-done.4
  180.5 6.4 %shard_map.78 = (bf16[128,1152]{1,0:T(8,128)(2,1)S(1)}, bf16[128,1792]{1,0:T(8,128)(2,1)S(1)}, f32[8,128,128]{2,1,0:T(8,128)S(1)}, bf16[128,576]{1,0:T(8,128)(2,1)S(1)}, f32[128,1]{1,0:T(8,128)S(1)}) custom-call(s32[12]{0:T(128)S(1)} %stack.72.place_ref, f32[3,8]{1,0:T(4,128)S(1)} %copy-done.57, bf16[128,1152]{1,0:T(8,128)(2,1)S(1)} %bitcast.63, ...), custom_call_target="tpu_custom_call" | custom-call | flops 679477248 | bytes 6291456 | tf_op jit(solution)/shard_map/pallas_call | solution.py:330
  190.5 6.0 %all-to-all-start.1 = ((bf16[8,16,1152]{2,1,0:T(8,128)(2,1)}), bf16[8,16,1152]{2,1,0:T(8,128)(2,1)}, u32[]{:S(2)}, u32[]{:S(2)}) async-start(bf16[8,16,1152]{2,1,0:T(8,128)(2,1)} %bitcast.69), calls=%async_computation.1 | async-start | bytes 589824 | tf_op jit(solution)/shard_map/all_to_all | solution.py:410
  196.5 2.1 pad_maximum_fusion.4.rest_0_
  199.3 5.7 %all-to-all-done.1 = bf16[8,16,1152]{2,1,0:T(8,128)(2,1)} async-done(((bf16[8,16,1152]{2,1,0:T(8,128)(2,1)}), bf16[8,16,1152]{2,1,0:T(8,128)(2,1)}, u32[]{:S(2)}, u32[]{:S(2)}) %all-to-all-start.1) | async-done | bytes 294944 | tf_op jit(solution)/shard_map/all_to_all | solution.py:410
  206.1 1.2 copy-done.36
  208.2 10.7 %shard_map.79 = bf16[128,1280]{1,0:T(8,128)(2,1)S(1)} custom-call(s32[12]{0:T(128)S(1)} %stack.72.place_ref, f32[3,8]{1,0:T(4,128)S(1)} %copy-done.57, bf16[128,1152]{1,0:T(8,128)(2,1)} %bitcast.33.x_ref, f32[3,1152]{1,0:T(4,128)S(1)} %copy-done.41, f32[128,128]{1,0:T(8,128)S(1)} %copy-done.48, bf16[128,1152]{1,0:T(8,128)(2,1)} %bitcast.35.outgrad_ref, ...), custom_call_target="tpu_custom_call" | custom-call | flops 1358954496 | bytes 6291456 | tf_op jit(solution)/shard_map/pallas_call | solution.py:330
  218.8 12.3 %all_to_all.65 = bf16[8,16,1280]{2,1,0:T(8,128)(2,1)S(1)} all-to-all(bf16[8,16,1280]{2,1,0:T(8,128)(2,1)S(1)} %bitcast.66), channel_id=1, replica_groups=mesh['ha'=4,'wa'=8] {'wa'}, dimensions={0} | all-to-all | bytes 655360 | tf_op jit(solution)/shard_map/all_to_all | solution.py:410
  231.3 8.0 %shard_map.80 = bf16[128,1280]{1,0:T(8,128)(2,1)S(1)} custom-call(s32[12]{0:T(128)S(1)} %stack.72.place_ref, f32[3,8]{1,0:T(4,128)S(1)} %copy-done.57, bf16[128,1152]{1,0:T(8,128)(2,1)S(1)} %bitcast.64, f32[3,1152]{1,0:T(4,128)S(1)} %copy-done.41, bf16[128,1280]{1,0:T(8,128)(2,1)S(1)} %bitcast.67, bf16[128,1792]{1,0:T(8,128)(2,1)S(1)} %copy-done.45, ...), custom_call_target="tpu_custom_call" | custom-call | flops 679477248 | bytes 6291456 | tf_op jit(solution)/shard_map/pallas_call | solution.py:330
  239.3 9.1 %all_to_all.66 = bf16[4,32,1280]{2,1,0:T(8,128)(2,1)S(1)} all-to-all(bf16[4,32,1280]{2,1,0:T(8,128)(2,1)S(1)} %bitcast.68), channel_id=1, replica_groups=mesh['ha'=4,'wa'=8] {'ha'}, dimensions={0} | all-to-all | bytes 655360 | tf_op jit(solution)/shard_map/all_to_all | solution.py:410
  248.5 6.9 %shard_map.81 = bf16[128,1280]{1,0:T(8,128)(2,1)S(1)} custom-call(s32[12]{0:T(128)S(1)} %stack.72.place_ref, f32[3,8]{1,0:T(4,128)S(1)} %copy-done.57, bf16[128,1152]{1,0:T(8,128)(2,1)S(1)} %copy-done.11, f32[3,1152]{1,0:T(4,128)S(1)} %copy-done.41, bf16[128,1280]{1,0:T(8,128)(2,1)S(1)} %bitcast.65, bf16[128,1792]{1,0:T(8,128)(2,1)S(1)} %copy-done.43, ...), custom_call_target="tpu_custom_call" | custom-call | flops 679477248 | bytes 6291456 | tf_op jit(solution)/shard_map/pallas_call | solution.py:330
  (213 shorter events, 36.0 us)
Async XLA Ops:
  4.2 8.8 %collective-permute-start.15 = (bf16[1,19,3,16,128]{4,3,2,1,0:T(8,128)(2,1)S(1)}, bf16[1,19,3,16,128]{4,3,2,1,0:T(8,128)(2,1)S(1)}, u32[]{:S(2)}, u32[]{:S(2)}) collective-permute-start(bf16[1,19,3,16,128]{4,3,2,1,0:T(8,128)(2,1)S(1)} %fusion.1), channel_id=1, source_target_pairs={{0,2},{1,3},{2,0},{3,1},{4,6},{5,7},{6,4},{7,5},{8,10},{9,11},{10,... | collective-permute-start | bytes 700424 | tf_op jit(solution)/shard_map/ppermute | solution.py:49
  13.8 29.2 %collective-permute-start.16 = (bf16[2,19,3,16,128]{4,3,2,1,0:T(8,128)(2,1)}, bf16[2,19,3,16,128]{4,3,2,1,0:T(8,128)(2,1)}, u32[]{:S(2)}, u32[]{:S(2)}) collective-permute-start(bf16[2,19,3,16,128]{4,3,2,1,0:T(8,128)(2,1)} %pad_maximum_fusion.7), channel_id=1, source_target_pairs={{0,4},{1,5},{2,6},{3,7},{4,0},{5,1},{6,2},{7,3},{8,12},{9,13},{10,... | collective-permute-start | bytes 1400840 | tf_op jit(solution)/shard_map/ppermute | solution.py:49
  18.2 27.5 %collective-permute-start.24 = (bf16[1,19,3,16,128]{4,3,2,1,0:T(8,128)(2,1)S(1)}, bf16[1,19,3,16,128]{4,3,2,1,0:T(8,128)(2,1)S(1)}, u32[]{:S(2)}, u32[]{:S(2)}) collective-permute-start(bf16[1,19,3,16,128]{4,3,2,1,0:T(8,128)(2,1)S(1)} %fusion), channel_id=1, source_target_pairs={{0,2},{1,3},{2,0},{3,1},{4,6},{5,7},{6,4},{7,5},{8,10},{9,11},{10,... | collective-permute-start | bytes 700424 | tf_op jit(solution)/shard_map/ppermute | solution.py:49
  20.2 22.8 %copy-start.65 = (bf16[1,19,3,16,128]{4,3,2,1,0:T(8,128)(2,1)S(1)}, bf16[1,19,3,16,128]{4,3,2,1,0:T(8,128)(2,1)}, u32[]{:S(2)}) copy-start(bf16[1,19,3,16,128]{4,3,2,1,0:T(8,128)(2,1)} %copy-done.64) | copy-start | bytes 700420
  20.8 27.9 %collective-permute-start.7 = (bf16[19,3,16,128]{3,2,1,0:T(8,128)(2,1)S(1)}, bf16[19,3,16,128]{3,2,1,0:T(8,128)(2,1)S(1)}, u32[]{:S(2)}, u32[]{:S(2)}) collective-permute-start(bf16[19,3,16,128]{3,2,1,0:T(8,128)(2,1)S(1)} %fusion.3), channel_id=1, source_target_pairs={{0,6},{1,7},{2,4},{3,5},{4,2},{5,3},{6,0},{7,1},{8,14},{9,15},{10,... | collective-permute-start | bytes 700424 | tf_op jit(solution)/shard_map/ppermute | solution.py:49
  20.9 28.3 %collective-permute-start = (bf16[19,3,16,128]{3,2,1,0:T(8,128)(2,1)S(1)}, bf16[19,3,16,128]{3,2,1,0:T(8,128)(2,1)S(1)}, u32[]{:S(2)}, u32[]{:S(2)}) collective-permute-start(bf16[19,3,16,128]{3,2,1,0:T(8,128)(2,1)S(1)} %fusion.3), channel_id=1, source_target_pairs={{0,2},{1,3},{2,0},{3,1},{4,6},{5,7},{6,4},{7,5},{8,10},{9,11},{10,... | collective-permute-start | bytes 700424 | tf_op jit(solution)/shard_map/ppermute | solution.py:49
  44.1 41.7 %collective-permute-start.20 = (bf16[4,19,3,16,128]{4,3,2,1,0:T(8,128)(2,1)S(1)}, bf16[4,19,3,16,128]{4,3,2,1,0:T(8,128)(2,1)S(1)}, u32[]{:S(2)}, u32[]{:S(2)}) collective-permute-start(bf16[4,19,3,16,128]{4,3,2,1,0:T(8,128)(2,1)S(1)} %pad_maximum_fusion.rest_1_), channel_id=1, source_target_pairs={{0,1},{1,0},{2,3},{3,2},{4,5},{5,4},{6,7},{7,6},{8,9},{9,8},{10,11... | collective-permute-start | bytes 2801672 | tf_op jit(solution)/shard_map/ppermute | solution.py:49
  45.7 23.1 %collective-permute-start.6 = (bf16[19,3,16,128]{3,2,1,0:T(8,128)(2,1)S(1)}, bf16[19,3,16,128]{3,2,1,0:T(8,128)(2,1)S(1)}, u32[]{:S(2)}, u32[]{:S(2)}) collective-permute-start(bf16[19,3,16,128]{3,2,1,0:T(8,128)(2,1)S(1)} %fusion.3), channel_id=1, source_target_pairs={{0,4},{1,5},{2,6},{3,7},{4,0},{5,1},{6,2},{7,3},{8,12},{9,13},{10,... | collective-permute-start | bytes 700424 | tf_op jit(solution)/shard_map/ppermute | solution.py:49
  45.8 33.7 %collective-permute-start.25 = (bf16[2,19,3,16,128]{4,3,2,1,0:T(8,128)(2,1)S(1)}, bf16[2,19,3,16,128]{4,3,2,1,0:T(8,128)(2,1)S(1)}, u32[]{:S(2)}, u32[]{:S(2)}) collective-permute-start(bf16[2,19,3,16,128]{4,3,2,1,0:T(8,128)(2,1)S(1)} %pad_maximum_fusion.8), channel_id=1, source_target_pairs={{0,4},{1,5},{2,6},{3,7},{4,0},{5,1},{6,2},{7,3},{8,12},{9,13},{10,... | collective-permute-start | bytes 1400840 | tf_op jit(solution)/shard_map/ppermute | solution.py:49
  48.8 24.1 %collective-permute-start.1 = (bf16[19,3,16,128]{3,2,1,0:T(8,128)(2,1)S(1)}, bf16[19,3,16,128]{3,2,1,0:T(8,128)(2,1)S(1)}, u32[]{:S(2)}, u32[]{:S(2)}) collective-permute-start(bf16[19,3,16,128]{3,2,1,0:T(8,128)(2,1)S(1)} %fusion.3), channel_id=1, source_target_pairs={{0,1},{1,0},{2,3},{3,2},{4,5},{5,4},{6,7},{7,6},{8,9},{9,8},{10,11... | collective-permute-start | bytes 700424 | tf_op jit(solution)/shard_map/ppermute | solution.py:49
  49.3 28.6 %collective-permute-start.2 = (bf16[19,3,16,128]{3,2,1,0:T(8,128)(2,1)S(1)}, bf16[19,3,16,128]{3,2,1,0:T(8,128)(2,1)S(1)}, u32[]{:S(2)}, u32[]{:S(2)}) collective-permute-start(bf16[19,3,16,128]{3,2,1,0:T(8,128)(2,1)S(1)} %collective-permute-done), channel_id=1, source_target_pairs={{0,1},{1,0},{2,3},{3,2},{4,5},{5,4},{6,7},{7,6},{8,9},{9,8},{10,11... | collective-permute-start | bytes 700424 | tf_op jit(solution)/shard_map/ppermute | solution.py:49
  68.8 17.0 %collective-permute-start.11 = (bf16[2,19,3,16,128]{4,3,2,1,0:T(8,128)(2,1)S(1)}, bf16[2,19,3,16,128]{4,3,2,1,0:T(8,128)(2,1)S(1)}, u32[]{:S(2)}, u32[]{:S(2)}) collective-permute-start(bf16[2,19,3,16,128]{4,3,2,1,0:T(8,128)(2,1)S(1)} %pad_maximum_fusion.6.rest_5_), channel_id=1, source_target_pairs={{0,1},{1,0},{2,3},{3,2},{4,5},{5,4},{6,7},{7,6},{8,9},{9,8},{10,11... | collective-permute-start | bytes 1400840 | tf_op jit(solution)/shard_map/ppermute | solution.py:49
  77.9 9.1 %collective-permute-start.4 = (bf16[3,19,3,16,128]{4,3,2,1,0:T(8,128)(2,1)S(1)}, bf16[3,19,3,16,128]{4,3,2,1,0:T(8,128)(2,1)}, u32[]{:S(2)}, u32[]{:S(2)}) collective-permute-start(bf16[3,19,3,16,128]{4,3,2,1,0:T(8,128)(2,1)S(1)} %pad_maximum_fusion.5.rest_1_), channel_id=1, source_target_pairs={{8,24},{9,25},{10,26},{11,27},{12,28},{13,29},{14,30},{15,31},{24,... | collective-permute-start | bytes 2101256 | tf_op jit(solution)/shard_map/ppermute | solution.py:49
  79.5 6.9 %collective-permute-start.8 = (bf16[2,19,3,16,128]{4,3,2,1,0:T(8,128)(2,1)S(1)}, bf16[2,19,3,16,128]{4,3,2,1,0:T(8,128)(2,1)S(1)}, u32[]{:S(2)}, u32[]{:S(2)}) collective-permute-start(bf16[2,19,3,16,128]{4,3,2,1,0:T(8,128)(2,1)S(1)} %pad_maximum_fusion.6.rest_5_), channel_id=1, source_target_pairs={{0,8},{1,9},{2,10},{3,11},{4,12},{5,13},{6,14},{7,15},{8,0},{9,1},... | collective-permute-start | bytes 1400840 | tf_op jit(solution)/shard_map/ppermute | solution.py:49
  80.5 58.6 %copy-start.41 = (f32[3,1152]{1,0:T(4,128)S(1)}, f32[3,1152]{1,0:T(4,128)}, u32[]{:S(2)}) copy-start(f32[3,1152]{1,0:T(4,128)} %gain_ref.9) | copy-start | bytes 41476
  80.5 58.7 %copy-start.57 = (f32[3,8]{1,0:T(4,128)S(1)}, f32[3,8]{1,0:T(4,128)}, u32[]{:S(2)}) copy-start(f32[3,8]{1,0:T(4,128)} %gates_ref.9) | copy-start | bytes 292
  80.5 24.4 %collective-permute-start.29 = (bf16[4,19,3,16,128]{4,3,2,1,0:T(8,128)(2,1)}, bf16[4,19,3,16,128]{4,3,2,1,0:T(8,128)(2,1)S(1)}, u32[]{:S(2)}, u32[]{:S(2)}) collective-permute-start(bf16[4,19,3,16,128]{4,3,2,1,0:T(8,128)(2,1)} %pad_maximum_fusion.1.rest_1_), channel_id=1, source_target_pairs={{0,1},{1,0},{2,3},{3,2},{4,5},{5,4},{6,7},{7,6},{8,9},{9,8},{10,11... | collective-permute-start | bytes 2801672 | tf_op jit(solution)/shard_map/ppermute | solution.py:49
  85.8 2.4 collective-permute-start.3
  85.9 51.9 %copy-start = (bf16[4,19,3,16,128]{4,3,2,1,0:T(8,128)(2,1)}, bf16[4,19,3,16,128]{4,3,2,1,0:T(8,128)(2,1)S(1)}, u32[]{:S(2)}) copy-start(bf16[4,19,3,16,128]{4,3,2,1,0:T(8,128)(2,1)S(1)} %collective-permute-done.20.rest_5_) | copy-start | bytes 2801668
  85.9 20.0 %collective-permute-start.21 = (bf16[4,19,3,16,128]{4,3,2,1,0:T(8,128)(2,1)S(1)}, bf16[4,19,3,16,128]{4,3,2,1,0:T(8,128)(2,1)}, u32[]{:S(2)}, u32[]{:S(2)}) collective-permute-start(bf16[4,19,3,16,128]{4,3,2,1,0:T(8,128)(2,1)S(1)} %collective-permute-done.20.rest_5_), channel_id=1, source_target_pairs={{0,8},{1,9},{2,10},{3,11},{4,12},{5,13},{6,14},{7,15},{8,0},{9,1},... | collective-permute-start | bytes 2801672 | tf_op jit(solution)/shard_map/ppermute | solution.py:49
  86.4 7.0 %collective-permute-start.13 = (bf16[2,19,3,16,128]{4,3,2,1,0:T(8,128)(2,1)S(1)}, bf16[2,19,3,16,128]{4,3,2,1,0:T(8,128)(2,1)S(1)}, u32[]{:S(2)}, u32[]{:S(2)}) collective-permute-start(bf16[2,19,3,16,128]{4,3,2,1,0:T(8,128)(2,1)S(1)} %collective-permute-done.11.rest_9_), channel_id=1, source_target_pairs={{8,24},{9,25},{10,26},{11,27},{12,28},{13,29},{14,30},{15,31},{24,... | collective-permute-start | bytes 1400840 | tf_op jit(solution)/shard_map/ppermute | solution.py:49
  87.1 26.1 %collective-permute-start.18 = (bf16[4,19,3,16,128]{4,3,2,1,0:T(8,128)(2,1)S(1)}, bf16[4,19,3,16,128]{4,3,2,1,0:T(8,128)(2,1)S(1)}, u32[]{:S(2)}, u32[]{:S(2)}) collective-permute-start(bf16[4,19,3,16,128]{4,3,2,1,0:T(8,128)(2,1)S(1)} %pad_maximum_fusion.rest_1_), channel_id=1, source_target_pairs={{8,24},{9,25},{10,26},{11,27},{12,28},{13,29},{14,30},{15,31},{24,... | collective-permute-start | bytes 2801672 | tf_op jit(solution)/shard_map/ppermute | solution.py:49
  89.1 19.8 %collective-permute-start.12 = (bf16[2,19,3,16,128]{4,3,2,1,0:T(8,128)(2,1)S(1)}, bf16[2,19,3,16,128]{4,3,2,1,0:T(8,128)(2,1)S(1)}, u32[]{:S(2)}, u32[]{:S(2)}) collective-permute-start(bf16[2,19,3,16,128]{4,3,2,1,0:T(8,128)(2,1)S(1)} %collective-permute-done.11.rest_9_), channel_id=1, source_target_pairs={{0,8},{1,9},{2,10},{3,11},{4,12},{5,13},{6,14},{7,15},{8,0},{9,1},... | collective-permute-start | bytes 1400840 | tf_op jit(solution)/shard_map/ppermute | solution.py:49
  93.4 17.7 %collective-permute-start.9 = (bf16[2,19,3,16,128]{4,3,2,1,0:T(8,128)(2,1)S(1)}, bf16[2,19,3,16,128]{4,3,2,1,0:T(8,128)(2,1)S(1)}, u32[]{:S(2)}, u32[]{:S(2)}) collective-permute-start(bf16[2,19,3,16,128]{4,3,2,1,0:T(8,128)(2,1)S(1)} %collective-permute-done.8.rest_6_), channel_id=1, source_target_pairs={{0,16},{1,17},{2,18},{3,19},{4,20},{5,21},{6,22},{7,23},{16,0},{17... | collective-permute-start | bytes 1400840 | tf_op jit(solution)/shard_map/ppermute | solution.py:49
  104.9 16.4 %collective-permute-start.30 = (bf16[4,19,3,16,128]{4,3,2,1,0:T(8,128)(2,1)S(1)}, bf16[4,19,3,16,128]{4,3,2,1,0:T(8,128)(2,1)}, u32[]{:S(2)}, u32[]{:S(2)}) collective-permute-start(bf16[4,19,3,16,128]{4,3,2,1,0:T(8,128)(2,1)S(1)} %collective-permute-done.29.rest_5_), channel_id=1, source_target_pairs={{0,8},{1,9},{2,10},{3,11},{4,12},{5,13},{6,14},{7,15},{8,0},{9,1},... | collective-permute-start | bytes 2801672 | tf_op jit(solution)/shard_map/ppermute | solution.py:49
  105.9 25.8 %collective-permute-start.22 = (bf16[4,19,3,16,128]{4,3,2,1,0:T(8,128)(2,1)}, bf16[4,19,3,16,128]{4,3,2,1,0:T(8,128)(2,1)}, u32[]{:S(2)}, u32[]{:S(2)}) collective-permute-start(bf16[4,19,3,16,128]{4,3,2,1,0:T(8,128)(2,1)} %collective-permute-done.21.rest_6_), channel_id=1, source_target_pairs={{0,16},{1,17},{2,18},{3,19},{4,20},{5,21},{6,22},{7,23},{16,0},{17... | collective-permute-start | bytes 2801672 | tf_op jit(solution)/shard_map/ppermute | solution.py:49
  109.7 20.6 %collective-permute-start.5 = (bf16[3,19,3,16,128]{4,3,2,1,0:T(8,128)(2,1)}, bf16[3,19,3,16,128]{4,3,2,1,0:T(8,128)(2,1)}, u32[]{:S(2)}, u32[]{:S(2)}) collective-permute-start(bf16[3,19,3,16,128]{4,3,2,1,0:T(8,128)(2,1)} %collective-permute-done.4.rest_3_), channel_id=1, source_target_pairs={{8,0},{9,1},{10,2},{11,3},{12,4},{13,5},{14,6},{15,7},{24,16},{25,... | collective-permute-start | bytes 2101256 | tf_op jit(solution)/shard_map/ppermute | solution.py:49
  111.0 6.8 %collective-permute-start.14 = (bf16[2,19,3,16,128]{4,3,2,1,0:T(8,128)(2,1)S(1)}, bf16[2,19,3,16,128]{4,3,2,1,0:T(8,128)(2,1)S(1)}, u32[]{:S(2)}, u32[]{:S(2)}) collective-permute-start(bf16[2,19,3,16,128]{4,3,2,1,0:T(8,128)(2,1)S(1)} %collective-permute-done.13.rest_11_), channel_id=1, source_target_pairs={{8,0},{9,1},{10,2},{11,3},{12,4},{13,5},{14,6},{15,7},{24,16},{25,... | collective-permute-start | bytes 1400840 | tf_op jit(solution)/shard_map/ppermute | solution.py:49
  113.1 7.1 %collective-permute-start.10 = (bf16[2,19,3,16,128]{4,3,2,1,0:T(8,128)(2,1)S(1)}, bf16[2,19,3,16,128]{4,3,2,1,0:T(8,128)(2,1)S(1)}, u32[]{:S(2)}, u32[]{:S(2)}) collective-permute-start(bf16[2,19,3,16,128]{4,3,2,1,0:T(8,128)(2,1)S(1)} %collective-permute-done.9.rest_7_), channel_id=1, source_target_pairs={{0,8},{1,9},{2,10},{3,11},{4,12},{5,13},{6,14},{7,15},{16,24},{17,... | collective-permute-start | bytes 1400840 | tf_op jit(solution)/shard_map/ppermute | solution.py:49
  118.6 52.8 %collective-permute-start.27 = (bf16[4,19,3,16,128]{4,3,2,1,0:T(8,128)(2,1)}, bf16[4,19,3,16,128]{4,3,2,1,0:T(8,128)(2,1)}, u32[]{:S(2)}, u32[]{:S(2)}) collective-permute-start(bf16[4,19,3,16,128]{4,3,2,1,0:T(8,128)(2,1)} %pad_maximum_fusion.1.rest_1_), channel_id=1, source_target_pairs={{8,24},{9,25},{10,26},{11,27},{12,28},{13,29},{14,30},{15,31},{24,... | collective-permute-start | bytes 2801672 | tf_op jit(solution)/shard_map/ppermute | solution.py:49
  121.0 50.5 %collective-permute-start.17 = (bf16[4,19,3,16,128]{4,3,2,1,0:T(8,128)(2,1)S(1)}, bf16[4,19,3,16,128]{4,3,2,1,0:T(8,128)(2,1)}, u32[]{:S(2)}, u32[]{:S(2)}) collective-permute-start(bf16[4,19,3,16,128]{4,3,2,1,0:T(8,128)(2,1)S(1)} %pad_maximum_fusion.rest_1_), channel_id=1, source_target_pairs={{0,8},{1,9},{2,10},{3,11},{4,12},{5,13},{6,14},{7,15},{8,0},{9,1},... | collective-permute-start | bytes 2801672 | tf_op jit(solution)/shard_map/ppermute | solution.py:49
  121.3 51.7 %collective-permute-start.31 = (bf16[4,19,3,16,128]{4,3,2,1,0:T(8,128)(2,1)}, bf16[4,19,3,16,128]{4,3,2,1,0:T(8,128)(2,1)}, u32[]{:S(2)}, u32[]{:S(2)}) collective-permute-start(bf16[4,19,3,16,128]{4,3,2,1,0:T(8,128)(2,1)} %collective-permute-done.30.rest_6_), channel_id=1, source_target_pairs={{0,16},{1,17},{2,18},{3,19},{4,20},{5,21},{6,22},{7,23},{16,0},{17... | collective-permute-start | bytes 2801672 | tf_op jit(solution)/shard_map/ppermute | solution.py:49
  126.2 27.9 %all-to-all-start.2 = ((bf16[4,32,1152]{2,1,0:T(8,128)(2,1)}), bf16[4,32,1152]{2,1,0:T(8,128)(2,1)}, u32[]{:S(2)}, u32[]{:S(2)}) async-start(bf16[4,32,1152]{2,1,0:T(8,128)(2,1)} %all_to_all.47), calls=%async_computation.2 | async-start | bytes 589824 | tf_op jit(solution)/shard_map/all_to_all | solution.py:410
  130.3 48.9 %collective-permute-start.19 = (bf16[4,19,3,16,128]{4,3,2,1,0:T(8,128)(2,1)}, bf16[4,19,3,16,128]{4,3,2,1,0:T(8,128)(2,1)}, u32[]{:S(2)}, u32[]{:S(2)}) collective-permute-start(bf16[4,19,3,16,128]{4,3,2,1,0:T(8,128)(2,1)} %copy-done.3), channel_id=1, source_target_pairs={{8,0},{9,1},{10,2},{11,3},{12,4},{13,5},{14,6},{15,7},{24,16},{25,... | collective-permute-start | bytes 2801672 | tf_op jit(solution)/shard_map/ppermute | solution.py:49
  131.6 47.6 %collective-permute-start.23 = (bf16[4,19,3,16,128]{4,3,2,1,0:T(8,128)(2,1)}, bf16[4,19,3,16,128]{4,3,2,1,0:T(8,128)(2,1)}, u32[]{:S(2)}, u32[]{:S(2)}) collective-permute-start(bf16[4,19,3,16,128]{4,3,2,1,0:T(8,128)(2,1)} %collective-permute-done.22.rest_7_), channel_id=1, source_target_pairs={{0,8},{1,9},{2,10},{3,11},{4,12},{5,13},{6,14},{7,15},{16,24},{17,... | collective-permute-start | bytes 2801672 | tf_op jit(solution)/shard_map/ppermute | solution.py:49
  154.1 18.9 %copy-start.49 = (bf16[128,576]{1,0:T(8,128)(2,1)}, bf16[128,576]{1,0:T(8,128)(2,1)S(1)}, u32[]{:S(2)}) copy-start(bf16[128,576]{1,0:T(8,128)(2,1)S(1)} %get-tuple-element.20.att_ref) | copy-start | bytes 442372
  164.7 25.8 %all-to-all-start.3 = ((bf16[8,16,1152]{2,1,0:T(8,128)(2,1)}), bf16[8,16,1152]{2,1,0:T(8,128)(2,1)}, u32[]{:S(2)}, u32[]{:S(2)}) async-start(bf16[8,16,1152]{2,1,0:T(8,128)(2,1)} %bitcast.34), calls=%async_computation.3 | async-start | bytes 589824 | tf_op jit(solution)/shard_map/all_to_all | solution.py:410
  171.5 27.8 %collective-permute-start.26 = (bf16[4,19,3,16,128]{4,3,2,1,0:T(8,128)(2,1)}, bf16[4,19,3,16,128]{4,3,2,1,0:T(8,128)(2,1)}, u32[]{:S(2)}, u32[]{:S(2)}) collective-permute-start(bf16[4,19,3,16,128]{4,3,2,1,0:T(8,128)(2,1)} %pad_maximum_fusion.1.rest_1_), channel_id=1, source_target_pairs={{0,8},{1,9},{2,10},{3,11},{4,12},{5,13},{6,14},{7,15},{8,0},{9,1},... | collective-permute-start | bytes 2801672 | tf_op jit(solution)/shard_map/ppermute | solution.py:49
  171.6 27.7 %collective-permute-start.28 = (bf16[4,19,3,16,128]{4,3,2,1,0:T(8,128)(2,1)}, bf16[4,19,3,16,128]{4,3,2,1,0:T(8,128)(2,1)}, u32[]{:S(2)}, u32[]{:S(2)}) collective-permute-start(bf16[4,19,3,16,128]{4,3,2,1,0:T(8,128)(2,1)} %collective-permute-done.27.rest_3_), channel_id=1, source_target_pairs={{8,0},{9,1},{10,2},{11,3},{12,4},{13,5},{14,6},{15,7},{24,16},{25,... | collective-permute-start | bytes 2801672 | tf_op jit(solution)/shard_map/ppermute | solution.py:49
  173.0 26.3 %collective-permute-start.32 = (bf16[4,19,3,16,128]{4,3,2,1,0:T(8,128)(2,1)}, bf16[4,19,3,16,128]{4,3,2,1,0:T(8,128)(2,1)}, u32[]{:S(2)}, u32[]{:S(2)}) collective-permute-start(bf16[4,19,3,16,128]{4,3,2,1,0:T(8,128)(2,1)} %collective-permute-done.31.rest_7_), channel_id=1, source_target_pairs={{0,8},{1,9},{2,10},{3,11},{4,12},{5,13},{6,14},{7,15},{16,24},{17,... | collective-permute-start | bytes 2801672 | tf_op jit(solution)/shard_map/ppermute | solution.py:49
  190.5 14.5 %all-to-all-start.1 = ((bf16[8,16,1152]{2,1,0:T(8,128)(2,1)}), bf16[8,16,1152]{2,1,0:T(8,128)(2,1)}, u32[]{:S(2)}, u32[]{:S(2)}) async-start(bf16[8,16,1152]{2,1,0:T(8,128)(2,1)} %bitcast.69), calls=%async_computation.1 | async-start | bytes 589824 | tf_op jit(solution)/shard_map/all_to_all | solution.py:410
  208.1 23.0 %copy-start.2 = (bf16[4,19,3,16,128]{4,3,2,1,0:T(8,128)(2,1)S(1)}, bf16[4,19,3,16,128]{4,3,2,1,0:T(8,128)(2,1)}, u32[]{:S(2)}) copy-start(bf16[4,19,3,16,128]{4,3,2,1,0:T(8,128)(2,1)} %copy-done) | copy-start | bytes 2801668
  208.1 23.0 %copy-start.5 = (bf16[4,19,3,16,128]{4,3,2,1,0:T(8,128)(2,1)S(1)}, bf16[4,19,3,16,128]{4,3,2,1,0:T(8,128)(2,1)}, u32[]{:S(2)}) copy-start(bf16[4,19,3,16,128]{4,3,2,1,0:T(8,128)(2,1)} %copy-done.3) | copy-start | bytes 2801668
  208.1 23.0 %copy-start.13 = (bf16[4,32,1152]{2,1,0:T(8,128)(2,1)S(1)}, bf16[4,32,1152]{2,1,0:T(8,128)(2,1)}, u32[]{:S(2)}) copy-start(bf16[4,32,1152]{2,1,0:T(8,128)(2,1)} %all_to_all.64) | copy-start | bytes 884740
  208.1 23.0 %copy-start.40 = (f32[8,128,128]{2,1,0:T(8,128)S(1)}, f32[8,128,128]{2,1,0:T(8,128)}, u32[]{:S(2)}) copy-start(f32[8,128,128]{2,1,0:T(8,128)} %copy-done.39) | copy-start | bytes 1572868
  208.1 23.0 %copy-start.45 = (bf16[128,1792]{1,0:T(8,128)(2,1)S(1)}, bf16[128,1792]{1,0:T(8,128)(2,1)}, u32[]{:S(2)}) copy-start(bf16[128,1792]{1,0:T(8,128)(2,1)} %copy-done.44) | copy-start | bytes 1376260
  208.1 23.0 %copy-start.52 = (bf16[128,576]{1,0:T(8,128)(2,1)S(1)}, bf16[128,576]{1,0:T(8,128)(2,1)}, u32[]{:S(2)}) copy-start(bf16[128,576]{1,0:T(8,128)(2,1)} %copy-done.51) | copy-start | bytes 442372
  208.2 23.0 %copy-start.56 = (f32[128,1]{1,0:T(8,128)S(1)}, f32[128,1]{1,0:T(8,128)}, u32[]{:S(2)}) copy-start(f32[128,1]{1,0:T(8,128)} %copy-done.55) | copy-start | bytes 1540
  (54 other events, 311.9 us)

commit v2 on v1

v2 whole, which is shorter than its diff:
```python
import functools

import jax
import jax.numpy as jnp
from jax import lax
from jax.experimental import pallas as pl
from jax.experimental.pallas import tpu as pltpu
from jax.sharding import PartitionSpec as P

LANES = 128
ROWS = 16
AXES = ("ha", "wa")
NT = (((1,), (1,)), ((), ()))
TN = (((0,), (0,)), ((), ()))


def ceil_to(value, unit):
    return -(-value // unit) * unit


def blocks_of(w):
    rows, cols = w.shape
    tall, wide = ceil_to(rows, ROWS), ceil_to(cols, LANES)
    w = jnp.pad(w, [(0, tall - rows), (0, wide - cols)])
    return jnp.moveaxis(w.reshape(tall // ROWS, ROWS, wide // LANES, LANES), 2, 0)


def flat_blocks(*arrays):
    return jnp.concatenate([a.reshape(-1, ROWS, LANES) for a in arrays])


HBM = pl.BlockSpec(memory_space=pltpu.HBM)


def hand_on(value, *after):
    def nothing(*refs):
        del refs

    return pl.pallas_call(
        nothing,
        out_shape=jax.ShapeDtypeStruct(value.shape, value.dtype),
        in_specs=[HBM] * (1 + len(after)),
        out_specs=HBM,
        input_output_aliases={0: 0},
        compiler_params=pltpu.CompilerParams(vmem_limit_bytes=60 * 2**20),
    )(value, *after)


class Routes:
    def __init__(self, n_ha, n_wa):
        self.n_ha, self.n_wa = n_ha, n_wa

    def send(self, value, ha_bits=0, wa_bits=0):
        pairs = [
            (a * self.n_wa + b, (a ^ ha_bits) * self.n_wa + (b ^ wa_bits))
            for a in range(self.n_ha)
            for b in range(self.n_wa)
        ]
        return lax.ppermute(value, AXES, pairs)

    def core(self, value):
        return self.send(value, ha_bits=1)

    def x(self, value):
        return self.send(value, ha_bits=2)

    def y(self, value):
        return self.send(value, wa_bits=1)

    def line(self, value):
        groups = [
            [a * self.n_wa + 2 * z + y for z in range(self.n_wa // 2)]
            for a in range(self.n_ha)
            for y in range(2)
        ]
        return lax.all_gather(value, AXES, axis=0, tiled=True, axis_index_groups=groups)


def over_square(routes, line, before, between):
    half = line.shape[0] // 2
    over_y, over_x = routes.y(line), routes.x(line)
    over_y, over_x = hand_on(over_y, *before), hand_on(over_x, *before)
    low, high = routes.y(over_x[:half]), routes.x(over_y[half:])
    there = between(over_y, over_x)
    low, high = hand_on(low, *there), hand_on(high, *there)
    mine = [hand_on(line, over_y, over_x), over_y, over_x, low, high]
    return mine + [routes.core(piece) for piece in mine]


def stack_kernel(n, slot_ref, *refs):
    ins, outs, held, sems = refs[:n], refs[n:-2], refs[-2], refs[-1]
    rows = held.shape[2]
    reads, writes = [], []
    for j, out in enumerate(outs):
        for i in range(n):
            slot = pl.ds(slot_ref[i] * rows, rows)
            piece = ins[i].at[pl.ds(j * rows, rows)]
            reads.append(pltpu.make_async_copy(piece, held.at[j, i], sems.at[0, j, i]))
            writes.append(pltpu.make_async_copy(held.at[j, i], out.at[slot], sems.at[1, j, i]))
    for read in reads:
        read.start()
    for read, write in zip(reads, writes):
        read.wait()
        write.start()
    for write in writes:
        write.wait()


def stacked(slots, arrays, outs, after):
    n, rows = len(arrays), arrays[0].shape[0] // outs
    anywhere = pl.BlockSpec(memory_space=pl.ANY)
    line = jax.ShapeDtypeStruct((n * rows, ROWS, LANES), jnp.bfloat16)
    return pl.pallas_call(
        lambda *refs: stack_kernel(n, *refs[: n + 1], *refs[n + 1 + len(after) :]),
        out_shape=[line] * outs,
        in_specs=[pl.BlockSpec(memory_space=pltpu.SMEM)] + [anywhere] * (n + len(after)),
        out_specs=[anywhere] * outs,
        scratch_shapes=[
            pltpu.VMEM((outs, n, rows, ROWS, LANES), jnp.bfloat16),
            pltpu.SemaphoreType.DMA((2, outs, n)),
        ],
        compiler_params=pltpu.CompilerParams(vmem_limit_bytes=60 * 2**20),
    )(slots, *arrays, *after)


def w_tile(plan, ref, tile, first=0, count=None):
    count = plan["D"] // ROWS - first if count is None else count
    return jnp.concatenate([ref[plan["w_at"](g, tile)] for g in range(first, first + count)], axis=0)


def o_tile(plan, ref, tile, heads):
    return jnp.concatenate(
        [ref[plan["o_at"](h, g, tile)] for h in heads for g in range(plan["og"])], axis=0
    )


class Weights:
    def __init__(self, plan, place_ref, refs, w_scr, sems, order):
        self.plan, self.w_scr, self.sems, self.here = plan, w_scr, sems, set()
        n_parts = plan["n_parts"]
        self.rows = w_scr.shape[0] // n_parts
        if not plan["square"]:
            for part in order if n_parts > 1 else [0]:
                self.copy(refs[0].at[pl.ds(part * self.rows, self.rows)], part * self.rows, part)
            return
        pieces = []
        for c in range(2):
            for which, ref in enumerate(refs[5 * c : 5 * c + 5]):
                spot = place_ref[4 * c + min(which, 3)]
                to = spot * plan["n_line"] + (ref.shape[0] if which == 4 else 0)
                pieces.append((ref, to, spot // 2))
        for wanted in order:
            for ref, to, part in pieces:

                @pl.when(part == wanted)
                def _():
                    self.copy(ref, to, part)

    def copy(self, ref, to, part):
        dst = self.w_scr.at[pl.ds(to, ref.shape[0])]
        pltpu.make_async_copy(ref, dst, self.sems.at[part]).start()

    def need(self, kind, tiles):
        per_tile, first = self.plan[kind]
        quarter = self.plan["quarter"]
        for part in range(self.plan["n_parts"]):
            used = any(
                first + t * per_tile < (part + 1) * quarter and first + (t + 1) * per_tile > part * quarter
                for t in tiles
            )
            if used and part not in self.here:
                self.here.add(part)
                rows = self.w_scr.at[pl.ds(part * self.rows, self.rows)]
                pltpu.make_async_copy(rows, rows, self.sems.at[part]).wait()


def dims_of(plan):
    return plan["T"], plan["D"], plan["heads"], plan["hd"], plan["tiles"] * LANES


def norm(x, gain):
    xf = x.astype(jnp.float32)
    inverse = lax.rsqrt(jnp.mean(xf * xf, axis=-1, keepdims=True) + 1e-06)
    return inverse, (xf * inverse * gain).astype(jnp.bfloat16)


def project(plan, normed, weights, w_ref, proj_scr):
    for j in range(0, plan["tiles"], 2):
        js = range(j, min(j + 2, plan["tiles"]))
        weights.need("w_tiles", js)
        w = jnp.concatenate([w_tile(plan, w_ref, i) for i in js], axis=1)
        proj_scr[:, j * LANES : j * LANES + LANES * len(js)] = jnp.dot(
            normed, w, preferred_element_type=jnp.float32
        ).astype(jnp.bfloat16)


def qkv_of(plan, proj_ref, h):
    hd, hidden = plan["hd"], plan["heads"] * plan["hd"]
    return [proj_ref[:, m * hidden + h * hd : m * hidden + (h + 1) * hd] for m in range(3)]


def attend(plan, h, proj_ref, bias):
    q, k, v = qkv_of(plan, proj_ref, h)
    scores = lax.dot_general(q, k, NT, preferred_element_type=jnp.float32)
    raised = jnp.exp(scores * plan["hd"] ** (-0.5) + bias)
    probs = raised / jnp.sum(raised, axis=-1, keepdims=True)
    attended = jnp.dot(probs.astype(jnp.bfloat16), v, preferred_element_type=jnp.float32)
    return probs, attended.astype(jnp.bfloat16)


def rows_of(plan, ref, second=False):
    if not plan["pairs"]:
        return ref[...]
    n = plan["T"] // plan["pairs"]
    at = n if second else 0
    return jnp.concatenate([ref[2 * n * i + at : 2 * n * i + at + n, :] for i in range(plan["pairs"])], axis=0)


def fwd_kernel(plan, place_ref, gates_ref, x_ref, gain_ref, bias_ref, cot_ref, *rest):
    n = plan["n_refs"]
    refs, rest = rest[:n], rest[n:]
    y_ref, proj_out, probs_out, att_out, w_ref, sems, proj_ref, probs_ref, att_ref, gated_scr = rest
    T, D, heads, hd, wide = dims_of(plan)
    layer, stride = plan["layer"], plan["og"] * ROWS
    weights = Weights(plan, place_ref, refs, w_ref, sems, (0, 1, 2, 3))
    x = rows_of(plan, x_ref)
    inverse, normed = norm(x, gain_ref[layer : layer + 1, :])
    project(plan, normed, weights, w_ref, proj_ref)
    free = 4
    saves = [pltpu.make_async_copy(proj_ref, proj_out, sems.at[free])]
    saves[0].start()
    bias = bias_ref[...]
    gated_scr[...] = jnp.zeros_like(gated_scr)
    for h in range(heads):
        probs, attended = attend(plan, h, proj_ref, bias)
        probs_ref[h] = probs
        saves.append(pltpu.make_async_copy(probs_ref.at[h], probs_out.at[h], sems.at[free + 2 + h]))
        saves[-1].start()
        att_ref[:, h * hd : (h + 1) * hd] = attended
        gated = (attended.astype(jnp.float32) * gates_ref[layer, h]).astype(jnp.bfloat16)
        gated_scr[:, h * stride : h * stride + hd] = gated
    saves.append(pltpu.make_async_copy(att_ref, att_out, sems.at[free + 1]))
    saves[-1].start()
    gated = gated_scr[...]
    lane_tiles = D // LANES
    for j in range(0, lane_tiles, 2):
        js = range(j, min(j + 2, lane_tiles))
        weights.need("o_tiles", js)
        w = jnp.concatenate([o_tile(plan, w_ref, i, range(heads)) for i in js], axis=1)
        cols = slice(j * LANES, j * LANES + LANES * len(js))
        y = (
            x[:, cols].astype(jnp.float32) + jnp.dot(gated, w, preferred_element_type=jnp.float32)
        ).astype(jnp.bfloat16)
        n = T // plan["to"]
        for i in range(plan["to"]):
            y_ref[2 * n * i : 2 * n * i + n, cols] = y[n * i : n * i + n]
    cot = rows_of(plan, cot_ref, True)
    for i in range(plan["to"]):
        y_ref[2 * n * i + n : 2 * n * i + 2 * n, :] = cot[n * i : n * i + n]
    for copy in saves:
        copy.wait()


def backward(plan, gates_ref, outgrad, x, gain, inverse, proj_ref, probs_of, att_of, sens,
             weights, w_ref, dgated_scr, dproj_scr, g_ref, sens_ref):
    T, D, heads, hd, wide = dims_of(plan)
    layer, stride, hidden = plan["layer"], plan["og"] * ROWS, heads * hd
    lane_tiles = D // LANES
    weights.need("o_tiles", range(lane_tiles))
    for r in range(0, heads, 2):
        hs = min(2, heads - r)
        w = jnp.concatenate(
            [o_tile(plan, w_ref, i, range(r, r + hs)) for i in range(lane_tiles)],
            axis=1,
        )
        out = lax.dot_general(outgrad, w, NT, preferred_element_type=jnp.float32)
        dgated_scr[:, r * stride : (r + hs) * stride] = out.astype(jnp.bfloat16)
    if wide > 3 * hidden:
        dproj_scr[:, wide - LANES :] = jnp.zeros((T, LANES), jnp.bfloat16)
    lane = lax.broadcasted_iota(jnp.int32, (T, LANES), 1)
    for h in range(heads):
        q, k, v = qkv_of(plan, proj_ref, h)
        probs = probs_of(h)
        dgated = dgated_scr[:, h * stride : h * stride + hd].astype(jnp.float32)
        own = jnp.sum(dgated * att_of(h).astype(jnp.float32), axis=-1, keepdims=True)
        sens = jnp.where(lane == layer * heads + h, own, sens)
        datt = (dgated * gates_ref[layer, h]).astype(jnp.bfloat16)
        dprobs = lax.dot_general(datt, v, NT, preferred_element_type=jnp.float32)
        dvalues = lax.dot_general(
            probs.astype(jnp.bfloat16), datt, TN, preferred_element_type=jnp.float32
        )
        inner = jnp.sum(dprobs * probs, axis=-1, keepdims=True)
        dscores = (probs * (dprobs - inner) * hd ** (-0.5)).astype(jnp.bfloat16)
        dqueries = jnp.dot(dscores, k, preferred_element_type=jnp.float32)
        dkeys = lax.dot_general(dscores, q, TN, preferred_element_type=jnp.float32)
        for m, d in enumerate((dqueries, dkeys, dvalues)):
            at = m * hidden + h * hd
            dproj_scr[:, at : at + hd] = d.astype(jnp.bfloat16)
    sens_ref[...] = sens.astype(jnp.bfloat16)
    weights.need("w_tiles", range(plan["tiles"]))
    dproj = dproj_scr[...]
    step = 2 * LANES
    parts = []
    for r in range(0, D, step):
        rr = min(step, D - r)
        w = jnp.concatenate(
            [
                w_tile(plan, w_ref, i, r // ROWS, rr // ROWS)
                for i in range(plan["tiles"])
            ],
            axis=1,
        )
        parts.append(lax.dot_general(dproj, w, NT, preferred_element_type=jnp.float32))
    dnormed = jnp.concatenate(parts, axis=1) * gain
    xf = x.astype(jnp.float32)
    mean = jnp.mean(xf * dnormed, axis=-1, keepdims=True)
    ingrad = (
        outgrad.astype(jnp.float32)
        + inverse * dnormed
        - xf * (inverse * inverse * inverse) * mean
    )
    g_ref[...] = ingrad.astype(jnp.bfloat16)


def both_kernel(plan, place_ref, gates_ref, x_ref, gain_ref, bias_ref, *rest):
    n = plan["n_refs"]
    refs, rest = rest[:n], rest[n:]
    g_ref, w_ref, sems, proj_scr, probs_scr, att_scr, dgated_scr, dproj_scr = rest
    T, D, heads, hd, wide = dims_of(plan)
    layer = plan["layer"]
    weights = Weights(plan, place_ref, refs, w_ref, sems, (0, 1, 2, 3))
    gain = gain_ref[layer : layer + 1, :]
    x = rows_of(plan, x_ref)
    inverse, normed = norm(x, gain)
    project(plan, normed, weights, w_ref, proj_scr)
    bias = bias_ref[...]
    for h in range(heads):
        probs, attended = attend(plan, h, proj_scr, bias)
        probs_scr[h] = probs
        att_scr[:, h * hd : (h + 1) * hd] = attended
    backward(
        plan, gates_ref, rows_of(plan, x_ref, True), x, gain, inverse, proj_scr,
        lambda h: probs_scr[h], lambda h: att_scr[:, h * hd : (h + 1) * hd],
        jnp.zeros((T, LANES), jnp.float32), weights, w_ref, dgated_scr, dproj_scr,
        g_ref.at[:, :D], g_ref.at[:, D : D + LANES],
    )


def bwd_kernel(plan, place_ref, gates_ref, x_ref, gain_ref, outgrad_ref, proj_in, probs_in, att_in,
               *rest):
    n = plan["n_refs"]
    refs, rest = rest[:n], rest[n:]
    if plan["apart"]:
        g_ref, sens_ref, *rest = rest
    else:
        g_ref, *rest = rest
    w_ref, sems, proj_ref, probs_ref, att_ref, dgated_scr, dproj_scr = rest
    T, D, heads, hd, wide = dims_of(plan)
    layer = plan["layer"]
    loads = []
    for src, dst in ((att_in, att_ref), (proj_in, proj_ref), (probs_in, probs_ref)):
        loads.append(pltpu.make_async_copy(src, dst, sems.at[4 + len(loads)]))
    for copy in loads:
        copy.start()
    weights = Weights(plan, place_ref, refs, w_ref, sems, (3, 2, 1, 0))
    gain = gain_ref[layer : layer + 1, :]
    x = rows_of(plan, x_ref)
    inverse, _ = norm(x, gain)
    for copy in loads:
        copy.wait()
    if not plan["apart"]:
        g_ref, sens_ref = g_ref.at[:, :D], g_ref.at[:, D : D + LANES]
    backward(
        plan, gates_ref, outgrad_ref[:, :D], x, gain, inverse,
        proj_ref, lambda h: probs_ref[h], lambda h: att_ref[:, h * hd : (h + 1) * hd],
        outgrad_ref[:, D : D + LANES].astype(jnp.float32),
        weights, w_ref, dgated_scr, dproj_scr, g_ref, sens_ref,
    )


def call(kernel, plan, place, gates, weights, arrays, saved, outs, saves, scratch, flops):
    vmem = pl.BlockSpec(memory_space=pltpu.VMEM)
    smem = pl.BlockSpec(memory_space=pltpu.SMEM)
    plan = dict(plan, n_refs=len(weights))
    n_sems = 4 + 2 + plan["heads"]
    return pl.pallas_call(
        functools.partial(kernel, plan),
        out_shape=list(outs) + list(saves),
        in_specs=[smem, smem]
        + [vmem] * len(arrays)
        + [pl.BlockSpec(memory_space=pl.ANY)] * (len(saved) + len(weights)),
        out_specs=[vmem] * len(outs) + [HBM] * len(saves),
        scratch_shapes=[
            pltpu.VMEM((plan["n_blocks"], ROWS, LANES), jnp.bfloat16),
            pltpu.SemaphoreType.DMA((n_sems,)),
        ]
        + scratch,
        compiler_params=pltpu.CompilerParams(vmem_limit_bytes=60 * 2**20),
        cost_estimate=pl.CostEstimate(flops=flops, bytes_accessed=12 * 2**20, transcendentals=0),
    )(place, gates, *arrays, *saved, *weights)


def per_device(n_ha, n_wa, tokens, cotangent, w_qkv, w_out, gains, gates):
    videos, frames, rows, cols, D = tokens.shape
    layers, heads = gates.shape
    T = videos * frames * rows * cols
    width = w_qkv.shape[2]
    hidden = width // 3
    hd = hidden // heads
    tiles = ceil_to(width, LANES) // LANES
    og = ceil_to(hd, ROWS) // ROWS
    lane_tiles = D // LANES
    wide = tiles * LANES

    def flat(value):
        return jnp.swapaxes(value, 0, 1).reshape(T, D)

    idx = jnp.arange(T)
    fl = frames // n_ha * videos
    lines = [
        idx % (videos * rows * cols),
        (idx // (rows * cols)) % fl * cols + idx % cols,
        (idx // cols) % (T // (n_wa * cols)),
    ]
    biases = [jnp.where(line[:, None] == line[None, :], 0.0, -1e30).astype(jnp.float32) for line in lines]

    def swap(value, axis):
        return lax.all_to_all(value, axis, split_axis=0, concat_axis=0, tiled=True)

    home, teacher = flat(tokens), flat(cotangent)

    shard = w_qkv.shape[1]
    base = dict(T=T, D=D, heads=heads, hd=hd, tiles=tiles, og=og, square=False, apart=False, pairs=0,
                w_tiles=(shard // ROWS, 0), o_tiles=(og, shard // ROWS * tiles))
    weights = []
    fast = n_ha == 4 and n_wa % 4 == 0 and shard % ROWS == 0 and w_out.shape[1] == hd
    if fast:
        routes = Routes(n_ha, n_wa)
        ha, wa = lax.axis_index("ha"), lax.axis_index("wa")
        n_z = n_wa // 2
        spot = ha * 2 + wa % 2
        spots = [spot ^ k for k in (0, 1, 4, 5, 2, 3, 6, 7)]
        place = jnp.stack(spots).astype(jnp.int32)
        rg = shard // ROWS
        quarter = -(-(rg * tiles + og * lane_tiles) // 4)

        def own_quarter(layer):
            own = flat_blocks(blocks_of(w_qkv[layer]), blocks_of(w_out[layer]))
            own = jnp.pad(own, [(0, 4 * quarter - own.shape[0]), (0, 0), (0, 0)])
            return lax.dynamic_slice_in_dim(own, ha * quarter, quarter, 0)

        def addresses(at):
            return dict(
                w_at=lambda g, t: at(g // rg, *divmod(t * rg + g % rg, quarter)),
                o_at=lambda h, g, t: at(h, *divmod(rg * tiles + t * og + g, quarter)),
            )

        squarewise = addresses(
            lambda slot, part, inner: ((part * 2 + slot % 2) * n_z + slot // 2) * quarter + inner
        )
        slots = jnp.stack([(wa // 2) ^ k for k in range(n_z)]).astype(jnp.int32)
        base.update(n_line=n_z * quarter, n_blocks=4 * quarter * n_wa, quarter=quarter, n_parts=4)
        plans = [dict(base, layer=layer, square=True, **squarewise) for layer in range(layers)]

        line = routes.line(own_quarter(0))
        later = hand_on(jnp.concatenate([own_quarter(1), own_quarter(2)]), line)
        far = [routes.send(later, wa_bits=2 * k) for k in range(1, n_z)]
        lines = []

        def stack_later(*squares):
            lines.extend(stacked(slots, [later] + far, 2, squares))
            return lines

        weights = [over_square(routes, line, [home, teacher] + biases, stack_later)]

        def gather(which, before, there):
            line = hand_on(lines[which], *weights[which][3:5])
            weights.append(over_square(routes, line, before, lambda *squares: there))

    else:
        full_qkv = lax.all_gather(w_qkv, "wa", axis=1, tiled=True)
        full_out = lax.all_gather(w_out, "wa", axis=1, tiled=True)
        n_rows = D // ROWS
        n_w = n_rows * tiles
        base["w_at"] = lambda g, t: t * n_rows + g
        base["o_at"] = lambda h, g, t: n_w + (h * lane_tiles + t) * og + g
        for layer in range(layers):
            by_head = full_out[layer].reshape(heads, hd, D)
            weights.append(
                [flat_blocks(blocks_of(full_qkv[layer]), *[blocks_of(by_head[h]) for h in range(heads)])]
            )
        n_blocks = weights[0][0].shape[0]
        base.update(n_blocks=n_blocks, quarter=n_blocks, n_parts=1)
        place = jnp.zeros((1,), jnp.int32)
        plans = [dict(base, layer=layer) for layer in range(layers)]

    bf16, f32 = jnp.bfloat16, jnp.float32
    act = jax.ShapeDtypeStruct((T, D), bf16)
    loaded = jax.ShapeDtypeStruct((T, D + LANES), bf16)
    dense = 2 * T * D * (width + hidden)

    keep = [
        jax.ShapeDtypeStruct((T, wide), bf16),
        jax.ShapeDtypeStruct((heads, T, T), f32),
        jax.ShapeDtypeStruct((T, hidden), bf16),
    ]
    kept = [pltpu.VMEM(array.shape, array.dtype) for array in keep]
    grads = [pltpu.VMEM((T, heads * og * ROWS), bf16), pltpu.VMEM((T, wide), bf16)]

    def forward(layer, x, cot, pairs, to):
        return call(
            fwd_kernel, dict(plans[layer], pairs=pairs, to=to), place, gates, weights[layer],
            [x, gains, biases[layer], cot], [], [jax.ShapeDtypeStruct((2 * T, D), bf16)], keep,
            kept + grads[:1], dense,
        )

    def back(layer, x, outgrad, saved, pairs, outs):
        plan = dict(plans[layer], pairs=pairs, apart=len(outs) > 1)
        return call(
            bwd_kernel, plan, place, gates, weights[layer], [x, gains, outgrad], saved, outs, [],
            kept + grads, dense,
        )

    after_time, *saved_time = forward(0, home, teacher, 0, n_ha)
    tall = swap(after_time, "ha")
    if fast:
        gather(0, [after_time], [tall])
    after_height, *saved_height = forward(1, tall, tall, n_ha, n_wa)
    if fast:
        gather(1, [after_height], [after_height])
    across = swap(after_height, "wa")
    (grad,) = call(
        both_kernel, dict(plans[2], pairs=n_wa), place, gates, weights[2],
        [across, gains, biases[2]], [], [loaded], [], kept + grads, 2 * dense,
    )
    (grad,) = back(1, tall, swap(grad, "wa"), saved_height, n_ha, [loaded])
    apart = [act, jax.ShapeDtypeStruct((T, LANES), bf16)]
    grad, sens = back(0, home, swap(grad, "ha"), saved_time, 0, apart)

    def unflat(value):
        value = value.reshape(frames, videos, rows, cols, value.shape[-1])
        return jnp.swapaxes(value, 0, 1)

    token_grad = unflat(grad)
    sens = unflat(sens[:, : layers * heads]).reshape(videos, frames, rows, cols, layers, heads)
    return (token_grad, jnp.moveaxis(sens, 4, 1))


def solution(mesh):
    spec = P(None, None, "ha", "wa", None)
    in_specs = (spec, spec, P(None, "wa", None), P(None, "wa", None), P(), P())
    out_specs = (spec, P(None, None, None, "ha", "wa", None))
    n_ha, n_wa = mesh.shape["ha"], mesh.shape["wa"]
    return jax.shard_map(
        functools.partial(per_device, n_ha, n_wa),
        mesh=mesh, in_specs=in_specs, out_specs=out_specs, check_vma=False,
    )
```

time: 259 us -> 203 us (0.78)
  starting transfers between devices: 70.9 us -> 29.2 us
  waiting for transfers between devices: 71.3 us -> 39 us
  blocking collectives: 31.9 us -> 47.8 us
  Pallas kernels: 37.6 us -> 45.8 us
  other arithmetic: 8.74 us -> 4.3 us
    ppermute x33 -> x30, starting transfers between devices: 54 us -> 21.6 us  [send(): return lax.ppermute(value, AXES, pairs)]
    ppermute x33 -> x30, waiting for transfers between devices: 65.6 us -> 39 us  [send(): return lax.ppermute(value, AXES, pairs)]
    all_gather x0 -> x1, blocking collectives: none -> 20.4 us  [line(): lax.all_gather(value, AXES, axis=0, tiled=True, axis_index_groups=groups)]
    unnamed x133 -> x63, local copies, waits for them, and re-layouts: 26.1 us -> 12.6 us
    all_to_all x3 -> x2, starting transfers between devices: 16.9 us -> 7.58 us  [swap(): return lax.all_to_all(value, axis, split_axis=0, concat_axis=0, tiled=True)]
    pallas_call x5 -> x24, Pallas kernels: 37.6 us -> 45.8 us  [the longest x5 42.9 us: call(): pl.pallas_call(functools.partial(kernel, plan), out_shape=list(outs) + li...]
    concatenate x9 -> x3, other arithmetic: 7.71 us -> 1.61 us  [the longest x2 0.85 us: flat_blocks(): return jnp.concatenate([a.reshape(-1, ROWS, LANES) for a in arrays])]
    all_to_all x3 -> x2, waiting for transfers between devices: 5.71 us -> 0.08 us  [swap(): return lax.all_to_all(value, axis, split_axis=0, concat_axis=0, tiled=True)]
  transfers between devices with their start and end apart: 36 -> 32, of which waited for: 9 -> 12; matrix products, arithmetic and copies ran while one was open for 4% -> 9% of each run, Pallas kernels for 5% -> 9%
where the time goes in v2:
time: 203 us; the launch traced here: 202 us
  blocking collectives  47.8 us (24%)
  Pallas kernels  45.8 us (23%)
  waiting for transfers between devices  39 us (19%)
  local copies, waits for them, and re-layouts  34.4 us (17%)
  starting transfers between devices  29.2 us (14%)
  other arithmetic  4.3 us (2%)
    pallas_call x5, Pallas kernels, call(): pl.pallas_call(functools.partial(kernel, plan), out_shape=list(outs) + li...  42.9 us
    ppermute x30, waiting for transfers between devices, send(): return lax.ppermute(value, AXES, pairs)  39 us
    all_to_all x2, blocking collectives, swap(): return lax.all_to_all(value, axis, split_axis=0, concat_axis=0, tiled=True)  27.4 us
    ppermute x30, starting transfers between devices, send(): return lax.ppermute(value, AXES, pairs)  21.6 us
    all_gather x1, blocking collectives, line(): lax.all_gather(value, AXES, axis=0, tiled=True, axis_index_groups=groups)  20.4 us
    unnamed x63, local copies, waits for them, and re-layouts  12.6 us
    all_to_all x2, starting transfers between devices, swap(): return lax.all_to_all(value, axis, split_axis=0, concat_axis=0, tiled=True)  7.58 us
    slice x6, local copies, waits for them, and re-layouts, over_square(): low, high = (routes.y(over_x[:half]), routes.x(over_y[half:]))  5.04 us
  transfers between devices with their start and end apart: 32, of which 12 were waited for; matrix products, arithmetic and copies ran while one was open for 9% of the time, Pallas kernels for 9%

profile of v2, /device:TPU:0, one launch (start us, length us, event | category | flops | bytes accessed | tf_op | source)
XLA Modules:
  0.0 201.6 jit_solution(6049327800761612154)
XLA Ops:
  0.6 1.8 slice_bitcast_fusion.4
  2.6 2.3 %slice_bitcast_fusion.1 = (bf16[144,1728]{1,0:T(8,128)(2,1)S(1)}, bf16[144,1728]{1,0:T(8,128)(2,1)S(1)}, bf16[144,1728]{1,0:T(8,128)(2,1)}) fusion(bf16[3,144,1728]{2,1,0:T(8,128)(2,1)} %param.8), kind=kLoop, calls=%fused_computation.7 | loop fusion | bytes 2985984 | tf_op jit(solution)/shard_map/squeeze | solution.py:448
  5.9 20.4 %all_gather.3.refs_0_.refs_1_ = bf16[172,16,128]{2,1,0:T(8,128)(2,1)S(1)} all-gather(bf16[43,16,128]{2,1,0:T(8,128)(2,1)S(1)} %fusion.6), channel_id=1, replica_groups={{0,2,4,6},{1,3,5,7},{8,10,12,14},{9,11,13,15},{16,18,20,22},{17,19,21,2..., dimensions={0}, use_global_device_ids=true | all-gather | bytes 880640 | tf_op jit(solution)/shard_map/all_gather | solution.py:76
  26.3 1.5 collective-permute-start.1
  27.8 1.5 collective-permute-start
  29.5 0.9 pad.37
  31.8 1.9 pad.36
  33.7 1.4 reshape.184
  36.5 2.3 %collective-permute-start.5 = (bf16[86,16,128]{2,1,0:T(8,128)(2,1)}, bf16[86,16,128]{2,1,0:T(8,128)(2,1)S(1)}, u32[]{:S(2)}, u32[]{:S(2)}) collective-permute-start(bf16[86,16,128]{2,1,0:T(8,128)(2,1)} %shard_map.80.refs_1_), channel_id=1, source_target_pairs={{0,6},{1,7},{2,4},{3,5},{4,2},{5,3},{6,0},{7,1},{8,14},{9,15},{10,... | collective-permute-start | bytes 1056776 | tf_op jit(solution)/shard_map/ppermute | solution.py:59
  41.8 1.8 reshape_transpose.7.refs_2_.cot_ref
  43.6 0.9 copy-done.2
  44.6 2.1 %collective-permute-start.3 = (bf16[86,16,128]{2,1,0:T(8,128)(2,1)S(1)}, bf16[86,16,128]{2,1,0:T(8,128)(2,1)}, u32[]{:S(2)}, u32[]{:S(2)}) collective-permute-start(bf16[86,16,128]{2,1,0:T(8,128)(2,1)S(1)} %copy-done.19), channel_id=1, source_target_pairs={{0,2},{1,3},{2,0},{3,1},{4,6},{5,7},{6,4},{7,5},{8,10},{9,11},{10,... | collective-permute-start | bytes 1056776 | tf_op jit(solution)/shard_map/ppermute | solution.py:59
  47.5 1.0 slice.53
  48.5 1.3 collective-permute-start.6
  51.0 14.8 %collective-permute-done.4.refs_3_ = bf16[86,16,128]{2,1,0:T(8,128)(2,1)} collective-permute-done((bf16[86,16,128]{2,1,0:T(8,128)(2,1)S(1)}, bf16[86,16,128]{2,1,0:T(8,128)(2,1)}, u32[]{:S(2)}, u32[]{:S(2)}) %collective-permute-start.4) | collective-permute-done | bytes 352288 | tf_op jit(solution)/shard_map/ppermute | solution.py:59
  65.8 2.9 %shard_map.81 = (bf16[172,16,128]{2,1,0:T(8,128)(2,1)}, bf16[172,16,128]{2,1,0:T(8,128)(2,1)}) custom-call(s32[4]{0:T(128)} %pad_add_fusion.refs_0_, bf16[86,16,128]{2,1,0:T(8,128)(2,1)} %shard_map.80.refs_1_, bf16[86,16,128]{2,1,0:T(8,128)(2,1)} %collective-permute-done.3.refs_2_, bf16[86,16,128]{2,1,0:T(8,128)(2,1)} %collective-permute-done.4.refs_3_, ...), custom_call_target="tpu_custom_call" | custom-call | tf_op jit(solution)/shard_map/pallas_call | solution.py:113
  71.3 1.4 collective-permute-start.13
  74.0 1.1 collective-permute-done.10.rest_8_
  76.0 7.2 %shard_map.84 = (bf16[256,1152]{1,0:T(8,128)(2,1)}, bf16[128,1792]{1,0:T(8,128)(2,1)}, f32[8,128,128]{2,1,0:T(8,128)}, bf16[128,576]{1,0:T(8,128)(2,1)}) custom-call(s32[8]{0:T(128)} %stack.50.place_ref, f32[3,8]{1,0:T(4,128)} %gates_ref.9, bf16[128,1152]{1,0:T(8,128)(2,1)} %reshape_transpose.6.refs_1_.x_ref, f32[3,1152]{1,0:T(4,128)} %gain_ref.9, ...), custom_call_target="tpu_custom_call" | custom-call | flops 679477248 | bytes 12582912 | tf_op jit(solution)/shard_map/pallas_call | solution.py:386
  83.2 3.5 %all-to-all-start = ((bf16[4,64,1152]{2,1,0:T(8,128)(2,1)}), bf16[4,64,1152]{2,1,0:T(8,128)(2,1)S(1)}, u32[]{:S(2)}, u32[]{:S(2)}) async-start(bf16[4,64,1152]{2,1,0:T(8,128)(2,1)} %bitcast.52), calls=%async_computation | async-start | bytes 1179648 | tf_op jit(solution)/shard_map/all_to_all | solution.py:428
  86.7 3.0 %collective-permute-done.13.refs_0_ = bf16[172,16,128]{2,1,0:T(8,128)(2,1)S(1)} collective-permute-done((bf16[172,16,128]{2,1,0:T(8,128)(2,1)}, bf16[172,16,128]{2,1,0:T(8,128)(2,1)S(1)}, u32[]{:S(2)}, u32[]{:S(2)}) %collective-permute-start.13) | collective-permute-done | bytes 704544 | tf_op jit(solution)/shard_map/ppermute | solution.py:59
  89.7 0.9 copy-done.8
  90.6 1.0 slice.54
  92.2 0.9 copy-done.6
  93.0 1.0 slice.55
  94.1 1.5 collective-permute-start.15
  96.2 5.3 %collective-permute-done.14.refs_0_ = bf16[86,16,128]{2,1,0:T(8,128)(2,1)S(1)} collective-permute-done((bf16[86,16,128]{2,1,0:T(8,128)(2,1)S(1)}, bf16[86,16,128]{2,1,0:T(8,128)(2,1)S(1)}, u32[]{:S(2)}, u32[]{:S(2)}) %collective-permute-start.14) | collective-permute-done | bytes 352288 | tf_op jit(solution)/shard_map/ppermute | solution.py:59
  102.3 1.5 collective-permute-done.15.refs_0_
  104.6 1.4 collective-permute-start.22
  106.4 1.5 collective-permute-start.21
  108.0 7.5 %shard_map.91 = (bf16[256,1152]{1,0:T(8,128)(2,1)}, bf16[128,1792]{1,0:T(8,128)(2,1)}, f32[8,128,128]{2,1,0:T(8,128)}, bf16[128,576]{1,0:T(8,128)(2,1)}) custom-call(s32[8]{0:T(128)} %stack.50.place_ref, f32[3,8]{1,0:T(4,128)} %gates_ref.9, bf16[256,1152]{1,0:T(8,128)(2,1)} %bitcast.48, f32[3,1152]{1,0:T(4,128)} %gain_ref.9, ...), custom_call_target="tpu_custom_call" | custom-call | flops 679477248 | bytes 12582912 | tf_op jit(solution)/shard_map/pallas_call | solution.py:386
  115.5 4.1 %all-to-all-start.1 = ((bf16[8,32,1152]{2,1,0:T(8,128)(2,1)}), bf16[8,32,1152]{2,1,0:T(8,128)(2,1)S(1)}, u32[]{:S(2)}, u32[]{:S(2)}) async-start(bf16[8,32,1152]{2,1,0:T(8,128)(2,1)} %bitcast.51), calls=%async_computation.1 | async-start | bytes 1179648 | tf_op jit(solution)/shard_map/all_to_all | solution.py:428
  119.6 3.4 %collective-permute-done.22.refs_0_ = bf16[172,16,128]{2,1,0:T(8,128)(2,1)S(1)} collective-permute-done((bf16[172,16,128]{2,1,0:T(8,128)(2,1)}, bf16[172,16,128]{2,1,0:T(8,128)(2,1)S(1)}, u32[]{:S(2)}, u32[]{:S(2)}) %collective-permute-start.22) | collective-permute-done | bytes 704544 | tf_op jit(solution)/shard_map/ppermute | solution.py:59
  123.0 0.9 copy-done.12
  123.9 1.0 slice.56
  124.9 1.6 collective-permute-start.23
  126.5 1.7 collective-permute-done.21.refs_0_
  128.2 0.9 copy-done.10
  129.1 1.0 slice.57
  130.1 1.4 collective-permute-start.24
  132.1 6.2 %collective-permute-done.23.refs_0_ = bf16[86,16,128]{2,1,0:T(8,128)(2,1)S(1)} collective-permute-done((bf16[86,16,128]{2,1,0:T(8,128)(2,1)S(1)}, bf16[86,16,128]{2,1,0:T(8,128)(2,1)S(1)}, u32[]{:S(2)}, u32[]{:S(2)}) %collective-permute-start.23) | collective-permute-done | bytes 352288 | tf_op jit(solution)/shard_map/ppermute | solution.py:59
  141.0 0.9 collective-permute-done.29.rest_9_
  142.6 10.6 %shard_map.98 = bf16[128,1280]{1,0:T(8,128)(2,1)} custom-call(s32[8]{0:T(128)} %stack.50.place_ref, f32[3,8]{1,0:T(4,128)} %gates_ref.9, bf16[256,1152]{1,0:T(8,128)(2,1)} %bitcast.53, f32[3,1152]{1,0:T(4,128)} %gain_ref.9, f32[128,128]{1,0:T(8,128)} %compare_select_fusion.refs_5_.bias_ref, bf16[172,16,128]{2,1,0:T(8,128)(2,1)} %shard_map.95.rest_0_, ...), custom_call_target="tpu_custom_call" | custom-call | flops 1358954496 | bytes 12582912 | tf_op jit(solution)/shard_map/pallas_call | solution.py:386
  153.2 16.5 %all_to_all.44 = bf16[8,16,1280]{2,1,0:T(8,128)(2,1)} all-to-all(bf16[8,16,1280]{2,1,0:T(8,128)(2,1)} %bitcast.61), channel_id=1, replica_groups=mesh['ha'=4,'wa'=8] {'wa'}, dimensions={0} | all-to-all | bytes 655360 | tf_op jit(solution)/shard_map/all_to_all | solution.py:428
  169.8 8.8 %shard_map.99 = bf16[128,1280]{1,0:T(8,128)(2,1)} custom-call(s32[8]{0:T(128)} %stack.50.place_ref, f32[3,8]{1,0:T(4,128)} %gates_ref.9, bf16[256,1152]{1,0:T(8,128)(2,1)} %bitcast.50, f32[3,1152]{1,0:T(4,128)} %gain_ref.9, bf16[128,1280]{1,0:T(8,128)(2,1)} %bitcast.65, bf16[128,1792]{1,0:T(8,128)(2,1)} %get-tuple-element.18.proj_in, ...), custom_call_target="tpu_custom_call" | custom-call | flops 679477248 | bytes 12582912 | tf_op jit(solution)/shard_map/pallas_call | solution.py:386
  178.6 10.9 %all_to_all.45 = bf16[4,32,1280]{2,1,0:T(8,128)(2,1)} all-to-all(bf16[4,32,1280]{2,1,0:T(8,128)(2,1)} %bitcast.66), channel_id=1, replica_groups=mesh['ha'=4,'wa'=8] {'ha'}, dimensions={0} | all-to-all | bytes 655360 | tf_op jit(solution)/shard_map/all_to_all | solution.py:428
  189.5 8.7 %shard_map.100 = (bf16[128,1152]{1,0:T(8,128)(2,1)}, bf16[128,128]{1,0:T(8,128)(2,1)}) custom-call(s32[8]{0:T(128)} %stack.50.place_ref, f32[3,8]{1,0:T(4,128)} %gates_ref.9, bf16[128,1152]{1,0:T(8,128)(2,1)} %reshape_transpose.6.refs_1_.x_ref, f32[3,1152]{1,0:T(4,128)} %gain_ref.9, bf16[128,1280]{1,0:T(8,128)(2,1)} %bitcast.60, ...), custom_call_target="tpu_custom_call" | custom-call | flops 679477248 | bytes 12582912 | tf_op jit(solution)/shard_map/pallas_call | solution.py:386
  198.2 1.8 transpose_reshape.3
  (146 shorter events, 22.5 us)
Async XLA Ops:
  26.3 5.0 %copy-start.5 = (bf16[172,16,128]{2,1,0:T(8,128)(2,1)}, bf16[172,16,128]{2,1,0:T(8,128)(2,1)S(1)}, u32[]{:S(2)}) copy-start(bf16[172,16,128]{2,1,0:T(8,128)(2,1)S(1)} %all_gather.3.refs_0_.refs_1_) | copy-start | bytes 2113540
  26.3 17.3 %collective-permute-start.1 = (bf16[172,16,128]{2,1,0:T(8,128)(2,1)S(1)}, bf16[172,16,128]{2,1,0:T(8,128)(2,1)S(1)}, u32[]{:S(2)}, u32[]{:S(2)}) collective-permute-start(bf16[172,16,128]{2,1,0:T(8,128)(2,1)S(1)} %all_gather.3.refs_0_.refs_1_), channel_id=1, source_target_pairs={{0,16},{1,17},{2,18},{3,19},{4,20},{5,21},{6,22},{7,23},{8,24},{9,... | collective-permute-start | bytes 2113544 | tf_op jit(solution)/shard_map/ppermute | solution.py:59
  27.8 18.9 %collective-permute-start = (bf16[172,16,128]{2,1,0:T(8,128)(2,1)S(1)}, bf16[172,16,128]{2,1,0:T(8,128)(2,1)S(1)}, u32[]{:S(2)}, u32[]{:S(2)}) collective-permute-start(bf16[172,16,128]{2,1,0:T(8,128)(2,1)S(1)} %all_gather.3.refs_0_.refs_1_), channel_id=1, source_target_pairs={{0,1},{1,0},{2,3},{3,2},{4,5},{5,4},{6,7},{7,6},{8,9},{9,8},{10,11... | collective-permute-start | bytes 2113544 | tf_op jit(solution)/shard_map/ppermute | solution.py:59
  35.8 5.2 %copy-start.30 = (bf16[1,8,8,2,1152]{4,3,2,1,0:T(2,128)(2,1)S(1)}, bf16[1,8,8,2,1152]{4,3,2,1,0:T(2,128)(2,1)}, u32[]{:S(2)}) copy-start(bf16[1,8,8,2,1152]{4,3,2,1,0:T(2,128)(2,1)} %param.6) | copy-start | bytes 884740
  36.5 13.3 %collective-permute-start.5 = (bf16[86,16,128]{2,1,0:T(8,128)(2,1)}, bf16[86,16,128]{2,1,0:T(8,128)(2,1)S(1)}, u32[]{:S(2)}, u32[]{:S(2)}) collective-permute-start(bf16[86,16,128]{2,1,0:T(8,128)(2,1)} %shard_map.80.refs_1_), channel_id=1, source_target_pairs={{0,6},{1,7},{2,4},{3,5},{4,2},{5,3},{6,0},{7,1},{8,14},{9,15},{10,... | collective-permute-start | bytes 1056776 | tf_op jit(solution)/shard_map/ppermute | solution.py:59
  41.0 3.5 %copy-start.19 = (bf16[86,16,128]{2,1,0:T(8,128)(2,1)S(1)}, bf16[86,16,128]{2,1,0:T(8,128)(2,1)}, u32[]{:S(2)}) copy-start(bf16[86,16,128]{2,1,0:T(8,128)(2,1)} %shard_map.80.refs_1_) | copy-start | bytes 1056772
  44.5 5.3 %copy-start.3 = (bf16[172,16,128]{2,1,0:T(8,128)(2,1)S(1)}, bf16[172,16,128]{2,1,0:T(8,128)(2,1)}, u32[]{:S(2)}) copy-start(bf16[172,16,128]{2,1,0:T(8,128)(2,1)} %shard_map.78.refs_2_.refs_6_.rest_2_) | copy-start | bytes 2113540
  44.5 28.3 %collective-permute-start.9 = (bf16[172,16,128]{2,1,0:T(8,128)(2,1)}, bf16[172,16,128]{2,1,0:T(8,128)(2,1)}, u32[]{:S(2)}, u32[]{:S(2)}) collective-permute-start(bf16[172,16,128]{2,1,0:T(8,128)(2,1)} %shard_map.78.refs_2_.refs_6_.rest_2_), channel_id=1, source_target_pairs={{0,8},{1,9},{2,10},{3,11},{4,12},{5,13},{6,14},{7,15},{8,0},{9,1},... | collective-permute-start | bytes 2113544 | tf_op jit(solution)/shard_map/ppermute | solution.py:59
  44.5 21.3 %collective-permute-start.4 = (bf16[86,16,128]{2,1,0:T(8,128)(2,1)S(1)}, bf16[86,16,128]{2,1,0:T(8,128)(2,1)}, u32[]{:S(2)}, u32[]{:S(2)}) collective-permute-start(bf16[86,16,128]{2,1,0:T(8,128)(2,1)S(1)} %copy-done.19), channel_id=1, source_target_pairs={{0,4},{1,5},{2,6},{3,7},{4,0},{5,1},{6,2},{7,3},{8,12},{9,13},{10,... | collective-permute-start | bytes 1056776 | tf_op jit(solution)/shard_map/ppermute | solution.py:59
  44.6 21.2 %collective-permute-start.3 = (bf16[86,16,128]{2,1,0:T(8,128)(2,1)S(1)}, bf16[86,16,128]{2,1,0:T(8,128)(2,1)}, u32[]{:S(2)}, u32[]{:S(2)}) collective-permute-start(bf16[86,16,128]{2,1,0:T(8,128)(2,1)S(1)} %copy-done.19), channel_id=1, source_target_pairs={{0,2},{1,3},{2,0},{3,1},{4,6},{5,7},{6,4},{7,5},{8,10},{9,11},{10,... | collective-permute-start | bytes 1056776 | tf_op jit(solution)/shard_map/ppermute | solution.py:59
  48.5 20.2 %collective-permute-start.6 = (bf16[86,16,128]{2,1,0:T(8,128)(2,1)S(1)}, bf16[86,16,128]{2,1,0:T(8,128)(2,1)S(1)}, u32[]{:S(2)}, u32[]{:S(2)}) collective-permute-start(bf16[86,16,128]{2,1,0:T(8,128)(2,1)S(1)} %slice.53), channel_id=1, source_target_pairs={{0,16},{1,17},{2,18},{3,19},{4,20},{5,21},{6,22},{7,23},{8,24},{9,... | collective-permute-start | bytes 1056776 | tf_op jit(solution)/shard_map/ppermute | solution.py:59
  49.9 16.0 %copy-start.27 = (bf16[86,16,128]{2,1,0:T(8,128)(2,1)}, bf16[86,16,128]{2,1,0:T(8,128)(2,1)S(1)}, u32[]{:S(2)}) copy-start(bf16[86,16,128]{2,1,0:T(8,128)(2,1)S(1)} %collective-permute-done.5.refs_4_) | copy-start | bytes 1056772
  49.9 20.7 %collective-permute-start.2 = (bf16[86,16,128]{2,1,0:T(8,128)(2,1)S(1)}, bf16[86,16,128]{2,1,0:T(8,128)(2,1)S(1)}, u32[]{:S(2)}, u32[]{:S(2)}) collective-permute-start(bf16[86,16,128]{2,1,0:T(8,128)(2,1)S(1)} %slice.52), channel_id=1, source_target_pairs={{0,1},{1,0},{2,3},{3,2},{4,5},{5,4},{6,7},{7,6},{8,9},{9,8},{10,11... | collective-permute-start | bytes 1056776 | tf_op jit(solution)/shard_map/ppermute | solution.py:59
  69.5 1.1 copy-start.1
  69.5 3.8 %collective-permute-start.11 = (bf16[86,16,128]{2,1,0:T(8,128)(2,1)}, bf16[86,16,128]{2,1,0:T(8,128)(2,1)S(1)}, u32[]{:S(2)}, u32[]{:S(2)}) collective-permute-start(bf16[86,16,128]{2,1,0:T(8,128)(2,1)} %shard_map.83.rest_4_.refs_2_), channel_id=1, source_target_pairs={{0,8},{1,9},{2,10},{3,11},{4,12},{5,13},{6,14},{7,15},{8,0},{9,1},... | collective-permute-start | bytes 1056776 | tf_op jit(solution)/shard_map/ppermute | solution.py:59
  69.5 5.7 %collective-permute-start.7 = (bf16[172,16,128]{2,1,0:T(8,128)(2,1)}, bf16[172,16,128]{2,1,0:T(8,128)(2,1)S(1)}, u32[]{:S(2)}, u32[]{:S(2)}) collective-permute-start(bf16[172,16,128]{2,1,0:T(8,128)(2,1)} %shard_map.79.rest_0_), channel_id=1, source_target_pairs={{0,8},{1,9},{2,10},{3,11},{4,12},{5,13},{6,14},{7,15},{8,0},{9,1},... | collective-permute-start | bytes 2113544 | tf_op jit(solution)/shard_map/ppermute | solution.py:59
  70.6 4.6 %collective-permute-start.8 = (bf16[172,16,128]{2,1,0:T(8,128)(2,1)S(1)}, bf16[172,16,128]{2,1,0:T(8,128)(2,1)}, u32[]{:S(2)}, u32[]{:S(2)}) collective-permute-start(bf16[172,16,128]{2,1,0:T(8,128)(2,1)S(1)} %copy-done.1), channel_id=1, source_target_pairs={{0,8},{1,9},{2,10},{3,11},{4,12},{5,13},{6,14},{7,15},{8,0},{9,1},... | collective-permute-start | bytes 2113544 | tf_op jit(solution)/shard_map/ppermute | solution.py:59
  71.3 2.0 copy-start.15
  71.3 18.4 %collective-permute-start.13 = (bf16[172,16,128]{2,1,0:T(8,128)(2,1)}, bf16[172,16,128]{2,1,0:T(8,128)(2,1)S(1)}, u32[]{:S(2)}, u32[]{:S(2)}) collective-permute-start(bf16[172,16,128]{2,1,0:T(8,128)(2,1)} %shard_map.85.refs_0_), channel_id=1, source_target_pairs={{0,16},{1,17},{2,18},{3,19},{4,20},{5,21},{6,22},{7,23},{8,24},{9,... | collective-permute-start | bytes 2113544 | tf_op jit(solution)/shard_map/ppermute | solution.py:59
  72.8 19.4 %collective-permute-start.12 = (bf16[172,16,128]{2,1,0:T(8,128)(2,1)}, bf16[172,16,128]{2,1,0:T(8,128)(2,1)S(1)}, u32[]{:S(2)}, u32[]{:S(2)}) collective-permute-start(bf16[172,16,128]{2,1,0:T(8,128)(2,1)} %shard_map.85.refs_0_), channel_id=1, source_target_pairs={{0,1},{1,0},{2,3},{3,2},{4,5},{5,4},{6,7},{7,6},{8,9},{9,8},{10,11... | collective-permute-start | bytes 2113544 | tf_op jit(solution)/shard_map/ppermute | solution.py:59
  73.3 1.9 copy-start.22
  73.3 1.9 collective-permute-start.10
  83.2 13.0 %all-to-all-start = ((bf16[4,64,1152]{2,1,0:T(8,128)(2,1)}), bf16[4,64,1152]{2,1,0:T(8,128)(2,1)S(1)}, u32[]{:S(2)}, u32[]{:S(2)}) async-start(bf16[4,64,1152]{2,1,0:T(8,128)(2,1)} %bitcast.52), calls=%async_computation | async-start | bytes 1179648 | tf_op jit(solution)/shard_map/all_to_all | solution.py:428
  91.6 9.9 %collective-permute-start.14 = (bf16[86,16,128]{2,1,0:T(8,128)(2,1)S(1)}, bf16[86,16,128]{2,1,0:T(8,128)(2,1)S(1)}, u32[]{:S(2)}, u32[]{:S(2)}) collective-permute-start(bf16[86,16,128]{2,1,0:T(8,128)(2,1)S(1)} %slice.54), channel_id=1, source_target_pairs={{0,1},{1,0},{2,3},{3,2},{4,5},{5,4},{6,7},{7,6},{8,9},{9,8},{10,11... | collective-permute-start | bytes 1056776 | tf_op jit(solution)/shard_map/ppermute | solution.py:59
  94.1 1.5 copy-start.7
  94.1 2.0 %copy-start.9 = (bf16[172,16,128]{2,1,0:T(8,128)(2,1)S(1)}, bf16[172,16,128]{2,1,0:T(8,128)(2,1)}, u32[]{:S(2)}) copy-start(bf16[172,16,128]{2,1,0:T(8,128)(2,1)} %shard_map.87.refs_2_.rest_2_) | copy-start | bytes 2113540
  94.1 9.7 %collective-permute-start.15 = (bf16[86,16,128]{2,1,0:T(8,128)(2,1)S(1)}, bf16[86,16,128]{2,1,0:T(8,128)(2,1)S(1)}, u32[]{:S(2)}, u32[]{:S(2)}) collective-permute-start(bf16[86,16,128]{2,1,0:T(8,128)(2,1)S(1)} %slice.55), channel_id=1, source_target_pairs={{0,16},{1,17},{2,18},{3,19},{4,20},{5,21},{6,22},{7,23},{8,24},{9,... | collective-permute-start | bytes 1056776 | tf_op jit(solution)/shard_map/ppermute | solution.py:59
  95.6 12.4 %collective-permute-start.16 = (bf16[172,16,128]{2,1,0:T(8,128)(2,1)}, bf16[172,16,128]{2,1,0:T(8,128)(2,1)}, u32[]{:S(2)}, u32[]{:S(2)}) collective-permute-start(bf16[172,16,128]{2,1,0:T(8,128)(2,1)} %shard_map.88.rest_0_), channel_id=1, source_target_pairs={{0,8},{1,9},{2,10},{3,11},{4,12},{5,13},{6,14},{7,15},{8,0},{9,1},... | collective-permute-start | bytes 2113544 | tf_op jit(solution)/shard_map/ppermute | solution.py:59
  95.6 12.4 %collective-permute-start.17 = (bf16[172,16,128]{2,1,0:T(8,128)(2,1)S(1)}, bf16[172,16,128]{2,1,0:T(8,128)(2,1)}, u32[]{:S(2)}, u32[]{:S(2)}) collective-permute-start(bf16[172,16,128]{2,1,0:T(8,128)(2,1)S(1)} %copy-done.7), channel_id=1, source_target_pairs={{0,8},{1,9},{2,10},{3,11},{4,12},{5,13},{6,14},{7,15},{8,0},{9,1},... | collective-permute-start | bytes 2113544 | tf_op jit(solution)/shard_map/ppermute | solution.py:59
  96.1 11.9 %collective-permute-start.18 = (bf16[172,16,128]{2,1,0:T(8,128)(2,1)S(1)}, bf16[172,16,128]{2,1,0:T(8,128)(2,1)}, u32[]{:S(2)}, u32[]{:S(2)}) collective-permute-start(bf16[172,16,128]{2,1,0:T(8,128)(2,1)S(1)} %copy-done.9), channel_id=1, source_target_pairs={{0,8},{1,9},{2,10},{3,11},{4,12},{5,13},{6,14},{7,15},{8,0},{9,1},... | collective-permute-start | bytes 2113544 | tf_op jit(solution)/shard_map/ppermute | solution.py:59
  96.2 5.3 %copy-start.4 = (bf16[4,64,1152]{2,1,0:T(8,128)(2,1)}, bf16[4,64,1152]{2,1,0:T(8,128)(2,1)S(1)}, u32[]{:S(2)}) copy-start(bf16[4,64,1152]{2,1,0:T(8,128)(2,1)S(1)} %all-to-all-done) | copy-start | bytes 1769476
  102.3 2.3 %collective-permute-start.19 = (bf16[86,16,128]{2,1,0:T(8,128)(2,1)}, bf16[86,16,128]{2,1,0:T(8,128)(2,1)S(1)}, u32[]{:S(2)}, u32[]{:S(2)}) collective-permute-start(bf16[86,16,128]{2,1,0:T(8,128)(2,1)} %shard_map.89.rest_3_.refs_1_), channel_id=1, source_target_pairs={{0,8},{1,9},{2,10},{3,11},{4,12},{5,13},{6,14},{7,15},{8,0},{9,1},... | collective-permute-start | bytes 1056776 | tf_op jit(solution)/shard_map/ppermute | solution.py:59
  104.6 1.9 collective-permute-start.20
  104.6 3.4 %copy-start.25 = (bf16[86,16,128]{2,1,0:T(8,128)(2,1)}, bf16[86,16,128]{2,1,0:T(8,128)(2,1)S(1)}, u32[]{:S(2)}) copy-start(bf16[86,16,128]{2,1,0:T(8,128)(2,1)S(1)} %collective-permute-done.19.rest_8_) | copy-start | bytes 1056772
  104.6 18.4 %collective-permute-start.22 = (bf16[172,16,128]{2,1,0:T(8,128)(2,1)}, bf16[172,16,128]{2,1,0:T(8,128)(2,1)S(1)}, u32[]{:S(2)}, u32[]{:S(2)}) collective-permute-start(bf16[172,16,128]{2,1,0:T(8,128)(2,1)} %shard_map.92.refs_0_), channel_id=1, source_target_pairs={{0,16},{1,17},{2,18},{3,19},{4,20},{5,21},{6,22},{7,23},{8,24},{9,... | collective-permute-start | bytes 2113544 | tf_op jit(solution)/shard_map/ppermute | solution.py:59
  106.4 1.5 copy-start.26
  106.4 21.7 %collective-permute-start.21 = (bf16[172,16,128]{2,1,0:T(8,128)(2,1)}, bf16[172,16,128]{2,1,0:T(8,128)(2,1)S(1)}, u32[]{:S(2)}, u32[]{:S(2)}) collective-permute-start(bf16[172,16,128]{2,1,0:T(8,128)(2,1)} %shard_map.92.refs_0_), channel_id=1, source_target_pairs={{0,1},{1,0},{2,3},{3,2},{4,5},{5,4},{6,7},{7,6},{8,9},{9,8},{10,11... | collective-permute-start | bytes 2113544 | tf_op jit(solution)/shard_map/ppermute | solution.py:59
  115.5 24.8 %all-to-all-start.1 = ((bf16[8,32,1152]{2,1,0:T(8,128)(2,1)}), bf16[8,32,1152]{2,1,0:T(8,128)(2,1)S(1)}, u32[]{:S(2)}, u32[]{:S(2)}) async-start(bf16[8,32,1152]{2,1,0:T(8,128)(2,1)} %bitcast.51), calls=%async_computation.1 | async-start | bytes 1179648 | tf_op jit(solution)/shard_map/all_to_all | solution.py:428
  124.9 13.4 %collective-permute-start.23 = (bf16[86,16,128]{2,1,0:T(8,128)(2,1)S(1)}, bf16[86,16,128]{2,1,0:T(8,128)(2,1)S(1)}, u32[]{:S(2)}, u32[]{:S(2)}) collective-permute-start(bf16[86,16,128]{2,1,0:T(8,128)(2,1)S(1)} %slice.56), channel_id=1, source_target_pairs={{0,1},{1,0},{2,3},{3,2},{4,5},{5,4},{6,7},{7,6},{8,9},{9,8},{10,11... | collective-permute-start | bytes 1056776 | tf_op jit(solution)/shard_map/ppermute | solution.py:59
  130.1 1.5 copy-start.11
  130.1 2.0 copy-start.13
  130.1 9.0 %collective-permute-start.24 = (bf16[86,16,128]{2,1,0:T(8,128)(2,1)S(1)}, bf16[86,16,128]{2,1,0:T(8,128)(2,1)S(1)}, u32[]{:S(2)}, u32[]{:S(2)}) collective-permute-start(bf16[86,16,128]{2,1,0:T(8,128)(2,1)S(1)} %slice.57), channel_id=1, source_target_pairs={{0,16},{1,17},{2,18},{3,19},{4,20},{5,21},{6,22},{7,23},{8,24},{9,... | collective-permute-start | bytes 1056776 | tf_op jit(solution)/shard_map/ppermute | solution.py:59
  131.5 10.3 %collective-permute-start.25 = (bf16[172,16,128]{2,1,0:T(8,128)(2,1)}, bf16[172,16,128]{2,1,0:T(8,128)(2,1)}, u32[]{:S(2)}, u32[]{:S(2)}) collective-permute-start(bf16[172,16,128]{2,1,0:T(8,128)(2,1)} %shard_map.95.rest_0_), channel_id=1, source_target_pairs={{0,8},{1,9},{2,10},{3,11},{4,12},{5,13},{6,14},{7,15},{8,0},{9,1},... | collective-permute-start | bytes 2113544 | tf_op jit(solution)/shard_map/ppermute | solution.py:59
  131.5 10.3 %collective-permute-start.26 = (bf16[172,16,128]{2,1,0:T(8,128)(2,1)S(1)}, bf16[172,16,128]{2,1,0:T(8,128)(2,1)}, u32[]{:S(2)}, u32[]{:S(2)}) collective-permute-start(bf16[172,16,128]{2,1,0:T(8,128)(2,1)S(1)} %copy-done.11), channel_id=1, source_target_pairs={{0,8},{1,9},{2,10},{3,11},{4,12},{5,13},{6,14},{7,15},{8,0},{9,1},... | collective-permute-start | bytes 2113544 | tf_op jit(solution)/shard_map/ppermute | solution.py:59
  132.0 9.8 %collective-permute-start.27 = (bf16[172,16,128]{2,1,0:T(8,128)(2,1)S(1)}, bf16[172,16,128]{2,1,0:T(8,128)(2,1)}, u32[]{:S(2)}, u32[]{:S(2)}) collective-permute-start(bf16[172,16,128]{2,1,0:T(8,128)(2,1)S(1)} %copy-done.13), channel_id=1, source_target_pairs={{0,8},{1,9},{2,10},{3,11},{4,12},{5,13},{6,14},{7,15},{8,0},{9,1},... | collective-permute-start | bytes 2113544 | tf_op jit(solution)/shard_map/ppermute | solution.py:59
  139.1 1.9 collective-permute-start.28
  139.8 2.0 collective-permute-start.29
  140.4 1.5 copy-start.21
  (15 other events, 12.2 us)

commit v3 on v2

--- a/solution.py
+++ b/solution.py
@@ -44,6 +44,55 @@
         input_output_aliases={0: 0},
         compiler_params=pltpu.CompilerParams(vmem_limit_bytes=60 * 2**20),
     )(value, *after)
+
+
+def pack_kernel(part_ref, q_ref, o_ref, *rest):
+    *outs, q_scr, o_scr = rest
+    layers, rows, width = q_ref.shape
+    hd = o_ref.shape[1]
+    q_scr[:, :, :width] = q_ref[...]
+    if q_scr.shape[2] > width:
+        q_scr[:, :, width:] = jnp.zeros((layers, rows, q_scr.shape[2] - width), q_scr.dtype)
+    o_scr[:, :hd, :] = o_ref[...]
+    if o_scr.shape[1] > hd:
+        o_scr[:, hd:, :] = jnp.zeros((layers, o_scr.shape[1] - hd, o_scr.shape[2]), o_scr.dtype)
+    rg, og = rows // ROWS, o_scr.shape[1] // ROWS
+    n_q, n_o = rg * (q_scr.shape[2] // LANES), og * (o_scr.shape[2] // LANES)
+    quarter = outs[0].shape[0]
+
+    def block(scr, layer, index, groups):
+        row = pl.multiple_of(lax.rem(index, groups) * ROWS, ROWS)
+        lane = pl.multiple_of(lax.div(index, groups) * LANES, LANES)
+        return scr[layer, pl.ds(row, ROWS), pl.ds(lane, LANES)]
+
+    def body(i, carry):
+        index = part_ref[0] * quarter + i
+        in_q = jnp.minimum(index, n_q - 1)
+        in_o = jnp.clip(index - n_q, 0, n_o - 1)
+        for layer in range(layers):
+            out = outs[min(layer, 1)]
+            out[i + max(layer - 1, 0) * quarter] = jnp.where(index < n_q, block(q_scr, layer, in_q, rg), block(o_scr, layer, in_o, og))
+        return carry
+
+    lax.fori_loop(0, quarter, body, 0)
+
+
+def own_quarters(part, w_qkv, w_out, quarter):
+    layers, rows, width = w_qkv.shape
+    vmem = pl.BlockSpec(memory_space=pltpu.VMEM)
+    return pl.pallas_call(
+        pack_kernel,
+        out_shape=[
+            jax.ShapeDtypeStruct((n * quarter, ROWS, LANES), w_qkv.dtype) for n in (1, layers - 1)
+        ],
+        in_specs=[pl.BlockSpec(memory_space=pltpu.SMEM), vmem, vmem],
+        out_specs=[vmem] * 2,
+        scratch_shapes=[
+            pltpu.VMEM((layers, rows, ceil_to(width, LANES)), w_qkv.dtype),
+            pltpu.VMEM((layers, ceil_to(w_out.shape[1], ROWS), w_out.shape[2]), w_out.dtype),
+        ],
+        compiler_params=pltpu.CompilerParams(vmem_limit_bytes=60 * 2**20),
+    )(part, w_qkv, w_out)
 
 
 class Routes:
@@ -262,7 +311,7 @@
 
 
 def backward(plan, gates_ref, outgrad, x, gain, inverse, proj_ref, probs_of, att_of, sens,
-             weights, w_ref, dgated_scr, dproj_scr, g_ref, sens_ref):
+             weights, w_ref, dgated_scr, dproj_scr):
     T, D, heads, hd, wide = dims_of(plan)
     layer, stride, hidden = plan["layer"], plan["og"] * ROWS, heads * hd
     lane_tiles = D // LANES
@@ -296,7 +345,6 @@
         for m, d in enumerate((dqueries, dkeys, dvalues)):
             at = m * hidden + h * hd
             dproj_scr[:, at : at + hd] = d.astype(jnp.bfloat16)
-    sens_ref[...] = sens.astype(jnp.bfloat16)
     weights.need("w_tiles", range(plan["tiles"]))
     dproj = dproj_scr[...]
     step = 2 * LANES
@@ -319,7 +367,7 @@
         + inverse * dnormed
         - xf * (inverse * inverse * inverse) * mean
     )
-    g_ref[...] = ingrad.astype(jnp.bfloat16)
+    return ingrad, sens
 
 
 def both_kernel(plan, place_ref, gates_ref, x_ref, gain_ref, bias_ref, *rest):
@@ -338,24 +386,23 @@
         probs, attended = attend(plan, h, proj_scr, bias)
         probs_scr[h] = probs
         att_scr[:, h * hd : (h + 1) * hd] = attended
-    backward(
+    ingrad, sens = backward(
         plan, gates_ref, rows_of(plan, x_ref, True), x, gain, inverse, proj_scr,
         lambda h: probs_scr[h], lambda h: att_scr[:, h * hd : (h + 1) * hd],
         jnp.zeros((T, LANES), jnp.float32), weights, w_ref, dgated_scr, dproj_scr,
-        g_ref.at[:, :D], g_ref.at[:, D : D + LANES],
     )
-
-
-def bwd_kernel(plan, place_ref, gates_ref, x_ref, gain_ref, outgrad_ref, proj_in, probs_in, att_in,
-               *rest):
+    g_ref[:, :D] = ingrad.astype(jnp.bfloat16)
+    g_ref[:, D:] = sens.astype(jnp.bfloat16)
+
+
+def bwd_kernel(plan, place_ref, gates_ref, x_ref, gain_ref, *rest):
+    T, D, heads, hd, wide = dims_of(plan)
+    n_in, n_out = plan["n_in"], plan["n_out"]
+    outgrad_refs, rest = rest[:n_in], rest[n_in:]
+    proj_in, probs_in, att_in, *rest = rest
     n = plan["n_refs"]
-    refs, rest = rest[:n], rest[n:]
-    if plan["apart"]:
-        g_ref, sens_ref, *rest = rest
-    else:
-        g_ref, *rest = rest
-    w_ref, sems, proj_ref, probs_ref, att_ref, dgated_scr, dproj_scr = rest
-    T, D, heads, hd, wide = dims_of(plan)
+    refs, outs, rest = rest[:n], rest[n : n + n_out], rest[n + n_out :]
+    w_ref, sems, proj_ref, probs_ref, att_ref, dgated_scr, dproj_scr, flow_scr = rest
     layer = plan["layer"]
     loads = []
     for src, dst in ((att_in, att_ref), (proj_in, proj_ref), (probs_in, probs_ref)):
@@ -366,16 +413,45 @@
     gain = gain_ref[layer : layer + 1, :]
     x = rows_of(plan, x_ref)
     inverse, _ = norm(x, gain)
+
+    def block(count, k):
+        rows = T // count
+        return pl.ds(pl.multiple_of(place_ref[8 + k] * rows, rows), rows)
+
+    outgrad_ref = outgrad_refs[0]
+    if n_in > 1:
+        outgrad_ref = dproj_scr.at[:, : D + LANES]
+        for k, ref in enumerate(outgrad_refs):
+            outgrad_ref[block(n_in, k), :] = ref[...]
+    outgrad, sens = outgrad_ref[:, :D], outgrad_ref[:, D : D + LANES].astype(jnp.float32)
     for copy in loads:
         copy.wait()
-    if not plan["apart"]:
-        g_ref, sens_ref = g_ref.at[:, :D], g_ref.at[:, D : D + LANES]
-    backward(
-        plan, gates_ref, outgrad_ref[:, :D], x, gain, inverse,
+    ingrad, sens = backward(
+        plan, gates_ref, outgrad, x, gain, inverse,
         proj_ref, lambda h: probs_ref[h], lambda h: att_ref[:, h * hd : (h + 1) * hd],
-        outgrad_ref[:, D : D + LANES].astype(jnp.float32),
-        weights, w_ref, dgated_scr, dproj_scr, g_ref, sens_ref,
+        sens, weights, w_ref, dgated_scr, dproj_scr,
     )
+    if plan["last"]:
+        g_ref, sens_ref = outs
+        cols, n_tiles = g_ref.shape[1], D // LANES
+        for t in range(n_tiles):
+            flow_scr[t] = ingrad[:, t * LANES : (t + 1) * LANES]
+        flow_scr[n_tiles] = sens
+        for j in range(cols):
+            rows = pl.ds(j, T // cols, stride=cols)
+            for t in range(n_tiles):
+                g_ref[:, j, t * LANES : (t + 1) * LANES] = flow_scr[t, rows, :].astype(jnp.bfloat16)
+            own = flow_scr[n_tiles, rows, :].astype(jnp.bfloat16)
+            for m in range(sens_ref.shape[0]):
+                sens_ref[m, :, j, :] = own[:, m * heads : (m + 1) * heads]
+    elif n_out > 1:
+        flow_scr[:, :D] = ingrad
+        flow_scr[:, D:] = sens
+        for k, out in enumerate(outs):
+            out[...] = flow_scr[block(n_out, k), :].astype(jnp.bfloat16)
+    else:
+        outs[0][:, :D] = ingrad.astype(jnp.bfloat16)
+        outs[0][:, D:] = sens.astype(jnp.bfloat16)
 
 
 def call(kernel, plan, place, gates, weights, arrays, saved, outs, saves, scratch, flops):
@@ -430,7 +506,7 @@
     home, teacher = flat(tokens), flat(cotangent)
 
     shard = w_qkv.shape[1]
-    base = dict(T=T, D=D, heads=heads, hd=hd, tiles=tiles, og=og, square=False, apart=False, pairs=0,
+    base = dict(T=T, D=D, heads=heads, hd=hd, tiles=tiles, og=og, square=False, pairs=0,
                 w_tiles=(shard // ROWS, 0), o_tiles=(og, shard // ROWS * tiles))
     weights = []
     fast = n_ha == 4 and n_wa % 4 == 0 and shard % ROWS == 0 and w_out.shape[1] == hd
@@ -440,14 +516,9 @@
         n_z = n_wa // 2
         spot = ha * 2 + wa % 2
         spots = [spot ^ k for k in (0, 1, 4, 5, 2, 3, 6, 7)]
-        place = jnp.stack(spots).astype(jnp.int32)
+        place = jnp.stack(spots + [ha ^ k for k in range(n_ha)]).astype(jnp.int32)
         rg = shard // ROWS
         quarter = -(-(rg * tiles + og * lane_tiles) // 4)
-
-        def own_quarter(layer):
-            own = flat_blocks(blocks_of(w_qkv[layer]), blocks_of(w_out[layer]))
-            own = jnp.pad(own, [(0, 4 * quarter - own.shape[0]), (0, 0), (0, 0)])
-            return lax.dynamic_slice_in_dim(own, ha * quarter, quarter, 0)
 
         def addresses(at):
             return dict(
@@ -462,8 +533,9 @@
         base.update(n_line=n_z * quarter, n_blocks=4 * quarter * n_wa, quarter=quarter, n_parts=4)
         plans = [dict(base, layer=layer, square=True, **squarewise) for layer in range(layers)]
 
-        line = routes.line(own_quarter(0))
-        later = hand_on(jnp.concatenate([own_quarter(1), own_quarter(2)]), line)
+        own, later = own_quarters(ha.astype(jnp.int32)[None], w_qkv, w_out, quarter)
+        line = routes.line(own)
+        later = hand_on(later, line)
         far = [routes.send(later, wa_bits=2 * k) for k in range(1, n_z)]
         lines = []
 
@@ -514,11 +586,12 @@
             kept + grads[:1], dense,
         )
 
-    def back(layer, x, outgrad, saved, pairs, outs):
-        plan = dict(plans[layer], pairs=pairs, apart=len(outs) > 1)
+    def back(layer, x, outgrads, saved, pairs, outs, last=False):
+        plan = dict(plans[layer], pairs=pairs, n_in=len(outgrads), n_out=len(outs), last=last)
+        flow = pltpu.VMEM((D // LANES + 1, T, LANES) if last else (T, D + LANES), f32)
         return call(
-            bwd_kernel, plan, place, gates, weights[layer], [x, gains, outgrad], saved, outs, [],
-            kept + grads, dense,
+            bwd_kernel, plan, place, gates, weights[layer], [x, gains] + outgrads, saved, outs, [],
+            kept + grads + [flow], dense,
         )
 
     after_time, *saved_time = forward(0, home, teacher, 0, n_ha)
@@ -533,17 +606,22 @@
         both_kernel, dict(plans[2], pairs=n_wa), place, gates, weights[2],
         [across, gains, biases[2]], [], [loaded], [], kept + grads, 2 * dense,
     )
-    (grad,) = back(1, tall, swap(grad, "wa"), saved_height, n_ha, [loaded])
-    apart = [act, jax.ShapeDtypeStruct((T, LANES), bf16)]
-    grad, sens = back(0, home, swap(grad, "ha"), saved_time, 0, apart)
-
-    def unflat(value):
-        value = value.reshape(frames, videos, rows, cols, value.shape[-1])
-        return jnp.swapaxes(value, 0, 1)
-
-    token_grad = unflat(grad)
-    sens = unflat(sens[:, : layers * heads]).reshape(videos, frames, rows, cols, layers, heads)
-    return (token_grad, jnp.moveaxis(sens, 4, 1))
+    grad = swap(grad, "wa")
+    if fast:
+        block = jax.ShapeDtypeStruct((T // n_ha, D + LANES), bf16)
+        blocks = back(1, tall, [grad], saved_height, n_ha, [block] * n_ha)
+        outgrads = [blocks[0]] + [routes.send(blocks[k], ha_bits=k) for k in range(1, n_ha)]
+    else:
+        (grad,) = back(1, tall, [grad], saved_height, n_ha, [loaded])
+        outgrads = [swap(grad, "ha")]
+    ends = [
+        jax.ShapeDtypeStruct((T // cols, cols, D), bf16),
+        jax.ShapeDtypeStruct((layers, T // cols, cols, heads), bf16),
+    ]
+    grad, sens = back(0, home, outgrads, saved_time, 0, ends, True)
+    token_grad = jnp.swapaxes(grad.reshape(frames, videos, rows, cols, D), 0, 1)
+    sens = sens.reshape(layers, frames, videos, rows, cols, heads)
+    return (token_grad, jnp.moveaxis(sens, 2, 0))
 
 
 def solution(mesh):

time: 203 us -> 191 us (0.941)
  local copies, waits for them, and re-layouts: 34.4 us -> 19.2 us
  blocking collectives: 47.8 us -> 36.6 us
  waiting for transfers between devices: 39 us -> 48.5 us
  Pallas kernels: 45.8 us -> 50.2 us
  starting transfers between devices: 29.2 us -> 32.5 us
  other arithmetic: 4.3 us -> 2.07 us
    all_to_all x2 -> x1, blocking collectives: 27.4 us -> 15.8 us  [swap(): return lax.all_to_all(value, axis, split_axis=0, concat_axis=0, tiled=True)]
    ppermute x30 -> x33, waiting for transfers between devices: 39 us -> 48.5 us  [send(): return lax.ppermute(value, AXES, pairs)]
    squeeze x2 -> x0, local copies, waits for them, and re-layouts: 4.04 us -> none  [own_quarter(): own = flat_blocks(blocks_of(w_qkv[layer]), blocks_of(w_out[layer]))]
    ppermute x30 -> x33, starting transfers between devices: 21.6 us -> 25.2 us  [send(): return lax.ppermute(value, AXES, pairs)]
    pallas_call x0 -> x1, Pallas kernels: none -> 3.41 us  [own_quarters(): pl.pallas_call(pack_kernel, out_shape=[jax.ShapeDtypeStruct((n * quarter,...]
    pad x6 -> x0, local copies, waits for them, and re-layouts: 2.92 us -> none  [blocks_of(): w = jnp.pad(w, [(0, tall - rows), (0, wide - cols)])]
    another operation x3 -> x1, local copies, waits for them, and re-layouts: 3.32 us -> 0.67 us  [per_device(): place = jnp.stack(spots + [ha ^ k for k in range(n_ha)]).astype(jnp.int32)]
    reshape x6 -> x0, local copies, waits for them, and re-layouts: 2.56 us -> none  [blocks_of(): w.reshape(tall // ROWS, ROWS, wide // LANES, LANES)]
  transfers between devices with their start and end apart: 32 -> 35, of which waited for: 12 -> 15; matrix products, arithmetic and copies ran while one was open for 9% -> 5% of each run, Pallas kernels for 9% -> 9%
where the time goes in v3:
time: 191 us; the launch traced here: 190 us
  Pallas kernels  50.2 us (26%)
  waiting for transfers between devices  48.5 us (25%)
  blocking collectives  36.6 us (19%)
  starting transfers between devices  32.5 us (17%)
  local copies, waits for them, and re-layouts  19.2 us (10%)
  other arithmetic  2.07 us (1%)
    ppermute x33, waiting for transfers between devices, send(): return lax.ppermute(value, AXES, pairs)  48.5 us
    pallas_call x5, Pallas kernels, call(): pl.pallas_call(functools.partial(kernel, plan), out_shape=list(outs) + li...  43.8 us
    ppermute x33, starting transfers between devices, send(): return lax.ppermute(value, AXES, pairs)  25.2 us
    all_gather x1, blocking collectives, line(): lax.all_gather(value, AXES, axis=0, tiled=True, axis_index_groups=groups)  20.7 us
    all_to_all x1, blocking collectives, swap(): return lax.all_to_all(value, axis, split_axis=0, concat_axis=0, tiled=True)  15.8 us
    unnamed x66, local copies, waits for them, and re-layouts  11.9 us
    all_to_all x2, starting transfers between devices, swap(): return lax.all_to_all(value, axis, split_axis=0, concat_axis=0, tiled=True)  7.22 us
    slice x6, local copies, waits for them, and re-layouts, over_square(): low, high = (routes.y(over_x[:half]), routes.x(over_y[half:]))  5.04 us
  transfers between devices with their start and end apart: 35, of which 15 were waited for; matrix products, arithmetic and copies ran while one was open for 5% of the time, Pallas kernels for 9%

profile of v3, /device:TPU:0, one launch (start us, length us, event | category | flops | bytes accessed | tf_op | source)
XLA Modules:
  0.0 190.1 jit_solution(12789097471057846751)
XLA Ops:
  0.6 3.4 %shard_map.77 = (bf16[43,16,128]{2,1,0:T(8,128)(2,1)}, bf16[86,16,128]{2,1,0:T(8,128)(2,1)}) custom-call(s32[1]{0:T(128)} %bitcast.8.part_ref, bf16[3,144,1728]{2,1,0:T(8,128)(2,1)} %q_ref.1, bf16[3,72,1152]{2,1,0:T(8,128)(2,1)} %o_ref.1), custom_call_target="tpu_custom_call" | custom-call | tf_op jit(solution)/shard_map/pallas_call | solution.py:83
  4.1 20.7 %all_gather.3.refs_0_.refs_1_ = bf16[172,16,128]{2,1,0:T(8,128)(2,1)S(1)} all-gather(bf16[43,16,128]{2,1,0:T(8,128)(2,1)} %get-tuple-element.20), channel_id=1, replica_groups={{0,2,4,6},{1,3,5,7},{8,10,12,14},{9,11,13,15},{16,18,20,22},{17,19,21,2..., dimensions={0}, use_global_device_ids=true | all-gather | bytes 880640 | tf_op jit(solution)/shard_map/all_gather | solution.py:125
  24.8 1.5 collective-permute-start.1
  26.3 1.5 collective-permute-start
  27.8 2.3 %collective-permute-start.5 = (bf16[86,16,128]{2,1,0:T(8,128)(2,1)}, bf16[86,16,128]{2,1,0:T(8,128)(2,1)}, u32[]{:S(2)}, u32[]{:S(2)}) collective-permute-start(bf16[86,16,128]{2,1,0:T(8,128)(2,1)} %shard_map.81.refs_1_), channel_id=1, source_target_pairs={{0,6},{1,7},{2,4},{3,5},{4,2},{5,3},{6,0},{7,1},{8,14},{9,15},{10,... | collective-permute-start | bytes 1056776 | tf_op jit(solution)/shard_map/ppermute | solution.py:108
  33.3 6.6 %collective-permute-done.1.refs_0_ = bf16[172,16,128]{2,1,0:T(8,128)(2,1)S(1)} collective-permute-done((bf16[172,16,128]{2,1,0:T(8,128)(2,1)S(1)}, bf16[172,16,128]{2,1,0:T(8,128)(2,1)S(1)}, u32[]{:S(2)}, u32[]{:S(2)}) %collective-permute-start.1) | collective-permute-done | bytes 704544 | tf_op jit(solution)/shard_map/ppermute | solution.py:108
  39.9 0.9 copy-done.2
  40.8 1.0 collective-permute-start.4
  41.8 0.9 collective-permute-start.3
  42.7 0.9 copy-done
  43.6 1.0 slice.25
  44.6 1.6 collective-permute-start.6
  46.2 1.6 collective-permute-start.2
  48.4 11.0 %collective-permute-done.4.refs_3_ = bf16[86,16,128]{2,1,0:T(8,128)(2,1)} collective-permute-done((bf16[86,16,128]{2,1,0:T(8,128)(2,1)}, bf16[86,16,128]{2,1,0:T(8,128)(2,1)}, u32[]{:S(2)}, u32[]{:S(2)}) %collective-permute-start.4) | collective-permute-done | bytes 352288 | tf_op jit(solution)/shard_map/ppermute | solution.py:108
  60.1 2.9 %shard_map.82 = (bf16[172,16,128]{2,1,0:T(8,128)(2,1)}, bf16[172,16,128]{2,1,0:T(8,128)(2,1)}) custom-call(s32[4]{0:T(128)} %pad_add_fusion.refs_0_, bf16[86,16,128]{2,1,0:T(8,128)(2,1)} %shard_map.81.refs_1_, bf16[86,16,128]{2,1,0:T(8,128)(2,1)} %collective-permute-done.3.refs_2_, bf16[86,16,128]{2,1,0:T(8,128)(2,1)} %collective-permute-done.4.refs_3_, ...), custom_call_target="tpu_custom_call" | custom-call | tf_op jit(solution)/shard_map/pallas_call | solution.py:162
  65.6 1.5 collective-permute-start.13
  67.1 1.5 collective-permute-start.12
  69.4 1.1 collective-permute-done.10.rest_8_.rest_15_
  70.5 7.2 %shard_map.85 = (bf16[256,1152]{1,0:T(8,128)(2,1)}, bf16[128,1792]{1,0:T(8,128)(2,1)}, f32[8,128,128]{2,1,0:T(8,128)}, bf16[128,576]{1,0:T(8,128)(2,1)}) custom-call(s32[12]{0:T(128)} %stack.66.place_ref, f32[3,8]{1,0:T(4,128)} %gates_ref.9, bf16[128,1152]{1,0:T(8,128)(2,1)} %reshape_transpose.6.refs_1_.x_ref, f32[3,1152]{1,0:T(4,128)} %gain_ref.9, ...), custom_call_target="tpu_custom_call" | custom-call | flops 679477248 | bytes 12582912 | tf_op jit(solution)/shard_map/pallas_call | solution.py:462
  77.7 3.5 %all-to-all-start = ((bf16[4,64,1152]{2,1,0:T(8,128)(2,1)}), bf16[4,64,1152]{2,1,0:T(8,128)(2,1)S(1)}, u32[]{:S(2)}, u32[]{:S(2)}) async-start(bf16[4,64,1152]{2,1,0:T(8,128)(2,1)} %bitcast.30), calls=%async_computation | async-start | bytes 1179648 | tf_op jit(solution)/shard_map/all_to_all | solution.py:504
  81.2 2.8 %collective-permute-done.13.refs_0_ = bf16[172,16,128]{2,1,0:T(8,128)(2,1)S(1)} collective-permute-done((bf16[172,16,128]{2,1,0:T(8,128)(2,1)}, bf16[172,16,128]{2,1,0:T(8,128)(2,1)S(1)}, u32[]{:S(2)}, u32[]{:S(2)}) %collective-permute-start.13) | collective-permute-done | bytes 704544 | tf_op jit(solution)/shard_map/ppermute | solution.py:108
  84.0 0.9 copy-done.8
  84.9 1.0 slice.26
  85.9 2.0 %collective-permute-start.14 = (bf16[86,16,128]{2,1,0:T(8,128)(2,1)S(1)}, bf16[86,16,128]{2,1,0:T(8,128)(2,1)S(1)}, u32[]{:S(2)}, u32[]{:S(2)}) collective-permute-start(bf16[86,16,128]{2,1,0:T(8,128)(2,1)S(1)} %slice.26), channel_id=1, source_target_pairs={{0,1},{1,0},{2,3},{3,2},{4,5},{5,4},{6,7},{7,6},{8,9},{9,8},{10,11... | collective-permute-start | bytes 1056776 | tf_op jit(solution)/shard_map/ppermute | solution.py:108
  87.9 0.9 copy-done.6
  88.7 1.0 slice.27
  89.7 1.5 collective-permute-start.15
  91.9 3.9 %collective-permute-done.14.refs_0_ = bf16[86,16,128]{2,1,0:T(8,128)(2,1)S(1)} collective-permute-done((bf16[86,16,128]{2,1,0:T(8,128)(2,1)S(1)}, bf16[86,16,128]{2,1,0:T(8,128)(2,1)S(1)}, u32[]{:S(2)}, u32[]{:S(2)}) %collective-permute-start.14) | collective-permute-done | bytes 352288 | tf_op jit(solution)/shard_map/ppermute | solution.py:108
  96.6 2.5 %collective-permute-done.15.refs_0_ = bf16[86,16,128]{2,1,0:T(8,128)(2,1)S(1)} collective-permute-done((bf16[86,16,128]{2,1,0:T(8,128)(2,1)S(1)}, bf16[86,16,128]{2,1,0:T(8,128)(2,1)S(1)}, u32[]{:S(2)}, u32[]{:S(2)}) %collective-permute-start.15) | collective-permute-done | bytes 352288 | tf_op jit(solution)/shard_map/ppermute | solution.py:108
  99.8 1.5 collective-permute-start.22
  102.4 7.5 %shard_map.92 = (bf16[256,1152]{1,0:T(8,128)(2,1)}, bf16[128,1792]{1,0:T(8,128)(2,1)}, f32[8,128,128]{2,1,0:T(8,128)}, bf16[128,576]{1,0:T(8,128)(2,1)}) custom-call(s32[12]{0:T(128)} %stack.66.place_ref, f32[3,8]{1,0:T(4,128)} %gates_ref.9, bf16[256,1152]{1,0:T(8,128)(2,1)} %bitcast.26, f32[3,1152]{1,0:T(4,128)} %gain_ref.9, ...), custom_call_target="tpu_custom_call" | custom-call | flops 679477248 | bytes 12582912 | tf_op jit(solution)/shard_map/pallas_call | solution.py:462
  109.9 3.7 %all-to-all-start.1 = ((bf16[8,32,1152]{2,1,0:T(8,128)(2,1)}), bf16[8,32,1152]{2,1,0:T(8,128)(2,1)S(1)}, u32[]{:S(2)}, u32[]{:S(2)}) async-start(bf16[8,32,1152]{2,1,0:T(8,128)(2,1)} %bitcast.29), calls=%async_computation.1 | async-start | bytes 1179648 | tf_op jit(solution)/shard_map/all_to_all | solution.py:504
  113.6 4.6 %collective-permute-done.22.refs_0_ = bf16[172,16,128]{2,1,0:T(8,128)(2,1)S(1)} collective-permute-done((bf16[172,16,128]{2,1,0:T(8,128)(2,1)}, bf16[172,16,128]{2,1,0:T(8,128)(2,1)S(1)}, u32[]{:S(2)}, u32[]{:S(2)}) %collective-permute-start.22) | collective-permute-done | bytes 704544 | tf_op jit(solution)/shard_map/ppermute | solution.py:108
  118.2 0.9 copy-done.12
  119.1 1.0 slice.28
  120.7 3.0 %collective-permute-done.21.refs_0_ = bf16[172,16,128]{2,1,0:T(8,128)(2,1)S(1)} collective-permute-done((bf16[172,16,128]{2,1,0:T(8,128)(2,1)}, bf16[172,16,128]{2,1,0:T(8,128)(2,1)S(1)}, u32[]{:S(2)}, u32[]{:S(2)}) %collective-permute-start.21) | collective-permute-done | bytes 704544 | tf_op jit(solution)/shard_map/ppermute | solution.py:108
  123.6 0.9 copy-done.10
  124.5 1.0 slice.29
  125.6 1.5 collective-permute-start.24
  127.7 5.9 %collective-permute-done.23.refs_0_ = bf16[86,16,128]{2,1,0:T(8,128)(2,1)S(1)} collective-permute-done((bf16[86,16,128]{2,1,0:T(8,128)(2,1)S(1)}, bf16[86,16,128]{2,1,0:T(8,128)(2,1)S(1)}, u32[]{:S(2)}, u32[]{:S(2)}) %collective-permute-start.23) | collective-permute-done | bytes 352288 | tf_op jit(solution)/shard_map/ppermute | solution.py:108
  136.2 0.9 collective-permute-done.29.rest_9_
  137.8 10.6 %shard_map.99 = bf16[128,1280]{1,0:T(8,128)(2,1)} custom-call(s32[12]{0:T(128)} %stack.66.place_ref, f32[3,8]{1,0:T(4,128)} %gates_ref.9, bf16[256,1152]{1,0:T(8,128)(2,1)} %bitcast.31, f32[3,1152]{1,0:T(4,128)} %gain_ref.9, f32[128,128]{1,0:T(8,128)} %get-tuple-element.38.refs_5_.bias_ref, bf16[172,16,128]{2,1,0:T(8,128)(2,1)} %shard_map.96.rest_0_, ...), custom_call_target="tpu_custom_call" | custom-call | flops 1358954496 | bytes 12582912 | tf_op jit(solution)/shard_map/pallas_call | solution.py:462
  148.4 15.8 %all_to_all.33 = bf16[8,16,1280]{2,1,0:T(8,128)(2,1)} all-to-all(bf16[8,16,1280]{2,1,0:T(8,128)(2,1)} %bitcast.33), channel_id=1, replica_groups=mesh['ha'=4,'wa'=8] {'wa'}, dimensions={0} | all-to-all | bytes 655360 | tf_op jit(solution)/shard_map/all_to_all | solution.py:504
  164.2 9.0 %shard_map.100 = (bf16[32,1280]{1,0:T(8,128)(2,1)}, bf16[32,1280]{1,0:T(8,128)(2,1)}, bf16[32,1280]{1,0:T(8,128)(2,1)}, bf16[32,1280]{1,0:T(8,128)(2,1)}) custom-call(s32[12]{0:T(128)} %stack.66.place_ref, f32[3,8]{1,0:T(4,128)} %gates_ref.9, bf16[256,1152]{1,0:T(8,128)(2,1)} %bitcast.28, f32[3,1152]{1,0:T(4,128)} %gain_ref.9, bf16[128,1280]{1,0:T(8,128)(2,1)} %bitcast.32, ...), custom_call_target="tpu_custom_call" | custom-call | flops 679477248 | bytes 12582912 | tf_op jit(solution)/shard_map/pallas_call | solution.py:462
  173.3 1.6 collective-permute-start.31
  175.2 3.5 %collective-permute-done.31.rest_2_ = bf16[32,1280]{1,0:T(8,128)(2,1)S(1)} collective-permute-done((bf16[32,1280]{1,0:T(8,128)(2,1)}, bf16[32,1280]{1,0:T(8,128)(2,1)S(1)}, u32[]{:S(2)}, u32[]{:S(2)}) %collective-permute-start.31) | collective-permute-done | bytes 81952 | tf_op jit(solution)/shard_map/ppermute | solution.py:108
  178.7 1.1 collective-permute-done.32.rest_3_
  180.4 9.5 %shard_map.101 = (bf16[64,2,1152]{2,1,0:T(2,128)(2,1)}, bf16[3,64,2,8]{3,2,1,0:T(2,128)(2,1)}) custom-call(s32[12]{0:T(128)} %stack.66.place_ref, f32[3,8]{1,0:T(4,128)} %gates_ref.9, bf16[128,1152]{1,0:T(8,128)(2,1)} %reshape_transpose.6.refs_1_.x_ref, f32[3,1152]{1,0:T(4,128)} %gain_ref.9, bf16[32,1280]{1,0:T(8,128)(2,1)} %get-tuple-element.29.rest_0_, ...), custom_call_target="tpu_custom_call" | custom-call | flops 679477248 | bytes 12582912 | tf_op jit(solution)/shard_map/pallas_call | solution.py:462
  (130 shorter events, 16.5 us)
Async XLA Ops:
  4.0 27.5 %copy-start.28 = (bf16[1,8,8,2,1152]{4,3,2,1,0:T(2,128)(2,1)S(1)}, bf16[1,8,8,2,1152]{4,3,2,1,0:T(2,128)(2,1)}, u32[]{:S(2)}) copy-start(bf16[1,8,8,2,1152]{4,3,2,1,0:T(2,128)(2,1)} %param.6) | copy-start | bytes 884740
  4.0 28.4 %copy-start.29 = (bf16[1,8,8,2,1152]{4,3,2,1,0:T(2,128)(2,1)S(1)}, bf16[1,8,8,2,1152]{4,3,2,1,0:T(2,128)(2,1)}, u32[]{:S(2)}) copy-start(bf16[1,8,8,2,1152]{4,3,2,1,0:T(2,128)(2,1)} %param.7) | copy-start | bytes 884740
  24.8 3.0 %copy-start.5 = (bf16[172,16,128]{2,1,0:T(8,128)(2,1)}, bf16[172,16,128]{2,1,0:T(8,128)(2,1)S(1)}, u32[]{:S(2)}) copy-start(bf16[172,16,128]{2,1,0:T(8,128)(2,1)S(1)} %all_gather.3.refs_0_.refs_1_) | copy-start | bytes 2113540
  24.8 15.1 %collective-permute-start.1 = (bf16[172,16,128]{2,1,0:T(8,128)(2,1)S(1)}, bf16[172,16,128]{2,1,0:T(8,128)(2,1)S(1)}, u32[]{:S(2)}, u32[]{:S(2)}) collective-permute-start(bf16[172,16,128]{2,1,0:T(8,128)(2,1)S(1)} %all_gather.3.refs_0_.refs_1_), channel_id=1, source_target_pairs={{0,16},{1,17},{2,18},{3,19},{4,20},{5,21},{6,22},{7,23},{8,24},{9,... | collective-permute-start | bytes 2113544 | tf_op jit(solution)/shard_map/ppermute | solution.py:108
  26.3 16.5 %collective-permute-start = (bf16[172,16,128]{2,1,0:T(8,128)(2,1)S(1)}, bf16[172,16,128]{2,1,0:T(8,128)(2,1)S(1)}, u32[]{:S(2)}, u32[]{:S(2)}) collective-permute-start(bf16[172,16,128]{2,1,0:T(8,128)(2,1)S(1)} %all_gather.3.refs_0_.refs_1_), channel_id=1, source_target_pairs={{0,1},{1,0},{2,3},{3,2},{4,5},{5,4},{6,7},{7,6},{8,9},{9,8},{10,11... | collective-permute-start | bytes 2113544 | tf_op jit(solution)/shard_map/ppermute | solution.py:108
  27.8 18.4 %collective-permute-start.5 = (bf16[86,16,128]{2,1,0:T(8,128)(2,1)}, bf16[86,16,128]{2,1,0:T(8,128)(2,1)}, u32[]{:S(2)}, u32[]{:S(2)}) collective-permute-start(bf16[86,16,128]{2,1,0:T(8,128)(2,1)} %shard_map.81.refs_1_), channel_id=1, source_target_pairs={{0,6},{1,7},{2,4},{3,5},{4,2},{5,3},{6,0},{7,1},{8,14},{9,15},{10,... | collective-permute-start | bytes 1056776 | tf_op jit(solution)/shard_map/ppermute | solution.py:108
  40.8 5.4 %copy-start.3 = (bf16[172,16,128]{2,1,0:T(8,128)(2,1)S(1)}, bf16[172,16,128]{2,1,0:T(8,128)(2,1)}, u32[]{:S(2)}) copy-start(bf16[172,16,128]{2,1,0:T(8,128)(2,1)} %shard_map.79.refs_2_.refs_6_.rest_2_.rest_9_) | copy-start | bytes 2113540
  40.8 26.3 %collective-permute-start.9 = (bf16[172,16,128]{2,1,0:T(8,128)(2,1)}, bf16[172,16,128]{2,1,0:T(8,128)(2,1)S(1)}, u32[]{:S(2)}, u32[]{:S(2)}) collective-permute-start(bf16[172,16,128]{2,1,0:T(8,128)(2,1)} %shard_map.79.refs_2_.refs_6_.rest_2_.rest_9_), channel_id=1, source_target_pairs={{0,8},{1,9},{2,10},{3,11},{4,12},{5,13},{6,14},{7,15},{8,0},{9,1},... | collective-permute-start | bytes 2113544 | tf_op jit(solution)/shard_map/ppermute | solution.py:108
  40.8 18.6 %collective-permute-start.4 = (bf16[86,16,128]{2,1,0:T(8,128)(2,1)}, bf16[86,16,128]{2,1,0:T(8,128)(2,1)}, u32[]{:S(2)}, u32[]{:S(2)}) collective-permute-start(bf16[86,16,128]{2,1,0:T(8,128)(2,1)} %shard_map.81.refs_1_), channel_id=1, source_target_pairs={{0,4},{1,5},{2,6},{3,7},{4,0},{5,1},{6,2},{7,3},{8,12},{9,13},{10,... | collective-permute-start | bytes 1056776 | tf_op jit(solution)/shard_map/ppermute | solution.py:108
  41.8 18.2 %collective-permute-start.3 = (bf16[86,16,128]{2,1,0:T(8,128)(2,1)}, bf16[86,16,128]{2,1,0:T(8,128)(2,1)}, u32[]{:S(2)}, u32[]{:S(2)}) collective-permute-start(bf16[86,16,128]{2,1,0:T(8,128)(2,1)} %shard_map.81.refs_1_), channel_id=1, source_target_pairs={{0,2},{1,3},{2,0},{3,1},{4,6},{5,7},{6,4},{7,5},{8,10},{9,11},{10,... | collective-permute-start | bytes 1056776 | tf_op jit(solution)/shard_map/ppermute | solution.py:108
  44.6 18.4 %collective-permute-start.6 = (bf16[86,16,128]{2,1,0:T(8,128)(2,1)S(1)}, bf16[86,16,128]{2,1,0:T(8,128)(2,1)S(1)}, u32[]{:S(2)}, u32[]{:S(2)}) collective-permute-start(bf16[86,16,128]{2,1,0:T(8,128)(2,1)S(1)} %slice.25), channel_id=1, source_target_pairs={{0,16},{1,17},{2,18},{3,19},{4,20},{5,21},{6,22},{7,23},{8,24},{9,... | collective-permute-start | bytes 1056776 | tf_op jit(solution)/shard_map/ppermute | solution.py:108
  46.2 18.7 %collective-permute-start.2 = (bf16[86,16,128]{2,1,0:T(8,128)(2,1)S(1)}, bf16[86,16,128]{2,1,0:T(8,128)(2,1)S(1)}, u32[]{:S(2)}, u32[]{:S(2)}) collective-permute-start(bf16[86,16,128]{2,1,0:T(8,128)(2,1)S(1)} %slice.24), channel_id=1, source_target_pairs={{0,1},{1,0},{2,3},{3,2},{4,5},{5,4},{6,7},{7,6},{8,9},{9,8},{10,11... | collective-permute-start | bytes 1056776 | tf_op jit(solution)/shard_map/ppermute | solution.py:108
  63.7 4.9 %collective-permute-start.11 = (bf16[86,16,128]{2,1,0:T(8,128)(2,1)}, bf16[86,16,128]{2,1,0:T(8,128)(2,1)S(1)}, u32[]{:S(2)}, u32[]{:S(2)}) collective-permute-start(bf16[86,16,128]{2,1,0:T(8,128)(2,1)} %shard_map.84.rest_4_.refs_2_.rest_11_), channel_id=1, source_target_pairs={{0,8},{1,9},{2,10},{3,11},{4,12},{5,13},{6,14},{7,15},{8,0},{9,1},... | collective-permute-start | bytes 1056776 | tf_op jit(solution)/shard_map/ppermute | solution.py:108
  63.8 6.7 %collective-permute-start.7 = (bf16[172,16,128]{2,1,0:T(8,128)(2,1)}, bf16[172,16,128]{2,1,0:T(8,128)(2,1)}, u32[]{:S(2)}, u32[]{:S(2)}) collective-permute-start(bf16[172,16,128]{2,1,0:T(8,128)(2,1)} %shard_map.80.rest_0_.rest_7_), channel_id=1, source_target_pairs={{0,8},{1,9},{2,10},{3,11},{4,12},{5,13},{6,14},{7,15},{8,0},{9,1},... | collective-permute-start | bytes 2113544 | tf_op jit(solution)/shard_map/ppermute | solution.py:108
  64.9 5.6 %collective-permute-start.8 = (bf16[172,16,128]{2,1,0:T(8,128)(2,1)S(1)}, bf16[172,16,128]{2,1,0:T(8,128)(2,1)}, u32[]{:S(2)}, u32[]{:S(2)}) collective-permute-start(bf16[172,16,128]{2,1,0:T(8,128)(2,1)S(1)} %copy-done.1), channel_id=1, source_target_pairs={{0,8},{1,9},{2,10},{3,11},{4,12},{5,13},{6,14},{7,15},{8,0},{9,1},... | collective-permute-start | bytes 2113544 | tf_op jit(solution)/shard_map/ppermute | solution.py:108
  65.6 3.0 %copy-start.17 = (bf16[86,16,128]{2,1,0:T(8,128)(2,1)S(1)}, bf16[86,16,128]{2,1,0:T(8,128)(2,1)}, u32[]{:S(2)}) copy-start(bf16[86,16,128]{2,1,0:T(8,128)(2,1)} %shard_map.83.rest_3_.refs_1_.rest_10_) | copy-start | bytes 1056772
  65.6 18.4 %collective-permute-start.13 = (bf16[172,16,128]{2,1,0:T(8,128)(2,1)}, bf16[172,16,128]{2,1,0:T(8,128)(2,1)S(1)}, u32[]{:S(2)}, u32[]{:S(2)}) collective-permute-start(bf16[172,16,128]{2,1,0:T(8,128)(2,1)} %shard_map.86.refs_0_), channel_id=1, source_target_pairs={{0,16},{1,17},{2,18},{3,19},{4,20},{5,21},{6,22},{7,23},{8,24},{9,... | collective-permute-start | bytes 2113544 | tf_op jit(solution)/shard_map/ppermute | solution.py:108
  67.1 3.4 %copy-start.19 = (bf16[172,16,128]{2,1,0:T(8,128)(2,1)}, bf16[172,16,128]{2,1,0:T(8,128)(2,1)S(1)}, u32[]{:S(2)}) copy-start(bf16[172,16,128]{2,1,0:T(8,128)(2,1)S(1)} %collective-permute-done.9.rest_7_.rest_14_) | copy-start | bytes 2113540
  67.1 20.8 %collective-permute-start.12 = (bf16[172,16,128]{2,1,0:T(8,128)(2,1)}, bf16[172,16,128]{2,1,0:T(8,128)(2,1)S(1)}, u32[]{:S(2)}, u32[]{:S(2)}) collective-permute-start(bf16[172,16,128]{2,1,0:T(8,128)(2,1)} %shard_map.86.refs_0_), channel_id=1, source_target_pairs={{0,1},{1,0},{2,3},{3,2},{4,5},{5,4},{6,7},{7,6},{8,9},{9,8},{10,11... | collective-permute-start | bytes 2113544 | tf_op jit(solution)/shard_map/ppermute | solution.py:108
  68.6 1.9 copy-start.21
  68.6 1.9 collective-permute-start.10
  77.7 14.1 %all-to-all-start = ((bf16[4,64,1152]{2,1,0:T(8,128)(2,1)}), bf16[4,64,1152]{2,1,0:T(8,128)(2,1)S(1)}, u32[]{:S(2)}, u32[]{:S(2)}) async-start(bf16[4,64,1152]{2,1,0:T(8,128)(2,1)} %bitcast.30), calls=%async_computation | async-start | bytes 1179648 | tf_op jit(solution)/shard_map/all_to_all | solution.py:504
  85.9 9.9 %collective-permute-start.14 = (bf16[86,16,128]{2,1,0:T(8,128)(2,1)S(1)}, bf16[86,16,128]{2,1,0:T(8,128)(2,1)S(1)}, u32[]{:S(2)}, u32[]{:S(2)}) collective-permute-start(bf16[86,16,128]{2,1,0:T(8,128)(2,1)S(1)} %slice.26), channel_id=1, source_target_pairs={{0,1},{1,0},{2,3},{3,2},{4,5},{5,4},{6,7},{7,6},{8,9},{9,8},{10,11... | collective-permute-start | bytes 1056776 | tf_op jit(solution)/shard_map/ppermute | solution.py:108
  89.7 2.1 %copy-start.9 = (bf16[172,16,128]{2,1,0:T(8,128)(2,1)S(1)}, bf16[172,16,128]{2,1,0:T(8,128)(2,1)}, u32[]{:S(2)}) copy-start(bf16[172,16,128]{2,1,0:T(8,128)(2,1)} %shard_map.88.refs_2_.rest_2_.rest_6_) | copy-start | bytes 2113540
  89.7 9.3 %collective-permute-start.15 = (bf16[86,16,128]{2,1,0:T(8,128)(2,1)S(1)}, bf16[86,16,128]{2,1,0:T(8,128)(2,1)S(1)}, u32[]{:S(2)}, u32[]{:S(2)}) collective-permute-start(bf16[86,16,128]{2,1,0:T(8,128)(2,1)S(1)} %slice.27), channel_id=1, source_target_pairs={{0,16},{1,17},{2,18},{3,19},{4,20},{5,21},{6,22},{7,23},{8,24},{9,... | collective-permute-start | bytes 1056776 | tf_op jit(solution)/shard_map/ppermute | solution.py:108
  91.3 10.9 %collective-permute-start.16 = (bf16[172,16,128]{2,1,0:T(8,128)(2,1)}, bf16[172,16,128]{2,1,0:T(8,128)(2,1)}, u32[]{:S(2)}, u32[]{:S(2)}) collective-permute-start(bf16[172,16,128]{2,1,0:T(8,128)(2,1)} %shard_map.89.rest_0_.rest_4_), channel_id=1, source_target_pairs={{0,8},{1,9},{2,10},{3,11},{4,12},{5,13},{6,14},{7,15},{8,0},{9,1},... | collective-permute-start | bytes 2113544 | tf_op jit(solution)/shard_map/ppermute | solution.py:108
  91.3 10.9 %collective-permute-start.17 = (bf16[172,16,128]{2,1,0:T(8,128)(2,1)S(1)}, bf16[172,16,128]{2,1,0:T(8,128)(2,1)}, u32[]{:S(2)}, u32[]{:S(2)}) collective-permute-start(bf16[172,16,128]{2,1,0:T(8,128)(2,1)S(1)} %copy-done.7), channel_id=1, source_target_pairs={{0,8},{1,9},{2,10},{3,11},{4,12},{5,13},{6,14},{7,15},{8,0},{9,1},... | collective-permute-start | bytes 2113544 | tf_op jit(solution)/shard_map/ppermute | solution.py:108
  91.8 10.4 %collective-permute-start.18 = (bf16[172,16,128]{2,1,0:T(8,128)(2,1)S(1)}, bf16[172,16,128]{2,1,0:T(8,128)(2,1)}, u32[]{:S(2)}, u32[]{:S(2)}) collective-permute-start(bf16[172,16,128]{2,1,0:T(8,128)(2,1)S(1)} %copy-done.9), channel_id=1, source_target_pairs={{0,8},{1,9},{2,10},{3,11},{4,12},{5,13},{6,14},{7,15},{8,0},{9,1},... | collective-permute-start | bytes 2113544 | tf_op jit(solution)/shard_map/ppermute | solution.py:108
  91.9 3.9 %copy-start.4 = (bf16[4,64,1152]{2,1,0:T(8,128)(2,1)}, bf16[4,64,1152]{2,1,0:T(8,128)(2,1)S(1)}, u32[]{:S(2)}) copy-start(bf16[4,64,1152]{2,1,0:T(8,128)(2,1)S(1)} %all-to-all-done) | copy-start | bytes 1769476
  96.6 3.2 %collective-permute-start.19 = (bf16[86,16,128]{2,1,0:T(8,128)(2,1)}, bf16[86,16,128]{2,1,0:T(8,128)(2,1)S(1)}, u32[]{:S(2)}, u32[]{:S(2)}) collective-permute-start(bf16[86,16,128]{2,1,0:T(8,128)(2,1)} %shard_map.90.rest_3_.refs_1_.rest_7_), channel_id=1, source_target_pairs={{0,8},{1,9},{2,10},{3,11},{4,12},{5,13},{6,14},{7,15},{8,0},{9,1},... | collective-permute-start | bytes 1056776 | tf_op jit(solution)/shard_map/ppermute | solution.py:108
  99.8 1.9 collective-permute-start.20
  99.8 2.4 %copy-start.22 = (bf16[86,16,128]{2,1,0:T(8,128)(2,1)}, bf16[86,16,128]{2,1,0:T(8,128)(2,1)S(1)}, u32[]{:S(2)}) copy-start(bf16[86,16,128]{2,1,0:T(8,128)(2,1)S(1)} %collective-permute-done.19.rest_8_.rest_12_) | copy-start | bytes 1056772
  99.8 18.4 %collective-permute-start.22 = (bf16[172,16,128]{2,1,0:T(8,128)(2,1)}, bf16[172,16,128]{2,1,0:T(8,128)(2,1)S(1)}, u32[]{:S(2)}, u32[]{:S(2)}) collective-permute-start(bf16[172,16,128]{2,1,0:T(8,128)(2,1)} %shard_map.93.refs_0_), channel_id=1, source_target_pairs={{0,16},{1,17},{2,18},{3,19},{4,20},{5,21},{6,22},{7,23},{8,24},{9,... | collective-permute-start | bytes 2113544 | tf_op jit(solution)/shard_map/ppermute | solution.py:108
  101.6 22.0 %collective-permute-start.21 = (bf16[172,16,128]{2,1,0:T(8,128)(2,1)}, bf16[172,16,128]{2,1,0:T(8,128)(2,1)S(1)}, u32[]{:S(2)}, u32[]{:S(2)}) collective-permute-start(bf16[172,16,128]{2,1,0:T(8,128)(2,1)} %shard_map.93.refs_0_), channel_id=1, source_target_pairs={{0,1},{1,0},{2,3},{3,2},{4,5},{5,4},{6,7},{7,6},{8,9},{9,8},{10,11... | collective-permute-start | bytes 2113544 | tf_op jit(solution)/shard_map/ppermute | solution.py:108
  109.9 25.6 %all-to-all-start.1 = ((bf16[8,32,1152]{2,1,0:T(8,128)(2,1)}), bf16[8,32,1152]{2,1,0:T(8,128)(2,1)S(1)}, u32[]{:S(2)}, u32[]{:S(2)}) async-start(bf16[8,32,1152]{2,1,0:T(8,128)(2,1)} %bitcast.29), calls=%async_computation.1 | async-start | bytes 1179648 | tf_op jit(solution)/shard_map/all_to_all | solution.py:504
  120.1 13.5 %collective-permute-start.23 = (bf16[86,16,128]{2,1,0:T(8,128)(2,1)S(1)}, bf16[86,16,128]{2,1,0:T(8,128)(2,1)S(1)}, u32[]{:S(2)}, u32[]{:S(2)}) collective-permute-start(bf16[86,16,128]{2,1,0:T(8,128)(2,1)S(1)} %slice.28), channel_id=1, source_target_pairs={{0,1},{1,0},{2,3},{3,2},{4,5},{5,4},{6,7},{7,6},{8,9},{9,8},{10,11... | collective-permute-start | bytes 1056776 | tf_op jit(solution)/shard_map/ppermute | solution.py:108
  125.5 1.6 copy-start.11
  125.5 2.1 %copy-start.13 = (bf16[172,16,128]{2,1,0:T(8,128)(2,1)S(1)}, bf16[172,16,128]{2,1,0:T(8,128)(2,1)}, u32[]{:S(2)}) copy-start(bf16[172,16,128]{2,1,0:T(8,128)(2,1)} %shard_map.95.refs_2_.rest_2_) | copy-start | bytes 2113540
  125.6 8.7 %collective-permute-start.24 = (bf16[86,16,128]{2,1,0:T(8,128)(2,1)S(1)}, bf16[86,16,128]{2,1,0:T(8,128)(2,1)S(1)}, u32[]{:S(2)}, u32[]{:S(2)}) collective-permute-start(bf16[86,16,128]{2,1,0:T(8,128)(2,1)S(1)} %slice.29), channel_id=1, source_target_pairs={{0,16},{1,17},{2,18},{3,19},{4,20},{5,21},{6,22},{7,23},{8,24},{9,... | collective-permute-start | bytes 1056776 | tf_op jit(solution)/shard_map/ppermute | solution.py:108
  127.1 9.9 %collective-permute-start.25 = (bf16[172,16,128]{2,1,0:T(8,128)(2,1)}, bf16[172,16,128]{2,1,0:T(8,128)(2,1)}, u32[]{:S(2)}, u32[]{:S(2)}) collective-permute-start(bf16[172,16,128]{2,1,0:T(8,128)(2,1)} %shard_map.96.rest_0_), channel_id=1, source_target_pairs={{0,8},{1,9},{2,10},{3,11},{4,12},{5,13},{6,14},{7,15},{8,0},{9,1},... | collective-permute-start | bytes 2113544 | tf_op jit(solution)/shard_map/ppermute | solution.py:108
  127.1 9.9 %collective-permute-start.26 = (bf16[172,16,128]{2,1,0:T(8,128)(2,1)S(1)}, bf16[172,16,128]{2,1,0:T(8,128)(2,1)}, u32[]{:S(2)}, u32[]{:S(2)}) collective-permute-start(bf16[172,16,128]{2,1,0:T(8,128)(2,1)S(1)} %copy-done.11), channel_id=1, source_target_pairs={{0,8},{1,9},{2,10},{3,11},{4,12},{5,13},{6,14},{7,15},{8,0},{9,1},... | collective-permute-start | bytes 2113544 | tf_op jit(solution)/shard_map/ppermute | solution.py:108
  127.6 9.4 %collective-permute-start.27 = (bf16[172,16,128]{2,1,0:T(8,128)(2,1)S(1)}, bf16[172,16,128]{2,1,0:T(8,128)(2,1)}, u32[]{:S(2)}, u32[]{:S(2)}) collective-permute-start(bf16[172,16,128]{2,1,0:T(8,128)(2,1)S(1)} %copy-done.13), channel_id=1, source_target_pairs={{0,8},{1,9},{2,10},{3,11},{4,12},{5,13},{6,14},{7,15},{8,0},{9,1},... | collective-permute-start | bytes 2113544 | tf_op jit(solution)/shard_map/ppermute | solution.py:108
  134.3 1.9 collective-permute-start.28
  135.0 2.0 %collective-permute-start.29 = (bf16[86,16,128]{2,1,0:T(8,128)(2,1)}, bf16[86,16,128]{2,1,0:T(8,128)(2,1)S(1)}, u32[]{:S(2)}, u32[]{:S(2)}) collective-permute-start(bf16[86,16,128]{2,1,0:T(8,128)(2,1)} %shard_map.98.rest_4_), channel_id=1, source_target_pairs={{0,8},{1,9},{2,10},{3,11},{4,12},{5,13},{6,14},{7,15},{8,0},{9,1},... | collective-permute-start | bytes 1056776 | tf_op jit(solution)/shard_map/ppermute | solution.py:108
  173.2 1.9 %collective-permute-start.30 = (bf16[32,1280]{1,0:T(8,128)(2,1)}, bf16[32,1280]{1,0:T(8,128)(2,1)S(1)}, u32[]{:S(2)}, u32[]{:S(2)}) collective-permute-start(bf16[32,1280]{1,0:T(8,128)(2,1)} %get-tuple-element.30), channel_id=1, source_target_pairs={{0,8},{1,9},{2,10},{3,11},{4,12},{5,13},{6,14},{7,15},{8,0},{9,1},... | collective-permute-start | bytes 245768 | tf_op jit(solution)/shard_map/ppermute | solution.py:108
  173.3 5.4 %collective-permute-start.31 = (bf16[32,1280]{1,0:T(8,128)(2,1)}, bf16[32,1280]{1,0:T(8,128)(2,1)S(1)}, u32[]{:S(2)}, u32[]{:S(2)}) collective-permute-start(bf16[32,1280]{1,0:T(8,128)(2,1)} %get-tuple-element.31), channel_id=1, source_target_pairs={{0,16},{1,17},{2,18},{3,19},{4,20},{5,21},{6,22},{7,23},{8,24},{9,... | collective-permute-start | bytes 245768 | tf_op jit(solution)/shard_map/ppermute | solution.py:108
  174.8 4.9 %collective-permute-start.32 = (bf16[32,1280]{1,0:T(8,128)(2,1)}, bf16[32,1280]{1,0:T(8,128)(2,1)S(1)}, u32[]{:S(2)}, u32[]{:S(2)}) collective-permute-start(bf16[32,1280]{1,0:T(8,128)(2,1)} %get-tuple-element.32), channel_id=1, source_target_pairs={{0,24},{1,25},{2,26},{3,27},{4,28},{5,29},{6,30},{7,31},{8,16},{9,... | collective-permute-start | bytes 245768 | tf_op jit(solution)/shard_map/ppermute | solution.py:108
  175.2 4.6 %copy-start.30 = (bf16[32,1280]{1,0:T(8,128)(2,1)}, bf16[32,1280]{1,0:T(8,128)(2,1)S(1)}, u32[]{:S(2)}) copy-start(bf16[32,1280]{1,0:T(8,128)(2,1)S(1)} %collective-permute-done.30.rest_1_) | copy-start | bytes 245764
  (20 other events, 18.0 us)

commit v4 on v3

--- a/solution.py
+++ b/solution.py
@@ -29,7 +29,7 @@
     return jnp.concatenate([a.reshape(-1, ROWS, LANES) for a in arrays])
 
 
-HBM = pl.BlockSpec(memory_space=pltpu.HBM)
+HBM = pl.BlockSpec(memory_space=pl.ANY)
 
 
 def hand_on(value, *after):
@@ -42,7 +42,7 @@
         in_specs=[HBM] * (1 + len(after)),
         out_specs=HBM,
         input_output_aliases={0: 0},
-        compiler_params=pltpu.CompilerParams(vmem_limit_bytes=60 * 2**20),
+        compiler_params=pltpu.CompilerParams(vmem_limit_bytes=2**20),
     )(value, *after)
 
 
@@ -131,7 +131,8 @@
     over_y, over_x = hand_on(over_y, *before), hand_on(over_x, *before)
     low, high = routes.y(over_x[:half]), routes.x(over_y[half:])
     there = between(over_y, over_x)
-    low, high = hand_on(low, *there), hand_on(high, *there)
+    if there:
+        low, high = hand_on(low, *there), hand_on(high, *there)
     mine = [hand_on(line, over_y, over_x), over_y, over_x, low, high]
     return mine + [routes.core(piece) for piece in mine]
 
@@ -168,7 +169,7 @@
             pltpu.VMEM((outs, n, rows, ROWS, LANES), jnp.bfloat16),
             pltpu.SemaphoreType.DMA((2, outs, n)),
         ],
-        compiler_params=pltpu.CompilerParams(vmem_limit_bytes=60 * 2**20),
+        compiler_params=pltpu.CompilerParams(vmem_limit_bytes=3 * 2**20),
     )(slots, *arrays, *after)
 
 
@@ -471,7 +472,7 @@
             pltpu.SemaphoreType.DMA((n_sems,)),
         ]
         + scratch,
-        compiler_params=pltpu.CompilerParams(vmem_limit_bytes=60 * 2**20),
+        compiler_params=pltpu.CompilerParams(vmem_limit_bytes=plan["vmem"] * 2**20),
         cost_estimate=pl.CostEstimate(flops=flops, bytes_accessed=12 * 2**20, transcendentals=0),
     )(place, gates, *arrays, *saved, *weights)
 
@@ -506,7 +507,7 @@
     home, teacher = flat(tokens), flat(cotangent)
 
     shard = w_qkv.shape[1]
-    base = dict(T=T, D=D, heads=heads, hd=hd, tiles=tiles, og=og, square=False, pairs=0,
+    base = dict(T=T, D=D, heads=heads, hd=hd, tiles=tiles, og=og, square=False, pairs=0, vmem=60,
                 w_tiles=(shard // ROWS, 0), o_tiles=(og, shard // ROWS * tiles))
     weights = []
     fast = n_ha == 4 and n_wa % 4 == 0 and shard % ROWS == 0 and w_out.shape[1] == hd
@@ -587,7 +588,7 @@
         )
 
     def back(layer, x, outgrads, saved, pairs, outs, last=False):
-        plan = dict(plans[layer], pairs=pairs, n_in=len(outgrads), n_out=len(outs), last=last)
+        plan = dict(plans[layer], vmem=24, pairs=pairs, n_in=len(outgrads), n_out=len(outs), last=last)
         flow = pltpu.VMEM((D // LANES + 1, T, LANES) if last else (T, D + LANES), f32)
         return call(
             bwd_kernel, plan, place, gates, weights[layer], [x, gains] + outgrads, saved, outs, [],
@@ -600,10 +601,10 @@
         gather(0, [after_time], [tall])
     after_height, *saved_height = forward(1, tall, tall, n_ha, n_wa)
     if fast:
-        gather(1, [after_height], [after_height])
+        gather(1, [after_height], [])
     across = swap(after_height, "wa")
     (grad,) = call(
-        both_kernel, dict(plans[2], pairs=n_wa), place, gates, weights[2],
+        both_kernel, dict(plans[2], pairs=n_wa, vmem=24), place, gates, weights[2],
         [across, gains, biases[2]], [], [loaded], [], kept + grads, 2 * dense,
     )
     grad = swap(grad, "wa")

time: 191 us -> 181 us (0.948)
  local copies, waits for them, and re-layouts: 19.2 us -> 8.61 us
  waiting for transfers between devices: 48.5 us -> 55.4 us
  Pallas kernels: 50.2 us -> 47.9 us
    unnamed x66 -> x80, local copies, waits for them, and re-layouts: 11.9 us -> 3.22 us
    ppermute x33, waiting for transfers between devices: 48.5 us -> 55.3 us  [send(): return lax.ppermute(value, AXES, pairs)]
    pallas_call x5, Pallas kernels: 43.8 us -> 41 us  [call(): pl.pallas_call(functools.partial(kernel, plan), out_shape=list(outs) + li...]
  transfers between devices with their start and end apart: 35 -> 35, of which waited for: 15 -> 14; matrix products, arithmetic and copies ran while one was open for 5% -> 3% of each run, Pallas kernels for 9% -> 10%
where the time goes in v4:
time: 181 us
  waiting for transfers between devices  55.4 us (31%)
  Pallas kernels  47.9 us (26%)
  blocking collectives  34.9 us (19%)
  starting transfers between devices  32.4 us (18%)
  local copies, waits for them, and re-layouts  8.61 us (5%)
    ppermute x33, waiting for transfers between devices, send(): return lax.ppermute(value, AXES, pairs)  55.3 us
    pallas_call x5, Pallas kernels, call(): pl.pallas_call(functools.partial(kernel, plan), out_shape=list(outs) + li...  41 us
    ppermute x33, starting transfers between devices, send(): return lax.ppermute(value, AXES, pairs)  25.3 us
    all_gather x1, blocking collectives, line(): lax.all_gather(value, AXES, axis=0, tiled=True, axis_index_groups=groups)  20.7 us
    all_to_all x1, blocking collectives, swap(): return lax.all_to_all(value, axis, split_axis=0, concat_axis=0, tiled=True)  14.2 us
    all_to_all x2, starting transfers between devices, swap(): return lax.all_to_all(value, axis, split_axis=0, concat_axis=0, tiled=True)  7.17 us
  transfers between devices with their start and end apart: 35, of which 14 were waited for; matrix products, arithmetic and copies ran while one was open for 3% of the time, Pallas kernels for 10%

profile of v4, /device:TPU:0, one launch (start us, length us, event | category | flops | bytes accessed | tf_op | source)
XLA Modules:
  0.0 180.9 jit_solution(15508635881716433896)
XLA Ops:
  0.6 3.4 %shard_map.77 = (bf16[43,16,128]{2,1,0:T(8,128)(2,1)}, bf16[86,16,128]{2,1,0:T(8,128)(2,1)}) custom-call(s32[1]{0:T(128)} %bitcast.8.part_ref, bf16[3,144,1728]{2,1,0:T(8,128)(2,1)} %q_ref.1, bf16[3,72,1152]{2,1,0:T(8,128)(2,1)} %o_ref.1), custom_call_target="tpu_custom_call" | custom-call | tf_op jit(solution)/shard_map/pallas_call | solution.py:83
  4.1 20.7 %all_gather.3.refs_0_.refs_1_ = bf16[172,16,128]{2,1,0:T(8,128)(2,1)S(1)} all-gather(bf16[43,16,128]{2,1,0:T(8,128)(2,1)} %get-tuple-element.20), channel_id=1, replica_groups={{0,2,4,6},{1,3,5,7},{8,10,12,14},{9,11,13,15},{16,18,20,22},{17,19,21,2..., dimensions={0}, use_global_device_ids=true | all-gather | bytes 880640 | tf_op jit(solution)/shard_map/all_gather | solution.py:125
  24.8 1.5 collective-permute-start.1
  26.3 1.5 collective-permute-start
  27.8 2.3 %collective-permute-start.5 = (bf16[86,16,128]{2,1,0:T(8,128)(2,1)}, bf16[86,16,128]{2,1,0:T(8,128)(2,1)S(1)}, u32[]{:S(2)}, u32[]{:S(2)}) collective-permute-start(bf16[86,16,128]{2,1,0:T(8,128)(2,1)} %shard_map.81.refs_1_), channel_id=1, source_target_pairs={{0,6},{1,7},{2,4},{3,5},{4,2},{5,3},{6,0},{7,1},{8,14},{9,15},{10,... | collective-permute-start | bytes 1056776 | tf_op jit(solution)/shard_map/ppermute | solution.py:108
  30.5 1.2 reshape_transpose.7.refs_2_.cot_ref
  31.7 8.2 %collective-permute-done.1.refs_0_ = bf16[172,16,128]{2,1,0:T(8,128)(2,1)S(1)} collective-permute-done((bf16[172,16,128]{2,1,0:T(8,128)(2,1)S(1)}, bf16[172,16,128]{2,1,0:T(8,128)(2,1)S(1)}, u32[]{:S(2)}, u32[]{:S(2)}) %collective-permute-start.1) | collective-permute-done | bytes 704544 | tf_op jit(solution)/shard_map/ppermute | solution.py:108
  39.9 1.0 collective-permute-start.4
  40.9 0.9 collective-permute-start.3
  41.9 0.8 slice.25
  42.7 1.5 collective-permute-start.6
  44.2 0.8 slice.24
  45.0 0.7 copy-done.33
  45.7 1.5 collective-permute-start.2
  47.3 11.2 %collective-permute-done.4.refs_3_ = bf16[86,16,128]{2,1,0:T(8,128)(2,1)} collective-permute-done((bf16[86,16,128]{2,1,0:T(8,128)(2,1)}, bf16[86,16,128]{2,1,0:T(8,128)(2,1)}, u32[]{:S(2)}, u32[]{:S(2)}) %collective-permute-start.4) | collective-permute-done | bytes 352288 | tf_op jit(solution)/shard_map/ppermute | solution.py:108
  58.5 0.7 collective-permute-done.3.refs_2_
  59.2 1.0 copy-done.34
  60.2 3.4 %shard_map.82 = (bf16[172,16,128]{2,1,0:T(8,128)(2,1)S(1)}, bf16[172,16,128]{2,1,0:T(8,128)(2,1)S(1)}) custom-call(s32[4]{0:T(128)S(1)} %pad_add_fusion.refs_0_, bf16[86,16,128]{2,1,0:T(8,128)(2,1)} %shard_map.81.refs_1_, bf16[86,16,128]{2,1,0:T(8,128)(2,1)} %collective-permute-done.3.refs_2_, bf16[86,16,128]{2,1,0:T(8,128)(2,1)} %collective-permute-done.4.refs_3_, ...), custom_call_target="tpu_custom_call" | custom-call | tf_op jit(solution)/shard_map/pallas_call | solution.py:163
  64.6 1.5 collective-permute-start.13
  66.0 1.5 collective-permute-start.12
  68.2 1.4 collective-permute-done.10.rest_8_.rest_15_
  69.6 7.2 %shard_map.85 = (bf16[256,1152]{1,0:T(8,128)(2,1)}, bf16[128,1792]{1,0:T(8,128)(2,1)}, f32[8,128,128]{2,1,0:T(8,128)}, bf16[128,576]{1,0:T(8,128)(2,1)}) custom-call(s32[12]{0:T(128)} %stack.66.place_ref, f32[3,8]{1,0:T(4,128)} %gates_ref.9, bf16[128,1152]{1,0:T(8,128)(2,1)} %copy-done.12, f32[3,1152]{1,0:T(4,128)} %gain_ref.9, f32[128,128]{1,0:T(8,128)} %copy-done.27, ...), custom_call_target="tpu_custom_call" | custom-call | flops 679477248 | bytes 12582912 | tf_op jit(solution)/shard_map/pallas_call | solution.py:463
  76.8 3.5 %all-to-all-start = ((bf16[4,64,1152]{2,1,0:T(8,128)(2,1)}), bf16[4,64,1152]{2,1,0:T(8,128)(2,1)S(1)}, u32[]{:S(2)}, u32[]{:S(2)}) async-start(bf16[4,64,1152]{2,1,0:T(8,128)(2,1)} %bitcast.30), calls=%async_computation | async-start | bytes 1179648 | tf_op jit(solution)/shard_map/all_to_all | solution.py:505
  80.3 2.6 %collective-permute-done.13.refs_0_ = bf16[172,16,128]{2,1,0:T(8,128)(2,1)} collective-permute-done((bf16[172,16,128]{2,1,0:T(8,128)(2,1)S(1)}, bf16[172,16,128]{2,1,0:T(8,128)(2,1)}, u32[]{:S(2)}, u32[]{:S(2)}) %collective-permute-start.13) | collective-permute-done | bytes 704544 | tf_op jit(solution)/shard_map/ppermute | solution.py:108
  82.8 1.1 copy-done.17
  83.9 1.1 slice.26
  85.0 1.8 collective-permute-start.14
  86.8 0.8 slice.27
  87.6 1.7 collective-permute-start.15
  89.9 5.0 %collective-permute-done.14.refs_0_ = bf16[86,16,128]{2,1,0:T(8,128)(2,1)S(1)} collective-permute-done((bf16[86,16,128]{2,1,0:T(8,128)(2,1)S(1)}, bf16[86,16,128]{2,1,0:T(8,128)(2,1)S(1)}, u32[]{:S(2)}, u32[]{:S(2)}) %collective-permute-start.14) | collective-permute-done | bytes 352288 | tf_op jit(solution)/shard_map/ppermute | solution.py:108
  94.9 2.6 %collective-permute-done.15.refs_0_ = bf16[86,16,128]{2,1,0:T(8,128)(2,1)} collective-permute-done((bf16[86,16,128]{2,1,0:T(8,128)(2,1)}, bf16[86,16,128]{2,1,0:T(8,128)(2,1)}, u32[]{:S(2)}, u32[]{:S(2)}) %collective-permute-start.15) | collective-permute-done | bytes 352288 | tf_op jit(solution)/shard_map/ppermute | solution.py:108
  97.5 1.3 collective-permute-start.22
  99.3 0.8 collective-permute-start.21
  100.1 7.5 %shard_map.92 = (bf16[256,1152]{1,0:T(8,128)(2,1)}, bf16[128,1792]{1,0:T(8,128)(2,1)}, f32[8,128,128]{2,1,0:T(8,128)}, bf16[128,576]{1,0:T(8,128)(2,1)}) custom-call(s32[12]{0:T(128)} %stack.66.place_ref, f32[3,8]{1,0:T(4,128)} %gates_ref.9, bf16[256,1152]{1,0:T(8,128)(2,1)} %bitcast.26, f32[3,1152]{1,0:T(4,128)} %gain_ref.9, f32[128,128]{1,0:T(8,128)} %copy-done.26, ...), custom_call_target="tpu_custom_call" | custom-call | flops 679477248 | bytes 12582912 | tf_op jit(solution)/shard_map/pallas_call | solution.py:463
  107.6 3.7 %all-to-all-start.1 = ((bf16[8,32,1152]{2,1,0:T(8,128)(2,1)}), bf16[8,32,1152]{2,1,0:T(8,128)(2,1)S(1)}, u32[]{:S(2)}, u32[]{:S(2)}) async-start(bf16[8,32,1152]{2,1,0:T(8,128)(2,1)} %bitcast.29), calls=%async_computation.1 | async-start | bytes 1179648 | tf_op jit(solution)/shard_map/all_to_all | solution.py:505
  111.3 4.4 %collective-permute-done.22.refs_0_ = bf16[172,16,128]{2,1,0:T(8,128)(2,1)S(1)} collective-permute-done((bf16[172,16,128]{2,1,0:T(8,128)(2,1)S(1)}, bf16[172,16,128]{2,1,0:T(8,128)(2,1)S(1)}, u32[]{:S(2)}, u32[]{:S(2)}) %collective-permute-start.22) | collective-permute-done | bytes 704544 | tf_op jit(solution)/shard_map/ppermute | solution.py:108
  115.8 0.9 collective-permute-start.23
  116.6 4.5 %collective-permute-done.21.refs_0_ = bf16[172,16,128]{2,1,0:T(8,128)(2,1)S(1)} collective-permute-done((bf16[172,16,128]{2,1,0:T(8,128)(2,1)S(1)}, bf16[172,16,128]{2,1,0:T(8,128)(2,1)S(1)}, u32[]{:S(2)}, u32[]{:S(2)}) %collective-permute-start.21) | collective-permute-done | bytes 704544 | tf_op jit(solution)/shard_map/ppermute | solution.py:108
  121.2 1.3 collective-permute-start.24
  123.0 8.1 %collective-permute-done.23.rest_3_ = bf16[86,16,128]{2,1,0:T(8,128)(2,1)} collective-permute-done((bf16[86,16,128]{2,1,0:T(8,128)(2,1)S(1)}, bf16[86,16,128]{2,1,0:T(8,128)(2,1)}, u32[]{:S(2)}, u32[]{:S(2)}) %collective-permute-start.23) | collective-permute-done | bytes 352288 | tf_op jit(solution)/shard_map/ppermute | solution.py:108
  131.6 1.9 %collective-permute-done.28.rest_8_ = bf16[86,16,128]{2,1,0:T(8,128)(2,1)} collective-permute-done((bf16[86,16,128]{2,1,0:T(8,128)(2,1)}, bf16[86,16,128]{2,1,0:T(8,128)(2,1)}, u32[]{:S(2)}, u32[]{:S(2)}) %collective-permute-start.28) | collective-permute-done | bytes 352288 | tf_op jit(solution)/shard_map/ppermute | solution.py:108
  133.7 9.5 %shard_map.97 = bf16[128,1280]{1,0:T(8,128)(2,1)S(1)} custom-call(s32[12]{0:T(128)S(1)} %copy-done.38, f32[3,8]{1,0:T(4,128)S(1)} %copy-done.37, bf16[256,1152]{1,0:T(8,128)(2,1)S(1)} %bitcast.31, f32[3,1152]{1,0:T(4,128)S(1)} %copy-done.30, f32[128,128]{1,0:T(8,128)S(1)} %copy-done.25, bf16[172,16,128]{2,1,0:T(8,128)(2,1)S(1)} %shard_map.96.rest_0_, ...), custom_call_target="tpu_custom_call" | custom-call | flops 1358954496 | bytes 12582912 | tf_op jit(solution)/shard_map/pallas_call | solution.py:463
  143.2 14.2 %all_to_all.33 = bf16[8,16,1280]{2,1,0:T(8,128)(2,1)S(1)} all-to-all(bf16[8,16,1280]{2,1,0:T(8,128)(2,1)S(1)} %bitcast.33), channel_id=1, replica_groups=mesh['ha'=4,'wa'=8] {'wa'}, dimensions={0} | all-to-all | bytes 655360 | tf_op jit(solution)/shard_map/all_to_all | solution.py:505
  157.5 7.8 %shard_map.98 = (bf16[32,1280]{1,0:T(8,128)(2,1)S(1)}, bf16[32,1280]{1,0:T(8,128)(2,1)S(1)}, bf16[32,1280]{1,0:T(8,128)(2,1)S(1)}, bf16[32,1280]{1,0:T(8,128)(2,1)S(1)}) custom-call(s32[12]{0:T(128)S(1)} %copy-done.38, f32[3,8]{1,0:T(4,128)S(1)} %copy-done.37, bf16[256,1152]{1,0:T(8,128)(2,1)S(1)} %bitcast.28, f32[3,1152]{1,0:T(4,128)S(1)} %copy-done.30, ...), custom_call_target="tpu_custom_call" | custom-call | flops 679477248 | bytes 12582912 | tf_op jit(solution)/shard_map/pallas_call | solution.py:463
  165.4 1.3 collective-permute-start.31
  167.3 3.4 %collective-permute-done.31.rest_2_ = bf16[32,1280]{1,0:T(8,128)(2,1)S(1)} collective-permute-done((bf16[32,1280]{1,0:T(8,128)(2,1)S(1)}, bf16[32,1280]{1,0:T(8,128)(2,1)S(1)}, u32[]{:S(2)}, u32[]{:S(2)}) %collective-permute-start.31) | collective-permute-done | bytes 81952 | tf_op jit(solution)/shard_map/ppermute | solution.py:108
  170.7 0.8 collective-permute-done.32.rest_3_
  171.6 9.0 %shard_map.99 = (bf16[64,2,1152]{2,1,0:T(2,128)(2,1)}, bf16[3,64,2,8]{3,2,1,0:T(2,128)(2,1)}) custom-call(s32[12]{0:T(128)S(1)} %copy-done.38, f32[3,8]{1,0:T(4,128)S(1)} %copy-done.37, bf16[128,1152]{1,0:T(8,128)(2,1)S(1)} %copy-done.13, f32[3,1152]{1,0:T(4,128)S(1)} %copy-done.30, bf16[32,1280]{1,0:T(8,128)(2,1)S(1)} %get-tuple-element.29.rest_0_, ...), custom_call_target="tpu_custom_call" | custom-call | flops 679477248 | bytes 12582912 | tf_op jit(solution)/shard_map/pallas_call | solution.py:463
  (142 shorter events, 5.0 us)
Async XLA Ops:
  4.1 26.3 %copy-start.39 = (bf16[1,8,8,2,1152]{4,3,2,1,0:T(2,128)(2,1)S(1)}, bf16[1,8,8,2,1152]{4,3,2,1,0:T(2,128)(2,1)}, u32[]{:S(2)}) copy-start(bf16[1,8,8,2,1152]{4,3,2,1,0:T(2,128)(2,1)} %param.6) | copy-start | bytes 884740
  24.8 15.1 %collective-permute-start.1 = (bf16[172,16,128]{2,1,0:T(8,128)(2,1)S(1)}, bf16[172,16,128]{2,1,0:T(8,128)(2,1)S(1)}, u32[]{:S(2)}, u32[]{:S(2)}) collective-permute-start(bf16[172,16,128]{2,1,0:T(8,128)(2,1)S(1)} %all_gather.3.refs_0_.refs_1_), channel_id=1, source_target_pairs={{0,16},{1,17},{2,18},{3,19},{4,20},{5,21},{6,22},{7,23},{8,24},{9,... | collective-permute-start | bytes 2113544 | tf_op jit(solution)/shard_map/ppermute | solution.py:108
  26.3 15.6 %collective-permute-start = (bf16[172,16,128]{2,1,0:T(8,128)(2,1)S(1)}, bf16[172,16,128]{2,1,0:T(8,128)(2,1)S(1)}, u32[]{:S(2)}, u32[]{:S(2)}) collective-permute-start(bf16[172,16,128]{2,1,0:T(8,128)(2,1)S(1)} %all_gather.3.refs_0_.refs_1_), channel_id=1, source_target_pairs={{0,1},{1,0},{2,3},{3,2},{4,5},{5,4},{6,7},{7,6},{8,9},{9,8},{10,11... | collective-permute-start | bytes 2113544 | tf_op jit(solution)/shard_map/ppermute | solution.py:108
  27.8 17.2 %collective-permute-start.5 = (bf16[86,16,128]{2,1,0:T(8,128)(2,1)}, bf16[86,16,128]{2,1,0:T(8,128)(2,1)S(1)}, u32[]{:S(2)}, u32[]{:S(2)}) collective-permute-start(bf16[86,16,128]{2,1,0:T(8,128)(2,1)} %shard_map.81.refs_1_), channel_id=1, source_target_pairs={{0,6},{1,7},{2,4},{3,5},{4,2},{5,3},{6,0},{7,1},{8,14},{9,15},{10,... | collective-permute-start | bytes 1056776 | tf_op jit(solution)/shard_map/ppermute | solution.py:108
  39.9 23.8 %copy-start.4 = (bf16[172,16,128]{2,1,0:T(8,128)(2,1)}, bf16[172,16,128]{2,1,0:T(8,128)(2,1)S(1)}, u32[]{:S(2)}) copy-start(bf16[172,16,128]{2,1,0:T(8,128)(2,1)S(1)} %shard_map.79.refs_2_.refs_6_.rest_2_.rest_9_) | copy-start | bytes 2113540
  39.9 26.1 %collective-permute-start.9 = (bf16[172,16,128]{2,1,0:T(8,128)(2,1)S(1)}, bf16[172,16,128]{2,1,0:T(8,128)(2,1)}, u32[]{:S(2)}, u32[]{:S(2)}) collective-permute-start(bf16[172,16,128]{2,1,0:T(8,128)(2,1)S(1)} %shard_map.79.refs_2_.refs_6_.rest_2_.rest_9_), channel_id=1, source_target_pairs={{0,8},{1,9},{2,10},{3,11},{4,12},{5,13},{6,14},{7,15},{8,0},{9,1},... | collective-permute-start | bytes 2113544 | tf_op jit(solution)/shard_map/ppermute | solution.py:108
  39.9 18.6 %collective-permute-start.4 = (bf16[86,16,128]{2,1,0:T(8,128)(2,1)}, bf16[86,16,128]{2,1,0:T(8,128)(2,1)}, u32[]{:S(2)}, u32[]{:S(2)}) collective-permute-start(bf16[86,16,128]{2,1,0:T(8,128)(2,1)} %shard_map.81.refs_1_), channel_id=1, source_target_pairs={{0,4},{1,5},{2,6},{3,7},{4,0},{5,1},{6,2},{7,3},{8,12},{9,13},{10,... | collective-permute-start | bytes 1056776 | tf_op jit(solution)/shard_map/ppermute | solution.py:108
  40.9 18.2 %collective-permute-start.3 = (bf16[86,16,128]{2,1,0:T(8,128)(2,1)}, bf16[86,16,128]{2,1,0:T(8,128)(2,1)}, u32[]{:S(2)}, u32[]{:S(2)}) collective-permute-start(bf16[86,16,128]{2,1,0:T(8,128)(2,1)} %shard_map.81.refs_1_), channel_id=1, source_target_pairs={{0,2},{1,3},{2,0},{3,1},{4,6},{5,7},{6,4},{7,5},{8,10},{9,11},{10,... | collective-permute-start | bytes 1056776 | tf_op jit(solution)/shard_map/ppermute | solution.py:108
  41.9 22.3 %copy-start.2 = (bf16[172,16,128]{2,1,0:T(8,128)(2,1)}, bf16[172,16,128]{2,1,0:T(8,128)(2,1)S(1)}, u32[]{:S(2)}) copy-start(bf16[172,16,128]{2,1,0:T(8,128)(2,1)S(1)} %shard_map.78.refs_1_.refs_5_.rest_1_.rest_8_) | copy-start | bytes 2113540
  42.7 20.8 %collective-permute-start.6 = (bf16[86,16,128]{2,1,0:T(8,128)(2,1)}, bf16[86,16,128]{2,1,0:T(8,128)(2,1)}, u32[]{:S(2)}, u32[]{:S(2)}) collective-permute-start(bf16[86,16,128]{2,1,0:T(8,128)(2,1)} %slice.25), channel_id=1, source_target_pairs={{0,16},{1,17},{2,18},{3,19},{4,20},{5,21},{6,22},{7,23},{8,24},{9,... | collective-permute-start | bytes 1056776 | tf_op jit(solution)/shard_map/ppermute | solution.py:108
  45.7 18.5 %collective-permute-start.2 = (bf16[86,16,128]{2,1,0:T(8,128)(2,1)}, bf16[86,16,128]{2,1,0:T(8,128)(2,1)}, u32[]{:S(2)}, u32[]{:S(2)}) collective-permute-start(bf16[86,16,128]{2,1,0:T(8,128)(2,1)} %slice.24), channel_id=1, source_target_pairs={{0,1},{1,0},{2,3},{3,2},{4,5},{5,4},{6,7},{7,6},{8,9},{9,8},{10,11... | collective-permute-start | bytes 1056776 | tf_op jit(solution)/shard_map/ppermute | solution.py:108
  63.6 4.0 %collective-permute-start.11 = (bf16[86,16,128]{2,1,0:T(8,128)(2,1)}, bf16[86,16,128]{2,1,0:T(8,128)(2,1)}, u32[]{:S(2)}, u32[]{:S(2)}) collective-permute-start(bf16[86,16,128]{2,1,0:T(8,128)(2,1)} %shard_map.84.rest_4_.refs_2_.rest_11_), channel_id=1, source_target_pairs={{0,8},{1,9},{2,10},{3,11},{4,12},{5,13},{6,14},{7,15},{8,0},{9,1},... | collective-permute-start | bytes 1056776 | tf_op jit(solution)/shard_map/ppermute | solution.py:108
  63.7 5.9 %collective-permute-start.7 = (bf16[172,16,128]{2,1,0:T(8,128)(2,1)S(1)}, bf16[172,16,128]{2,1,0:T(8,128)(2,1)}, u32[]{:S(2)}, u32[]{:S(2)}) collective-permute-start(bf16[172,16,128]{2,1,0:T(8,128)(2,1)S(1)} %shard_map.80.rest_0_.rest_7_), channel_id=1, source_target_pairs={{0,8},{1,9},{2,10},{3,11},{4,12},{5,13},{6,14},{7,15},{8,0},{9,1},... | collective-permute-start | bytes 2113544 | tf_op jit(solution)/shard_map/ppermute | solution.py:108
  64.2 5.4 %collective-permute-start.8 = (bf16[172,16,128]{2,1,0:T(8,128)(2,1)S(1)}, bf16[172,16,128]{2,1,0:T(8,128)(2,1)}, u32[]{:S(2)}, u32[]{:S(2)}) collective-permute-start(bf16[172,16,128]{2,1,0:T(8,128)(2,1)S(1)} %shard_map.78.refs_1_.refs_5_.rest_1_.rest_8_), channel_id=1, source_target_pairs={{0,8},{1,9},{2,10},{3,11},{4,12},{5,13},{6,14},{7,15},{8,0},{9,1},... | collective-permute-start | bytes 2113544 | tf_op jit(solution)/shard_map/ppermute | solution.py:108
  64.6 18.3 %collective-permute-start.13 = (bf16[172,16,128]{2,1,0:T(8,128)(2,1)S(1)}, bf16[172,16,128]{2,1,0:T(8,128)(2,1)}, u32[]{:S(2)}, u32[]{:S(2)}) collective-permute-start(bf16[172,16,128]{2,1,0:T(8,128)(2,1)S(1)} %shard_map.86.refs_0_), channel_id=1, source_target_pairs={{0,16},{1,17},{2,18},{3,19},{4,20},{5,21},{6,22},{7,23},{8,24},{9,... | collective-permute-start | bytes 2113544 | tf_op jit(solution)/shard_map/ppermute | solution.py:108
  66.0 20.7 %collective-permute-start.12 = (bf16[172,16,128]{2,1,0:T(8,128)(2,1)S(1)}, bf16[172,16,128]{2,1,0:T(8,128)(2,1)S(1)}, u32[]{:S(2)}, u32[]{:S(2)}) collective-permute-start(bf16[172,16,128]{2,1,0:T(8,128)(2,1)S(1)} %shard_map.86.refs_0_), channel_id=1, source_target_pairs={{0,1},{1,0},{2,3},{3,2},{4,5},{5,4},{6,7},{7,6},{8,9},{9,8},{10,11... | collective-permute-start | bytes 2113544 | tf_op jit(solution)/shard_map/ppermute | solution.py:108
  67.6 2.0 %collective-permute-start.10 = (bf16[86,16,128]{2,1,0:T(8,128)(2,1)}, bf16[86,16,128]{2,1,0:T(8,128)(2,1)}, u32[]{:S(2)}, u32[]{:S(2)}) collective-permute-start(bf16[86,16,128]{2,1,0:T(8,128)(2,1)} %shard_map.83.rest_3_.refs_1_.rest_10_), channel_id=1, source_target_pairs={{0,8},{1,9},{2,10},{3,11},{4,12},{5,13},{6,14},{7,15},{8,0},{9,1},... | collective-permute-start | bytes 1056776 | tf_op jit(solution)/shard_map/ppermute | solution.py:108
  76.8 13.1 %all-to-all-start = ((bf16[4,64,1152]{2,1,0:T(8,128)(2,1)}), bf16[4,64,1152]{2,1,0:T(8,128)(2,1)S(1)}, u32[]{:S(2)}, u32[]{:S(2)}) async-start(bf16[4,64,1152]{2,1,0:T(8,128)(2,1)} %bitcast.30), calls=%async_computation | async-start | bytes 1179648 | tf_op jit(solution)/shard_map/all_to_all | solution.py:505
  85.0 9.9 %collective-permute-start.14 = (bf16[86,16,128]{2,1,0:T(8,128)(2,1)S(1)}, bf16[86,16,128]{2,1,0:T(8,128)(2,1)S(1)}, u32[]{:S(2)}, u32[]{:S(2)}) collective-permute-start(bf16[86,16,128]{2,1,0:T(8,128)(2,1)S(1)} %slice.26), channel_id=1, source_target_pairs={{0,1},{1,0},{2,3},{3,2},{4,5},{5,4},{6,7},{7,6},{8,9},{9,8},{10,11... | collective-permute-start | bytes 1056776 | tf_op jit(solution)/shard_map/ppermute | solution.py:108
  87.6 9.8 %collective-permute-start.15 = (bf16[86,16,128]{2,1,0:T(8,128)(2,1)}, bf16[86,16,128]{2,1,0:T(8,128)(2,1)}, u32[]{:S(2)}, u32[]{:S(2)}) collective-permute-start(bf16[86,16,128]{2,1,0:T(8,128)(2,1)} %slice.27), channel_id=1, source_target_pairs={{0,16},{1,17},{2,18},{3,19},{4,20},{5,21},{6,22},{7,23},{8,24},{9,... | collective-permute-start | bytes 1056776 | tf_op jit(solution)/shard_map/ppermute | solution.py:108
  89.3 10.8 %collective-permute-start.16 = (bf16[172,16,128]{2,1,0:T(8,128)(2,1)S(1)}, bf16[172,16,128]{2,1,0:T(8,128)(2,1)}, u32[]{:S(2)}, u32[]{:S(2)}) collective-permute-start(bf16[172,16,128]{2,1,0:T(8,128)(2,1)S(1)} %shard_map.89.rest_0_.rest_4_), channel_id=1, source_target_pairs={{0,8},{1,9},{2,10},{3,11},{4,12},{5,13},{6,14},{7,15},{8,0},{9,1},... | collective-permute-start | bytes 2113544 | tf_op jit(solution)/shard_map/ppermute | solution.py:108
  89.3 10.8 %collective-permute-start.17 = (bf16[172,16,128]{2,1,0:T(8,128)(2,1)S(1)}, bf16[172,16,128]{2,1,0:T(8,128)(2,1)}, u32[]{:S(2)}, u32[]{:S(2)}) collective-permute-start(bf16[172,16,128]{2,1,0:T(8,128)(2,1)S(1)} %shard_map.87.refs_1_.rest_1_.rest_5_), channel_id=1, source_target_pairs={{0,8},{1,9},{2,10},{3,11},{4,12},{5,13},{6,14},{7,15},{8,0},{9,1},... | collective-permute-start | bytes 2113544 | tf_op jit(solution)/shard_map/ppermute | solution.py:108
  89.8 10.3 %collective-permute-start.18 = (bf16[172,16,128]{2,1,0:T(8,128)(2,1)}, bf16[172,16,128]{2,1,0:T(8,128)(2,1)}, u32[]{:S(2)}, u32[]{:S(2)}) collective-permute-start(bf16[172,16,128]{2,1,0:T(8,128)(2,1)} %shard_map.88.refs_2_.rest_2_.rest_6_), channel_id=1, source_target_pairs={{0,8},{1,9},{2,10},{3,11},{4,12},{5,13},{6,14},{7,15},{8,0},{9,1},... | collective-permute-start | bytes 2113544 | tf_op jit(solution)/shard_map/ppermute | solution.py:108
  94.9 2.6 %collective-permute-start.19 = (bf16[86,16,128]{2,1,0:T(8,128)(2,1)S(1)}, bf16[86,16,128]{2,1,0:T(8,128)(2,1)S(1)}, u32[]{:S(2)}, u32[]{:S(2)}) collective-permute-start(bf16[86,16,128]{2,1,0:T(8,128)(2,1)S(1)} %shard_map.90.rest_3_.refs_1_.rest_7_), channel_id=1, source_target_pairs={{0,8},{1,9},{2,10},{3,11},{4,12},{5,13},{6,14},{7,15},{8,0},{9,1},... | collective-permute-start | bytes 1056776 | tf_op jit(solution)/shard_map/ppermute | solution.py:108
  97.4 1.9 %collective-permute-start.20 = (bf16[86,16,128]{2,1,0:T(8,128)(2,1)}, bf16[86,16,128]{2,1,0:T(8,128)(2,1)S(1)}, u32[]{:S(2)}, u32[]{:S(2)}) collective-permute-start(bf16[86,16,128]{2,1,0:T(8,128)(2,1)} %shard_map.91.rest_4_.refs_2_.rest_8_), channel_id=1, source_target_pairs={{0,8},{1,9},{2,10},{3,11},{4,12},{5,13},{6,14},{7,15},{8,0},{9,1},... | collective-permute-start | bytes 1056776 | tf_op jit(solution)/shard_map/ppermute | solution.py:108
  97.5 18.2 %collective-permute-start.22 = (bf16[172,16,128]{2,1,0:T(8,128)(2,1)S(1)}, bf16[172,16,128]{2,1,0:T(8,128)(2,1)S(1)}, u32[]{:S(2)}, u32[]{:S(2)}) collective-permute-start(bf16[172,16,128]{2,1,0:T(8,128)(2,1)S(1)} %shard_map.93.refs_0_), channel_id=1, source_target_pairs={{0,16},{1,17},{2,18},{3,19},{4,20},{5,21},{6,22},{7,23},{8,24},{9,... | collective-permute-start | bytes 2113544 | tf_op jit(solution)/shard_map/ppermute | solution.py:108
  99.3 21.8 %collective-permute-start.21 = (bf16[172,16,128]{2,1,0:T(8,128)(2,1)S(1)}, bf16[172,16,128]{2,1,0:T(8,128)(2,1)S(1)}, u32[]{:S(2)}, u32[]{:S(2)}) collective-permute-start(bf16[172,16,128]{2,1,0:T(8,128)(2,1)S(1)} %shard_map.93.refs_0_), channel_id=1, source_target_pairs={{0,1},{1,0},{2,3},{3,2},{4,5},{5,4},{6,7},{7,6},{8,9},{9,8},{10,11... | collective-permute-start | bytes 2113544 | tf_op jit(solution)/shard_map/ppermute | solution.py:108
  107.6 24.0 %all-to-all-start.1 = ((bf16[8,32,1152]{2,1,0:T(8,128)(2,1)}), bf16[8,32,1152]{2,1,0:T(8,128)(2,1)S(1)}, u32[]{:S(2)}, u32[]{:S(2)}) async-start(bf16[8,32,1152]{2,1,0:T(8,128)(2,1)} %bitcast.29), calls=%async_computation.1 | async-start | bytes 1179648 | tf_op jit(solution)/shard_map/all_to_all | solution.py:505
  115.8 15.3 %collective-permute-start.23 = (bf16[86,16,128]{2,1,0:T(8,128)(2,1)S(1)}, bf16[86,16,128]{2,1,0:T(8,128)(2,1)}, u32[]{:S(2)}, u32[]{:S(2)}) collective-permute-start(bf16[86,16,128]{2,1,0:T(8,128)(2,1)S(1)} %slice.28), channel_id=1, source_target_pairs={{0,1},{1,0},{2,3},{3,2},{4,5},{5,4},{6,7},{7,6},{8,9},{9,8},{10,11... | collective-permute-start | bytes 1056776 | tf_op jit(solution)/shard_map/ppermute | solution.py:108
  121.2 9.9 %collective-permute-start.24 = (bf16[86,16,128]{2,1,0:T(8,128)(2,1)S(1)}, bf16[86,16,128]{2,1,0:T(8,128)(2,1)S(1)}, u32[]{:S(2)}, u32[]{:S(2)}) collective-permute-start(bf16[86,16,128]{2,1,0:T(8,128)(2,1)S(1)} %slice.29), channel_id=1, source_target_pairs={{0,16},{1,17},{2,18},{3,19},{4,20},{5,21},{6,22},{7,23},{8,24},{9,... | collective-permute-start | bytes 1056776 | tf_op jit(solution)/shard_map/ppermute | solution.py:108
  122.5 11.0 %collective-permute-start.25 = (bf16[172,16,128]{2,1,0:T(8,128)(2,1)S(1)}, bf16[172,16,128]{2,1,0:T(8,128)(2,1)}, u32[]{:S(2)}, u32[]{:S(2)}) collective-permute-start(bf16[172,16,128]{2,1,0:T(8,128)(2,1)S(1)} %shard_map.96.rest_0_), channel_id=1, source_target_pairs={{0,8},{1,9},{2,10},{3,11},{4,12},{5,13},{6,14},{7,15},{8,0},{9,1},... | collective-permute-start | bytes 2113544 | tf_op jit(solution)/shard_map/ppermute | solution.py:108
  122.5 11.0 %collective-permute-start.26 = (bf16[172,16,128]{2,1,0:T(8,128)(2,1)S(1)}, bf16[172,16,128]{2,1,0:T(8,128)(2,1)}, u32[]{:S(2)}, u32[]{:S(2)}) collective-permute-start(bf16[172,16,128]{2,1,0:T(8,128)(2,1)S(1)} %shard_map.94.refs_1_.rest_1_), channel_id=1, source_target_pairs={{0,8},{1,9},{2,10},{3,11},{4,12},{5,13},{6,14},{7,15},{8,0},{9,1},... | collective-permute-start | bytes 2113544 | tf_op jit(solution)/shard_map/ppermute | solution.py:108
  123.0 10.5 %collective-permute-start.27 = (bf16[172,16,128]{2,1,0:T(8,128)(2,1)S(1)}, bf16[172,16,128]{2,1,0:T(8,128)(2,1)}, u32[]{:S(2)}, u32[]{:S(2)}) collective-permute-start(bf16[172,16,128]{2,1,0:T(8,128)(2,1)S(1)} %shard_map.95.refs_2_.rest_2_), channel_id=1, source_target_pairs={{0,8},{1,9},{2,10},{3,11},{4,12},{5,13},{6,14},{7,15},{8,0},{9,1},... | collective-permute-start | bytes 2113544 | tf_op jit(solution)/shard_map/ppermute | solution.py:108
  131.1 2.4 %collective-permute-start.28 = (bf16[86,16,128]{2,1,0:T(8,128)(2,1)}, bf16[86,16,128]{2,1,0:T(8,128)(2,1)}, u32[]{:S(2)}, u32[]{:S(2)}) collective-permute-start(bf16[86,16,128]{2,1,0:T(8,128)(2,1)} %collective-permute-done.23.rest_3_), channel_id=1, source_target_pairs={{0,8},{1,9},{2,10},{3,11},{4,12},{5,13},{6,14},{7,15},{8,0},{9,1},... | collective-permute-start | bytes 1056776 | tf_op jit(solution)/shard_map/ppermute | solution.py:108
  131.1 2.4 %collective-permute-start.29 = (bf16[86,16,128]{2,1,0:T(8,128)(2,1)S(1)}, bf16[86,16,128]{2,1,0:T(8,128)(2,1)}, u32[]{:S(2)}, u32[]{:S(2)}) collective-permute-start(bf16[86,16,128]{2,1,0:T(8,128)(2,1)S(1)} %collective-permute-done.24.rest_4_), channel_id=1, source_target_pairs={{0,8},{1,9},{2,10},{3,11},{4,12},{5,13},{6,14},{7,15},{8,0},{9,1},... | collective-permute-start | bytes 1056776 | tf_op jit(solution)/shard_map/ppermute | solution.py:108
  133.6 23.8 %copy-start.1 = (bf16[172,16,128]{2,1,0:T(8,128)(2,1)S(1)}, bf16[172,16,128]{2,1,0:T(8,128)(2,1)}, u32[]{:S(2)}) copy-start(bf16[172,16,128]{2,1,0:T(8,128)(2,1)} %copy-done) | copy-start | bytes 2113540
  133.6 23.8 %copy-start.7 = (bf16[4,64,1152]{2,1,0:T(8,128)(2,1)S(1)}, bf16[4,64,1152]{2,1,0:T(8,128)(2,1)}, u32[]{:S(2)}) copy-start(bf16[4,64,1152]{2,1,0:T(8,128)(2,1)} %copy-done.6) | copy-start | bytes 1769476
  133.6 23.8 %copy-start.11 = (bf16[172,16,128]{2,1,0:T(8,128)(2,1)S(1)}, bf16[172,16,128]{2,1,0:T(8,128)(2,1)}, u32[]{:S(2)}) copy-start(bf16[172,16,128]{2,1,0:T(8,128)(2,1)} %copy-done.10) | copy-start | bytes 2113540
  133.6 23.8 %copy-start.15 = (bf16[86,16,128]{2,1,0:T(8,128)(2,1)S(1)}, bf16[86,16,128]{2,1,0:T(8,128)(2,1)}, u32[]{:S(2)}) copy-start(bf16[86,16,128]{2,1,0:T(8,128)(2,1)} %copy-done.14) | copy-start | bytes 1056772
  133.6 23.8 %copy-start.21 = (bf16[86,16,128]{2,1,0:T(8,128)(2,1)S(1)}, bf16[86,16,128]{2,1,0:T(8,128)(2,1)}, u32[]{:S(2)}) copy-start(bf16[86,16,128]{2,1,0:T(8,128)(2,1)} %copy-done.20) | copy-start | bytes 1056772
  133.7 23.8 %copy-start.23 = (bf16[86,16,128]{2,1,0:T(8,128)(2,1)S(1)}, bf16[86,16,128]{2,1,0:T(8,128)(2,1)}, u32[]{:S(2)}) copy-start(bf16[86,16,128]{2,1,0:T(8,128)(2,1)} %copy-done.22) | copy-start | bytes 1056772
  133.7 23.8 %copy-start.29 = (f32[8,128,128]{2,1,0:T(8,128)S(1)}, f32[8,128,128]{2,1,0:T(8,128)}, u32[]{:S(2)}) copy-start(f32[8,128,128]{2,1,0:T(8,128)} %get-tuple-element.27.rest_2_) | copy-start | bytes 1572868
  133.7 23.8 %copy-start.32 = (bf16[128,1792]{1,0:T(8,128)(2,1)S(1)}, bf16[128,1792]{1,0:T(8,128)(2,1)}, u32[]{:S(2)}) copy-start(bf16[128,1792]{1,0:T(8,128)(2,1)} %get-tuple-element.26.rest_1_) | copy-start | bytes 1376260
  133.7 23.8 %copy-start.36 = (bf16[128,576]{1,0:T(8,128)(2,1)S(1)}, bf16[128,576]{1,0:T(8,128)(2,1)}, u32[]{:S(2)}) copy-start(bf16[128,576]{1,0:T(8,128)(2,1)} %get-tuple-element.28.rest_3_) | copy-start | bytes 442372
  157.4 14.1 %copy-start.3 = (bf16[172,16,128]{2,1,0:T(8,128)(2,1)S(1)}, bf16[172,16,128]{2,1,0:T(8,128)(2,1)}, u32[]{:S(2)}) copy-start(bf16[172,16,128]{2,1,0:T(8,128)(2,1)} %copy-done.2) | copy-start | bytes 2113540
  165.4 1.9 %collective-permute-start.30 = (bf16[32,1280]{1,0:T(8,128)(2,1)S(1)}, bf16[32,1280]{1,0:T(8,128)(2,1)S(1)}, u32[]{:S(2)}, u32[]{:S(2)}) collective-permute-start(bf16[32,1280]{1,0:T(8,128)(2,1)S(1)} %get-tuple-element.30), channel_id=1, source_target_pairs={{0,8},{1,9},{2,10},{3,11},{4,12},{5,13},{6,14},{7,15},{8,0},{9,1},... | collective-permute-start | bytes 245768 | tf_op jit(solution)/shard_map/ppermute | solution.py:108
  165.4 5.3 %collective-permute-start.31 = (bf16[32,1280]{1,0:T(8,128)(2,1)S(1)}, bf16[32,1280]{1,0:T(8,128)(2,1)S(1)}, u32[]{:S(2)}, u32[]{:S(2)}) collective-permute-start(bf16[32,1280]{1,0:T(8,128)(2,1)S(1)} %get-tuple-element.31), channel_id=1, source_target_pairs={{0,16},{1,17},{2,18},{3,19},{4,20},{5,21},{6,22},{7,23},{8,24},{9,... | collective-permute-start | bytes 245768 | tf_op jit(solution)/shard_map/ppermute | solution.py:108
  166.7 4.9 %collective-permute-start.32 = (bf16[32,1280]{1,0:T(8,128)(2,1)S(1)}, bf16[32,1280]{1,0:T(8,128)(2,1)S(1)}, u32[]{:S(2)}, u32[]{:S(2)}) collective-permute-start(bf16[32,1280]{1,0:T(8,128)(2,1)S(1)} %get-tuple-element.32), channel_id=1, source_target_pairs={{0,24},{1,25},{2,26},{3,27},{4,28},{5,29},{6,30},{7,31},{8,16},{9,... | collective-permute-start | bytes 245768 | tf_op jit(solution)/shard_map/ppermute | solution.py:108
  (27 other events, 229.9 us)

commit v5 on v4

--- a/solution.py
+++ b/solution.py
@@ -138,38 +138,23 @@
 
 
 def stack_kernel(n, slot_ref, *refs):
-    ins, outs, held, sems = refs[:n], refs[n:-2], refs[-2], refs[-1]
-    rows = held.shape[2]
-    reads, writes = [], []
+    ins, outs = refs[:n], refs[n:]
+    rows = ins[0].shape[0] // len(outs)
     for j, out in enumerate(outs):
         for i in range(n):
-            slot = pl.ds(slot_ref[i] * rows, rows)
-            piece = ins[i].at[pl.ds(j * rows, rows)]
-            reads.append(pltpu.make_async_copy(piece, held.at[j, i], sems.at[0, j, i]))
-            writes.append(pltpu.make_async_copy(held.at[j, i], out.at[slot], sems.at[1, j, i]))
-    for read in reads:
-        read.start()
-    for read, write in zip(reads, writes):
-        read.wait()
-        write.start()
-    for write in writes:
-        write.wait()
+            out[pl.ds(slot_ref[i] * rows, rows)] = ins[i][j * rows : (j + 1) * rows]
 
 
 def stacked(slots, arrays, outs, after):
     n, rows = len(arrays), arrays[0].shape[0] // outs
-    anywhere = pl.BlockSpec(memory_space=pl.ANY)
+    vmem = pl.BlockSpec(memory_space=pltpu.VMEM)
     line = jax.ShapeDtypeStruct((n * rows, ROWS, LANES), jnp.bfloat16)
     return pl.pallas_call(
         lambda *refs: stack_kernel(n, *refs[: n + 1], *refs[n + 1 + len(after) :]),
         out_shape=[line] * outs,
-        in_specs=[pl.BlockSpec(memory_space=pltpu.SMEM)] + [anywhere] * (n + len(after)),
-        out_specs=[anywhere] * outs,
-        scratch_shapes=[
-            pltpu.VMEM((outs, n, rows, ROWS, LANES), jnp.bfloat16),
-            pltpu.SemaphoreType.DMA((2, outs, n)),
-        ],
-        compiler_params=pltpu.CompilerParams(vmem_limit_bytes=3 * 2**20),
+        in_specs=[pl.BlockSpec(memory_space=pltpu.SMEM)] + [vmem] * n + [HBM] * len(after),
+        out_specs=[vmem] * outs,
+        compiler_params=pltpu.CompilerParams(vmem_limit_bytes=6 * 2**20),
     )(slots, *arrays, *after)
 
 

time: 181 us -> 179 us (0.989)
  Pallas kernels: 47.9 us -> 45.7 us
    pallas_call x1, Pallas kernels: 3.4 us -> 1.3 us  [stacked(): pl.pallas_call(lambda *refs: stack_kernel(n, *refs[:n + 1], *refs[n + 1 +...]
  transfers between devices with their start and end apart: 35 -> 35, of which waited for: 14 -> 15; matrix products, arithmetic and copies ran while one was open for 3% -> 3% of each run, Pallas kernels for 10% -> 9%
where the time goes in v5:
time: 179 us
  waiting for transfers between devices  55.4 us (31%)
  Pallas kernels  45.7 us (26%)
  blocking collectives  34.9 us (19%)
  starting transfers between devices  32.4 us (18%)
  local copies, waits for them, and re-layouts  8.61 us (5%)
    ppermute x33, waiting for transfers between devices, send(): return lax.ppermute(value, AXES, pairs)  55.3 us
    pallas_call x5, Pallas kernels, call(): pl.pallas_call(functools.partial(kernel, plan), out_shape=list(outs) + li...  41 us
    ppermute x33, starting transfers between devices, send(): return lax.ppermute(value, AXES, pairs)  25.2 us
    all_gather x1, blocking collectives, line(): lax.all_gather(value, AXES, axis=0, tiled=True, axis_index_groups=groups)  20.7 us
    all_to_all x1, blocking collectives, swap(): return lax.all_to_all(value, axis, split_axis=0, concat_axis=0, tiled=True)  14.1 us
    all_to_all x2, starting transfers between devices, swap(): return lax.all_to_all(value, axis, split_axis=0, concat_axis=0, tiled=True)  7.17 us
  transfers between devices with their start and end apart: 35, of which 15 were waited for; matrix products, arithmetic and copies ran while one was open for 3% of the time, Pallas kernels for 9%

profile of v5, /device:TPU:0, one launch (start us, length us, event | category | flops | bytes accessed | tf_op | source)
XLA Modules:
  0.0 178.7 jit_solution(6337766486403981522)
XLA Ops:
  0.6 3.4 %shard_map.77 = (bf16[43,16,128]{2,1,0:T(8,128)(2,1)}, bf16[86,16,128]{2,1,0:T(8,128)(2,1)}) custom-call(s32[1]{0:T(128)} %bitcast.8.part_ref, bf16[3,144,1728]{2,1,0:T(8,128)(2,1)} %q_ref.1, bf16[3,72,1152]{2,1,0:T(8,128)(2,1)} %o_ref.1), custom_call_target="tpu_custom_call" | custom-call | tf_op jit(solution)/shard_map/pallas_call | solution.py:83
  4.1 20.7 %all_gather.3.refs_0_.refs_1_ = bf16[172,16,128]{2,1,0:T(8,128)(2,1)S(1)} all-gather(bf16[43,16,128]{2,1,0:T(8,128)(2,1)} %get-tuple-element.20), channel_id=1, replica_groups={{0,2,4,6},{1,3,5,7},{8,10,12,14},{9,11,13,15},{16,18,20,22},{17,19,21,2..., dimensions={0}, use_global_device_ids=true | all-gather | bytes 880640 | tf_op jit(solution)/shard_map/all_gather | solution.py:125
  24.8 1.5 collective-permute-start.1
  26.3 1.5 collective-permute-start
  27.8 2.3 %collective-permute-start.5 = (bf16[86,16,128]{2,1,0:T(8,128)(2,1)}, bf16[86,16,128]{2,1,0:T(8,128)(2,1)S(1)}, u32[]{:S(2)}, u32[]{:S(2)}) collective-permute-start(bf16[86,16,128]{2,1,0:T(8,128)(2,1)} %shard_map.81.refs_1_), channel_id=1, source_target_pairs={{0,6},{1,7},{2,4},{3,5},{4,2},{5,3},{6,0},{7,1},{8,14},{9,15},{10,... | collective-permute-start | bytes 1056776 | tf_op jit(solution)/shard_map/ppermute | solution.py:108
  30.5 1.2 reshape_transpose.7.refs_2_.cot_ref
  31.7 8.2 %collective-permute-done.1.refs_0_ = bf16[172,16,128]{2,1,0:T(8,128)(2,1)S(1)} collective-permute-done((bf16[172,16,128]{2,1,0:T(8,128)(2,1)S(1)}, bf16[172,16,128]{2,1,0:T(8,128)(2,1)S(1)}, u32[]{:S(2)}, u32[]{:S(2)}) %collective-permute-start.1) | collective-permute-done | bytes 704544 | tf_op jit(solution)/shard_map/ppermute | solution.py:108
  39.9 1.0 collective-permute-start.4
  40.9 0.9 collective-permute-start.3
  41.9 0.8 slice.25
  42.7 1.5 collective-permute-start.6
  44.2 0.8 slice.24
  45.0 0.7 copy-done.33
  45.7 1.5 collective-permute-start.2
  47.3 11.2 %collective-permute-done.4.refs_3_ = bf16[86,16,128]{2,1,0:T(8,128)(2,1)} collective-permute-done((bf16[86,16,128]{2,1,0:T(8,128)(2,1)}, bf16[86,16,128]{2,1,0:T(8,128)(2,1)}, u32[]{:S(2)}, u32[]{:S(2)}) %collective-permute-start.4) | collective-permute-done | bytes 352288 | tf_op jit(solution)/shard_map/ppermute | solution.py:108
  58.5 0.7 collective-permute-done.3.refs_2_
  59.2 1.0 copy-done.34
  60.2 1.3 shard_map.82
  62.5 1.5 collective-permute-start.13
  63.9 1.5 collective-permute-start.12
  66.1 1.4 collective-permute-done.10.rest_8_.rest_15_
  67.5 7.2 %shard_map.85 = (bf16[256,1152]{1,0:T(8,128)(2,1)}, bf16[128,1792]{1,0:T(8,128)(2,1)}, f32[8,128,128]{2,1,0:T(8,128)}, bf16[128,576]{1,0:T(8,128)(2,1)}) custom-call(s32[12]{0:T(128)} %stack.66.place_ref, f32[3,8]{1,0:T(4,128)} %gates_ref.9, bf16[128,1152]{1,0:T(8,128)(2,1)} %copy-done.12, f32[3,1152]{1,0:T(4,128)} %gain_ref.9, f32[128,128]{1,0:T(8,128)} %copy-done.27, ...), custom_call_target="tpu_custom_call" | custom-call | flops 679477248 | bytes 12582912 | tf_op jit(solution)/shard_map/pallas_call | solution.py:448
  74.7 3.5 %all-to-all-start = ((bf16[4,64,1152]{2,1,0:T(8,128)(2,1)}), bf16[4,64,1152]{2,1,0:T(8,128)(2,1)S(1)}, u32[]{:S(2)}, u32[]{:S(2)}) async-start(bf16[4,64,1152]{2,1,0:T(8,128)(2,1)} %bitcast.30), calls=%async_computation | async-start | bytes 1179648 | tf_op jit(solution)/shard_map/all_to_all | solution.py:490
  78.2 2.6 %collective-permute-done.13.refs_0_ = bf16[172,16,128]{2,1,0:T(8,128)(2,1)} collective-permute-done((bf16[172,16,128]{2,1,0:T(8,128)(2,1)S(1)}, bf16[172,16,128]{2,1,0:T(8,128)(2,1)}, u32[]{:S(2)}, u32[]{:S(2)}) %collective-permute-start.13) | collective-permute-done | bytes 704544 | tf_op jit(solution)/shard_map/ppermute | solution.py:108
  80.7 1.1 copy-done.17
  81.8 1.1 slice.26
  82.9 1.8 %collective-permute-start.14 = (bf16[86,16,128]{2,1,0:T(8,128)(2,1)S(1)}, bf16[86,16,128]{2,1,0:T(8,128)(2,1)S(1)}, u32[]{:S(2)}, u32[]{:S(2)}) collective-permute-start(bf16[86,16,128]{2,1,0:T(8,128)(2,1)S(1)} %slice.26), channel_id=1, source_target_pairs={{0,1},{1,0},{2,3},{3,2},{4,5},{5,4},{6,7},{7,6},{8,9},{9,8},{10,11... | collective-permute-start | bytes 1056776 | tf_op jit(solution)/shard_map/ppermute | solution.py:108
  84.7 0.8 slice.27
  85.5 1.7 collective-permute-start.15
  87.8 5.0 %collective-permute-done.14.refs_0_ = bf16[86,16,128]{2,1,0:T(8,128)(2,1)S(1)} collective-permute-done((bf16[86,16,128]{2,1,0:T(8,128)(2,1)S(1)}, bf16[86,16,128]{2,1,0:T(8,128)(2,1)S(1)}, u32[]{:S(2)}, u32[]{:S(2)}) %collective-permute-start.14) | collective-permute-done | bytes 352288 | tf_op jit(solution)/shard_map/ppermute | solution.py:108
  92.8 2.6 %collective-permute-done.15.refs_0_ = bf16[86,16,128]{2,1,0:T(8,128)(2,1)} collective-permute-done((bf16[86,16,128]{2,1,0:T(8,128)(2,1)}, bf16[86,16,128]{2,1,0:T(8,128)(2,1)}, u32[]{:S(2)}, u32[]{:S(2)}) %collective-permute-start.15) | collective-permute-done | bytes 352288 | tf_op jit(solution)/shard_map/ppermute | solution.py:108
  95.4 1.3 collective-permute-start.22
  97.2 0.8 collective-permute-start.21
  98.0 7.5 %shard_map.92 = (bf16[256,1152]{1,0:T(8,128)(2,1)}, bf16[128,1792]{1,0:T(8,128)(2,1)}, f32[8,128,128]{2,1,0:T(8,128)}, bf16[128,576]{1,0:T(8,128)(2,1)}) custom-call(s32[12]{0:T(128)} %stack.66.place_ref, f32[3,8]{1,0:T(4,128)} %gates_ref.9, bf16[256,1152]{1,0:T(8,128)(2,1)} %bitcast.26, f32[3,1152]{1,0:T(4,128)} %gain_ref.9, f32[128,128]{1,0:T(8,128)} %copy-done.26, ...), custom_call_target="tpu_custom_call" | custom-call | flops 679477248 | bytes 12582912 | tf_op jit(solution)/shard_map/pallas_call | solution.py:448
  105.5 3.7 %all-to-all-start.1 = ((bf16[8,32,1152]{2,1,0:T(8,128)(2,1)}), bf16[8,32,1152]{2,1,0:T(8,128)(2,1)S(1)}, u32[]{:S(2)}, u32[]{:S(2)}) async-start(bf16[8,32,1152]{2,1,0:T(8,128)(2,1)} %bitcast.29), calls=%async_computation.1 | async-start | bytes 1179648 | tf_op jit(solution)/shard_map/all_to_all | solution.py:490
  109.2 4.4 %collective-permute-done.22.refs_0_ = bf16[172,16,128]{2,1,0:T(8,128)(2,1)S(1)} collective-permute-done((bf16[172,16,128]{2,1,0:T(8,128)(2,1)S(1)}, bf16[172,16,128]{2,1,0:T(8,128)(2,1)S(1)}, u32[]{:S(2)}, u32[]{:S(2)}) %collective-permute-start.22) | collective-permute-done | bytes 704544 | tf_op jit(solution)/shard_map/ppermute | solution.py:108
  113.7 0.9 collective-permute-start.23
  114.5 4.5 %collective-permute-done.21.refs_0_ = bf16[172,16,128]{2,1,0:T(8,128)(2,1)S(1)} collective-permute-done((bf16[172,16,128]{2,1,0:T(8,128)(2,1)S(1)}, bf16[172,16,128]{2,1,0:T(8,128)(2,1)S(1)}, u32[]{:S(2)}, u32[]{:S(2)}) %collective-permute-start.21) | collective-permute-done | bytes 704544 | tf_op jit(solution)/shard_map/ppermute | solution.py:108
  119.1 1.3 collective-permute-start.24
  120.9 8.1 %collective-permute-done.23.rest_3_ = bf16[86,16,128]{2,1,0:T(8,128)(2,1)} collective-permute-done((bf16[86,16,128]{2,1,0:T(8,128)(2,1)S(1)}, bf16[86,16,128]{2,1,0:T(8,128)(2,1)}, u32[]{:S(2)}, u32[]{:S(2)}) %collective-permute-start.23) | collective-permute-done | bytes 352288 | tf_op jit(solution)/shard_map/ppermute | solution.py:108
  129.5 1.9 %collective-permute-done.28.rest_8_ = bf16[86,16,128]{2,1,0:T(8,128)(2,1)} collective-permute-done((bf16[86,16,128]{2,1,0:T(8,128)(2,1)}, bf16[86,16,128]{2,1,0:T(8,128)(2,1)}, u32[]{:S(2)}, u32[]{:S(2)}) %collective-permute-start.28) | collective-permute-done | bytes 352288 | tf_op jit(solution)/shard_map/ppermute | solution.py:108
  131.6 9.5 %shard_map.97 = bf16[128,1280]{1,0:T(8,128)(2,1)S(1)} custom-call(s32[12]{0:T(128)S(1)} %copy-done.38, f32[3,8]{1,0:T(4,128)S(1)} %copy-done.37, bf16[256,1152]{1,0:T(8,128)(2,1)S(1)} %bitcast.31, f32[3,1152]{1,0:T(4,128)S(1)} %copy-done.30, f32[128,128]{1,0:T(8,128)S(1)} %copy-done.25, bf16[172,16,128]{2,1,0:T(8,128)(2,1)S(1)} %shard_map.96.rest_0_, ...), custom_call_target="tpu_custom_call" | custom-call | flops 1358954496 | bytes 12582912 | tf_op jit(solution)/shard_map/pallas_call | solution.py:448
  141.1 14.1 %all_to_all.33 = bf16[8,16,1280]{2,1,0:T(8,128)(2,1)S(1)} all-to-all(bf16[8,16,1280]{2,1,0:T(8,128)(2,1)S(1)} %bitcast.33), channel_id=1, replica_groups=mesh['ha'=4,'wa'=8] {'wa'}, dimensions={0} | all-to-all | bytes 655360 | tf_op jit(solution)/shard_map/all_to_all | solution.py:490
  155.4 7.8 %shard_map.98 = (bf16[32,1280]{1,0:T(8,128)(2,1)S(1)}, bf16[32,1280]{1,0:T(8,128)(2,1)S(1)}, bf16[32,1280]{1,0:T(8,128)(2,1)S(1)}, bf16[32,1280]{1,0:T(8,128)(2,1)S(1)}) custom-call(s32[12]{0:T(128)S(1)} %copy-done.38, f32[3,8]{1,0:T(4,128)S(1)} %copy-done.37, bf16[256,1152]{1,0:T(8,128)(2,1)S(1)} %bitcast.28, f32[3,1152]{1,0:T(4,128)S(1)} %copy-done.30, ...), custom_call_target="tpu_custom_call" | custom-call | flops 679477248 | bytes 12582912 | tf_op jit(solution)/shard_map/pallas_call | solution.py:448
  163.3 1.3 collective-permute-start.31
  165.2 3.4 %collective-permute-done.31.rest_2_ = bf16[32,1280]{1,0:T(8,128)(2,1)S(1)} collective-permute-done((bf16[32,1280]{1,0:T(8,128)(2,1)S(1)}, bf16[32,1280]{1,0:T(8,128)(2,1)S(1)}, u32[]{:S(2)}, u32[]{:S(2)}) %collective-permute-start.31) | collective-permute-done | bytes 81952 | tf_op jit(solution)/shard_map/ppermute | solution.py:108
  168.6 0.8 collective-permute-done.32.rest_3_
  169.5 9.0 %shard_map.99 = (bf16[64,2,1152]{2,1,0:T(2,128)(2,1)}, bf16[3,64,2,8]{3,2,1,0:T(2,128)(2,1)}) custom-call(s32[12]{0:T(128)S(1)} %copy-done.38, f32[3,8]{1,0:T(4,128)S(1)} %copy-done.37, bf16[128,1152]{1,0:T(8,128)(2,1)S(1)} %copy-done.13, f32[3,1152]{1,0:T(4,128)S(1)} %copy-done.30, bf16[32,1280]{1,0:T(8,128)(2,1)S(1)} %get-tuple-element.29.rest_0_, ...), custom_call_target="tpu_custom_call" | custom-call | flops 679477248 | bytes 12582912 | tf_op jit(solution)/shard_map/pallas_call | solution.py:448
  (142 shorter events, 5.0 us)
Async XLA Ops:
  4.1 26.3 %copy-start.39 = (bf16[1,8,8,2,1152]{4,3,2,1,0:T(2,128)(2,1)S(1)}, bf16[1,8,8,2,1152]{4,3,2,1,0:T(2,128)(2,1)}, u32[]{:S(2)}) copy-start(bf16[1,8,8,2,1152]{4,3,2,1,0:T(2,128)(2,1)} %param.6) | copy-start | bytes 884740
  24.8 15.1 %collective-permute-start.1 = (bf16[172,16,128]{2,1,0:T(8,128)(2,1)S(1)}, bf16[172,16,128]{2,1,0:T(8,128)(2,1)S(1)}, u32[]{:S(2)}, u32[]{:S(2)}) collective-permute-start(bf16[172,16,128]{2,1,0:T(8,128)(2,1)S(1)} %all_gather.3.refs_0_.refs_1_), channel_id=1, source_target_pairs={{0,16},{1,17},{2,18},{3,19},{4,20},{5,21},{6,22},{7,23},{8,24},{9,... | collective-permute-start | bytes 2113544 | tf_op jit(solution)/shard_map/ppermute | solution.py:108
  26.3 15.6 %collective-permute-start = (bf16[172,16,128]{2,1,0:T(8,128)(2,1)S(1)}, bf16[172,16,128]{2,1,0:T(8,128)(2,1)S(1)}, u32[]{:S(2)}, u32[]{:S(2)}) collective-permute-start(bf16[172,16,128]{2,1,0:T(8,128)(2,1)S(1)} %all_gather.3.refs_0_.refs_1_), channel_id=1, source_target_pairs={{0,1},{1,0},{2,3},{3,2},{4,5},{5,4},{6,7},{7,6},{8,9},{9,8},{10,11... | collective-permute-start | bytes 2113544 | tf_op jit(solution)/shard_map/ppermute | solution.py:108
  27.8 17.2 %collective-permute-start.5 = (bf16[86,16,128]{2,1,0:T(8,128)(2,1)}, bf16[86,16,128]{2,1,0:T(8,128)(2,1)S(1)}, u32[]{:S(2)}, u32[]{:S(2)}) collective-permute-start(bf16[86,16,128]{2,1,0:T(8,128)(2,1)} %shard_map.81.refs_1_), channel_id=1, source_target_pairs={{0,6},{1,7},{2,4},{3,5},{4,2},{5,3},{6,0},{7,1},{8,14},{9,15},{10,... | collective-permute-start | bytes 1056776 | tf_op jit(solution)/shard_map/ppermute | solution.py:108
  39.9 21.7 %copy-start.4 = (bf16[172,16,128]{2,1,0:T(8,128)(2,1)}, bf16[172,16,128]{2,1,0:T(8,128)(2,1)S(1)}, u32[]{:S(2)}) copy-start(bf16[172,16,128]{2,1,0:T(8,128)(2,1)S(1)} %shard_map.79.refs_2_.refs_6_.rest_2_.rest_9_) | copy-start | bytes 2113540
  39.9 24.0 %collective-permute-start.9 = (bf16[172,16,128]{2,1,0:T(8,128)(2,1)S(1)}, bf16[172,16,128]{2,1,0:T(8,128)(2,1)}, u32[]{:S(2)}, u32[]{:S(2)}) collective-permute-start(bf16[172,16,128]{2,1,0:T(8,128)(2,1)S(1)} %shard_map.79.refs_2_.refs_6_.rest_2_.rest_9_), channel_id=1, source_target_pairs={{0,8},{1,9},{2,10},{3,11},{4,12},{5,13},{6,14},{7,15},{8,0},{9,1},... | collective-permute-start | bytes 2113544 | tf_op jit(solution)/shard_map/ppermute | solution.py:108
  39.9 18.6 %collective-permute-start.4 = (bf16[86,16,128]{2,1,0:T(8,128)(2,1)}, bf16[86,16,128]{2,1,0:T(8,128)(2,1)}, u32[]{:S(2)}, u32[]{:S(2)}) collective-permute-start(bf16[86,16,128]{2,1,0:T(8,128)(2,1)} %shard_map.81.refs_1_), channel_id=1, source_target_pairs={{0,4},{1,5},{2,6},{3,7},{4,0},{5,1},{6,2},{7,3},{8,12},{9,13},{10,... | collective-permute-start | bytes 1056776 | tf_op jit(solution)/shard_map/ppermute | solution.py:108
  40.9 18.2 %collective-permute-start.3 = (bf16[86,16,128]{2,1,0:T(8,128)(2,1)}, bf16[86,16,128]{2,1,0:T(8,128)(2,1)}, u32[]{:S(2)}, u32[]{:S(2)}) collective-permute-start(bf16[86,16,128]{2,1,0:T(8,128)(2,1)} %shard_map.81.refs_1_), channel_id=1, source_target_pairs={{0,2},{1,3},{2,0},{3,1},{4,6},{5,7},{6,4},{7,5},{8,10},{9,11},{10,... | collective-permute-start | bytes 1056776 | tf_op jit(solution)/shard_map/ppermute | solution.py:108
  41.9 20.2 %copy-start.2 = (bf16[172,16,128]{2,1,0:T(8,128)(2,1)}, bf16[172,16,128]{2,1,0:T(8,128)(2,1)S(1)}, u32[]{:S(2)}) copy-start(bf16[172,16,128]{2,1,0:T(8,128)(2,1)S(1)} %shard_map.78.refs_1_.refs_5_.rest_1_.rest_8_) | copy-start | bytes 2113540
  42.7 18.7 %collective-permute-start.6 = (bf16[86,16,128]{2,1,0:T(8,128)(2,1)}, bf16[86,16,128]{2,1,0:T(8,128)(2,1)}, u32[]{:S(2)}, u32[]{:S(2)}) collective-permute-start(bf16[86,16,128]{2,1,0:T(8,128)(2,1)} %slice.25), channel_id=1, source_target_pairs={{0,16},{1,17},{2,18},{3,19},{4,20},{5,21},{6,22},{7,23},{8,24},{9,... | collective-permute-start | bytes 1056776 | tf_op jit(solution)/shard_map/ppermute | solution.py:108
  45.7 16.4 %collective-permute-start.2 = (bf16[86,16,128]{2,1,0:T(8,128)(2,1)}, bf16[86,16,128]{2,1,0:T(8,128)(2,1)}, u32[]{:S(2)}, u32[]{:S(2)}) collective-permute-start(bf16[86,16,128]{2,1,0:T(8,128)(2,1)} %slice.24), channel_id=1, source_target_pairs={{0,1},{1,0},{2,3},{3,2},{4,5},{5,4},{6,7},{7,6},{8,9},{9,8},{10,11... | collective-permute-start | bytes 1056776 | tf_op jit(solution)/shard_map/ppermute | solution.py:108
  61.5 4.0 %collective-permute-start.11 = (bf16[86,16,128]{2,1,0:T(8,128)(2,1)}, bf16[86,16,128]{2,1,0:T(8,128)(2,1)}, u32[]{:S(2)}, u32[]{:S(2)}) collective-permute-start(bf16[86,16,128]{2,1,0:T(8,128)(2,1)} %shard_map.84.rest_4_.refs_2_.rest_11_), channel_id=1, source_target_pairs={{0,8},{1,9},{2,10},{3,11},{4,12},{5,13},{6,14},{7,15},{8,0},{9,1},... | collective-permute-start | bytes 1056776 | tf_op jit(solution)/shard_map/ppermute | solution.py:108
  61.6 5.9 %collective-permute-start.7 = (bf16[172,16,128]{2,1,0:T(8,128)(2,1)S(1)}, bf16[172,16,128]{2,1,0:T(8,128)(2,1)}, u32[]{:S(2)}, u32[]{:S(2)}) collective-permute-start(bf16[172,16,128]{2,1,0:T(8,128)(2,1)S(1)} %shard_map.80.rest_0_.rest_7_), channel_id=1, source_target_pairs={{0,8},{1,9},{2,10},{3,11},{4,12},{5,13},{6,14},{7,15},{8,0},{9,1},... | collective-permute-start | bytes 2113544 | tf_op jit(solution)/shard_map/ppermute | solution.py:108
  62.1 5.4 %collective-permute-start.8 = (bf16[172,16,128]{2,1,0:T(8,128)(2,1)S(1)}, bf16[172,16,128]{2,1,0:T(8,128)(2,1)}, u32[]{:S(2)}, u32[]{:S(2)}) collective-permute-start(bf16[172,16,128]{2,1,0:T(8,128)(2,1)S(1)} %shard_map.78.refs_1_.refs_5_.rest_1_.rest_8_), channel_id=1, source_target_pairs={{0,8},{1,9},{2,10},{3,11},{4,12},{5,13},{6,14},{7,15},{8,0},{9,1},... | collective-permute-start | bytes 2113544 | tf_op jit(solution)/shard_map/ppermute | solution.py:108
  62.5 18.3 %collective-permute-start.13 = (bf16[172,16,128]{2,1,0:T(8,128)(2,1)S(1)}, bf16[172,16,128]{2,1,0:T(8,128)(2,1)}, u32[]{:S(2)}, u32[]{:S(2)}) collective-permute-start(bf16[172,16,128]{2,1,0:T(8,128)(2,1)S(1)} %shard_map.86.refs_0_), channel_id=1, source_target_pairs={{0,16},{1,17},{2,18},{3,19},{4,20},{5,21},{6,22},{7,23},{8,24},{9,... | collective-permute-start | bytes 2113544 | tf_op jit(solution)/shard_map/ppermute | solution.py:108
  63.9 20.7 %collective-permute-start.12 = (bf16[172,16,128]{2,1,0:T(8,128)(2,1)S(1)}, bf16[172,16,128]{2,1,0:T(8,128)(2,1)S(1)}, u32[]{:S(2)}, u32[]{:S(2)}) collective-permute-start(bf16[172,16,128]{2,1,0:T(8,128)(2,1)S(1)} %shard_map.86.refs_0_), channel_id=1, source_target_pairs={{0,1},{1,0},{2,3},{3,2},{4,5},{5,4},{6,7},{7,6},{8,9},{9,8},{10,11... | collective-permute-start | bytes 2113544 | tf_op jit(solution)/shard_map/ppermute | solution.py:108
  65.5 2.0 %collective-permute-start.10 = (bf16[86,16,128]{2,1,0:T(8,128)(2,1)}, bf16[86,16,128]{2,1,0:T(8,128)(2,1)}, u32[]{:S(2)}, u32[]{:S(2)}) collective-permute-start(bf16[86,16,128]{2,1,0:T(8,128)(2,1)} %shard_map.83.rest_3_.refs_1_.rest_10_), channel_id=1, source_target_pairs={{0,8},{1,9},{2,10},{3,11},{4,12},{5,13},{6,14},{7,15},{8,0},{9,1},... | collective-permute-start | bytes 1056776 | tf_op jit(solution)/shard_map/ppermute | solution.py:108
  74.7 13.1 %all-to-all-start = ((bf16[4,64,1152]{2,1,0:T(8,128)(2,1)}), bf16[4,64,1152]{2,1,0:T(8,128)(2,1)S(1)}, u32[]{:S(2)}, u32[]{:S(2)}) async-start(bf16[4,64,1152]{2,1,0:T(8,128)(2,1)} %bitcast.30), calls=%async_computation | async-start | bytes 1179648 | tf_op jit(solution)/shard_map/all_to_all | solution.py:490
  82.9 9.9 %collective-permute-start.14 = (bf16[86,16,128]{2,1,0:T(8,128)(2,1)S(1)}, bf16[86,16,128]{2,1,0:T(8,128)(2,1)S(1)}, u32[]{:S(2)}, u32[]{:S(2)}) collective-permute-start(bf16[86,16,128]{2,1,0:T(8,128)(2,1)S(1)} %slice.26), channel_id=1, source_target_pairs={{0,1},{1,0},{2,3},{3,2},{4,5},{5,4},{6,7},{7,6},{8,9},{9,8},{10,11... | collective-permute-start | bytes 1056776 | tf_op jit(solution)/shard_map/ppermute | solution.py:108
  85.5 9.8 %collective-permute-start.15 = (bf16[86,16,128]{2,1,0:T(8,128)(2,1)}, bf16[86,16,128]{2,1,0:T(8,128)(2,1)}, u32[]{:S(2)}, u32[]{:S(2)}) collective-permute-start(bf16[86,16,128]{2,1,0:T(8,128)(2,1)} %slice.27), channel_id=1, source_target_pairs={{0,16},{1,17},{2,18},{3,19},{4,20},{5,21},{6,22},{7,23},{8,24},{9,... | collective-permute-start | bytes 1056776 | tf_op jit(solution)/shard_map/ppermute | solution.py:108
  87.2 10.8 %collective-permute-start.16 = (bf16[172,16,128]{2,1,0:T(8,128)(2,1)S(1)}, bf16[172,16,128]{2,1,0:T(8,128)(2,1)}, u32[]{:S(2)}, u32[]{:S(2)}) collective-permute-start(bf16[172,16,128]{2,1,0:T(8,128)(2,1)S(1)} %shard_map.89.rest_0_.rest_4_), channel_id=1, source_target_pairs={{0,8},{1,9},{2,10},{3,11},{4,12},{5,13},{6,14},{7,15},{8,0},{9,1},... | collective-permute-start | bytes 2113544 | tf_op jit(solution)/shard_map/ppermute | solution.py:108
  87.2 10.8 %collective-permute-start.17 = (bf16[172,16,128]{2,1,0:T(8,128)(2,1)S(1)}, bf16[172,16,128]{2,1,0:T(8,128)(2,1)}, u32[]{:S(2)}, u32[]{:S(2)}) collective-permute-start(bf16[172,16,128]{2,1,0:T(8,128)(2,1)S(1)} %shard_map.87.refs_1_.rest_1_.rest_5_), channel_id=1, source_target_pairs={{0,8},{1,9},{2,10},{3,11},{4,12},{5,13},{6,14},{7,15},{8,0},{9,1},... | collective-permute-start | bytes 2113544 | tf_op jit(solution)/shard_map/ppermute | solution.py:108
  87.7 10.3 %collective-permute-start.18 = (bf16[172,16,128]{2,1,0:T(8,128)(2,1)}, bf16[172,16,128]{2,1,0:T(8,128)(2,1)}, u32[]{:S(2)}, u32[]{:S(2)}) collective-permute-start(bf16[172,16,128]{2,1,0:T(8,128)(2,1)} %shard_map.88.refs_2_.rest_2_.rest_6_), channel_id=1, source_target_pairs={{0,8},{1,9},{2,10},{3,11},{4,12},{5,13},{6,14},{7,15},{8,0},{9,1},... | collective-permute-start | bytes 2113544 | tf_op jit(solution)/shard_map/ppermute | solution.py:108
  92.8 2.6 %collective-permute-start.19 = (bf16[86,16,128]{2,1,0:T(8,128)(2,1)S(1)}, bf16[86,16,128]{2,1,0:T(8,128)(2,1)S(1)}, u32[]{:S(2)}, u32[]{:S(2)}) collective-permute-start(bf16[86,16,128]{2,1,0:T(8,128)(2,1)S(1)} %shard_map.90.rest_3_.refs_1_.rest_7_), channel_id=1, source_target_pairs={{0,8},{1,9},{2,10},{3,11},{4,12},{5,13},{6,14},{7,15},{8,0},{9,1},... | collective-permute-start | bytes 1056776 | tf_op jit(solution)/shard_map/ppermute | solution.py:108
  95.3 1.9 %collective-permute-start.20 = (bf16[86,16,128]{2,1,0:T(8,128)(2,1)}, bf16[86,16,128]{2,1,0:T(8,128)(2,1)S(1)}, u32[]{:S(2)}, u32[]{:S(2)}) collective-permute-start(bf16[86,16,128]{2,1,0:T(8,128)(2,1)} %shard_map.91.rest_4_.refs_2_.rest_8_), channel_id=1, source_target_pairs={{0,8},{1,9},{2,10},{3,11},{4,12},{5,13},{6,14},{7,15},{8,0},{9,1},... | collective-permute-start | bytes 1056776 | tf_op jit(solution)/shard_map/ppermute | solution.py:108
  95.4 18.2 %collective-permute-start.22 = (bf16[172,16,128]{2,1,0:T(8,128)(2,1)S(1)}, bf16[172,16,128]{2,1,0:T(8,128)(2,1)S(1)}, u32[]{:S(2)}, u32[]{:S(2)}) collective-permute-start(bf16[172,16,128]{2,1,0:T(8,128)(2,1)S(1)} %shard_map.93.refs_0_), channel_id=1, source_target_pairs={{0,16},{1,17},{2,18},{3,19},{4,20},{5,21},{6,22},{7,23},{8,24},{9,... | collective-permute-start | bytes 2113544 | tf_op jit(solution)/shard_map/ppermute | solution.py:108
  97.2 21.8 %collective-permute-start.21 = (bf16[172,16,128]{2,1,0:T(8,128)(2,1)S(1)}, bf16[172,16,128]{2,1,0:T(8,128)(2,1)S(1)}, u32[]{:S(2)}, u32[]{:S(2)}) collective-permute-start(bf16[172,16,128]{2,1,0:T(8,128)(2,1)S(1)} %shard_map.93.refs_0_), channel_id=1, source_target_pairs={{0,1},{1,0},{2,3},{3,2},{4,5},{5,4},{6,7},{7,6},{8,9},{9,8},{10,11... | collective-permute-start | bytes 2113544 | tf_op jit(solution)/shard_map/ppermute | solution.py:108
  105.5 24.0 %all-to-all-start.1 = ((bf16[8,32,1152]{2,1,0:T(8,128)(2,1)}), bf16[8,32,1152]{2,1,0:T(8,128)(2,1)S(1)}, u32[]{:S(2)}, u32[]{:S(2)}) async-start(bf16[8,32,1152]{2,1,0:T(8,128)(2,1)} %bitcast.29), calls=%async_computation.1 | async-start | bytes 1179648 | tf_op jit(solution)/shard_map/all_to_all | solution.py:490
  113.7 15.3 %collective-permute-start.23 = (bf16[86,16,128]{2,1,0:T(8,128)(2,1)S(1)}, bf16[86,16,128]{2,1,0:T(8,128)(2,1)}, u32[]{:S(2)}, u32[]{:S(2)}) collective-permute-start(bf16[86,16,128]{2,1,0:T(8,128)(2,1)S(1)} %slice.28), channel_id=1, source_target_pairs={{0,1},{1,0},{2,3},{3,2},{4,5},{5,4},{6,7},{7,6},{8,9},{9,8},{10,11... | collective-permute-start | bytes 1056776 | tf_op jit(solution)/shard_map/ppermute | solution.py:108
  119.1 9.9 %collective-permute-start.24 = (bf16[86,16,128]{2,1,0:T(8,128)(2,1)S(1)}, bf16[86,16,128]{2,1,0:T(8,128)(2,1)S(1)}, u32[]{:S(2)}, u32[]{:S(2)}) collective-permute-start(bf16[86,16,128]{2,1,0:T(8,128)(2,1)S(1)} %slice.29), channel_id=1, source_target_pairs={{0,16},{1,17},{2,18},{3,19},{4,20},{5,21},{6,22},{7,23},{8,24},{9,... | collective-permute-start | bytes 1056776 | tf_op jit(solution)/shard_map/ppermute | solution.py:108
  120.4 11.0 %collective-permute-start.25 = (bf16[172,16,128]{2,1,0:T(8,128)(2,1)S(1)}, bf16[172,16,128]{2,1,0:T(8,128)(2,1)}, u32[]{:S(2)}, u32[]{:S(2)}) collective-permute-start(bf16[172,16,128]{2,1,0:T(8,128)(2,1)S(1)} %shard_map.96.rest_0_), channel_id=1, source_target_pairs={{0,8},{1,9},{2,10},{3,11},{4,12},{5,13},{6,14},{7,15},{8,0},{9,1},... | collective-permute-start | bytes 2113544 | tf_op jit(solution)/shard_map/ppermute | solution.py:108
  120.4 11.0 %collective-permute-start.26 = (bf16[172,16,128]{2,1,0:T(8,128)(2,1)S(1)}, bf16[172,16,128]{2,1,0:T(8,128)(2,1)}, u32[]{:S(2)}, u32[]{:S(2)}) collective-permute-start(bf16[172,16,128]{2,1,0:T(8,128)(2,1)S(1)} %shard_map.94.refs_1_.rest_1_), channel_id=1, source_target_pairs={{0,8},{1,9},{2,10},{3,11},{4,12},{5,13},{6,14},{7,15},{8,0},{9,1},... | collective-permute-start | bytes 2113544 | tf_op jit(solution)/shard_map/ppermute | solution.py:108
  120.9 10.5 %collective-permute-start.27 = (bf16[172,16,128]{2,1,0:T(8,128)(2,1)S(1)}, bf16[172,16,128]{2,1,0:T(8,128)(2,1)}, u32[]{:S(2)}, u32[]{:S(2)}) collective-permute-start(bf16[172,16,128]{2,1,0:T(8,128)(2,1)S(1)} %shard_map.95.refs_2_.rest_2_), channel_id=1, source_target_pairs={{0,8},{1,9},{2,10},{3,11},{4,12},{5,13},{6,14},{7,15},{8,0},{9,1},... | collective-permute-start | bytes 2113544 | tf_op jit(solution)/shard_map/ppermute | solution.py:108
  129.0 2.4 %collective-permute-start.28 = (bf16[86,16,128]{2,1,0:T(8,128)(2,1)}, bf16[86,16,128]{2,1,0:T(8,128)(2,1)}, u32[]{:S(2)}, u32[]{:S(2)}) collective-permute-start(bf16[86,16,128]{2,1,0:T(8,128)(2,1)} %collective-permute-done.23.rest_3_), channel_id=1, source_target_pairs={{0,8},{1,9},{2,10},{3,11},{4,12},{5,13},{6,14},{7,15},{8,0},{9,1},... | collective-permute-start | bytes 1056776 | tf_op jit(solution)/shard_map/ppermute | solution.py:108
  129.0 2.4 %collective-permute-start.29 = (bf16[86,16,128]{2,1,0:T(8,128)(2,1)S(1)}, bf16[86,16,128]{2,1,0:T(8,128)(2,1)}, u32[]{:S(2)}, u32[]{:S(2)}) collective-permute-start(bf16[86,16,128]{2,1,0:T(8,128)(2,1)S(1)} %collective-permute-done.24.rest_4_), channel_id=1, source_target_pairs={{0,8},{1,9},{2,10},{3,11},{4,12},{5,13},{6,14},{7,15},{8,0},{9,1},... | collective-permute-start | bytes 1056776 | tf_op jit(solution)/shard_map/ppermute | solution.py:108
  131.5 23.8 %copy-start.1 = (bf16[172,16,128]{2,1,0:T(8,128)(2,1)S(1)}, bf16[172,16,128]{2,1,0:T(8,128)(2,1)}, u32[]{:S(2)}) copy-start(bf16[172,16,128]{2,1,0:T(8,128)(2,1)} %copy-done) | copy-start | bytes 2113540
  131.5 23.8 %copy-start.7 = (bf16[4,64,1152]{2,1,0:T(8,128)(2,1)S(1)}, bf16[4,64,1152]{2,1,0:T(8,128)(2,1)}, u32[]{:S(2)}) copy-start(bf16[4,64,1152]{2,1,0:T(8,128)(2,1)} %copy-done.6) | copy-start | bytes 1769476
  131.5 23.7 %copy-start.11 = (bf16[172,16,128]{2,1,0:T(8,128)(2,1)S(1)}, bf16[172,16,128]{2,1,0:T(8,128)(2,1)}, u32[]{:S(2)}) copy-start(bf16[172,16,128]{2,1,0:T(8,128)(2,1)} %copy-done.10) | copy-start | bytes 2113540
  131.5 23.7 %copy-start.15 = (bf16[86,16,128]{2,1,0:T(8,128)(2,1)S(1)}, bf16[86,16,128]{2,1,0:T(8,128)(2,1)}, u32[]{:S(2)}) copy-start(bf16[86,16,128]{2,1,0:T(8,128)(2,1)} %copy-done.14) | copy-start | bytes 1056772
  131.6 23.7 %copy-start.21 = (bf16[86,16,128]{2,1,0:T(8,128)(2,1)S(1)}, bf16[86,16,128]{2,1,0:T(8,128)(2,1)}, u32[]{:S(2)}) copy-start(bf16[86,16,128]{2,1,0:T(8,128)(2,1)} %copy-done.20) | copy-start | bytes 1056772
  131.6 23.7 %copy-start.23 = (bf16[86,16,128]{2,1,0:T(8,128)(2,1)S(1)}, bf16[86,16,128]{2,1,0:T(8,128)(2,1)}, u32[]{:S(2)}) copy-start(bf16[86,16,128]{2,1,0:T(8,128)(2,1)} %copy-done.22) | copy-start | bytes 1056772
  131.6 23.7 %copy-start.29 = (f32[8,128,128]{2,1,0:T(8,128)S(1)}, f32[8,128,128]{2,1,0:T(8,128)}, u32[]{:S(2)}) copy-start(f32[8,128,128]{2,1,0:T(8,128)} %get-tuple-element.27.rest_2_) | copy-start | bytes 1572868
  131.6 23.7 %copy-start.32 = (bf16[128,1792]{1,0:T(8,128)(2,1)S(1)}, bf16[128,1792]{1,0:T(8,128)(2,1)}, u32[]{:S(2)}) copy-start(bf16[128,1792]{1,0:T(8,128)(2,1)} %get-tuple-element.26.rest_1_) | copy-start | bytes 1376260
  131.6 23.7 %copy-start.36 = (bf16[128,576]{1,0:T(8,128)(2,1)S(1)}, bf16[128,576]{1,0:T(8,128)(2,1)}, u32[]{:S(2)}) copy-start(bf16[128,576]{1,0:T(8,128)(2,1)} %get-tuple-element.28.rest_3_) | copy-start | bytes 442372
  155.3 14.1 %copy-start.3 = (bf16[172,16,128]{2,1,0:T(8,128)(2,1)S(1)}, bf16[172,16,128]{2,1,0:T(8,128)(2,1)}, u32[]{:S(2)}) copy-start(bf16[172,16,128]{2,1,0:T(8,128)(2,1)} %copy-done.2) | copy-start | bytes 2113540
  163.2 1.9 %collective-permute-start.30 = (bf16[32,1280]{1,0:T(8,128)(2,1)S(1)}, bf16[32,1280]{1,0:T(8,128)(2,1)S(1)}, u32[]{:S(2)}, u32[]{:S(2)}) collective-permute-start(bf16[32,1280]{1,0:T(8,128)(2,1)S(1)} %get-tuple-element.30), channel_id=1, source_target_pairs={{0,8},{1,9},{2,10},{3,11},{4,12},{5,13},{6,14},{7,15},{8,0},{9,1},... | collective-permute-start | bytes 245768 | tf_op jit(solution)/shard_map/ppermute | solution.py:108
  163.3 5.3 %collective-permute-start.31 = (bf16[32,1280]{1,0:T(8,128)(2,1)S(1)}, bf16[32,1280]{1,0:T(8,128)(2,1)S(1)}, u32[]{:S(2)}, u32[]{:S(2)}) collective-permute-start(bf16[32,1280]{1,0:T(8,128)(2,1)S(1)} %get-tuple-element.31), channel_id=1, source_target_pairs={{0,16},{1,17},{2,18},{3,19},{4,20},{5,21},{6,22},{7,23},{8,24},{9,... | collective-permute-start | bytes 245768 | tf_op jit(solution)/shard_map/ppermute | solution.py:108
  164.6 4.9 %collective-permute-start.32 = (bf16[32,1280]{1,0:T(8,128)(2,1)S(1)}, bf16[32,1280]{1,0:T(8,128)(2,1)S(1)}, u32[]{:S(2)}, u32[]{:S(2)}) collective-permute-start(bf16[32,1280]{1,0:T(8,128)(2,1)S(1)} %get-tuple-element.32), channel_id=1, source_target_pairs={{0,24},{1,25},{2,26},{3,27},{4,28},{5,29},{6,30},{7,31},{8,16},{9,... | collective-permute-start | bytes 245768 | tf_op jit(solution)/shard_map/ppermute | solution.py:108
  (27 other events, 229.8 us)

commit v6 on v5

--- a/solution.py
+++ b/solution.py
@@ -495,7 +495,7 @@
     base = dict(T=T, D=D, heads=heads, hd=hd, tiles=tiles, og=og, square=False, pairs=0, vmem=60,
                 w_tiles=(shard // ROWS, 0), o_tiles=(og, shard // ROWS * tiles))
     weights = []
-    fast = n_ha == 4 and n_wa % 4 == 0 and shard % ROWS == 0 and w_out.shape[1] == hd
+    fast = n_ha == 4 and n_wa % 4 == 0 and n_wa & (n_wa - 1) == 0 and shard % ROWS == 0 and w_out.shape[1] == hd
     if fast:
         routes = Routes(n_ha, n_wa)
         ha, wa = lax.axis_index("ha"), lax.axis_index("wa")
@@ -522,14 +522,18 @@
         own, later = own_quarters(ha.astype(jnp.int32)[None], w_qkv, w_out, quarter)
         line = routes.line(own)
         later = hand_on(later, line)
-        far = [routes.send(later, wa_bits=2 * k) for k in range(1, n_z)]
+        got, bit = {0: later}, n_z // 2
+        while bit:
+            got.update({k ^ bit: routes.send(got[k], wa_bits=2 * bit) for k in list(got)})
+            bit //= 2
+        far = [got[k] for k in range(1, n_z)]
         lines = []
 
         def stack_later(*squares):
             lines.extend(stacked(slots, [later] + far, 2, squares))
             return lines
 
-        weights = [over_square(routes, line, [home, teacher] + biases, stack_later)]
+        weights = [over_square(routes, line, [home, teacher] + biases + far[:1], stack_later)]
 
         def gather(which, before, there):
             line = hand_on(lines[which], *weights[which][3:5])

time: 179 us -> 173 us (0.966)
  waiting for transfers between devices: 55.4 us -> 49.3 us
    ppermute x33, waiting for transfers between devices: 55.3 us -> 49 us  [send(): return lax.ppermute(value, AXES, pairs)]
  transfers between devices with their start and end apart: 35 -> 35, of which waited for: 15 -> 16; matrix products, arithmetic and copies ran while one was open for 3% -> 3% of each run, Pallas kernels for 9% -> 9%
where the time goes in v6:
time: 173 us
  waiting for transfers between devices  49.3 us (28%)
  Pallas kernels  45.8 us (26%)
  blocking collectives  35.8 us (21%)
  starting transfers between devices  32.6 us (19%)
  local copies, waits for them, and re-layouts  7.6 us (4%)
    ppermute x33, waiting for transfers between devices, send(): return lax.ppermute(value, AXES, pairs)  49 us
    pallas_call x5, Pallas kernels, call(): pl.pallas_call(functools.partial(kernel, plan), out_shape=list(outs) + li...  41 us
    ppermute x33, starting transfers between devices, send(): return lax.ppermute(value, AXES, pairs)  24.6 us
    all_gather x1, blocking collectives, line(): lax.all_gather(value, AXES, axis=0, tiled=True, axis_index_groups=groups)  20.7 us
    all_to_all x1, blocking collectives, swap(): return lax.all_to_all(value, axis, split_axis=0, concat_axis=0, tiled=True)  15.1 us
    all_to_all x2, starting transfers between devices, swap(): return lax.all_to_all(value, axis, split_axis=0, concat_axis=0, tiled=True)  8.02 us
    slice x6, local copies, waits for them, and re-layouts, over_square(): low, high = (routes.y(over_x[:half]), routes.x(over_y[half:]))  3.49 us
  transfers between devices with their start and end apart: 35, of which 16 were waited for; matrix products, arithmetic and copies ran while one was open for 3% of the time, Pallas kernels for 9%

profile of v6, /device:TPU:0, one launch (start us, length us, event | category | flops | bytes accessed | tf_op | source)
XLA Modules:
  0.0 172.8 jit_solution(15101687621100280155)
XLA Ops:
  0.6 3.4 %shard_map.77 = (bf16[43,16,128]{2,1,0:T(8,128)(2,1)}, bf16[86,16,128]{2,1,0:T(8,128)(2,1)}) custom-call(s32[1]{0:T(128)} %bitcast.8.part_ref, bf16[3,144,1728]{2,1,0:T(8,128)(2,1)} %q_ref.1, bf16[3,72,1152]{2,1,0:T(8,128)(2,1)} %o_ref.1), custom_call_target="tpu_custom_call" | custom-call | tf_op jit(solution)/shard_map/pallas_call | solution.py:83
  4.1 20.7 %all_gather.3.refs_1_.refs_0_ = bf16[172,16,128]{2,1,0:T(8,128)(2,1)S(1)} all-gather(bf16[43,16,128]{2,1,0:T(8,128)(2,1)} %get-tuple-element.20), channel_id=1, replica_groups={{0,2,4,6},{1,3,5,7},{8,10,12,14},{9,11,13,15},{16,18,20,22},{17,19,21,2..., dimensions={0}, use_global_device_ids=true | all-gather | bytes 880640 | tf_op jit(solution)/shard_map/all_gather | solution.py:125
  24.8 0.9 collective-permute-start.4
  25.7 1.9 %collective-permute-start.1 = (bf16[86,16,128]{2,1,0:T(8,128)(2,1)}, bf16[86,16,128]{2,1,0:T(8,128)(2,1)S(1)}, u32[]{:S(2)}, u32[]{:S(2)}) collective-permute-start(bf16[86,16,128]{2,1,0:T(8,128)(2,1)} %shard_map.78.refs_1_), channel_id=1, source_target_pairs={{0,2},{1,3},{2,0},{3,1},{4,6},{5,7},{6,4},{7,5},{8,10},{9,11},{10,... | collective-permute-start | bytes 1056776 | tf_op jit(solution)/shard_map/ppermute | solution.py:108
  27.6 1.5 collective-permute-start.2
  29.1 1.5 collective-permute-start
  30.9 1.2 reshape_transpose.7.refs_2_.cot_ref
  32.3 8.6 %collective-permute-done.1.refs_6_.refs_2_ = bf16[86,16,128]{2,1,0:T(8,128)(2,1)S(1)} collective-permute-done((bf16[86,16,128]{2,1,0:T(8,128)(2,1)}, bf16[86,16,128]{2,1,0:T(8,128)(2,1)S(1)}, u32[]{:S(2)}, u32[]{:S(2)}) %collective-permute-start.1) | collective-permute-done | bytes 352288 | tf_op jit(solution)/shard_map/ppermute | solution.py:108
  41.3 1.2 collective-permute-start.5
  42.6 0.8 slice.25
  43.4 1.5 collective-permute-start.6
  44.9 0.8 slice.24
  45.6 1.5 collective-permute-start.3
  47.2 5.1 %collective-permute-done.5.refs_4_ = bf16[86,16,128]{2,1,0:T(8,128)(2,1)} collective-permute-done((bf16[86,16,128]{2,1,0:T(8,128)(2,1)}, bf16[86,16,128]{2,1,0:T(8,128)(2,1)}, u32[]{:S(2)}, u32[]{:S(2)}) %collective-permute-start.5) | collective-permute-done | bytes 352288 | tf_op jit(solution)/shard_map/ppermute | solution.py:108
  52.3 1.0 copy-done.21
  53.3 1.3 shard_map.82
  55.3 0.7 collective-permute-done.3.refs_0_
  56.0 1.1 collective-permute-start.13
  57.0 1.5 collective-permute-start.12
  59.2 1.4 collective-permute-done.10.rest_8_.rest_15_
  60.6 7.2 %shard_map.85 = (bf16[256,1152]{1,0:T(8,128)(2,1)}, bf16[128,1792]{1,0:T(8,128)(2,1)}, f32[8,128,128]{2,1,0:T(8,128)}, bf16[128,576]{1,0:T(8,128)(2,1)}) custom-call(s32[12]{0:T(128)} %stack.66.place_ref, f32[3,8]{1,0:T(4,128)} %gates_ref.9, bf16[128,1152]{1,0:T(8,128)(2,1)} %copy-done.12, f32[3,1152]{1,0:T(4,128)} %gain_ref.9, f32[128,128]{1,0:T(8,128)} %copy-done.29, ...), custom_call_target="tpu_custom_call" | custom-call | flops 679477248 | bytes 12582912 | tf_op jit(solution)/shard_map/pallas_call | solution.py:448
  67.8 3.5 %all-to-all-start = ((bf16[4,64,1152]{2,1,0:T(8,128)(2,1)}), bf16[4,64,1152]{2,1,0:T(8,128)(2,1)S(1)}, u32[]{:S(2)}, u32[]{:S(2)}) async-start(bf16[4,64,1152]{2,1,0:T(8,128)(2,1)} %bitcast.30), calls=%async_computation | async-start | bytes 1179648 | tf_op jit(solution)/shard_map/all_to_all | solution.py:490
  71.3 2.6 %collective-permute-done.13.refs_0_ = bf16[172,16,128]{2,1,0:T(8,128)(2,1)} collective-permute-done((bf16[172,16,128]{2,1,0:T(8,128)(2,1)S(1)}, bf16[172,16,128]{2,1,0:T(8,128)(2,1)}, u32[]{:S(2)}, u32[]{:S(2)}) %collective-permute-start.13) | collective-permute-done | bytes 704544 | tf_op jit(solution)/shard_map/ppermute | solution.py:108
  73.8 1.1 copy-done.17
  74.9 1.1 slice.26
  76.0 1.8 %collective-permute-start.14 = (bf16[86,16,128]{2,1,0:T(8,128)(2,1)S(1)}, bf16[86,16,128]{2,1,0:T(8,128)(2,1)S(1)}, u32[]{:S(2)}, u32[]{:S(2)}) collective-permute-start(bf16[86,16,128]{2,1,0:T(8,128)(2,1)S(1)} %slice.26), channel_id=1, source_target_pairs={{0,1},{1,0},{2,3},{3,2},{4,5},{5,4},{6,7},{7,6},{8,9},{9,8},{10,11... | collective-permute-start | bytes 1056776 | tf_op jit(solution)/shard_map/ppermute | solution.py:108
  77.8 0.8 slice.27
  78.6 1.7 collective-permute-start.15
  81.2 4.2 %collective-permute-done.14.refs_0_ = bf16[86,16,128]{2,1,0:T(8,128)(2,1)S(1)} collective-permute-done((bf16[86,16,128]{2,1,0:T(8,128)(2,1)S(1)}, bf16[86,16,128]{2,1,0:T(8,128)(2,1)S(1)}, u32[]{:S(2)}, u32[]{:S(2)}) %collective-permute-start.14) | collective-permute-done | bytes 352288 | tf_op jit(solution)/shard_map/ppermute | solution.py:108
  85.4 3.0 %collective-permute-done.15.refs_0_ = bf16[86,16,128]{2,1,0:T(8,128)(2,1)} collective-permute-done((bf16[86,16,128]{2,1,0:T(8,128)(2,1)}, bf16[86,16,128]{2,1,0:T(8,128)(2,1)}, u32[]{:S(2)}, u32[]{:S(2)}) %collective-permute-start.15) | collective-permute-done | bytes 352288 | tf_op jit(solution)/shard_map/ppermute | solution.py:108
  88.5 1.3 collective-permute-start.22
  90.3 0.8 collective-permute-start.21
  91.1 7.5 %shard_map.92 = (bf16[256,1152]{1,0:T(8,128)(2,1)}, bf16[128,1792]{1,0:T(8,128)(2,1)}, f32[8,128,128]{2,1,0:T(8,128)}, bf16[128,576]{1,0:T(8,128)(2,1)}) custom-call(s32[12]{0:T(128)} %stack.66.place_ref, f32[3,8]{1,0:T(4,128)} %gates_ref.9, bf16[256,1152]{1,0:T(8,128)(2,1)} %bitcast.26, f32[3,1152]{1,0:T(4,128)} %gain_ref.9, f32[128,128]{1,0:T(8,128)} %copy-done.28, ...), custom_call_target="tpu_custom_call" | custom-call | flops 679477248 | bytes 12582912 | tf_op jit(solution)/shard_map/pallas_call | solution.py:448
  98.6 4.5 %all-to-all-start.1 = ((bf16[8,32,1152]{2,1,0:T(8,128)(2,1)}), bf16[8,32,1152]{2,1,0:T(8,128)(2,1)S(1)}, u32[]{:S(2)}, u32[]{:S(2)}) async-start(bf16[8,32,1152]{2,1,0:T(8,128)(2,1)} %bitcast.29), calls=%async_computation.1 | async-start | bytes 1179648 | tf_op jit(solution)/shard_map/all_to_all | solution.py:490
  103.1 3.6 %collective-permute-done.22.refs_0_ = bf16[172,16,128]{2,1,0:T(8,128)(2,1)S(1)} collective-permute-done((bf16[172,16,128]{2,1,0:T(8,128)(2,1)S(1)}, bf16[172,16,128]{2,1,0:T(8,128)(2,1)S(1)}, u32[]{:S(2)}, u32[]{:S(2)}) %collective-permute-start.22) | collective-permute-done | bytes 704544 | tf_op jit(solution)/shard_map/ppermute | solution.py:108
  106.8 0.8 collective-permute-start.23
  107.6 4.3 %collective-permute-done.21.refs_0_ = bf16[172,16,128]{2,1,0:T(8,128)(2,1)S(1)} collective-permute-done((bf16[172,16,128]{2,1,0:T(8,128)(2,1)S(1)}, bf16[172,16,128]{2,1,0:T(8,128)(2,1)S(1)}, u32[]{:S(2)}, u32[]{:S(2)}) %collective-permute-start.21) | collective-permute-done | bytes 704544 | tf_op jit(solution)/shard_map/ppermute | solution.py:108
  111.9 1.3 collective-permute-start.24
  113.8 8.3 %collective-permute-done.23.rest_3_ = bf16[86,16,128]{2,1,0:T(8,128)(2,1)} collective-permute-done((bf16[86,16,128]{2,1,0:T(8,128)(2,1)S(1)}, bf16[86,16,128]{2,1,0:T(8,128)(2,1)}, u32[]{:S(2)}, u32[]{:S(2)}) %collective-permute-start.23) | collective-permute-done | bytes 352288 | tf_op jit(solution)/shard_map/ppermute | solution.py:108
  122.6 1.9 %collective-permute-done.28.rest_8_ = bf16[86,16,128]{2,1,0:T(8,128)(2,1)} collective-permute-done((bf16[86,16,128]{2,1,0:T(8,128)(2,1)}, bf16[86,16,128]{2,1,0:T(8,128)(2,1)}, u32[]{:S(2)}, u32[]{:S(2)}) %collective-permute-start.28) | collective-permute-done | bytes 352288 | tf_op jit(solution)/shard_map/ppermute | solution.py:108
  124.7 9.5 %shard_map.97 = bf16[128,1280]{1,0:T(8,128)(2,1)S(1)} custom-call(s32[12]{0:T(128)S(1)} %copy-done.38, f32[3,8]{1,0:T(4,128)S(1)} %copy-done.37, bf16[256,1152]{1,0:T(8,128)(2,1)S(1)} %bitcast.31, f32[3,1152]{1,0:T(4,128)S(1)} %copy-done.32, f32[128,128]{1,0:T(8,128)S(1)} %copy-done.27, bf16[172,16,128]{2,1,0:T(8,128)(2,1)S(1)} %shard_map.96.rest_0_, ...), custom_call_target="tpu_custom_call" | custom-call | flops 1358954496 | bytes 12582912 | tf_op jit(solution)/shard_map/pallas_call | solution.py:448
  134.2 15.1 %all_to_all.33 = bf16[8,16,1280]{2,1,0:T(8,128)(2,1)S(1)} all-to-all(bf16[8,16,1280]{2,1,0:T(8,128)(2,1)S(1)} %bitcast.33), channel_id=1, replica_groups=mesh['ha'=4,'wa'=8] {'wa'}, dimensions={0} | all-to-all | bytes 655360 | tf_op jit(solution)/shard_map/all_to_all | solution.py:490
  149.4 7.8 %shard_map.98 = (bf16[32,1280]{1,0:T(8,128)(2,1)S(1)}, bf16[32,1280]{1,0:T(8,128)(2,1)S(1)}, bf16[32,1280]{1,0:T(8,128)(2,1)S(1)}, bf16[32,1280]{1,0:T(8,128)(2,1)S(1)}) custom-call(s32[12]{0:T(128)S(1)} %copy-done.38, f32[3,8]{1,0:T(4,128)S(1)} %copy-done.37, bf16[256,1152]{1,0:T(8,128)(2,1)S(1)} %bitcast.28, f32[3,1152]{1,0:T(4,128)S(1)} %copy-done.32, ...), custom_call_target="tpu_custom_call" | custom-call | flops 679477248 | bytes 12582912 | tf_op jit(solution)/shard_map/pallas_call | solution.py:448
  157.3 1.3 collective-permute-start.31
  158.6 0.6 collective-permute-start.32
  159.2 3.4 %collective-permute-done.31.rest_2_ = bf16[32,1280]{1,0:T(8,128)(2,1)S(1)} collective-permute-done((bf16[32,1280]{1,0:T(8,128)(2,1)S(1)}, bf16[32,1280]{1,0:T(8,128)(2,1)S(1)}, u32[]{:S(2)}, u32[]{:S(2)}) %collective-permute-start.31) | collective-permute-done | bytes 81952 | tf_op jit(solution)/shard_map/ppermute | solution.py:108
  162.6 0.8 collective-permute-done.32.rest_3_
  163.5 9.0 %shard_map.99 = (bf16[64,2,1152]{2,1,0:T(2,128)(2,1)}, bf16[3,64,2,8]{3,2,1,0:T(2,128)(2,1)}) custom-call(s32[12]{0:T(128)S(1)} %copy-done.38, f32[3,8]{1,0:T(4,128)S(1)} %copy-done.37, bf16[128,1152]{1,0:T(8,128)(2,1)S(1)} %copy-done.13, f32[3,1152]{1,0:T(4,128)S(1)} %copy-done.32, bf16[32,1280]{1,0:T(8,128)(2,1)S(1)} %get-tuple-element.29.rest_0_, ...), custom_call_target="tpu_custom_call" | custom-call | flops 679477248 | bytes 12582912 | tf_op jit(solution)/shard_map/pallas_call | solution.py:448
  (142 shorter events, 4.8 us)
Async XLA Ops:
  4.1 26.7 %copy-start.39 = (bf16[1,8,8,2,1152]{4,3,2,1,0:T(2,128)(2,1)S(1)}, bf16[1,8,8,2,1152]{4,3,2,1,0:T(2,128)(2,1)}, u32[]{:S(2)}) copy-start(bf16[1,8,8,2,1152]{4,3,2,1,0:T(2,128)(2,1)} %param.6) | copy-start | bytes 884740
  24.8 16.5 %collective-permute-start.4 = (bf16[86,16,128]{2,1,0:T(8,128)(2,1)}, bf16[86,16,128]{2,1,0:T(8,128)(2,1)}, u32[]{:S(2)}, u32[]{:S(2)}) collective-permute-start(bf16[86,16,128]{2,1,0:T(8,128)(2,1)} %shard_map.78.refs_1_), channel_id=1, source_target_pairs={{0,4},{1,5},{2,6},{3,7},{4,0},{5,1},{6,2},{7,3},{8,12},{9,13},{10,... | collective-permute-start | bytes 1056776 | tf_op jit(solution)/shard_map/ppermute | solution.py:108
  25.7 15.2 %collective-permute-start.1 = (bf16[86,16,128]{2,1,0:T(8,128)(2,1)}, bf16[86,16,128]{2,1,0:T(8,128)(2,1)S(1)}, u32[]{:S(2)}, u32[]{:S(2)}) collective-permute-start(bf16[86,16,128]{2,1,0:T(8,128)(2,1)} %shard_map.78.refs_1_), channel_id=1, source_target_pairs={{0,2},{1,3},{2,0},{3,1},{4,6},{5,7},{6,4},{7,5},{8,10},{9,11},{10,... | collective-permute-start | bytes 1056776 | tf_op jit(solution)/shard_map/ppermute | solution.py:108
  27.6 13.7 %collective-permute-start.2 = (bf16[172,16,128]{2,1,0:T(8,128)(2,1)S(1)}, bf16[172,16,128]{2,1,0:T(8,128)(2,1)S(1)}, u32[]{:S(2)}, u32[]{:S(2)}) collective-permute-start(bf16[172,16,128]{2,1,0:T(8,128)(2,1)S(1)} %all_gather.3.refs_1_.refs_0_), channel_id=1, source_target_pairs={{0,16},{1,17},{2,18},{3,19},{4,20},{5,21},{6,22},{7,23},{8,24},{9,... | collective-permute-start | bytes 2113544 | tf_op jit(solution)/shard_map/ppermute | solution.py:108
  29.1 13.4 %collective-permute-start = (bf16[172,16,128]{2,1,0:T(8,128)(2,1)S(1)}, bf16[172,16,128]{2,1,0:T(8,128)(2,1)S(1)}, u32[]{:S(2)}, u32[]{:S(2)}) collective-permute-start(bf16[172,16,128]{2,1,0:T(8,128)(2,1)S(1)} %all_gather.3.refs_1_.refs_0_), channel_id=1, source_target_pairs={{0,1},{1,0},{2,3},{3,2},{4,5},{5,4},{6,7},{7,6},{8,9},{9,8},{10,11... | collective-permute-start | bytes 2113544 | tf_op jit(solution)/shard_map/ppermute | solution.py:108
  41.3 15.7 %collective-permute-start.9 = (bf16[172,16,128]{2,1,0:T(8,128)(2,1)S(1)}, bf16[172,16,128]{2,1,0:T(8,128)(2,1)}, u32[]{:S(2)}, u32[]{:S(2)}) collective-permute-start(bf16[172,16,128]{2,1,0:T(8,128)(2,1)S(1)} %shard_map.80.refs_2_.refs_6_.rest_2_.rest_9_), channel_id=1, source_target_pairs={{0,8},{1,9},{2,10},{3,11},{4,12},{5,13},{6,14},{7,15},{8,0},{9,1},... | collective-permute-start | bytes 2113544 | tf_op jit(solution)/shard_map/ppermute | solution.py:108
  41.3 11.0 %collective-permute-start.5 = (bf16[86,16,128]{2,1,0:T(8,128)(2,1)}, bf16[86,16,128]{2,1,0:T(8,128)(2,1)}, u32[]{:S(2)}, u32[]{:S(2)}) collective-permute-start(bf16[86,16,128]{2,1,0:T(8,128)(2,1)} %collective-permute-done.4.refs_3_), channel_id=1, source_target_pairs={{0,2},{1,3},{2,0},{3,1},{4,6},{5,7},{6,4},{7,5},{8,10},{9,11},{10,... | collective-permute-start | bytes 1056776 | tf_op jit(solution)/shard_map/ppermute | solution.py:108
  43.4 11.2 %collective-permute-start.6 = (bf16[86,16,128]{2,1,0:T(8,128)(2,1)}, bf16[86,16,128]{2,1,0:T(8,128)(2,1)}, u32[]{:S(2)}, u32[]{:S(2)}) collective-permute-start(bf16[86,16,128]{2,1,0:T(8,128)(2,1)} %slice.25), channel_id=1, source_target_pairs={{0,16},{1,17},{2,18},{3,19},{4,20},{5,21},{6,22},{7,23},{8,24},{9,... | collective-permute-start | bytes 1056776 | tf_op jit(solution)/shard_map/ppermute | solution.py:108
  45.6 10.3 %collective-permute-start.3 = (bf16[86,16,128]{2,1,0:T(8,128)(2,1)}, bf16[86,16,128]{2,1,0:T(8,128)(2,1)}, u32[]{:S(2)}, u32[]{:S(2)}) collective-permute-start(bf16[86,16,128]{2,1,0:T(8,128)(2,1)} %slice.24), channel_id=1, source_target_pairs={{0,1},{1,0},{2,3},{3,2},{4,5},{5,4},{6,7},{7,6},{8,9},{9,8},{10,11... | collective-permute-start | bytes 1056776 | tf_op jit(solution)/shard_map/ppermute | solution.py:108
  54.6 4.0 %collective-permute-start.11 = (bf16[86,16,128]{2,1,0:T(8,128)(2,1)}, bf16[86,16,128]{2,1,0:T(8,128)(2,1)}, u32[]{:S(2)}, u32[]{:S(2)}) collective-permute-start(bf16[86,16,128]{2,1,0:T(8,128)(2,1)} %shard_map.84.rest_4_.refs_2_.rest_11_), channel_id=1, source_target_pairs={{0,8},{1,9},{2,10},{3,11},{4,12},{5,13},{6,14},{7,15},{8,0},{9,1},... | collective-permute-start | bytes 1056776 | tf_op jit(solution)/shard_map/ppermute | solution.py:108
  54.7 5.9 %collective-permute-start.7 = (bf16[172,16,128]{2,1,0:T(8,128)(2,1)S(1)}, bf16[172,16,128]{2,1,0:T(8,128)(2,1)}, u32[]{:S(2)}, u32[]{:S(2)}) collective-permute-start(bf16[172,16,128]{2,1,0:T(8,128)(2,1)S(1)} %shard_map.81.rest_0_.rest_7_), channel_id=1, source_target_pairs={{0,8},{1,9},{2,10},{3,11},{4,12},{5,13},{6,14},{7,15},{8,0},{9,1},... | collective-permute-start | bytes 2113544 | tf_op jit(solution)/shard_map/ppermute | solution.py:108
  55.2 5.4 %collective-permute-start.8 = (bf16[172,16,128]{2,1,0:T(8,128)(2,1)S(1)}, bf16[172,16,128]{2,1,0:T(8,128)(2,1)}, u32[]{:S(2)}, u32[]{:S(2)}) collective-permute-start(bf16[172,16,128]{2,1,0:T(8,128)(2,1)S(1)} %shard_map.79.refs_1_.refs_5_.rest_1_.rest_8_), channel_id=1, source_target_pairs={{0,8},{1,9},{2,10},{3,11},{4,12},{5,13},{6,14},{7,15},{8,0},{9,1},... | collective-permute-start | bytes 2113544 | tf_op jit(solution)/shard_map/ppermute | solution.py:108
  56.0 17.9 %collective-permute-start.13 = (bf16[172,16,128]{2,1,0:T(8,128)(2,1)S(1)}, bf16[172,16,128]{2,1,0:T(8,128)(2,1)}, u32[]{:S(2)}, u32[]{:S(2)}) collective-permute-start(bf16[172,16,128]{2,1,0:T(8,128)(2,1)S(1)} %shard_map.86.refs_0_), channel_id=1, source_target_pairs={{0,16},{1,17},{2,18},{3,19},{4,20},{5,21},{6,22},{7,23},{8,24},{9,... | collective-permute-start | bytes 2113544 | tf_op jit(solution)/shard_map/ppermute | solution.py:108
  57.0 20.7 %collective-permute-start.12 = (bf16[172,16,128]{2,1,0:T(8,128)(2,1)S(1)}, bf16[172,16,128]{2,1,0:T(8,128)(2,1)S(1)}, u32[]{:S(2)}, u32[]{:S(2)}) collective-permute-start(bf16[172,16,128]{2,1,0:T(8,128)(2,1)S(1)} %shard_map.86.refs_0_), channel_id=1, source_target_pairs={{0,1},{1,0},{2,3},{3,2},{4,5},{5,4},{6,7},{7,6},{8,9},{9,8},{10,11... | collective-permute-start | bytes 2113544 | tf_op jit(solution)/shard_map/ppermute | solution.py:108
  58.6 2.0 %collective-permute-start.10 = (bf16[86,16,128]{2,1,0:T(8,128)(2,1)}, bf16[86,16,128]{2,1,0:T(8,128)(2,1)}, u32[]{:S(2)}, u32[]{:S(2)}) collective-permute-start(bf16[86,16,128]{2,1,0:T(8,128)(2,1)} %shard_map.83.rest_3_.refs_1_.rest_10_), channel_id=1, source_target_pairs={{0,8},{1,9},{2,10},{3,11},{4,12},{5,13},{6,14},{7,15},{8,0},{9,1},... | collective-permute-start | bytes 1056776 | tf_op jit(solution)/shard_map/ppermute | solution.py:108
  67.8 13.4 %all-to-all-start = ((bf16[4,64,1152]{2,1,0:T(8,128)(2,1)}), bf16[4,64,1152]{2,1,0:T(8,128)(2,1)S(1)}, u32[]{:S(2)}, u32[]{:S(2)}) async-start(bf16[4,64,1152]{2,1,0:T(8,128)(2,1)} %bitcast.30), calls=%async_computation | async-start | bytes 1179648 | tf_op jit(solution)/shard_map/all_to_all | solution.py:490
  76.0 9.4 %collective-permute-start.14 = (bf16[86,16,128]{2,1,0:T(8,128)(2,1)S(1)}, bf16[86,16,128]{2,1,0:T(8,128)(2,1)S(1)}, u32[]{:S(2)}, u32[]{:S(2)}) collective-permute-start(bf16[86,16,128]{2,1,0:T(8,128)(2,1)S(1)} %slice.26), channel_id=1, source_target_pairs={{0,1},{1,0},{2,3},{3,2},{4,5},{5,4},{6,7},{7,6},{8,9},{9,8},{10,11... | collective-permute-start | bytes 1056776 | tf_op jit(solution)/shard_map/ppermute | solution.py:108
  78.6 9.9 %collective-permute-start.15 = (bf16[86,16,128]{2,1,0:T(8,128)(2,1)}, bf16[86,16,128]{2,1,0:T(8,128)(2,1)}, u32[]{:S(2)}, u32[]{:S(2)}) collective-permute-start(bf16[86,16,128]{2,1,0:T(8,128)(2,1)} %slice.27), channel_id=1, source_target_pairs={{0,16},{1,17},{2,18},{3,19},{4,20},{5,21},{6,22},{7,23},{8,24},{9,... | collective-permute-start | bytes 1056776 | tf_op jit(solution)/shard_map/ppermute | solution.py:108
  80.3 10.8 %collective-permute-start.16 = (bf16[172,16,128]{2,1,0:T(8,128)(2,1)S(1)}, bf16[172,16,128]{2,1,0:T(8,128)(2,1)}, u32[]{:S(2)}, u32[]{:S(2)}) collective-permute-start(bf16[172,16,128]{2,1,0:T(8,128)(2,1)S(1)} %shard_map.89.rest_0_.rest_4_), channel_id=1, source_target_pairs={{0,8},{1,9},{2,10},{3,11},{4,12},{5,13},{6,14},{7,15},{8,0},{9,1},... | collective-permute-start | bytes 2113544 | tf_op jit(solution)/shard_map/ppermute | solution.py:108
  80.3 10.8 %collective-permute-start.17 = (bf16[172,16,128]{2,1,0:T(8,128)(2,1)S(1)}, bf16[172,16,128]{2,1,0:T(8,128)(2,1)}, u32[]{:S(2)}, u32[]{:S(2)}) collective-permute-start(bf16[172,16,128]{2,1,0:T(8,128)(2,1)S(1)} %shard_map.87.refs_1_.rest_1_.rest_5_), channel_id=1, source_target_pairs={{0,8},{1,9},{2,10},{3,11},{4,12},{5,13},{6,14},{7,15},{8,0},{9,1},... | collective-permute-start | bytes 2113544 | tf_op jit(solution)/shard_map/ppermute | solution.py:108
  80.8 10.3 %collective-permute-start.18 = (bf16[172,16,128]{2,1,0:T(8,128)(2,1)}, bf16[172,16,128]{2,1,0:T(8,128)(2,1)}, u32[]{:S(2)}, u32[]{:S(2)}) collective-permute-start(bf16[172,16,128]{2,1,0:T(8,128)(2,1)} %shard_map.88.refs_2_.rest_2_.rest_6_), channel_id=1, source_target_pairs={{0,8},{1,9},{2,10},{3,11},{4,12},{5,13},{6,14},{7,15},{8,0},{9,1},... | collective-permute-start | bytes 2113544 | tf_op jit(solution)/shard_map/ppermute | solution.py:108
  85.4 3.1 %collective-permute-start.19 = (bf16[86,16,128]{2,1,0:T(8,128)(2,1)S(1)}, bf16[86,16,128]{2,1,0:T(8,128)(2,1)S(1)}, u32[]{:S(2)}, u32[]{:S(2)}) collective-permute-start(bf16[86,16,128]{2,1,0:T(8,128)(2,1)S(1)} %shard_map.90.rest_3_.refs_1_.rest_7_), channel_id=1, source_target_pairs={{0,8},{1,9},{2,10},{3,11},{4,12},{5,13},{6,14},{7,15},{8,0},{9,1},... | collective-permute-start | bytes 1056776 | tf_op jit(solution)/shard_map/ppermute | solution.py:108
  88.4 1.9 %collective-permute-start.20 = (bf16[86,16,128]{2,1,0:T(8,128)(2,1)}, bf16[86,16,128]{2,1,0:T(8,128)(2,1)S(1)}, u32[]{:S(2)}, u32[]{:S(2)}) collective-permute-start(bf16[86,16,128]{2,1,0:T(8,128)(2,1)} %shard_map.91.rest_4_.refs_2_.rest_8_), channel_id=1, source_target_pairs={{0,8},{1,9},{2,10},{3,11},{4,12},{5,13},{6,14},{7,15},{8,0},{9,1},... | collective-permute-start | bytes 1056776 | tf_op jit(solution)/shard_map/ppermute | solution.py:108
  88.5 18.2 %collective-permute-start.22 = (bf16[172,16,128]{2,1,0:T(8,128)(2,1)S(1)}, bf16[172,16,128]{2,1,0:T(8,128)(2,1)S(1)}, u32[]{:S(2)}, u32[]{:S(2)}) collective-permute-start(bf16[172,16,128]{2,1,0:T(8,128)(2,1)S(1)} %shard_map.93.refs_0_), channel_id=1, source_target_pairs={{0,16},{1,17},{2,18},{3,19},{4,20},{5,21},{6,22},{7,23},{8,24},{9,... | collective-permute-start | bytes 2113544 | tf_op jit(solution)/shard_map/ppermute | solution.py:108
  90.3 21.6 %collective-permute-start.21 = (bf16[172,16,128]{2,1,0:T(8,128)(2,1)S(1)}, bf16[172,16,128]{2,1,0:T(8,128)(2,1)S(1)}, u32[]{:S(2)}, u32[]{:S(2)}) collective-permute-start(bf16[172,16,128]{2,1,0:T(8,128)(2,1)S(1)} %shard_map.93.refs_0_), channel_id=1, source_target_pairs={{0,1},{1,0},{2,3},{3,2},{4,5},{5,4},{6,7},{7,6},{8,9},{9,8},{10,11... | collective-permute-start | bytes 2113544 | tf_op jit(solution)/shard_map/ppermute | solution.py:108
  98.6 24.0 %all-to-all-start.1 = ((bf16[8,32,1152]{2,1,0:T(8,128)(2,1)}), bf16[8,32,1152]{2,1,0:T(8,128)(2,1)S(1)}, u32[]{:S(2)}, u32[]{:S(2)}) async-start(bf16[8,32,1152]{2,1,0:T(8,128)(2,1)} %bitcast.29), calls=%async_computation.1 | async-start | bytes 1179648 | tf_op jit(solution)/shard_map/all_to_all | solution.py:490
  106.8 15.3 %collective-permute-start.23 = (bf16[86,16,128]{2,1,0:T(8,128)(2,1)S(1)}, bf16[86,16,128]{2,1,0:T(8,128)(2,1)}, u32[]{:S(2)}, u32[]{:S(2)}) collective-permute-start(bf16[86,16,128]{2,1,0:T(8,128)(2,1)S(1)} %slice.28), channel_id=1, source_target_pairs={{0,1},{1,0},{2,3},{3,2},{4,5},{5,4},{6,7},{7,6},{8,9},{9,8},{10,11... | collective-permute-start | bytes 1056776 | tf_op jit(solution)/shard_map/ppermute | solution.py:108
  111.9 10.2 %collective-permute-start.24 = (bf16[86,16,128]{2,1,0:T(8,128)(2,1)S(1)}, bf16[86,16,128]{2,1,0:T(8,128)(2,1)S(1)}, u32[]{:S(2)}, u32[]{:S(2)}) collective-permute-start(bf16[86,16,128]{2,1,0:T(8,128)(2,1)S(1)} %slice.29), channel_id=1, source_target_pairs={{0,16},{1,17},{2,18},{3,19},{4,20},{5,21},{6,22},{7,23},{8,24},{9,... | collective-permute-start | bytes 1056776 | tf_op jit(solution)/shard_map/ppermute | solution.py:108
  113.3 11.3 %collective-permute-start.25 = (bf16[172,16,128]{2,1,0:T(8,128)(2,1)S(1)}, bf16[172,16,128]{2,1,0:T(8,128)(2,1)}, u32[]{:S(2)}, u32[]{:S(2)}) collective-permute-start(bf16[172,16,128]{2,1,0:T(8,128)(2,1)S(1)} %shard_map.96.rest_0_), channel_id=1, source_target_pairs={{0,8},{1,9},{2,10},{3,11},{4,12},{5,13},{6,14},{7,15},{8,0},{9,1},... | collective-permute-start | bytes 2113544 | tf_op jit(solution)/shard_map/ppermute | solution.py:108
  113.3 11.3 %collective-permute-start.26 = (bf16[172,16,128]{2,1,0:T(8,128)(2,1)S(1)}, bf16[172,16,128]{2,1,0:T(8,128)(2,1)}, u32[]{:S(2)}, u32[]{:S(2)}) collective-permute-start(bf16[172,16,128]{2,1,0:T(8,128)(2,1)S(1)} %shard_map.94.refs_1_.rest_1_), channel_id=1, source_target_pairs={{0,8},{1,9},{2,10},{3,11},{4,12},{5,13},{6,14},{7,15},{8,0},{9,1},... | collective-permute-start | bytes 2113544 | tf_op jit(solution)/shard_map/ppermute | solution.py:108
  113.8 10.8 %collective-permute-start.27 = (bf16[172,16,128]{2,1,0:T(8,128)(2,1)S(1)}, bf16[172,16,128]{2,1,0:T(8,128)(2,1)}, u32[]{:S(2)}, u32[]{:S(2)}) collective-permute-start(bf16[172,16,128]{2,1,0:T(8,128)(2,1)S(1)} %shard_map.95.refs_2_.rest_2_), channel_id=1, source_target_pairs={{0,8},{1,9},{2,10},{3,11},{4,12},{5,13},{6,14},{7,15},{8,0},{9,1},... | collective-permute-start | bytes 2113544 | tf_op jit(solution)/shard_map/ppermute | solution.py:108
  122.1 2.4 %collective-permute-start.28 = (bf16[86,16,128]{2,1,0:T(8,128)(2,1)}, bf16[86,16,128]{2,1,0:T(8,128)(2,1)}, u32[]{:S(2)}, u32[]{:S(2)}) collective-permute-start(bf16[86,16,128]{2,1,0:T(8,128)(2,1)} %collective-permute-done.23.rest_3_), channel_id=1, source_target_pairs={{0,8},{1,9},{2,10},{3,11},{4,12},{5,13},{6,14},{7,15},{8,0},{9,1},... | collective-permute-start | bytes 1056776 | tf_op jit(solution)/shard_map/ppermute | solution.py:108
  122.1 2.4 %collective-permute-start.29 = (bf16[86,16,128]{2,1,0:T(8,128)(2,1)S(1)}, bf16[86,16,128]{2,1,0:T(8,128)(2,1)}, u32[]{:S(2)}, u32[]{:S(2)}) collective-permute-start(bf16[86,16,128]{2,1,0:T(8,128)(2,1)S(1)} %collective-permute-done.24.rest_4_), channel_id=1, source_target_pairs={{0,8},{1,9},{2,10},{3,11},{4,12},{5,13},{6,14},{7,15},{8,0},{9,1},... | collective-permute-start | bytes 1056776 | tf_op jit(solution)/shard_map/ppermute | solution.py:108
  124.6 24.7 %copy-start.1 = (bf16[172,16,128]{2,1,0:T(8,128)(2,1)S(1)}, bf16[172,16,128]{2,1,0:T(8,128)(2,1)}, u32[]{:S(2)}) copy-start(bf16[172,16,128]{2,1,0:T(8,128)(2,1)} %copy-done) | copy-start | bytes 2113540
  124.6 24.7 %copy-start.7 = (bf16[4,64,1152]{2,1,0:T(8,128)(2,1)S(1)}, bf16[4,64,1152]{2,1,0:T(8,128)(2,1)}, u32[]{:S(2)}) copy-start(bf16[4,64,1152]{2,1,0:T(8,128)(2,1)} %copy-done.6) | copy-start | bytes 1769476
  124.6 24.7 %copy-start.11 = (bf16[172,16,128]{2,1,0:T(8,128)(2,1)S(1)}, bf16[172,16,128]{2,1,0:T(8,128)(2,1)}, u32[]{:S(2)}) copy-start(bf16[172,16,128]{2,1,0:T(8,128)(2,1)} %copy-done.10) | copy-start | bytes 2113540
  124.6 24.7 %copy-start.15 = (bf16[86,16,128]{2,1,0:T(8,128)(2,1)S(1)}, bf16[86,16,128]{2,1,0:T(8,128)(2,1)}, u32[]{:S(2)}) copy-start(bf16[86,16,128]{2,1,0:T(8,128)(2,1)} %copy-done.14) | copy-start | bytes 1056772
  124.7 24.7 %copy-start.23 = (bf16[86,16,128]{2,1,0:T(8,128)(2,1)S(1)}, bf16[86,16,128]{2,1,0:T(8,128)(2,1)}, u32[]{:S(2)}) copy-start(bf16[86,16,128]{2,1,0:T(8,128)(2,1)} %copy-done.22) | copy-start | bytes 1056772
  124.7 24.7 %copy-start.25 = (bf16[86,16,128]{2,1,0:T(8,128)(2,1)S(1)}, bf16[86,16,128]{2,1,0:T(8,128)(2,1)}, u32[]{:S(2)}) copy-start(bf16[86,16,128]{2,1,0:T(8,128)(2,1)} %copy-done.24) | copy-start | bytes 1056772
  124.7 24.7 %copy-start.31 = (f32[8,128,128]{2,1,0:T(8,128)S(1)}, f32[8,128,128]{2,1,0:T(8,128)}, u32[]{:S(2)}) copy-start(f32[8,128,128]{2,1,0:T(8,128)} %get-tuple-element.27.rest_2_) | copy-start | bytes 1572868
  124.7 24.7 %copy-start.34 = (bf16[128,1792]{1,0:T(8,128)(2,1)S(1)}, bf16[128,1792]{1,0:T(8,128)(2,1)}, u32[]{:S(2)}) copy-start(bf16[128,1792]{1,0:T(8,128)(2,1)} %get-tuple-element.26.rest_1_) | copy-start | bytes 1376260
  124.7 24.7 %copy-start.36 = (bf16[128,576]{1,0:T(8,128)(2,1)S(1)}, bf16[128,576]{1,0:T(8,128)(2,1)}, u32[]{:S(2)}) copy-start(bf16[128,576]{1,0:T(8,128)(2,1)} %get-tuple-element.28.rest_3_) | copy-start | bytes 442372
  149.4 14.1 %copy-start.3 = (bf16[172,16,128]{2,1,0:T(8,128)(2,1)S(1)}, bf16[172,16,128]{2,1,0:T(8,128)(2,1)}, u32[]{:S(2)}) copy-start(bf16[172,16,128]{2,1,0:T(8,128)(2,1)} %copy-done.2) | copy-start | bytes 2113540
  149.4 14.1 %copy-start.5 = (bf16[172,16,128]{2,1,0:T(8,128)(2,1)S(1)}, bf16[172,16,128]{2,1,0:T(8,128)(2,1)}, u32[]{:S(2)}) copy-start(bf16[172,16,128]{2,1,0:T(8,128)(2,1)} %copy-done.4) | copy-start | bytes 2113540
  149.4 14.1 %copy-start.9 = (bf16[172,16,128]{2,1,0:T(8,128)(2,1)S(1)}, bf16[172,16,128]{2,1,0:T(8,128)(2,1)}, u32[]{:S(2)}) copy-start(bf16[172,16,128]{2,1,0:T(8,128)(2,1)} %copy-done.8) | copy-start | bytes 2113540
  157.3 1.9 %collective-permute-start.30 = (bf16[32,1280]{1,0:T(8,128)(2,1)S(1)}, bf16[32,1280]{1,0:T(8,128)(2,1)S(1)}, u32[]{:S(2)}, u32[]{:S(2)}) collective-permute-start(bf16[32,1280]{1,0:T(8,128)(2,1)S(1)} %get-tuple-element.30), channel_id=1, source_target_pairs={{0,8},{1,9},{2,10},{3,11},{4,12},{5,13},{6,14},{7,15},{8,0},{9,1},... | collective-permute-start | bytes 245768 | tf_op jit(solution)/shard_map/ppermute | solution.py:108
  157.3 5.3 %collective-permute-start.31 = (bf16[32,1280]{1,0:T(8,128)(2,1)S(1)}, bf16[32,1280]{1,0:T(8,128)(2,1)S(1)}, u32[]{:S(2)}, u32[]{:S(2)}) collective-permute-start(bf16[32,1280]{1,0:T(8,128)(2,1)S(1)} %get-tuple-element.31), channel_id=1, source_target_pairs={{0,16},{1,17},{2,18},{3,19},{4,20},{5,21},{6,22},{7,23},{8,24},{9,... | collective-permute-start | bytes 245768 | tf_op jit(solution)/shard_map/ppermute | solution.py:108
  158.6 4.9 %collective-permute-start.32 = (bf16[32,1280]{1,0:T(8,128)(2,1)S(1)}, bf16[32,1280]{1,0:T(8,128)(2,1)S(1)}, u32[]{:S(2)}, u32[]{:S(2)}) collective-permute-start(bf16[32,1280]{1,0:T(8,128)(2,1)S(1)} %get-tuple-element.32), channel_id=1, source_target_pairs={{0,24},{1,25},{2,26},{3,27},{4,28},{5,29},{6,30},{7,31},{8,16},{9,... | collective-permute-start | bytes 245768 | tf_op jit(solution)/shard_map/ppermute | solution.py:108
  (27 other events, 229.4 us)

commit v7 on v6

--- a/solution.py
+++ b/solution.py
@@ -125,11 +125,27 @@
         return lax.all_gather(value, AXES, axis=0, tiled=True, axis_index_groups=groups)
 
 
+def half_of(value, second):
+    n = value.shape[0] // 2
+    first = n if second else 0
+
+    def kernel(source, out):
+        out[...] = source[first : first + n]
+
+    vmem = pl.BlockSpec(memory_space=pltpu.VMEM)
+    return pl.pallas_call(
+        kernel,
+        out_shape=jax.ShapeDtypeStruct((n,) + value.shape[1:], value.dtype),
+        in_specs=[vmem],
+        out_specs=vmem,
+        compiler_params=pltpu.CompilerParams(vmem_limit_bytes=3 * 2**20),
+    )(value)
+
+
 def over_square(routes, line, before, between):
-    half = line.shape[0] // 2
     over_y, over_x = routes.y(line), routes.x(line)
     over_y, over_x = hand_on(over_y, *before), hand_on(over_x, *before)
-    low, high = routes.y(over_x[:half]), routes.x(over_y[half:])
+    low, high = routes.y(half_of(over_x, False)), routes.x(half_of(over_y, True))
     there = between(over_y, over_x)
     if there:
         low, high = hand_on(low, *there), hand_on(high, *there)

time: 173 us -> 174 us (level)
  Pallas kernels: 45.8 us -> 49.3 us
  local copies, waits for them, and re-layouts: 7.6 us -> 4.11 us
    pallas_call x0 -> x6, Pallas kernels: none -> 3.58 us  [half_of(): pl.pallas_call(kernel, out_shape=jax.ShapeDtypeStruct((n,) + value.shape[...]
    slice x6 -> x0, local copies, waits for them, and re-layouts: 3.49 us -> none  [over_square(): low, high = (routes.y(over_x[:half]), routes.x(over_y[half:]))]
  transfers between devices with their start and end apart: 35 -> 35, of which waited for: 16 -> 16; matrix products, arithmetic and copies ran while one was open for 3% -> 1% of each run, Pallas kernels for 9% -> 11%
where the time goes in v7:
time: 174 us; the launch traced here: 173 us
  Pallas kernels  49.3 us (28%)
  waiting for transfers between devices  49 us (28%)
  blocking collectives  35.9 us (21%)
  starting transfers between devices  32.8 us (19%)
  local copies, waits for them, and re-layouts  4.11 us (2%)
    ppermute x33, waiting for transfers between devices, send(): return lax.ppermute(value, AXES, pairs)  48.7 us
    pallas_call x5, Pallas kernels, call(): pl.pallas_call(functools.partial(kernel, plan), out_shape=list(outs) + li...  41 us
    ppermute x33, starting transfers between devices, send(): return lax.ppermute(value, AXES, pairs)  25.2 us
    all_gather x1, blocking collectives, line(): lax.all_gather(value, AXES, axis=0, tiled=True, axis_index_groups=groups)  20.7 us
    all_to_all x1, blocking collectives, swap(): return lax.all_to_all(value, axis, split_axis=0, concat_axis=0, tiled=True)  15.2 us
    all_to_all x2, starting transfers between devices, swap(): return lax.all_to_all(value, axis, split_axis=0, concat_axis=0, tiled=True)  7.56 us
    pallas_call x6, Pallas kernels, half_of(): pl.pallas_call(kernel, out_shape=jax.ShapeDtypeStruct((n,) + value.shape[...  3.58 us
  transfers between devices with their start and end apart: 35, of which 16 were waited for; matrix products, arithmetic and copies ran while one was open for 1% of the time, Pallas kernels for 11%

profile of v7, /device:TPU:0, one launch (start us, length us, event | category | flops | bytes accessed | tf_op | source)
XLA Modules:
  0.0 172.9 jit_solution(10445726674455233812)
XLA Ops:
  0.6 3.4 %shard_map.77 = (bf16[43,16,128]{2,1,0:T(8,128)(2,1)}, bf16[86,16,128]{2,1,0:T(8,128)(2,1)}) custom-call(s32[1]{0:T(128)} %bitcast.8.part_ref, bf16[3,144,1728]{2,1,0:T(8,128)(2,1)} %q_ref.1, bf16[3,72,1152]{2,1,0:T(8,128)(2,1)} %o_ref.1), custom_call_target="tpu_custom_call" | custom-call | tf_op jit(solution)/shard_map/pallas_call | solution.py:83
  4.1 20.7 %all_gather.3.refs_1_.refs_0_ = bf16[172,16,128]{2,1,0:T(8,128)(2,1)S(1)} all-gather(bf16[43,16,128]{2,1,0:T(8,128)(2,1)} %get-tuple-element.20), channel_id=1, replica_groups={{0,2,4,6},{1,3,5,7},{8,10,12,14},{9,11,13,15},{16,18,20,22},{17,19,21,2..., dimensions={0}, use_global_device_ids=true | all-gather | bytes 880640 | tf_op jit(solution)/shard_map/all_gather | solution.py:125
  24.8 0.9 collective-permute-start.4
  25.7 1.9 %collective-permute-start.1 = (bf16[86,16,128]{2,1,0:T(8,128)(2,1)}, bf16[86,16,128]{2,1,0:T(8,128)(2,1)S(1)}, u32[]{:S(2)}, u32[]{:S(2)}) collective-permute-start(bf16[86,16,128]{2,1,0:T(8,128)(2,1)} %shard_map.78.refs_1_), channel_id=1, source_target_pairs={{0,2},{1,3},{2,0},{3,1},{4,6},{5,7},{6,4},{7,5},{8,10},{9,11},{10,... | collective-permute-start | bytes 1056776 | tf_op jit(solution)/shard_map/ppermute | solution.py:108
  27.6 1.5 collective-permute-start.2
  29.1 1.5 collective-permute-start
  30.9 1.2 reshape_transpose.7.refs_2_.cot_ref
  32.3 8.6 %collective-permute-done.1.refs_6_.refs_2_ = bf16[86,16,128]{2,1,0:T(8,128)(2,1)S(1)} collective-permute-done((bf16[86,16,128]{2,1,0:T(8,128)(2,1)}, bf16[86,16,128]{2,1,0:T(8,128)(2,1)S(1)}, u32[]{:S(2)}, u32[]{:S(2)}) %collective-permute-start.1) | collective-permute-done | bytes 352288 | tf_op jit(solution)/shard_map/ppermute | solution.py:108
  41.3 1.2 collective-permute-start.5
  42.6 0.8 shard_map.85
  43.4 1.5 collective-permute-start.6
  44.9 0.8 shard_map.82
  45.6 1.5 collective-permute-start.3
  47.2 5.1 %collective-permute-done.5.refs_4_ = bf16[86,16,128]{2,1,0:T(8,128)(2,1)} collective-permute-done((bf16[86,16,128]{2,1,0:T(8,128)(2,1)}, bf16[86,16,128]{2,1,0:T(8,128)(2,1)}, u32[]{:S(2)}, u32[]{:S(2)}) %collective-permute-start.5) | collective-permute-done | bytes 352288 | tf_op jit(solution)/shard_map/ppermute | solution.py:108
  52.3 1.0 copy-done.21
  53.3 1.3 shard_map.83
  55.3 0.7 collective-permute-done.3.refs_0_
  56.0 1.1 collective-permute-start.13
  57.0 1.5 collective-permute-start.12
  58.6 0.6 stack.66.place_ref
  59.2 1.4 collective-permute-done.10.rest_8_.rest_15_
  60.6 7.2 %shard_map.87 = (bf16[256,1152]{1,0:T(8,128)(2,1)}, bf16[128,1792]{1,0:T(8,128)(2,1)}, f32[8,128,128]{2,1,0:T(8,128)}, bf16[128,576]{1,0:T(8,128)(2,1)}) custom-call(s32[12]{0:T(128)} %stack.66.place_ref, f32[3,8]{1,0:T(4,128)} %gates_ref.9, bf16[128,1152]{1,0:T(8,128)(2,1)} %copy-done.12, f32[3,1152]{1,0:T(4,128)} %gain_ref.9, f32[128,128]{1,0:T(8,128)} %copy-done.29, ...), custom_call_target="tpu_custom_call" | custom-call | flops 679477248 | bytes 12582912 | tf_op jit(solution)/shard_map/pallas_call | solution.py:464
  67.8 3.5 %all-to-all-start = ((bf16[4,64,1152]{2,1,0:T(8,128)(2,1)}), bf16[4,64,1152]{2,1,0:T(8,128)(2,1)S(1)}, u32[]{:S(2)}, u32[]{:S(2)}) async-start(bf16[4,64,1152]{2,1,0:T(8,128)(2,1)} %bitcast.30), calls=%async_computation | async-start | bytes 1179648 | tf_op jit(solution)/shard_map/all_to_all | solution.py:506
  71.3 2.6 %collective-permute-done.13.refs_0_ = bf16[172,16,128]{2,1,0:T(8,128)(2,1)} collective-permute-done((bf16[172,16,128]{2,1,0:T(8,128)(2,1)S(1)}, bf16[172,16,128]{2,1,0:T(8,128)(2,1)}, u32[]{:S(2)}, u32[]{:S(2)}) %collective-permute-start.13) | collective-permute-done | bytes 704544 | tf_op jit(solution)/shard_map/ppermute | solution.py:108
  73.8 1.1 copy-done.17
  74.9 1.9 %shard_map.92 = bf16[86,16,128]{2,1,0:T(8,128)(2,1)} custom-call(bf16[172,16,128]{2,1,0:T(8,128)(2,1)} %shard_map.90.refs_2_.source.rest_2_.rest_6_), custom_call_target="tpu_custom_call" | custom-call | tf_op jit(solution)/shard_map/pallas_call | solution.py:136
  76.8 1.7 collective-permute-start.14
  78.6 1.8 %collective-permute-start.15 = (bf16[86,16,128]{2,1,0:T(8,128)(2,1)S(1)}, bf16[86,16,128]{2,1,0:T(8,128)(2,1)}, u32[]{:S(2)}, u32[]{:S(2)}) collective-permute-start(bf16[86,16,128]{2,1,0:T(8,128)(2,1)S(1)} %shard_map.94), channel_id=1, source_target_pairs={{0,16},{1,17},{2,18},{3,19},{4,20},{5,21},{6,22},{7,23},{8,24},{9,... | collective-permute-start | bytes 1056776 | tf_op jit(solution)/shard_map/ppermute | solution.py:108
  81.3 5.1 %collective-permute-done.14.refs_0_ = bf16[86,16,128]{2,1,0:T(8,128)(2,1)S(1)} collective-permute-done((bf16[86,16,128]{2,1,0:T(8,128)(2,1)}, bf16[86,16,128]{2,1,0:T(8,128)(2,1)S(1)}, u32[]{:S(2)}, u32[]{:S(2)}) %collective-permute-start.14) | collective-permute-done | bytes 352288 | tf_op jit(solution)/shard_map/ppermute | solution.py:108
  86.4 2.0 %collective-permute-done.15.refs_0_ = bf16[86,16,128]{2,1,0:T(8,128)(2,1)} collective-permute-done((bf16[86,16,128]{2,1,0:T(8,128)(2,1)S(1)}, bf16[86,16,128]{2,1,0:T(8,128)(2,1)}, u32[]{:S(2)}, u32[]{:S(2)}) %collective-permute-start.15) | collective-permute-done | bytes 352288 | tf_op jit(solution)/shard_map/ppermute | solution.py:108
  88.5 1.5 collective-permute-start.22
  90.3 1.2 collective-permute-start.21
  91.6 7.5 %shard_map.96 = (bf16[256,1152]{1,0:T(8,128)(2,1)}, bf16[128,1792]{1,0:T(8,128)(2,1)}, f32[8,128,128]{2,1,0:T(8,128)}, bf16[128,576]{1,0:T(8,128)(2,1)}) custom-call(s32[12]{0:T(128)} %stack.66.place_ref, f32[3,8]{1,0:T(4,128)} %gates_ref.9, bf16[256,1152]{1,0:T(8,128)(2,1)} %bitcast.26, f32[3,1152]{1,0:T(4,128)} %gain_ref.9, f32[128,128]{1,0:T(8,128)} %copy-done.28, ...), custom_call_target="tpu_custom_call" | custom-call | flops 679477248 | bytes 12582912 | tf_op jit(solution)/shard_map/pallas_call | solution.py:464
  99.1 4.1 %all-to-all-start.1 = ((bf16[8,32,1152]{2,1,0:T(8,128)(2,1)}), bf16[8,32,1152]{2,1,0:T(8,128)(2,1)S(1)}, u32[]{:S(2)}, u32[]{:S(2)}) async-start(bf16[8,32,1152]{2,1,0:T(8,128)(2,1)} %bitcast.29), calls=%async_computation.1 | async-start | bytes 1179648 | tf_op jit(solution)/shard_map/all_to_all | solution.py:506
  103.1 3.6 %collective-permute-done.22.refs_0_ = bf16[172,16,128]{2,1,0:T(8,128)(2,1)S(1)} collective-permute-done((bf16[172,16,128]{2,1,0:T(8,128)(2,1)S(1)}, bf16[172,16,128]{2,1,0:T(8,128)(2,1)S(1)}, u32[]{:S(2)}, u32[]{:S(2)}) %collective-permute-start.22) | collective-permute-done | bytes 704544 | tf_op jit(solution)/shard_map/ppermute | solution.py:108
  106.8 1.0 collective-permute-start.23
  107.7 4.1 %collective-permute-done.21.refs_0_ = bf16[172,16,128]{2,1,0:T(8,128)(2,1)S(1)} collective-permute-done((bf16[172,16,128]{2,1,0:T(8,128)(2,1)S(1)}, bf16[172,16,128]{2,1,0:T(8,128)(2,1)S(1)}, u32[]{:S(2)}, u32[]{:S(2)}) %collective-permute-start.21) | collective-permute-done | bytes 704544 | tf_op jit(solution)/shard_map/ppermute | solution.py:108
  111.9 1.2 collective-permute-start.24
  113.6 8.5 %collective-permute-done.23.rest_3_ = bf16[86,16,128]{2,1,0:T(8,128)(2,1)} collective-permute-done((bf16[86,16,128]{2,1,0:T(8,128)(2,1)S(1)}, bf16[86,16,128]{2,1,0:T(8,128)(2,1)}, u32[]{:S(2)}, u32[]{:S(2)}) %collective-permute-start.23) | collective-permute-done | bytes 352288 | tf_op jit(solution)/shard_map/ppermute | solution.py:108
  122.6 1.9 %collective-permute-done.28.rest_8_ = bf16[86,16,128]{2,1,0:T(8,128)(2,1)} collective-permute-done((bf16[86,16,128]{2,1,0:T(8,128)(2,1)}, bf16[86,16,128]{2,1,0:T(8,128)(2,1)}, u32[]{:S(2)}, u32[]{:S(2)}) %collective-permute-start.28) | collective-permute-done | bytes 352288 | tf_op jit(solution)/shard_map/ppermute | solution.py:108
  124.7 9.5 %shard_map.103 = bf16[128,1280]{1,0:T(8,128)(2,1)S(1)} custom-call(s32[12]{0:T(128)S(1)} %copy-done.38, f32[3,8]{1,0:T(4,128)S(1)} %copy-done.37, bf16[256,1152]{1,0:T(8,128)(2,1)S(1)} %bitcast.31, f32[3,1152]{1,0:T(4,128)S(1)} %copy-done.32, f32[128,128]{1,0:T(8,128)S(1)} %copy-done.27, bf16[172,16,128]{2,1,0:T(8,128)(2,1)S(1)} %shard_map.100.rest_0_, ...), custom_call_target="tpu_custom_call" | custom-call | flops 1358954496 | bytes 12582912 | tf_op jit(solution)/shard_map/pallas_call | solution.py:464
  134.2 15.2 %all_to_all.33 = bf16[8,16,1280]{2,1,0:T(8,128)(2,1)S(1)} all-to-all(bf16[8,16,1280]{2,1,0:T(8,128)(2,1)S(1)} %bitcast.33), channel_id=1, replica_groups=mesh['ha'=4,'wa'=8] {'wa'}, dimensions={0} | all-to-all | bytes 655360 | tf_op jit(solution)/shard_map/all_to_all | solution.py:506
  149.6 7.8 %shard_map.104 = (bf16[32,1280]{1,0:T(8,128)(2,1)S(1)}, bf16[32,1280]{1,0:T(8,128)(2,1)S(1)}, bf16[32,1280]{1,0:T(8,128)(2,1)S(1)}, bf16[32,1280]{1,0:T(8,128)(2,1)S(1)}) custom-call(s32[12]{0:T(128)S(1)} %copy-done.38, f32[3,8]{1,0:T(4,128)S(1)} %copy-done.37, bf16[256,1152]{1,0:T(8,128)(2,1)S(1)} %bitcast.28, f32[3,1152]{1,0:T(4,128)S(1)} %copy-done.32, ...), custom_call_target="tpu_custom_call" | custom-call | flops 679477248 | bytes 12582912 | tf_op jit(solution)/shard_map/pallas_call | solution.py:464
  157.5 1.1 collective-permute-start.31
  158.6 0.8 collective-permute-start.32
  159.4 3.4 %collective-permute-done.31.rest_2_ = bf16[32,1280]{1,0:T(8,128)(2,1)S(1)} collective-permute-done((bf16[32,1280]{1,0:T(8,128)(2,1)S(1)}, bf16[32,1280]{1,0:T(8,128)(2,1)S(1)}, u32[]{:S(2)}, u32[]{:S(2)}) %collective-permute-start.31) | collective-permute-done | bytes 81952 | tf_op jit(solution)/shard_map/ppermute | solution.py:108
  162.8 0.8 collective-permute-done.32.rest_3_
  163.7 9.0 %shard_map.105 = (bf16[64,2,1152]{2,1,0:T(2,128)(2,1)}, bf16[3,64,2,8]{3,2,1,0:T(2,128)(2,1)}) custom-call(s32[12]{0:T(128)S(1)} %copy-done.38, f32[3,8]{1,0:T(4,128)S(1)} %copy-done.37, bf16[128,1152]{1,0:T(8,128)(2,1)S(1)} %copy-done.13, f32[3,1152]{1,0:T(4,128)S(1)} %copy-done.32, bf16[32,1280]{1,0:T(8,128)(2,1)S(1)} %get-tuple-element.29.rest_0_, ...), custom_call_target="tpu_custom_call" | custom-call | flops 679477248 | bytes 12582912 | tf_op jit(solution)/shard_map/pallas_call | solution.py:464
  (142 shorter events, 4.0 us)
Async XLA Ops:
  4.1 26.7 %copy-start.39 = (bf16[1,8,8,2,1152]{4,3,2,1,0:T(2,128)(2,1)S(1)}, bf16[1,8,8,2,1152]{4,3,2,1,0:T(2,128)(2,1)}, u32[]{:S(2)}) copy-start(bf16[1,8,8,2,1152]{4,3,2,1,0:T(2,128)(2,1)} %param.6) | copy-start | bytes 884740
  24.8 16.5 %collective-permute-start.4 = (bf16[86,16,128]{2,1,0:T(8,128)(2,1)}, bf16[86,16,128]{2,1,0:T(8,128)(2,1)}, u32[]{:S(2)}, u32[]{:S(2)}) collective-permute-start(bf16[86,16,128]{2,1,0:T(8,128)(2,1)} %shard_map.78.refs_1_), channel_id=1, source_target_pairs={{0,4},{1,5},{2,6},{3,7},{4,0},{5,1},{6,2},{7,3},{8,12},{9,13},{10,... | collective-permute-start | bytes 1056776 | tf_op jit(solution)/shard_map/ppermute | solution.py:108
  25.7 15.2 %collective-permute-start.1 = (bf16[86,16,128]{2,1,0:T(8,128)(2,1)}, bf16[86,16,128]{2,1,0:T(8,128)(2,1)S(1)}, u32[]{:S(2)}, u32[]{:S(2)}) collective-permute-start(bf16[86,16,128]{2,1,0:T(8,128)(2,1)} %shard_map.78.refs_1_), channel_id=1, source_target_pairs={{0,2},{1,3},{2,0},{3,1},{4,6},{5,7},{6,4},{7,5},{8,10},{9,11},{10,... | collective-permute-start | bytes 1056776 | tf_op jit(solution)/shard_map/ppermute | solution.py:108
  27.6 13.7 %collective-permute-start.2 = (bf16[172,16,128]{2,1,0:T(8,128)(2,1)S(1)}, bf16[172,16,128]{2,1,0:T(8,128)(2,1)S(1)}, u32[]{:S(2)}, u32[]{:S(2)}) collective-permute-start(bf16[172,16,128]{2,1,0:T(8,128)(2,1)S(1)} %all_gather.3.refs_1_.refs_0_), channel_id=1, source_target_pairs={{0,16},{1,17},{2,18},{3,19},{4,20},{5,21},{6,22},{7,23},{8,24},{9,... | collective-permute-start | bytes 2113544 | tf_op jit(solution)/shard_map/ppermute | solution.py:108
  29.1 13.4 %collective-permute-start = (bf16[172,16,128]{2,1,0:T(8,128)(2,1)S(1)}, bf16[172,16,128]{2,1,0:T(8,128)(2,1)S(1)}, u32[]{:S(2)}, u32[]{:S(2)}) collective-permute-start(bf16[172,16,128]{2,1,0:T(8,128)(2,1)S(1)} %all_gather.3.refs_1_.refs_0_), channel_id=1, source_target_pairs={{0,1},{1,0},{2,3},{3,2},{4,5},{5,4},{6,7},{7,6},{8,9},{9,8},{10,11... | collective-permute-start | bytes 2113544 | tf_op jit(solution)/shard_map/ppermute | solution.py:108
  41.3 15.7 %collective-permute-start.9 = (bf16[172,16,128]{2,1,0:T(8,128)(2,1)S(1)}, bf16[172,16,128]{2,1,0:T(8,128)(2,1)}, u32[]{:S(2)}, u32[]{:S(2)}) collective-permute-start(bf16[172,16,128]{2,1,0:T(8,128)(2,1)S(1)} %shard_map.80.refs_2_.source.refs_6_.rest_2_.rest_9_), channel_id=1, source_target_pairs={{0,8},{1,9},{2,10},{3,11},{4,12},{5,13},{6,14},{7,15},{8,0},{9,1},... | collective-permute-start | bytes 2113544 | tf_op jit(solution)/shard_map/ppermute | solution.py:108
  41.3 11.0 %collective-permute-start.5 = (bf16[86,16,128]{2,1,0:T(8,128)(2,1)}, bf16[86,16,128]{2,1,0:T(8,128)(2,1)}, u32[]{:S(2)}, u32[]{:S(2)}) collective-permute-start(bf16[86,16,128]{2,1,0:T(8,128)(2,1)} %collective-permute-done.4.refs_3_), channel_id=1, source_target_pairs={{0,2},{1,3},{2,0},{3,1},{4,6},{5,7},{6,4},{7,5},{8,10},{9,11},{10,... | collective-permute-start | bytes 1056776 | tf_op jit(solution)/shard_map/ppermute | solution.py:108
  43.4 11.2 %collective-permute-start.6 = (bf16[86,16,128]{2,1,0:T(8,128)(2,1)}, bf16[86,16,128]{2,1,0:T(8,128)(2,1)}, u32[]{:S(2)}, u32[]{:S(2)}) collective-permute-start(bf16[86,16,128]{2,1,0:T(8,128)(2,1)} %shard_map.85), channel_id=1, source_target_pairs={{0,16},{1,17},{2,18},{3,19},{4,20},{5,21},{6,22},{7,23},{8,24},{9,... | collective-permute-start | bytes 1056776 | tf_op jit(solution)/shard_map/ppermute | solution.py:108
  45.6 10.3 %collective-permute-start.3 = (bf16[86,16,128]{2,1,0:T(8,128)(2,1)}, bf16[86,16,128]{2,1,0:T(8,128)(2,1)}, u32[]{:S(2)}, u32[]{:S(2)}) collective-permute-start(bf16[86,16,128]{2,1,0:T(8,128)(2,1)} %shard_map.82), channel_id=1, source_target_pairs={{0,1},{1,0},{2,3},{3,2},{4,5},{5,4},{6,7},{7,6},{8,9},{9,8},{10,11... | collective-permute-start | bytes 1056776 | tf_op jit(solution)/shard_map/ppermute | solution.py:108
  54.6 4.0 %collective-permute-start.11 = (bf16[86,16,128]{2,1,0:T(8,128)(2,1)}, bf16[86,16,128]{2,1,0:T(8,128)(2,1)}, u32[]{:S(2)}, u32[]{:S(2)}) collective-permute-start(bf16[86,16,128]{2,1,0:T(8,128)(2,1)} %shard_map.86.rest_4_.refs_2_.rest_11_), channel_id=1, source_target_pairs={{0,8},{1,9},{2,10},{3,11},{4,12},{5,13},{6,14},{7,15},{8,0},{9,1},... | collective-permute-start | bytes 1056776 | tf_op jit(solution)/shard_map/ppermute | solution.py:108
  54.7 5.9 %collective-permute-start.7 = (bf16[172,16,128]{2,1,0:T(8,128)(2,1)S(1)}, bf16[172,16,128]{2,1,0:T(8,128)(2,1)}, u32[]{:S(2)}, u32[]{:S(2)}) collective-permute-start(bf16[172,16,128]{2,1,0:T(8,128)(2,1)S(1)} %shard_map.81.rest_0_.rest_7_), channel_id=1, source_target_pairs={{0,8},{1,9},{2,10},{3,11},{4,12},{5,13},{6,14},{7,15},{8,0},{9,1},... | collective-permute-start | bytes 2113544 | tf_op jit(solution)/shard_map/ppermute | solution.py:108
  55.2 5.4 %collective-permute-start.8 = (bf16[172,16,128]{2,1,0:T(8,128)(2,1)S(1)}, bf16[172,16,128]{2,1,0:T(8,128)(2,1)}, u32[]{:S(2)}, u32[]{:S(2)}) collective-permute-start(bf16[172,16,128]{2,1,0:T(8,128)(2,1)S(1)} %shard_map.79.refs_1_.refs_5_.source.rest_1_.rest_8_), channel_id=1, source_target_pairs={{0,8},{1,9},{2,10},{3,11},{4,12},{5,13},{6,14},{7,15},{8,0},{9,1},... | collective-permute-start | bytes 2113544 | tf_op jit(solution)/shard_map/ppermute | solution.py:108
  56.0 17.9 %collective-permute-start.13 = (bf16[172,16,128]{2,1,0:T(8,128)(2,1)S(1)}, bf16[172,16,128]{2,1,0:T(8,128)(2,1)}, u32[]{:S(2)}, u32[]{:S(2)}) collective-permute-start(bf16[172,16,128]{2,1,0:T(8,128)(2,1)S(1)} %shard_map.88.refs_0_), channel_id=1, source_target_pairs={{0,16},{1,17},{2,18},{3,19},{4,20},{5,21},{6,22},{7,23},{8,24},{9,... | collective-permute-start | bytes 2113544 | tf_op jit(solution)/shard_map/ppermute | solution.py:108
  57.0 21.5 %collective-permute-start.12 = (bf16[172,16,128]{2,1,0:T(8,128)(2,1)S(1)}, bf16[172,16,128]{2,1,0:T(8,128)(2,1)S(1)}, u32[]{:S(2)}, u32[]{:S(2)}) collective-permute-start(bf16[172,16,128]{2,1,0:T(8,128)(2,1)S(1)} %shard_map.88.refs_0_), channel_id=1, source_target_pairs={{0,1},{1,0},{2,3},{3,2},{4,5},{5,4},{6,7},{7,6},{8,9},{9,8},{10,11... | collective-permute-start | bytes 2113544 | tf_op jit(solution)/shard_map/ppermute | solution.py:108
  58.6 2.0 %collective-permute-start.10 = (bf16[86,16,128]{2,1,0:T(8,128)(2,1)}, bf16[86,16,128]{2,1,0:T(8,128)(2,1)}, u32[]{:S(2)}, u32[]{:S(2)}) collective-permute-start(bf16[86,16,128]{2,1,0:T(8,128)(2,1)} %shard_map.84.rest_3_.refs_1_.rest_10_), channel_id=1, source_target_pairs={{0,8},{1,9},{2,10},{3,11},{4,12},{5,13},{6,14},{7,15},{8,0},{9,1},... | collective-permute-start | bytes 1056776 | tf_op jit(solution)/shard_map/ppermute | solution.py:108
  67.8 13.5 %all-to-all-start = ((bf16[4,64,1152]{2,1,0:T(8,128)(2,1)}), bf16[4,64,1152]{2,1,0:T(8,128)(2,1)S(1)}, u32[]{:S(2)}, u32[]{:S(2)}) async-start(bf16[4,64,1152]{2,1,0:T(8,128)(2,1)} %bitcast.30), calls=%async_computation | async-start | bytes 1179648 | tf_op jit(solution)/shard_map/all_to_all | solution.py:506
  76.8 9.6 %collective-permute-start.14 = (bf16[86,16,128]{2,1,0:T(8,128)(2,1)}, bf16[86,16,128]{2,1,0:T(8,128)(2,1)S(1)}, u32[]{:S(2)}, u32[]{:S(2)}) collective-permute-start(bf16[86,16,128]{2,1,0:T(8,128)(2,1)} %shard_map.92), channel_id=1, source_target_pairs={{0,1},{1,0},{2,3},{3,2},{4,5},{5,4},{6,7},{7,6},{8,9},{9,8},{10,11... | collective-permute-start | bytes 1056776 | tf_op jit(solution)/shard_map/ppermute | solution.py:108
  78.6 9.8 %collective-permute-start.15 = (bf16[86,16,128]{2,1,0:T(8,128)(2,1)S(1)}, bf16[86,16,128]{2,1,0:T(8,128)(2,1)}, u32[]{:S(2)}, u32[]{:S(2)}) collective-permute-start(bf16[86,16,128]{2,1,0:T(8,128)(2,1)S(1)} %shard_map.94), channel_id=1, source_target_pairs={{0,16},{1,17},{2,18},{3,19},{4,20},{5,21},{6,22},{7,23},{8,24},{9,... | collective-permute-start | bytes 1056776 | tf_op jit(solution)/shard_map/ppermute | solution.py:108
  80.4 11.2 %collective-permute-start.16 = (bf16[172,16,128]{2,1,0:T(8,128)(2,1)S(1)}, bf16[172,16,128]{2,1,0:T(8,128)(2,1)}, u32[]{:S(2)}, u32[]{:S(2)}) collective-permute-start(bf16[172,16,128]{2,1,0:T(8,128)(2,1)S(1)} %shard_map.91.rest_0_.rest_4_), channel_id=1, source_target_pairs={{0,8},{1,9},{2,10},{3,11},{4,12},{5,13},{6,14},{7,15},{8,0},{9,1},... | collective-permute-start | bytes 2113544 | tf_op jit(solution)/shard_map/ppermute | solution.py:108
  80.4 11.2 %collective-permute-start.17 = (bf16[172,16,128]{2,1,0:T(8,128)(2,1)S(1)}, bf16[172,16,128]{2,1,0:T(8,128)(2,1)}, u32[]{:S(2)}, u32[]{:S(2)}) collective-permute-start(bf16[172,16,128]{2,1,0:T(8,128)(2,1)S(1)} %shard_map.89.refs_1_.source.rest_1_.rest_5_), channel_id=1, source_target_pairs={{0,8},{1,9},{2,10},{3,11},{4,12},{5,13},{6,14},{7,15},{8,0},{9,1},... | collective-permute-start | bytes 2113544 | tf_op jit(solution)/shard_map/ppermute | solution.py:108
  80.9 10.7 %collective-permute-start.18 = (bf16[172,16,128]{2,1,0:T(8,128)(2,1)}, bf16[172,16,128]{2,1,0:T(8,128)(2,1)}, u32[]{:S(2)}, u32[]{:S(2)}) collective-permute-start(bf16[172,16,128]{2,1,0:T(8,128)(2,1)} %shard_map.90.refs_2_.source.rest_2_.rest_6_), channel_id=1, source_target_pairs={{0,8},{1,9},{2,10},{3,11},{4,12},{5,13},{6,14},{7,15},{8,0},{9,1},... | collective-permute-start | bytes 2113544 | tf_op jit(solution)/shard_map/ppermute | solution.py:108
  86.4 2.1 %collective-permute-start.19 = (bf16[86,16,128]{2,1,0:T(8,128)(2,1)S(1)}, bf16[86,16,128]{2,1,0:T(8,128)(2,1)S(1)}, u32[]{:S(2)}, u32[]{:S(2)}) collective-permute-start(bf16[86,16,128]{2,1,0:T(8,128)(2,1)S(1)} %shard_map.93.rest_3_.refs_1_.rest_7_), channel_id=1, source_target_pairs={{0,8},{1,9},{2,10},{3,11},{4,12},{5,13},{6,14},{7,15},{8,0},{9,1},... | collective-permute-start | bytes 1056776 | tf_op jit(solution)/shard_map/ppermute | solution.py:108
  88.4 1.9 %collective-permute-start.20 = (bf16[86,16,128]{2,1,0:T(8,128)(2,1)}, bf16[86,16,128]{2,1,0:T(8,128)(2,1)S(1)}, u32[]{:S(2)}, u32[]{:S(2)}) collective-permute-start(bf16[86,16,128]{2,1,0:T(8,128)(2,1)} %shard_map.95.rest_4_.refs_2_.rest_8_), channel_id=1, source_target_pairs={{0,8},{1,9},{2,10},{3,11},{4,12},{5,13},{6,14},{7,15},{8,0},{9,1},... | collective-permute-start | bytes 1056776 | tf_op jit(solution)/shard_map/ppermute | solution.py:108
  88.5 18.2 %collective-permute-start.22 = (bf16[172,16,128]{2,1,0:T(8,128)(2,1)S(1)}, bf16[172,16,128]{2,1,0:T(8,128)(2,1)S(1)}, u32[]{:S(2)}, u32[]{:S(2)}) collective-permute-start(bf16[172,16,128]{2,1,0:T(8,128)(2,1)S(1)} %shard_map.97.refs_0_), channel_id=1, source_target_pairs={{0,16},{1,17},{2,18},{3,19},{4,20},{5,21},{6,22},{7,23},{8,24},{9,... | collective-permute-start | bytes 2113544 | tf_op jit(solution)/shard_map/ppermute | solution.py:108
  90.3 21.6 %collective-permute-start.21 = (bf16[172,16,128]{2,1,0:T(8,128)(2,1)S(1)}, bf16[172,16,128]{2,1,0:T(8,128)(2,1)S(1)}, u32[]{:S(2)}, u32[]{:S(2)}) collective-permute-start(bf16[172,16,128]{2,1,0:T(8,128)(2,1)S(1)} %shard_map.97.refs_0_), channel_id=1, source_target_pairs={{0,1},{1,0},{2,3},{3,2},{4,5},{5,4},{6,7},{7,6},{8,9},{9,8},{10,11... | collective-permute-start | bytes 2113544 | tf_op jit(solution)/shard_map/ppermute | solution.py:108
  99.1 23.6 %all-to-all-start.1 = ((bf16[8,32,1152]{2,1,0:T(8,128)(2,1)}), bf16[8,32,1152]{2,1,0:T(8,128)(2,1)S(1)}, u32[]{:S(2)}, u32[]{:S(2)}) async-start(bf16[8,32,1152]{2,1,0:T(8,128)(2,1)} %bitcast.29), calls=%async_computation.1 | async-start | bytes 1179648 | tf_op jit(solution)/shard_map/all_to_all | solution.py:506
  106.8 15.3 %collective-permute-start.23 = (bf16[86,16,128]{2,1,0:T(8,128)(2,1)S(1)}, bf16[86,16,128]{2,1,0:T(8,128)(2,1)}, u32[]{:S(2)}, u32[]{:S(2)}) collective-permute-start(bf16[86,16,128]{2,1,0:T(8,128)(2,1)S(1)} %shard_map.101), channel_id=1, source_target_pairs={{0,1},{1,0},{2,3},{3,2},{4,5},{5,4},{6,7},{7,6},{8,9},{9,8},{10,11... | collective-permute-start | bytes 1056776 | tf_op jit(solution)/shard_map/ppermute | solution.py:108
  111.9 10.2 %collective-permute-start.24 = (bf16[86,16,128]{2,1,0:T(8,128)(2,1)S(1)}, bf16[86,16,128]{2,1,0:T(8,128)(2,1)S(1)}, u32[]{:S(2)}, u32[]{:S(2)}) collective-permute-start(bf16[86,16,128]{2,1,0:T(8,128)(2,1)S(1)} %shard_map.102), channel_id=1, source_target_pairs={{0,16},{1,17},{2,18},{3,19},{4,20},{5,21},{6,22},{7,23},{8,24},{9,... | collective-permute-start | bytes 1056776 | tf_op jit(solution)/shard_map/ppermute | solution.py:108
  113.1 11.4 %collective-permute-start.25 = (bf16[172,16,128]{2,1,0:T(8,128)(2,1)S(1)}, bf16[172,16,128]{2,1,0:T(8,128)(2,1)}, u32[]{:S(2)}, u32[]{:S(2)}) collective-permute-start(bf16[172,16,128]{2,1,0:T(8,128)(2,1)S(1)} %shard_map.100.rest_0_), channel_id=1, source_target_pairs={{0,8},{1,9},{2,10},{3,11},{4,12},{5,13},{6,14},{7,15},{8,0},{9,1},... | collective-permute-start | bytes 2113544 | tf_op jit(solution)/shard_map/ppermute | solution.py:108
  113.1 11.4 %collective-permute-start.26 = (bf16[172,16,128]{2,1,0:T(8,128)(2,1)S(1)}, bf16[172,16,128]{2,1,0:T(8,128)(2,1)}, u32[]{:S(2)}, u32[]{:S(2)}) collective-permute-start(bf16[172,16,128]{2,1,0:T(8,128)(2,1)S(1)} %shard_map.98.refs_1_.source.rest_1_), channel_id=1, source_target_pairs={{0,8},{1,9},{2,10},{3,11},{4,12},{5,13},{6,14},{7,15},{8,0},{9,1},... | collective-permute-start | bytes 2113544 | tf_op jit(solution)/shard_map/ppermute | solution.py:108
  113.6 10.9 %collective-permute-start.27 = (bf16[172,16,128]{2,1,0:T(8,128)(2,1)S(1)}, bf16[172,16,128]{2,1,0:T(8,128)(2,1)}, u32[]{:S(2)}, u32[]{:S(2)}) collective-permute-start(bf16[172,16,128]{2,1,0:T(8,128)(2,1)S(1)} %shard_map.99.refs_2_.source.rest_2_), channel_id=1, source_target_pairs={{0,8},{1,9},{2,10},{3,11},{4,12},{5,13},{6,14},{7,15},{8,0},{9,1},... | collective-permute-start | bytes 2113544 | tf_op jit(solution)/shard_map/ppermute | solution.py:108
  122.1 2.4 %collective-permute-start.28 = (bf16[86,16,128]{2,1,0:T(8,128)(2,1)}, bf16[86,16,128]{2,1,0:T(8,128)(2,1)}, u32[]{:S(2)}, u32[]{:S(2)}) collective-permute-start(bf16[86,16,128]{2,1,0:T(8,128)(2,1)} %collective-permute-done.23.rest_3_), channel_id=1, source_target_pairs={{0,8},{1,9},{2,10},{3,11},{4,12},{5,13},{6,14},{7,15},{8,0},{9,1},... | collective-permute-start | bytes 1056776 | tf_op jit(solution)/shard_map/ppermute | solution.py:108
  122.1 2.4 %collective-permute-start.29 = (bf16[86,16,128]{2,1,0:T(8,128)(2,1)S(1)}, bf16[86,16,128]{2,1,0:T(8,128)(2,1)}, u32[]{:S(2)}, u32[]{:S(2)}) collective-permute-start(bf16[86,16,128]{2,1,0:T(8,128)(2,1)S(1)} %collective-permute-done.24.rest_4_), channel_id=1, source_target_pairs={{0,8},{1,9},{2,10},{3,11},{4,12},{5,13},{6,14},{7,15},{8,0},{9,1},... | collective-permute-start | bytes 1056776 | tf_op jit(solution)/shard_map/ppermute | solution.py:108
  124.6 24.8 %copy-start.3 = (bf16[172,16,128]{2,1,0:T(8,128)(2,1)S(1)}, bf16[172,16,128]{2,1,0:T(8,128)(2,1)}, u32[]{:S(2)}) copy-start(bf16[172,16,128]{2,1,0:T(8,128)(2,1)} %copy-done.2) | copy-start | bytes 2113540
  124.6 24.8 %copy-start.7 = (bf16[4,64,1152]{2,1,0:T(8,128)(2,1)S(1)}, bf16[4,64,1152]{2,1,0:T(8,128)(2,1)}, u32[]{:S(2)}) copy-start(bf16[4,64,1152]{2,1,0:T(8,128)(2,1)} %copy-done.6) | copy-start | bytes 1769476
  124.6 24.8 %copy-start.11 = (bf16[172,16,128]{2,1,0:T(8,128)(2,1)S(1)}, bf16[172,16,128]{2,1,0:T(8,128)(2,1)}, u32[]{:S(2)}) copy-start(bf16[172,16,128]{2,1,0:T(8,128)(2,1)} %copy-done.10) | copy-start | bytes 2113540
  124.6 24.8 %copy-start.15 = (bf16[86,16,128]{2,1,0:T(8,128)(2,1)S(1)}, bf16[86,16,128]{2,1,0:T(8,128)(2,1)}, u32[]{:S(2)}) copy-start(bf16[86,16,128]{2,1,0:T(8,128)(2,1)} %copy-done.14) | copy-start | bytes 1056772
  124.7 24.8 %copy-start.23 = (bf16[86,16,128]{2,1,0:T(8,128)(2,1)S(1)}, bf16[86,16,128]{2,1,0:T(8,128)(2,1)}, u32[]{:S(2)}) copy-start(bf16[86,16,128]{2,1,0:T(8,128)(2,1)} %copy-done.22) | copy-start | bytes 1056772
  124.7 24.8 %copy-start.25 = (bf16[86,16,128]{2,1,0:T(8,128)(2,1)S(1)}, bf16[86,16,128]{2,1,0:T(8,128)(2,1)}, u32[]{:S(2)}) copy-start(bf16[86,16,128]{2,1,0:T(8,128)(2,1)} %copy-done.24) | copy-start | bytes 1056772
  124.7 24.8 %copy-start.31 = (f32[8,128,128]{2,1,0:T(8,128)S(1)}, f32[8,128,128]{2,1,0:T(8,128)}, u32[]{:S(2)}) copy-start(f32[8,128,128]{2,1,0:T(8,128)} %get-tuple-element.27.rest_2_) | copy-start | bytes 1572868
  124.7 24.8 %copy-start.34 = (bf16[128,1792]{1,0:T(8,128)(2,1)S(1)}, bf16[128,1792]{1,0:T(8,128)(2,1)}, u32[]{:S(2)}) copy-start(bf16[128,1792]{1,0:T(8,128)(2,1)} %get-tuple-element.26.rest_1_) | copy-start | bytes 1376260
  124.7 24.8 %copy-start.36 = (bf16[128,576]{1,0:T(8,128)(2,1)S(1)}, bf16[128,576]{1,0:T(8,128)(2,1)}, u32[]{:S(2)}) copy-start(bf16[128,576]{1,0:T(8,128)(2,1)} %get-tuple-element.28.rest_3_) | copy-start | bytes 442372
  149.5 14.1 %copy-start.1 = (bf16[172,16,128]{2,1,0:T(8,128)(2,1)S(1)}, bf16[172,16,128]{2,1,0:T(8,128)(2,1)}, u32[]{:S(2)}) copy-start(bf16[172,16,128]{2,1,0:T(8,128)(2,1)} %copy-done) | copy-start | bytes 2113540
  149.5 14.1 %copy-start.5 = (bf16[172,16,128]{2,1,0:T(8,128)(2,1)S(1)}, bf16[172,16,128]{2,1,0:T(8,128)(2,1)}, u32[]{:S(2)}) copy-start(bf16[172,16,128]{2,1,0:T(8,128)(2,1)} %copy-done.4) | copy-start | bytes 2113540
  149.6 14.1 %copy-start.9 = (bf16[172,16,128]{2,1,0:T(8,128)(2,1)S(1)}, bf16[172,16,128]{2,1,0:T(8,128)(2,1)}, u32[]{:S(2)}) copy-start(bf16[172,16,128]{2,1,0:T(8,128)(2,1)} %copy-done.8) | copy-start | bytes 2113540
  157.4 1.9 %collective-permute-start.30 = (bf16[32,1280]{1,0:T(8,128)(2,1)S(1)}, bf16[32,1280]{1,0:T(8,128)(2,1)S(1)}, u32[]{:S(2)}, u32[]{:S(2)}) collective-permute-start(bf16[32,1280]{1,0:T(8,128)(2,1)S(1)} %get-tuple-element.30), channel_id=1, source_target_pairs={{0,8},{1,9},{2,10},{3,11},{4,12},{5,13},{6,14},{7,15},{8,0},{9,1},... | collective-permute-start | bytes 245768 | tf_op jit(solution)/shard_map/ppermute | solution.py:108
  157.5 5.3 %collective-permute-start.31 = (bf16[32,1280]{1,0:T(8,128)(2,1)S(1)}, bf16[32,1280]{1,0:T(8,128)(2,1)S(1)}, u32[]{:S(2)}, u32[]{:S(2)}) collective-permute-start(bf16[32,1280]{1,0:T(8,128)(2,1)S(1)} %get-tuple-element.31), channel_id=1, source_target_pairs={{0,16},{1,17},{2,18},{3,19},{4,20},{5,21},{6,22},{7,23},{8,24},{9,... | collective-permute-start | bytes 245768 | tf_op jit(solution)/shard_map/ppermute | solution.py:108
  158.6 5.1 %collective-permute-start.32 = (bf16[32,1280]{1,0:T(8,128)(2,1)S(1)}, bf16[32,1280]{1,0:T(8,128)(2,1)S(1)}, u32[]{:S(2)}, u32[]{:S(2)}) collective-permute-start(bf16[32,1280]{1,0:T(8,128)(2,1)S(1)} %get-tuple-element.32), channel_id=1, source_target_pairs={{0,24},{1,25},{2,26},{3,27},{4,28},{5,29},{6,30},{7,31},{8,16},{9,... | collective-permute-start | bytes 245768 | tf_op jit(solution)/shard_map/ppermute | solution.py:108
  (27 other events, 228.7 us)
